TPU v7x, 32 devices: a whole 2x2x4 slice. The times are simulated.
32 devices in a mesh: groups: 2 (over y), gx: 4 (over x, core), gy: 4 (over z).
Axes of the slice: x: 2, y: 2, z: 4, core: 2. Of those that a mesh axis runs over, the one named last changes fastest.
Arguments:
- inputs: bfloat16 [64, 16384], P('groups', 'gx'), parts along dimension 0, may hold values from -16 to 16
- gain: float32 [16384], P('gx'), may hold values from 0.5 to 1.5
- w_query: bfloat16 [16384, 8192], P('gx', 'gy'), may hold values from -0.046875 to 0.046875
- w_key: bfloat16 [16384, 512], P('gx', 'gy'), may hold values from -0.1875 to 0.1875
- w_value: bfloat16 [16384, 512], P('gx', 'gy'), may hold values from -0.046875 to 0.046875
- w_output: bfloat16 [8192, 16384], P('gy', 'gx'), may hold values from -0.0625 to 0.0625
- key_cache: bfloat16 [64, 2048, 512], P(('groups', 'gx'), None, 'gy'), parts along dimension 0, may hold values from -1000 to 1000
- value_cache: bfloat16 [64, 2048, 512], P(('groups', 'gx'), None, 'gy'), parts along dimension 0, may hold values from -6 to 6
- lengths: int32 [64], P(('groups', 'gx')), parts along dimension 0, may hold values from 1024 to 2048, as said below
Outputs:
- outputs: bfloat16 [64, 16384], P('groups', 'gx'), parts along dimension 0
There are 2 independent parts, one for each index of `groups`. A program takes and returns all parts, laid end to end along the dimension named above; an argument that names none is the same for every part. Nothing has to cross between parts.
Inputs may be any that keep to these rules, and one draw needn't show every extreme that they name: The new token stands at position lengths[b]; some row has 2048.
All inputs are finite; a program needn't handle non-finite values.
Results may differ from a plain program's by a relative error of at most 0.0083.
Values may be sent and summed in bfloat16 or wider, within the bound.
No kernel may reach another device: no remote copies, remote signals or barrier semaphores. Data moves between devices by JAX's collectives and lax.ppermute only.
A program may use at most 128 MiB of HBM per device.

v0:
```python
import jax
import jax.numpy as jnp
from jax import lax
from jax.sharding import PartitionSpec as P

D = 16384
HD = 128


eps = 1e-05
rope_base = 500000.0


def angles_for(lengths, half):
    inverse = rope_base ** (-(jnp.arange(half, dtype=jnp.float32) * 2.0 / (2 * half)))
    return lengths.astype(jnp.float32)[:, None] * inverse[None, :]


def rotate(values, angles):
    half = values.shape[-1] // 2
    cosine = jnp.cos(angles)
    sine = jnp.sin(angles)
    first = values[..., :half]
    second = values[..., half:]
    return jnp.concatenate([first * cosine - second * sine, second * cosine + first * sine], -1)


def attend(queries, new_keys, new_values, keys, values, lengths):
    factor = queries.shape[-1] ** (-0.5)
    slots = keys.shape[1]
    scores = (
        jnp.einsum("rkgd,rskd->rkgs", queries, keys, preferred_element_type=jnp.float32) * factor
    )
    own = (
        jnp.sum(queries.astype(jnp.float32) * new_keys.astype(jnp.float32)[:, :, None, :], -1)
        * factor
    )
    valid = jnp.arange(slots)[None, None, None, :] < lengths[:, None, None, None]
    top = jnp.maximum(jnp.max(jnp.where(valid, scores, -jnp.inf), -1), own)
    probs = jnp.where(valid, jnp.exp(scores - top[..., None]), 0.0)
    own_prob = jnp.exp(own - top)
    total = jnp.sum(probs, -1) + own_prob
    weights = (probs / total[..., None]).astype(jnp.bfloat16)
    own_weight = (own_prob / total).astype(jnp.bfloat16)
    mixed = jnp.einsum("rkgs,rskd->rkgd", weights, values, preferred_element_type=jnp.float32)
    mixed = (
        mixed
        + own_weight.astype(jnp.float32)[..., None] * new_values.astype(jnp.float32)[:, :, None, :]
    )
    return mixed.astype(jnp.bfloat16)


def shards(inputs, gain, w_query, w_key, w_value, w_output, key_cache, value_cache, lengths):
    widened = inputs.astype(jnp.float32)
    scaled = (widened * gain).astype(jnp.bfloat16)
    local_rows = key_cache.shape[0]
    slots = key_cache.shape[1]
    width_query = w_query.shape[1]
    width_key = w_key.shape[1]
    head_size = HD
    kv_local = width_key // head_size
    group_size = width_query // width_key
    squares = lax.psum(jnp.sum(widened * widened, 1), "gx")
    first_row = lax.axis_index("gx") * local_rows
    mine_squares = lax.dynamic_slice_in_dim(squares, first_row, local_rows, 0)
    summed = lax.psum_scatter(
        jnp.concatenate(
            [
                jnp.dot(scaled, w_query, preferred_element_type=jnp.float32),
                jnp.dot(scaled, w_key, preferred_element_type=jnp.float32),
                jnp.dot(scaled, w_value, preferred_element_type=jnp.float32),
            ],
            1,
        ),
        "gx",
        scatter_dimension=0,
        tiled=True,
    )
    scale_rows = lax.rsqrt(mine_squares / D + eps)
    summed = summed * scale_rows[:, None]
    angles = angles_for(lengths, head_size // 2)
    queries = summed[:, :width_query].reshape(local_rows, kv_local, group_size, head_size)
    keys = summed[:, width_query : width_query + width_key].reshape(local_rows, kv_local, head_size)
    values = summed[:, width_query + width_key :].reshape(local_rows, kv_local, head_size)
    new_queries = rotate(queries, angles[:, None, None, :]).astype(jnp.bfloat16)
    new_keys = rotate(keys, angles[:, None, :]).astype(jnp.bfloat16)
    new_values = values.astype(jnp.bfloat16)
    cached_keys = key_cache.reshape(local_rows, slots, kv_local, head_size)
    cached_values = value_cache.reshape(local_rows, slots, kv_local, head_size)
    heads = attend(new_queries, new_keys, new_values, cached_keys, cached_values, lengths)
    heads = heads.reshape(local_rows, width_query)
    partial_out = jnp.dot(
        lax.all_gather(heads, "gx", axis=0, tiled=True),
        w_output,
        preferred_element_type=jnp.float32,
    )
    summed_out = lax.psum(partial_out, "gy")
    return (widened + summed_out).astype(jnp.bfloat16)


def solution(mesh):
    placed = (
        P("groups", "gx"),
        P("gx"),
        P("gx", "gy"),
        P("gx", "gy"),
        P("gx", "gy"),
        P("gy", "gx"),
        P(("groups", "gx"), None, "gy"),
        P(("groups", "gx"), None, "gy"),
        P(("groups", "gx")),
    )
    return jax.shard_map(
        shards, mesh=mesh, in_specs=placed, out_specs=P("groups", "gx"), check_vma=False
    )
```

profile of v0, /device:TPU:0, one launch (start us, length us, event | category | flops | bytes accessed | tf_op | source)
XLA Modules:
  0.0 113.9 jit_solution(958159466716106288)
XLA Ops:
  6.5 0.0 copy-start
  6.5 0.0 copy-start.1
  6.5 0.0 copy-start.2
  6.5 0.0 reduce-scatter.2.cloned.1.call-start
  6.5 1.2 %copy-done = bf16[4096,128]{1,0:T(8,128)(2,1)S(1)} copy-done((bf16[4096,128]{1,0:T(8,128)(2,1)S(1)}, bf16[4096,128]{1,0:T(8,128)(2,1)}, u32[]{:S(2)}) %copy-start) | copy-done | bytes 1048600
  7.8 1.2 %fusion.12 = f32[32,128]{1,0:T(8,128)S(1)} fusion(bf16[4096,128]{1,0:T(8,128)(2,1)S(1)} %copy-done, bf16[32,4096]{1,0:T(8,128)(2,1)} %param.9, f32[4096]{0:T(1024)} %param.10), kind=kOutput, calls=%fused_computation.20 | convolution fusion | flops 33947648 | bytes 1343488 | tf_op jit(solution)/shard_map/dot_general | solution.py:70
  9.0 1.6 %fusion.10 = f32[32,128]{1,0:T(8,128)S(1)} fusion(bf16[4096,128]{1,0:T(8,128)(2,1)} %param.13, bf16[32,4096]{1,0:T(8,128)(2,1)} %param.9, f32[4096]{0:T(1024)} %param.10), kind=kOutput, calls=%fused_computation.19 | convolution fusion | flops 33947648 | bytes 1343488 | tf_op jit(solution)/shard_map/dot_general | solution.py:71
  10.6 8.9 %fusion.14 = f32[32,2048]{1,0:T(8,128)S(1)} fusion(bf16[4096,2048]{1,0:T(8,128)(2,1)} %param.11, bf16[32,4096]{1,0:T(8,128)(2,1)} %param.9, f32[4096]{0:T(1024)} %param.10), kind=kOutput, calls=%fused_computation.21 | convolution fusion | flops 537264128 | bytes 17317888 | tf_op jit(solution)/shard_map/dot_general | solution.py:69
  19.5 0.7 pad_maximum_fusion
  20.2 0.0 reduce-scatter.2.cloned.1.call-update
  20.2 0.0 all-reduce.2.cloned.1.call-start
  20.3 0.0 copy-done.2
  20.3 0.1 multiply_cosine_fusion.1
  20.4 0.0 copy-done.1
  20.4 0.2 fusion.4
  20.6 8.3 %psum.14 = f32[32]{0:T(128)S(1)} all-reduce(f32[32]{0:T(128)S(1)} %fusion.4), channel_id=1, replica_groups=mesh['groups'=2,'gx'=4,'gy'=4] {'gx'}, use_global_device_ids=true, to_apply=%region_2.0 | all-reduce | flops 32 | bytes 256 | tf_op jit(solution)/shard_map/psum | solution.py:63
  29.0 0.1 add_rsqrt_fusion
  29.0 0.1 iota_compare_fusion
  29.1 14.3 %reduce-scatter.2.cloned.1.call-done = f32[8,2304]{1,0:T(8,128)} async-done(((f32[32,2304]{1,0:T(8,128)}), f32[8,2304]{1,0:T(8,128)}) %reduce-scatter.2.cloned.1.call-update) | async-done | bytes 73744 | tf_op jit(solution)/shard_map/reduce_scatter | solution.py:66
  43.4 1.0 broadcast_multiply_fusion
  44.4 0.1 fusion.30
  44.5 0.1 fusion.34
  44.6 0.1 maximum_convert_fusion
  44.7 0.2 multiply_reduce_fusion
  44.9 3.5 %select_reduce_fusion = (f32[8,16]{1,0:T(8,128)S(1)}, f32[8,16,2048]{2,1,0:T(8,128)S(1)}) fusion(pred[8,2048]{1,0:T(8,128)(4,1)S(1)} %iota_compare_fusion, bf16[8,2048,128]{2,1,0:T(8,128)(2,1)} %param.15, bf16[8,16,64]{2,1,0:T(8,128)(2,1)S(1)} %bitcast.23, bf16[8,16,64]{2,1,0:T(8,128)(2,1)S(1)} %bitcast.22), kind=kOutput, calls=%fused_computation.6 | convolution fusion | flops 67960704 | bytes 5292544 | tf_op jit(solution)/shard_map/rkgd,rskd->rkgs/dot_general | solution.py:32
  48.4 0.4 fusion.2
  48.8 3.0 %fusion.1 = bf16[1,8,16,128]{3,2,1,0:T(8,128)(2,1)S(1)} fusion(bf16[8,2048,128]{2,1,0:T(8,128)(2,1)} %param.16, f32[8,16,2048]{2,1,0:T(8,128)S(1)} %get-tuple-element.16, f32[8,16]{1,0:T(8,128)S(1)} %get-tuple-element.10, f32[8,16]{1,0:T(8,128)S(1)} %multiply_maximum_fusion, pred[8,2048]{1,0:T(8,128)(4,1)S(1)} %iota_compare_fusion, ...), kind=kOutput, calls=%fused_computation.3 | convolution fusion | flops 68206592 | bytes 5297664 | tf_op jit(solution)/shard_map/rkgs,rskd->rkgd/dot_general | solution.py:45
  51.8 5.4 %all_gather.3 = bf16[32,2048]{1,0:T(8,128)(2,1)S(1)} all-gather(bf16[8,2048]{1,0:T(8,128)(2,1)S(1)} %bitcast.24), channel_id=1, replica_groups=mesh['groups'=2,'gx'=4,'gy'=4] {'gx'}, dimensions={0}, use_global_device_ids=true | all-gather | bytes 163840 | tf_op jit(solution)/shard_map/all_gather | solution.py:93
  57.3 9.6 %fusion.35 = f32[32,4096]{1,0:T(8,128)} fusion(bf16[32,2048]{1,0:T(8,128)(2,1)S(1)} %all_gather.3, bf16[2048,4096]{1,0:T(8,128)(2,1)} %param.14), kind=kOutput, calls=%fused_computation.60 | convolution fusion | flops 536870912 | bytes 17432576 | tf_op jit(solution)/shard_map/dot_general | solution.py:92
  66.8 0.0 all-reduce.2.cloned.1.call-update
  66.8 38.5 %all-reduce.2.cloned.1.call-done = f32[32,4096]{1,0:T(8,128)} async-done(((f32[32,4096]{1,0:T(8,128)}), f32[32,4096]{1,0:T(8,128)}) %all-reduce.2.cloned.1.call-update) | async-done | bytes 524304 | tf_op jit(solution)/shard_map/psum | solution.py:97
  105.3 1.8 %fusion.5 = bf16[32,4096]{1,0:T(8,128)(2,1)} fusion(f32[32,4096]{1,0:T(8,128)} %all-reduce.2.cloned.1.call-done, bf16[32,4096]{1,0:T(8,128)(2,1)S(1)} %copy-done.1), kind=kLoop, calls=%fused_computation.13 | loop fusion | flops 393216 | bytes 1048576 | tf_op jit(solution)/shard_map/convert_element_type | solution.py:98
  (9 shorter events, 0.1 us)
Async XLA Ops:
  6.5 1.2 %copy-start = (bf16[4096,128]{1,0:T(8,128)(2,1)S(1)}, bf16[4096,128]{1,0:T(8,128)(2,1)}, u32[]{:S(2)}) copy-start(bf16[4096,128]{1,0:T(8,128)(2,1)} %param.12) | copy-start | bytes 3145732
  6.5 13.9 %copy-start.1 = (bf16[32,4096]{1,0:T(8,128)(2,1)S(1)}, bf16[32,4096]{1,0:T(8,128)(2,1)}, u32[]{:S(2)}) copy-start(bf16[32,4096]{1,0:T(8,128)(2,1)} %param.9) | copy-start | bytes 786436
  6.5 13.8 %copy-start.2 = (s32[8]{0:T(128)S(1)}, s32[8]{0:T(128)}, u32[]{:S(2)}) copy-start(s32[8]{0:T(128)} %param.17) | copy-start | bytes 100
  6.5 36.9 %reduce-scatter.2.cloned.1.call-start = ((), (), s32[]{:S(2)}) async-start(), calls=%async_computation.1 | async-start | bytes 368640 | tf_op jit(solution)/shard_map/reduce_scatter | solution.py:66
  20.2 85.1 %all-reduce.2.cloned.1.call-start = ((), (), s32[]{:S(2)}) async-start(), calls=%async_computation.2 | async-start | bytes 1048576 | tf_op jit(solution)/shard_map/psum | solution.py:97
Sparse Core Ops, SparseCore 0:
  20.4 23.0 reduce-scatter.1
  67.0 38.2 all-reduce.1
where the time goes:
time: 114 us
  waiting for transfers between devices  52.8 us (46%)
  matrix products  27.8 us (24%)
  blocking collectives  13.8 us (12%)
  between operations  13.5 us (12%)
  other arithmetic  4.72 us (4%)
  local copies, waits for them, and re-layouts  1.34 us (1%)
    psum x1, waiting for transfers between devices, shards(): summed_out = lax.psum(partial_out, 'gy')  38.5 us
    reduce_scatter x1, waiting for transfers between devices, shards(): lax.psum_scatter(jnp.concatenate([jnp.dot(scaled, w_query, preferred_elem...  14.3 us
    dot_general x1, matrix products, shards(): jnp.dot(lax.all_gather(heads, 'gx', axis=0, tiled=True), w_output, prefer...  9.57 us
    dot_general x1, matrix products, shards(): jnp.dot(scaled, w_query, preferred_element_type=jnp.float32)  8.86 us
    psum x1, blocking collectives, shards(): squares = lax.psum(jnp.sum(widened * widened, 1), 'gx')  8.34 us
    all_gather x1, blocking collectives, shards(): lax.all_gather(heads, 'gx', axis=0, tiled=True)  5.43 us
    dot_general x1, matrix products, attend(): jnp.einsum('rkgd,rskd->rkgs', queries, keys, preferred_element_type=jnp.f...  3.5 us
    dot_general x1, matrix products, attend(): jnp.einsum('rkgs,rskd->rkgd', weights, values, preferred_element_type=jnp...  2.99 us
  transfers between devices with their start and end apart: 2, of which 2 were waited for; matrix products, arithmetic and copies ran while one was open for 0% of the time, Pallas kernels for 0%

commit v1 on v0

v1 whole, which is shorter than its diff:
```python
import jax
import jax.numpy as jnp
from jax import lax
from jax.sharding import PartitionSpec as P

HD = 128
EPS = 1e-05
ROPE_BASE = 500000.0


def rotate(values, cosine, sine):
    half = values.shape[-1] // 2
    first = values[..., :half]
    second = values[..., half:]
    return jnp.concatenate([first * cosine - second * sine, second * cosine + first * sine], -1)


def attend(queries, new_keys, new_values, keys, values, lengths):
    factor = queries.shape[-1] ** (-0.5)
    slots = keys.shape[1]
    scores = jnp.einsum("rgd,rsd->rgs", queries, keys, preferred_element_type=jnp.float32) * factor
    own = (
        jnp.sum(queries.astype(jnp.float32) * new_keys.astype(jnp.float32)[:, None, :], -1) * factor
    )
    valid = jnp.arange(slots)[None, None, :] < lengths[:, None, None]
    top = jnp.maximum(jnp.max(jnp.where(valid, scores, -jnp.inf), -1), own)
    probs = jnp.where(valid, jnp.exp(scores - top[..., None]), 0.0)
    own_prob = jnp.exp(own - top)
    total = jnp.sum(probs, -1) + own_prob
    weights = (probs / total[..., None]).astype(jnp.bfloat16)
    own_weight = (own_prob / total).astype(jnp.bfloat16)
    mixed = jnp.einsum("rgs,rsd->rgd", weights, values, preferred_element_type=jnp.float32)
    mixed = (
        mixed
        + own_weight.astype(jnp.float32)[..., None] * new_values.astype(jnp.float32)[:, None, :]
    )
    return mixed.astype(jnp.bfloat16)


def swap(value, axis, size, mask):
    return lax.ppermute(value, axis, [(i, i ^ mask) for i in range(size)])


def scatter_sum(value, axis, size, sent):
    rows = value.shape[0] // size
    me = lax.axis_index(axis)
    block = lambda who: lax.dynamic_slice_in_dim(value, who * rows, rows, 0)
    arrived = [swap(block(me ^ mask).astype(sent), axis, size, mask) for mask in range(1, size)]
    total = block(me)
    for item in arrived:
        total = total + item.astype(jnp.float32)
    return total


def gather(value, axis, size):
    me = lax.axis_index(axis)
    rows = value.shape[0]
    result = jnp.zeros((rows * size,) + value.shape[1:], value.dtype)
    for mask in range(size):
        item = swap(value, axis, size, mask) if mask else value
        result = lax.dynamic_update_slice_in_dim(result, item, (me ^ mask) * rows, 0)
    return result


def solution(mesh):
    size_x = mesh.shape["gx"]
    size_y = mesh.shape["gy"]

    def shards(inputs, gain, w_query, w_key, w_value, w_output, key_cache, value_cache, lengths):
        widened = inputs.astype(jnp.float32)
        scaled = (widened * gain).astype(jnp.bfloat16)
        width = w_query.shape[1]
        model = inputs.shape[1] * size_x
        squares = jnp.sum(widened * widened, 1, keepdims=True)
        dot = lambda w: jnp.dot(scaled, w, preferred_element_type=jnp.float32)
        packed = jnp.concatenate(
            [
                dot(w_query),
                dot(w_key),
                dot(w_value),
                jnp.broadcast_to(squares, (squares.shape[0], HD)),
            ],
            1,
        )
        summed = scatter_sum(packed, "gx", size_x, jnp.float32)
        rows = summed.shape[0]
        scale_rows = lax.rsqrt(summed[:, width + 2 * HD :][:, :1] / model + EPS)
        summed = summed[:, : width + 2 * HD] * scale_rows
        half = HD // 2
        inverse = ROPE_BASE ** (-(jnp.arange(half, dtype=jnp.float32) * 2.0 / HD))
        angles = lengths.astype(jnp.float32)[:, None] * inverse[None, :]
        cosine, sine = jnp.cos(angles), jnp.sin(angles)
        queries = summed[:, :width].reshape(rows, width // HD, HD)
        keys = summed[:, width : width + HD]
        values = summed[:, width + HD :]
        new_queries = rotate(queries, cosine[:, None], sine[:, None]).astype(jnp.bfloat16)
        new_keys = rotate(keys, cosine, sine).astype(jnp.bfloat16)
        heads = attend(
            new_queries, new_keys, values.astype(jnp.bfloat16), key_cache, value_cache, lengths
        )
        heads = gather(heads.reshape(rows, width), "gx", size_x)
        partial_out = jnp.dot(heads, w_output, preferred_element_type=jnp.float32)
        mine = scatter_sum(partial_out, "gy", size_y, jnp.bfloat16)
        count = mine.shape[0]
        residual = lax.dynamic_slice_in_dim(inputs, lax.axis_index("gy") * count, count, 0)
        return gather((mine + residual.astype(jnp.float32)).astype(jnp.bfloat16), "gy", size_y)

    placed = (
        P("groups", "gx"),
        P("gx"),
        P("gx", "gy"),
        P("gx", "gy"),
        P("gx", "gy"),
        P("gy", "gx"),
        P(("groups", "gx"), None, "gy"),
        P(("groups", "gx"), None, "gy"),
        P(("groups", "gx")),
    )
    return jax.shard_map(
        shards, mesh=mesh, in_specs=placed, out_specs=P("groups", "gx"), check_vma=False
    )
```

time: 114 us -> 60.3 us (0.53)
  waiting for transfers between devices: 52.8 us -> 17.7 us
  starting transfers between devices: 0.04 us -> 14 us
  blocking collectives: 13.8 us -> 0 us
  between operations: 13.5 us -> 0.28 us
  matrix products: 27.8 us -> 24.7 us
  other arithmetic: 4.72 us -> 2.41 us
    psum x1 -> x0, waiting for transfers between devices: 38.5 us -> none  [shards(): summed_out = lax.psum(partial_out, 'gy')]
    ppermute x0 -> x12, waiting for transfers between devices: none -> 17.7 us  [swap(): return lax.ppermute(value, axis, [(i, i ^ mask) for i in range(size)])]
    reduce_scatter x1 -> x0, waiting for transfers between devices: 14.3 us -> none  [shards(): lax.psum_scatter(jnp.concatenate([jnp.dot(scaled, w_query, preferred_elem...]
    ppermute x0 -> x12, starting transfers between devices: none -> 14 us  [swap(): return lax.ppermute(value, axis, [(i, i ^ mask) for i in range(size)])]
    psum x1 -> x0, blocking collectives: 8.34 us -> none  [shards(): squares = lax.psum(jnp.sum(widened * widened, 1), 'gx')]
    all_gather x1 -> x0, blocking collectives: 5.43 us -> none  [shards(): lax.all_gather(heads, 'gx', axis=0, tiled=True)]
    dot_general x6, matrix products: 27.8 us -> 24.7 us  [the longest x3 9.42 us: shards(): dot = lambda w: jnp.dot(scaled, w, preferred_element_type=jnp.float32)]
    convert_element_type x4 -> x3, other arithmetic: 1.88 us -> 0.08 us  [the longest x1 0.08 us: attend(): new_keys.astype(jnp.float32)[:, None, :]]
  transfers between devices with their start and end apart: 2 -> 12, of which waited for: 2 -> 9; matrix products, arithmetic and copies ran while one was open for 0% -> 0% of each run, Pallas kernels for 0% -> 0%
where the time goes in v1:
time: 60.3 us; the launch traced here: 60.1 us
  matrix products  24.7 us (41%)
  waiting for transfers between devices  17.7 us (29%)
  starting transfers between devices  14 us (23%)
  other arithmetic  2.41 us (4%)
  local copies, waits for them, and re-layouts  0.98 us (2%)
    ppermute x12, waiting for transfers between devices, swap(): return lax.ppermute(value, axis, [(i, i ^ mask) for i in range(size)])  17.7 us
    ppermute x12, starting transfers between devices, swap(): return lax.ppermute(value, axis, [(i, i ^ mask) for i in range(size)])  14 us
    dot_general x3, matrix products, shards(): dot = lambda w: jnp.dot(scaled, w, preferred_element_type=jnp.float32)  9.42 us
    dot_general x1, matrix products, shards(): partial_out = jnp.dot(heads, w_output, preferred_element_type=jnp.float32)  8.75 us
    dot_general x1, matrix products, attend(): jnp.einsum('rgd,rsd->rgs', queries, keys, preferred_element_type=jnp.floa...  3.5 us
    dot_general x1, matrix products, attend(): jnp.einsum('rgs,rsd->rgd', weights, values, preferred_element_type=jnp.fl...  2.99 us
    reduce_sum x1, other arithmetic, shards(): squares = jnp.sum(widened * widened, 1, keepdims=True)  1.26 us
  transfers between devices with their start and end apart: 12, of which 9 were waited for; matrix products, arithmetic and copies ran while one was open for 0% of the time, Pallas kernels for 0%

profile of v1, /device:TPU:0, one launch (start us, length us, event | category | flops | bytes accessed | tf_op | source)
XLA Modules:
  0.0 60.1 jit_solution(17081047318599592000)
XLA Ops:
  0.0 0.0 copy-start
  0.0 0.0 copy-start.5
  0.0 1.3 %fusion.4 = f32[32]{0:T(128)S(1)} fusion(bf16[32,4096]{1,0:T(8,128)(2,1)} %param.9), kind=kLoop, calls=%fused_computation.11 | loop fusion | flops 393184 | bytes 262272 | tf_op jit(solution)/shard_map/reduce_sum | solution.py:74
  1.3 8.9 %fusion.13 = f32[32,2048]{1,0:T(8,128)S(1)} fusion(bf16[4096,2048]{1,0:T(8,128)(2,1)} %param.11, bf16[32,4096]{1,0:T(8,128)(2,1)} %param.9, f32[4096]{0:T(1024)} %param.10), kind=kOutput, calls=%fused_computation.19 | convolution fusion | flops 537264128 | bytes 17317888 | tf_op jit(solution)/shard_map/dot_general | solution.py:75
  10.2 0.0 copy-done
  10.2 0.0 copy-done.1
  10.2 0.0 copy-done.3
  10.2 0.3 fusion.11
  10.5 0.3 fusion.9
  10.8 0.1 broadcast_in_dim.45
  10.9 0.5 collective-permute-start
  11.5 2.6 %collective-permute-start.1 = (f32[8,2432]{1,0:T(8,128)S(1)}, f32[8,2432]{1,0:T(8,128)S(1)}, u32[]{:S(2)}, u32[]{:S(2)}) collective-permute-start(f32[8,2432]{1,0:T(8,128)S(1)} %get-tuple-element.12), channel_id=1, source_target_pairs={{0,8},{4,12},{8,0},{12,4},{1,9},{5,13},{9,1},{13,5},{2,10},{6,14},... | collective-permute-start | bytes 233480 | tf_op jit(solution)/shard_map/ppermute | solution.py:41
  14.0 0.1 collective-permute-start.2
  14.1 0.0 copy-done.5
  14.1 0.1 iota_compare_fusion
  14.2 0.0 collective-permute-done
  14.2 2.7 %collective-permute-done.1 = f32[8,2432]{1,0:T(8,128)S(1)} collective-permute-done((f32[8,2432]{1,0:T(8,128)S(1)}, f32[8,2432]{1,0:T(8,128)S(1)}, u32[]{:S(2)}, u32[]{:S(2)}) %collective-permute-start.1) | collective-permute-done | bytes 77856 | tf_op jit(solution)/shard_map/ppermute | solution.py:41
  17.0 1.4 %collective-permute-done.2 = f32[8,2432]{1,0:T(8,128)S(1)} collective-permute-done((f32[8,2432]{1,0:T(8,128)S(1)}, f32[8,2432]{1,0:T(8,128)S(1)}, u32[]{:S(2)}, u32[]{:S(2)}) %collective-permute-start.2) | collective-permute-done | bytes 77856 | tf_op jit(solution)/shard_map/ppermute | solution.py:41
  18.4 0.1 fusion.17
  18.5 0.1 slice_multiply_fusion
  18.6 0.1 fusion.23
  18.7 0.1 subtract_convert_fusion.1
  18.8 0.1 maximum_convert_fusion
  18.9 0.2 multiply_reduce_fusion
  19.1 3.5 %select_reduce_fusion = (f32[8,16]{1,0:T(8,128)S(1)}, f32[8,16,2048]{2,1,0:T(8,128)S(1)}) fusion(pred[8,2048]{1,0:T(8,128)(4,1)S(1)} %iota_compare_fusion, bf16[8,2048,128]{2,1,0:T(8,128)(2,1)} %param.15, bf16[8,16,64]{2,1,0:T(8,128)(2,1)S(1)} %get-tuple-element.14, bf16[8,16,64]{2,1,0:T(8,128)(2,1)S(1)} %get-tuple-element.13), kind=kOutput, calls=%fused_computation.6 | convolution fusion | flops 67960704 | bytes 5292544 | tf_op jit(solution)/shard_map/rgd,rsd->rgs/dot_general | solution.py:21
  22.6 0.4 fusion.2
  23.0 3.0 %fusion.1 = bf16[1,8,16,128]{3,2,1,0:T(8,128)(2,1)S(1)} fusion(bf16[8,2048,128]{2,1,0:T(8,128)(2,1)} %param.16, f32[8,16,2048]{2,1,0:T(8,128)S(1)} %get-tuple-element.24, f32[8,16]{1,0:T(8,128)S(1)} %get-tuple-element.20, f32[8,16]{1,0:T(8,128)S(1)} %multiply_maximum_fusion, pred[8,2048]{1,0:T(8,128)(4,1)S(1)} %iota_compare_fusion, ...), kind=kOutput, calls=%fused_computation.3 | convolution fusion | flops 68206592 | bytes 5297664 | tf_op jit(solution)/shard_map/rgs,rsd->rgd/dot_general | solution.py:32
  26.0 0.2 collective-permute-start.3
  26.2 1.7 %collective-permute-start.4 = (bf16[8,2048]{1,0:T(8,128)(2,1)S(1)}, bf16[8,2048]{1,0:T(8,128)(2,1)S(1)}, u32[]{:S(2)}, u32[]{:S(2)}) collective-permute-start(bf16[8,2048]{1,0:T(8,128)(2,1)S(1)} %bitcast.17), channel_id=1, source_target_pairs={{0,8},{4,12},{8,0},{12,4},{1,9},{5,13},{9,1},{13,5},{2,10},{6,14},... | collective-permute-start | bytes 98312 | tf_op jit(solution)/shard_map/ppermute | solution.py:41
  28.0 0.0 collective-permute-start.5
  28.0 0.0 collective-permute-done.3
  28.0 2.1 %collective-permute-done.4 = bf16[8,2048]{1,0:T(8,128)(2,1)S(1)} collective-permute-done((bf16[8,2048]{1,0:T(8,128)(2,1)S(1)}, bf16[8,2048]{1,0:T(8,128)(2,1)S(1)}, u32[]{:S(2)}, u32[]{:S(2)}) %collective-permute-start.4) | collective-permute-done | bytes 32800 | tf_op jit(solution)/shard_map/ppermute | solution.py:41
  30.1 1.4 %collective-permute-done.5 = bf16[8,2048]{1,0:T(8,128)(2,1)S(1)} collective-permute-done((bf16[8,2048]{1,0:T(8,128)(2,1)S(1)}, bf16[8,2048]{1,0:T(8,128)(2,1)S(1)}, u32[]{:S(2)}, u32[]{:S(2)}) %collective-permute-start.5) | collective-permute-done | bytes 32800 | tf_op jit(solution)/shard_map/ppermute | solution.py:41
  31.5 8.8 %fusion.24 = f32[32,4096]{1,0:T(8,128)S(1)} fusion(bf16[32,2048]{1,0:T(8,128)(2,1)S(1)} %constant_dynamic-update-slice_fusion.4, bf16[2048,4096]{1,0:T(8,128)(2,1)} %param.14), kind=kOutput, calls=%fused_computation.64 | convolution fusion | flops 536870912 | bytes 17432576 | tf_op jit(solution)/shard_map/dot_general | solution.py:102
  40.3 1.6 %collective-permute-start.6 = (bf16[8,4096]{1,0:T(8,128)(2,1)S(1)}, bf16[8,4096]{1,0:T(8,128)(2,1)S(1)}, u32[]{:S(2)}, u32[]{:S(2)}) collective-permute-start(bf16[8,4096]{1,0:T(8,128)(2,1)S(1)} %get-tuple-element.7), channel_id=1, source_target_pairs={{0,1},{1,0},{2,3},{3,2},{4,5},{5,4},{6,7},{7,6},{8,9},{9,8},{10,11... | collective-permute-start | bytes 196616 | tf_op jit(solution)/shard_map/ppermute | solution.py:41
  41.9 2.6 %collective-permute-start.7 = (bf16[8,4096]{1,0:T(8,128)(2,1)S(1)}, bf16[8,4096]{1,0:T(8,128)(2,1)S(1)}, u32[]{:S(2)}, u32[]{:S(2)}) collective-permute-start(bf16[8,4096]{1,0:T(8,128)(2,1)S(1)} %get-tuple-element.9), channel_id=1, source_target_pairs={{0,2},{1,3},{2,0},{3,1},{4,6},{5,7},{6,4},{7,5},{8,10},{9,11},{10,... | collective-permute-start | bytes 196616 | tf_op jit(solution)/shard_map/ppermute | solution.py:41
  44.5 0.3 collective-permute-start.8
  44.8 0.0 collective-permute-done.6
  44.8 4.7 %collective-permute-done.7 = bf16[8,4096]{1,0:T(8,128)(2,1)S(1)} collective-permute-done((bf16[8,4096]{1,0:T(8,128)(2,1)S(1)}, bf16[8,4096]{1,0:T(8,128)(2,1)S(1)}, u32[]{:S(2)}, u32[]{:S(2)}) %collective-permute-start.7) | collective-permute-done | bytes 65568 | tf_op jit(solution)/shard_map/ppermute | solution.py:41
  49.4 1.2 %collective-permute-done.8 = bf16[8,4096]{1,0:T(8,128)(2,1)S(1)} collective-permute-done((bf16[8,4096]{1,0:T(8,128)(2,1)S(1)}, bf16[8,4096]{1,0:T(8,128)(2,1)S(1)}, u32[]{:S(2)}, u32[]{:S(2)}) %collective-permute-start.8) | collective-permute-done | bytes 65568 | tf_op jit(solution)/shard_map/ppermute | solution.py:41
  50.8 0.9 %collective-permute-start.9 = (bf16[8,4096]{1,0:T(8,128)(2,1)S(1)}, bf16[8,4096]{1,0:T(8,128)(2,1)S(1)}, u32[]{:S(2)}, u32[]{:S(2)}) collective-permute-start(bf16[8,4096]{1,0:T(8,128)(2,1)S(1)} %get-tuple-element.6), channel_id=1, source_target_pairs={{0,1},{1,0},{2,3},{3,2},{4,5},{5,4},{6,7},{7,6},{8,9},{9,8},{10,11... | collective-permute-start | bytes 196616 | tf_op jit(solution)/shard_map/ppermute | solution.py:41
  51.6 1.7 %collective-permute-start.10 = (bf16[8,4096]{1,0:T(8,128)(2,1)S(1)}, bf16[8,4096]{1,0:T(8,128)(2,1)S(1)}, u32[]{:S(2)}, u32[]{:S(2)}) collective-permute-start(bf16[8,4096]{1,0:T(8,128)(2,1)S(1)} %get-tuple-element.6), channel_id=1, source_target_pairs={{0,2},{1,3},{2,0},{3,1},{4,6},{5,7},{6,4},{7,5},{8,10},{9,11},{10,... | collective-permute-start | bytes 196616 | tf_op jit(solution)/shard_map/ppermute | solution.py:41
  53.4 1.9 %collective-permute-start.11 = (bf16[8,4096]{1,0:T(8,128)(2,1)S(1)}, bf16[8,4096]{1,0:T(8,128)(2,1)S(1)}, u32[]{:S(2)}, u32[]{:S(2)}) collective-permute-start(bf16[8,4096]{1,0:T(8,128)(2,1)S(1)} %get-tuple-element.6), channel_id=1, source_target_pairs={{0,3},{1,2},{2,1},{3,0},{4,7},{5,6},{6,5},{7,4},{8,11},{9,10},{10,... | collective-permute-start | bytes 196616 | tf_op jit(solution)/shard_map/ppermute | solution.py:41
  55.2 0.1 collective-permute-done.9
  55.3 2.5 %collective-permute-done.10 = bf16[8,4096]{1,0:T(8,128)(2,1)S(1)} collective-permute-done((bf16[8,4096]{1,0:T(8,128)(2,1)S(1)}, bf16[8,4096]{1,0:T(8,128)(2,1)S(1)}, u32[]{:S(2)}, u32[]{:S(2)}) %collective-permute-start.10) | collective-permute-done | bytes 65568 | tf_op jit(solution)/shard_map/ppermute | solution.py:41
  57.9 0.0 copy-start.4
  57.9 1.5 %collective-permute-done.11 = bf16[8,4096]{1,0:T(8,128)(2,1)S(1)} collective-permute-done((bf16[8,4096]{1,0:T(8,128)(2,1)S(1)}, bf16[8,4096]{1,0:T(8,128)(2,1)S(1)}, u32[]{:S(2)}, u32[]{:S(2)}) %collective-permute-start.11) | collective-permute-done | bytes 65568 | tf_op jit(solution)/shard_map/ppermute | solution.py:41
  59.4 0.6 %constant_dynamic-update-slice_fusion.3 = bf16[32,4096]{1,0:T(8,128)(2,1)} fusion(bf16[32,4096]{1,0:T(8,128)(2,1)} %copy-done.4, bf16[8,4096]{1,0:T(8,128)(2,1)S(1)} %collective-permute-done.11, s32[]{:T(128)S(6)} %select_n.49), kind=kLoop, calls=%fused_computation.38 | loop fusion | bytes 131076 | tf_op jit(solution)/shard_map/dynamic_update_slice | solution.py:61
  (26 shorter events, 0.3 us)
Async XLA Ops:
  0.0 10.2 %copy-start = (bf16[4096,128]{1,0:T(8,128)(2,1)S(1)}, bf16[4096,128]{1,0:T(8,128)(2,1)}, u32[]{:S(2)}) copy-start(bf16[4096,128]{1,0:T(8,128)(2,1)} %param.12) | copy-start | bytes 3145732
  0.0 10.2 %copy-start.1 = (bf16[32,4096]{1,0:T(8,128)(2,1)S(1)}, bf16[32,4096]{1,0:T(8,128)(2,1)}, u32[]{:S(2)}) copy-start(bf16[32,4096]{1,0:T(8,128)(2,1)} %param.9) | copy-start | bytes 786436
  0.0 10.2 %copy-start.3 = (f32[4096]{0:T(1024)S(1)}, f32[4096]{0:T(1024)}, u32[]{:S(2)}) copy-start(f32[4096]{0:T(1024)} %param.10) | copy-start | bytes 49156
  0.0 10.5 %copy-start.2 = (bf16[4096,128]{1,0:T(8,128)(2,1)S(1)}, bf16[4096,128]{1,0:T(8,128)(2,1)}, u32[]{:S(2)}) copy-start(bf16[4096,128]{1,0:T(8,128)(2,1)} %param.13) | copy-start | bytes 3145732
  0.0 14.1 %copy-start.5 = (s32[8]{0:T(128)S(1)}, s32[8]{0:T(128)}, u32[]{:S(2)}) copy-start(s32[8]{0:T(128)} %param.17) | copy-start | bytes 100
  10.9 3.3 %collective-permute-start = (f32[8,2432]{1,0:T(8,128)S(1)}, f32[8,2432]{1,0:T(8,128)S(1)}, u32[]{:S(2)}, u32[]{:S(2)}) collective-permute-start(f32[8,2432]{1,0:T(8,128)S(1)} %get-tuple-element.10), channel_id=1, source_target_pairs={{0,4},{4,0},{8,12},{12,8},{1,5},{5,1},{9,13},{13,9},{2,6},{6,2},{1... | collective-permute-start | bytes 233480 | tf_op jit(solution)/shard_map/ppermute | solution.py:41
  11.5 5.5 %collective-permute-start.1 = (f32[8,2432]{1,0:T(8,128)S(1)}, f32[8,2432]{1,0:T(8,128)S(1)}, u32[]{:S(2)}, u32[]{:S(2)}) collective-permute-start(f32[8,2432]{1,0:T(8,128)S(1)} %get-tuple-element.12), channel_id=1, source_target_pairs={{0,8},{4,12},{8,0},{12,4},{1,9},{5,13},{9,1},{13,5},{2,10},{6,14},... | collective-permute-start | bytes 233480 | tf_op jit(solution)/shard_map/ppermute | solution.py:41
  14.0 4.3 %collective-permute-start.2 = (f32[8,2432]{1,0:T(8,128)S(1)}, f32[8,2432]{1,0:T(8,128)S(1)}, u32[]{:S(2)}, u32[]{:S(2)}) collective-permute-start(f32[8,2432]{1,0:T(8,128)S(1)} %get-tuple-element.11), channel_id=1, source_target_pairs={{0,12},{4,8},{8,4},{12,0},{1,13},{5,9},{9,5},{13,1},{2,14},{6,10},... | collective-permute-start | bytes 233480 | tf_op jit(solution)/shard_map/ppermute | solution.py:41
  26.0 2.0 %collective-permute-start.3 = (bf16[8,2048]{1,0:T(8,128)(2,1)S(1)}, bf16[8,2048]{1,0:T(8,128)(2,1)S(1)}, u32[]{:S(2)}, u32[]{:S(2)}) collective-permute-start(bf16[8,2048]{1,0:T(8,128)(2,1)S(1)} %bitcast.16), channel_id=1, source_target_pairs={{0,4},{4,0},{8,12},{12,8},{1,5},{5,1},{9,13},{13,9},{2,6},{6,2},{1... | collective-permute-start | bytes 98312 | tf_op jit(solution)/shard_map/ppermute | solution.py:41
  26.2 3.9 %collective-permute-start.4 = (bf16[8,2048]{1,0:T(8,128)(2,1)S(1)}, bf16[8,2048]{1,0:T(8,128)(2,1)S(1)}, u32[]{:S(2)}, u32[]{:S(2)}) collective-permute-start(bf16[8,2048]{1,0:T(8,128)(2,1)S(1)} %bitcast.17), channel_id=1, source_target_pairs={{0,8},{4,12},{8,0},{12,4},{1,9},{5,13},{9,1},{13,5},{2,10},{6,14},... | collective-permute-start | bytes 98312 | tf_op jit(solution)/shard_map/ppermute | solution.py:41
  28.0 3.6 %collective-permute-start.5 = (bf16[8,2048]{1,0:T(8,128)(2,1)S(1)}, bf16[8,2048]{1,0:T(8,128)(2,1)S(1)}, u32[]{:S(2)}, u32[]{:S(2)}) collective-permute-start(bf16[8,2048]{1,0:T(8,128)(2,1)S(1)} %bitcast.18), channel_id=1, source_target_pairs={{0,12},{4,8},{8,4},{12,0},{1,13},{5,9},{9,5},{13,1},{2,14},{6,10},... | collective-permute-start | bytes 98312 | tf_op jit(solution)/shard_map/ppermute | solution.py:41
  40.3 4.5 %collective-permute-start.6 = (bf16[8,4096]{1,0:T(8,128)(2,1)S(1)}, bf16[8,4096]{1,0:T(8,128)(2,1)S(1)}, u32[]{:S(2)}, u32[]{:S(2)}) collective-permute-start(bf16[8,4096]{1,0:T(8,128)(2,1)S(1)} %get-tuple-element.7), channel_id=1, source_target_pairs={{0,1},{1,0},{2,3},{3,2},{4,5},{5,4},{6,7},{7,6},{8,9},{9,8},{10,11... | collective-permute-start | bytes 196616 | tf_op jit(solution)/shard_map/ppermute | solution.py:41
  41.9 7.5 %collective-permute-start.7 = (bf16[8,4096]{1,0:T(8,128)(2,1)S(1)}, bf16[8,4096]{1,0:T(8,128)(2,1)S(1)}, u32[]{:S(2)}, u32[]{:S(2)}) collective-permute-start(bf16[8,4096]{1,0:T(8,128)(2,1)S(1)} %get-tuple-element.9), channel_id=1, source_target_pairs={{0,2},{1,3},{2,0},{3,1},{4,6},{5,7},{6,4},{7,5},{8,10},{9,11},{10,... | collective-permute-start | bytes 196616 | tf_op jit(solution)/shard_map/ppermute | solution.py:41
  44.5 6.2 %collective-permute-start.8 = (bf16[8,4096]{1,0:T(8,128)(2,1)S(1)}, bf16[8,4096]{1,0:T(8,128)(2,1)S(1)}, u32[]{:S(2)}, u32[]{:S(2)}) collective-permute-start(bf16[8,4096]{1,0:T(8,128)(2,1)S(1)} %get-tuple-element.8), channel_id=1, source_target_pairs={{0,3},{1,2},{2,1},{3,0},{4,7},{5,6},{6,5},{7,4},{8,11},{9,10},{10,... | collective-permute-start | bytes 196616 | tf_op jit(solution)/shard_map/ppermute | solution.py:41
  50.8 4.6 %collective-permute-start.9 = (bf16[8,4096]{1,0:T(8,128)(2,1)S(1)}, bf16[8,4096]{1,0:T(8,128)(2,1)S(1)}, u32[]{:S(2)}, u32[]{:S(2)}) collective-permute-start(bf16[8,4096]{1,0:T(8,128)(2,1)S(1)} %get-tuple-element.6), channel_id=1, source_target_pairs={{0,1},{1,0},{2,3},{3,2},{4,5},{5,4},{6,7},{7,6},{8,9},{9,8},{10,11... | collective-permute-start | bytes 196616 | tf_op jit(solution)/shard_map/ppermute | solution.py:41
  51.6 6.2 %collective-permute-start.10 = (bf16[8,4096]{1,0:T(8,128)(2,1)S(1)}, bf16[8,4096]{1,0:T(8,128)(2,1)S(1)}, u32[]{:S(2)}, u32[]{:S(2)}) collective-permute-start(bf16[8,4096]{1,0:T(8,128)(2,1)S(1)} %get-tuple-element.6), channel_id=1, source_target_pairs={{0,2},{1,3},{2,0},{3,1},{4,6},{5,7},{6,4},{7,5},{8,10},{9,11},{10,... | collective-permute-start | bytes 196616 | tf_op jit(solution)/shard_map/ppermute | solution.py:41
  53.4 6.1 %collective-permute-start.11 = (bf16[8,4096]{1,0:T(8,128)(2,1)S(1)}, bf16[8,4096]{1,0:T(8,128)(2,1)S(1)}, u32[]{:S(2)}, u32[]{:S(2)}) collective-permute-start(bf16[8,4096]{1,0:T(8,128)(2,1)S(1)} %get-tuple-element.6), channel_id=1, source_target_pairs={{0,3},{1,2},{2,1},{3,0},{4,7},{5,6},{6,5},{7,4},{8,11},{9,10},{10,... | collective-permute-start | bytes 196616 | tf_op jit(solution)/shard_map/ppermute | solution.py:41
  57.9 1.6 %copy-start.4 = (bf16[32,4096]{1,0:T(8,128)(2,1)}, bf16[32,4096]{1,0:T(8,128)(2,1)S(1)}, u32[]{:S(2)}) copy-start(bf16[32,4096]{1,0:T(8,128)(2,1)S(1)} %constant_dynamic-update-slice_fusion) | copy-start | bytes 786436

commit v2 on v1

--- a/solution.py
+++ b/solution.py
@@ -37,29 +37,18 @@
     return mixed.astype(jnp.bfloat16)
 
 
-def swap(value, axis, size, mask):
-    return lax.ppermute(value, axis, [(i, i ^ mask) for i in range(size)])
-
-
 def scatter_sum(value, axis, size, sent):
     rows = value.shape[0] // size
-    me = lax.axis_index(axis)
-    block = lambda who: lax.dynamic_slice_in_dim(value, who * rows, rows, 0)
-    arrived = [swap(block(me ^ mask).astype(sent), axis, size, mask) for mask in range(1, size)]
-    total = block(me)
-    for item in arrived:
-        total = total + item.astype(jnp.float32)
-    return total
+    blocks = value.reshape((size, rows) + value.shape[1:]).astype(sent)
+    arrived = lax.all_to_all(blocks, axis, 0, 0, tiled=True)
+    return jnp.sum(arrived.astype(jnp.float32), 0)
 
 
 def gather(value, axis, size):
-    me = lax.axis_index(axis)
     rows = value.shape[0]
-    result = jnp.zeros((rows * size,) + value.shape[1:], value.dtype)
-    for mask in range(size):
-        item = swap(value, axis, size, mask) if mask else value
-        result = lax.dynamic_update_slice_in_dim(result, item, (me ^ mask) * rows, 0)
-    return result
+    blocks = jnp.broadcast_to(value[None], (size,) + value.shape)
+    arrived = lax.all_to_all(blocks, axis, 0, 0, tiled=True)
+    return arrived.reshape((rows * size,) + value.shape[1:])
 
 
 def solution(mesh):

time: 60.3 us -> 75.5 us (1.25)
  blocking collectives: 0 us -> 17.7 us
  starting transfers between devices: 14 us -> 9.74 us
  matrix products: 24.7 us -> 27.5 us
  waiting for transfers between devices: 17.7 us -> 15 us
  other arithmetic: 2.41 us -> 3.98 us
    ppermute x12 -> x0, waiting for transfers between devices: 17.7 us -> none  [swap(): return lax.ppermute(value, axis, [(i, i ^ mask) for i in range(size)])]
    all_to_all x0 -> x2, blocking collectives: none -> 17.7 us  [gather(): arrived = lax.all_to_all(blocks, axis, 0, 0, tiled=True)]
    all_to_all x0 -> x2, waiting for transfers between devices: none -> 15 us  [scatter_sum(): arrived = lax.all_to_all(blocks, axis, 0, 0, tiled=True)]
    ppermute x12 -> x0, starting transfers between devices: 14 us -> none  [swap(): return lax.ppermute(value, axis, [(i, i ^ mask) for i in range(size)])]
    all_to_all x0 -> x2, starting transfers between devices: none -> 9.74 us  [scatter_sum(): arrived = lax.all_to_all(blocks, axis, 0, 0, tiled=True)]
    dot_general x3, matrix products: 9.42 us -> 11.7 us  [shards(): dot = lambda w: jnp.dot(scaled, w, preferred_element_type=jnp.float32)]
    convert_element_type x0 -> x1, other arithmetic: none -> 0.87 us  [shards(): (mine + residual.astype(jnp.float32)).astype(jnp.bfloat16)]
    unnamed x13 -> x8, local copies, waits for them, and re-layouts: 0.05 us -> 0.85 us
  transfers between devices with their start and end apart: 12 -> 2, of which waited for: 9 -> 2; matrix products, arithmetic and copies ran while one was open for 0% -> 0% of each run, Pallas kernels for 0% -> 0%
where the time goes in v2:
time: 75.5 us; the launch traced here: 74.9 us
  matrix products  27.5 us (36%)
  blocking collectives  17.7 us (23%)
  waiting for transfers between devices  15 us (20%)
  starting transfers between devices  9.74 us (13%)
  other arithmetic  3.98 us (5%)
  local copies, waits for them, and re-layouts  0.95 us (1%)
    all_to_all x2, blocking collectives, gather(): arrived = lax.all_to_all(blocks, axis, 0, 0, tiled=True)  17.7 us
    all_to_all x2, waiting for transfers between devices, scatter_sum(): arrived = lax.all_to_all(blocks, axis, 0, 0, tiled=True)  15 us
    dot_general x3, matrix products, shards(): dot = lambda w: jnp.dot(scaled, w, preferred_element_type=jnp.float32)  11.7 us
    all_to_all x2, starting transfers between devices, scatter_sum(): arrived = lax.all_to_all(blocks, axis, 0, 0, tiled=True)  9.74 us
    dot_general x1, matrix products, shards(): partial_out = jnp.dot(heads, w_output, preferred_element_type=jnp.float32)  9.34 us
    dot_general x1, matrix products, attend(): jnp.einsum('rgd,rsd->rgs', queries, keys, preferred_element_type=jnp.floa...  3.5 us
    dot_general x1, matrix products, attend(): jnp.einsum('rgs,rsd->rgd', weights, values, preferred_element_type=jnp.fl...  2.99 us
  transfers between devices with their start and end apart: 2, of which 2 were waited for; matrix products, arithmetic and copies ran while one was open for 0% of the time, Pallas kernels for 0%

profile of v2, /device:TPU:0, one launch (start us, length us, event | category | flops | bytes accessed | tf_op | source)
XLA Modules:
  0.0 74.9 jit_solution(1250286610350980655)
XLA Ops:
  0.0 0.0 copy-start
  0.0 0.0 copy-start.1
  0.0 1.2 %fusion.9 = f32[32]{0:T(128)S(1)} fusion(bf16[32,4096]{1,0:T(8,128)(2,1)} %param.9), kind=kLoop, calls=%fused_computation.14 | loop fusion | flops 393184 | bytes 262272 | tf_op jit(solution)/shard_map/reduce_sum | solution.py:63
  1.2 0.1 copy-done
  1.3 1.2 %fusion.16 = f32[32,128]{1,0:T(8,128)S(1)} fusion(bf16[4096,128]{1,0:T(8,128)(2,1)S(1)} %copy-done, bf16[32,4096]{1,0:T(8,128)(2,1)} %param.9, f32[4096]{0:T(1024)} %param.10), kind=kOutput, calls=%fused_computation.22 | convolution fusion | flops 33947648 | bytes 1343488 | tf_op jit(solution)/shard_map/dot_general | solution.py:64
  2.5 1.6 %fusion.14 = f32[32,128]{1,0:T(8,128)S(1)} fusion(bf16[4096,128]{1,0:T(8,128)(2,1)} %param.13, bf16[32,4096]{1,0:T(8,128)(2,1)} %param.9, f32[4096]{0:T(1024)} %param.10), kind=kOutput, calls=%fused_computation.21 | convolution fusion | flops 33947648 | bytes 1343488 | tf_op jit(solution)/shard_map/dot_general | solution.py:64
  4.1 8.9 %fusion.18 = f32[32,2048]{1,0:T(8,128)S(1)} fusion(bf16[4096,2048]{1,0:T(8,128)(2,1)} %param.11, bf16[32,4096]{1,0:T(8,128)(2,1)} %param.9, f32[4096]{0:T(1024)} %param.10), kind=kOutput, calls=%fused_computation.23 | convolution fusion | flops 537264128 | bytes 17317888 | tf_op jit(solution)/shard_map/dot_general | solution.py:64
  13.0 0.1 broadcast_in_dim.27
  13.1 0.7 maximum_bitcast_fusion
  13.8 4.2 %all-to-all-start = ((f32[4,8,2432]{2,1,0:T(8,128)}), f32[4,8,2432]{2,1,0:T(8,128)S(1)}, u32[]{:S(2)}, u32[]{:S(2)}) async-start(f32[4,8,2432]{2,1,0:T(8,128)} %maximum_bitcast_fusion), calls=%async_computation | async-start | bytes 622592 | tf_op jit(solution)/shard_map/all_to_all | solution.py:43
  18.0 0.0 copy-done.1
  18.0 0.1 iota_compare_fusion
  18.1 6.5 %all-to-all-done = f32[4,8,2432]{2,1,0:T(8,128)S(1)} async-done(((f32[4,8,2432]{2,1,0:T(8,128)}), f32[4,8,2432]{2,1,0:T(8,128)S(1)}, u32[]{:S(2)}, u32[]{:S(2)}) %all-to-all-start) | async-done | bytes 311328 | tf_op jit(solution)/shard_map/all_to_all | solution.py:43
  24.6 0.1 fusion.22
  24.7 0.1 slice_multiply_fusion
  24.9 0.1 subtract_convert_fusion.1
  25.0 0.1 maximum_convert_fusion
  25.0 0.1 subtract_convert_fusion
  25.1 0.2 multiply_reduce_fusion
  25.3 3.5 %select_reduce_fusion = (f32[8,16]{1,0:T(8,128)S(1)}, f32[8,16,2048]{2,1,0:T(8,128)S(1)}) fusion(pred[8,2048]{1,0:T(8,128)(4,1)S(1)} %iota_compare_fusion, bf16[8,2048,128]{2,1,0:T(8,128)(2,1)} %param.15, bf16[8,16,64]{2,1,0:T(8,128)(2,1)S(1)} %get-tuple-element.8, bf16[8,16,64]{2,1,0:T(8,128)(2,1)S(1)} %get-tuple-element.7), kind=kOutput, calls=%fused_computation.9 | convolution fusion | flops 67960704 | bytes 5292544 | tf_op jit(solution)/shard_map/rgd,rsd->rgs/dot_general | solution.py:21
  28.8 0.4 fusion.7
  29.2 3.0 %fusion.6 = bf16[1,8,16,128]{3,2,1,0:T(8,128)(2,1)S(1)} fusion(bf16[8,2048,128]{2,1,0:T(8,128)(2,1)} %param.16, f32[8,16,2048]{2,1,0:T(8,128)S(1)} %get-tuple-element.14, f32[8,16]{1,0:T(8,128)S(1)} %get-tuple-element.10, f32[8,16]{1,0:T(8,128)S(1)} %multiply_maximum_fusion, pred[8,2048]{1,0:T(8,128)(4,1)S(1)} %iota_compare_fusion, ...), kind=kOutput, calls=%fused_computation.6 | convolution fusion | flops 68206592 | bytes 5297664 | tf_op jit(solution)/shard_map/rgs,rsd->rgd/dot_general | solution.py:32
  32.3 7.0 %all_to_all.20 = bf16[4,8,2048]{2,1,0:T(8,128)(2,1)S(1)} all-to-all(bf16[4,8,2048]{2,1,0:T(8,128)(2,1)S(1)} %broadcast_in_dim.54), channel_id=1, replica_groups=mesh['groups'=2,'gx'=4,'gy'=4] {'gx'}, dimensions={0} | all-to-all | bytes 262144 | tf_op jit(solution)/shard_map/all_to_all | solution.py:50
  39.3 9.3 %fusion.2 = bf16[4,8,4096]{2,1,0:T(8,128)(2,1)} fusion(bf16[4,8,2048]{2,1,0:T(8,128)(2,1)S(1)} %all_to_all.20, bf16[2048,4096]{1,0:T(8,128)(2,1)} %param.14), kind=kOutput, calls=%fused_computation.2 | convolution fusion | flops 537001984 | bytes 17170432 | tf_op jit(solution)/shard_map/dot_general | solution.py:91
  48.6 5.5 %all-to-all-start.2 = ((bf16[4,8,4096]{2,1,0:T(8,128)(2,1)}), bf16[4,8,4096]{2,1,0:T(8,128)(2,1)S(1)}, u32[]{:S(2)}, u32[]{:S(2)}) async-start(bf16[4,8,4096]{2,1,0:T(8,128)(2,1)} %fusion.2), calls=%async_computation.2 | async-start | bytes 524288 | tf_op jit(solution)/shard_map/all_to_all | solution.py:43
  54.2 8.5 %all-to-all-done.2 = bf16[4,8,4096]{2,1,0:T(8,128)(2,1)S(1)} async-done(((bf16[4,8,4096]{2,1,0:T(8,128)(2,1)}), bf16[4,8,4096]{2,1,0:T(8,128)(2,1)S(1)}, u32[]{:S(2)}, u32[]{:S(2)}) %all-to-all-start.2) | async-done | bytes 262176 | tf_op jit(solution)/shard_map/all_to_all | solution.py:43
  62.7 0.9 %add_convert_fusion = bf16[8,4096]{1,0:T(8,128)(2,1)S(1)} fusion(f32[8,4096]{1,0:T(8,128)S(1)} %convert_reduce_fusion, bf16[32,4096]{1,0:T(8,128)(2,1)} %param.9, s32[]{:T(128)S(6)} %select_n.12), kind=kLoop, calls=%fused_computation.24 | loop fusion | flops 98304 | bytes 262148 | tf_op jit(solution)/shard_map/convert_element_type | solution.py:95
  63.6 10.7 %all_to_all.21 = bf16[4,8,4096]{2,1,0:T(8,128)(2,1)S(1)} all-to-all(bf16[4,8,4096]{2,1,0:T(8,128)(2,1)S(1)} %broadcast_in_dim.55), channel_id=1, replica_groups=mesh['groups'=2,'gx'=4,'gy'=4] {'gy'}, dimensions={0} | all-to-all | bytes 524288 | tf_op jit(solution)/shard_map/all_to_all | solution.py:50
  74.2 0.7 copy.22
  (12 shorter events, 0.2 us)
Async XLA Ops:
  0.0 1.3 %copy-start = (bf16[4096,128]{1,0:T(8,128)(2,1)S(1)}, bf16[4096,128]{1,0:T(8,128)(2,1)}, u32[]{:S(2)}) copy-start(bf16[4096,128]{1,0:T(8,128)(2,1)} %param.12) | copy-start | bytes 3145732
  0.0 18.0 %copy-start.1 = (s32[8]{0:T(128)S(1)}, s32[8]{0:T(128)}, u32[]{:S(2)}) copy-start(s32[8]{0:T(128)} %param.17) | copy-start | bytes 100
  13.8 10.8 %all-to-all-start = ((f32[4,8,2432]{2,1,0:T(8,128)}), f32[4,8,2432]{2,1,0:T(8,128)S(1)}, u32[]{:S(2)}, u32[]{:S(2)}) async-start(f32[4,8,2432]{2,1,0:T(8,128)} %maximum_bitcast_fusion), calls=%async_computation | async-start | bytes 622592 | tf_op jit(solution)/shard_map/all_to_all | solution.py:43
  48.6 14.0 %all-to-all-start.2 = ((bf16[4,8,4096]{2,1,0:T(8,128)(2,1)}), bf16[4,8,4096]{2,1,0:T(8,128)(2,1)S(1)}, u32[]{:S(2)}, u32[]{:S(2)}) async-start(bf16[4,8,4096]{2,1,0:T(8,128)(2,1)} %fusion.2), calls=%async_computation.2 | async-start | bytes 524288 | tf_op jit(solution)/shard_map/all_to_all | solution.py:43

commit v3 on v2

v3 whole, which is shorter than its diff:
```python
import functools

import jax
import jax.numpy as jnp
from jax import lax
from jax.experimental import pallas as pl
from jax.experimental.pallas import tpu as pltpu
from jax.sharding import PartitionSpec as P

HD = 128
EPS = 1e-05
ROPE_BASE = 500000.0
CHUNK = 256
F32 = jnp.float32
BF16 = jnp.bfloat16

ANY = pl.BlockSpec(memory_space=pl.ANY)
VMEM = pl.BlockSpec(memory_space=pltpu.VMEM)
SMEM = pl.BlockSpec(memory_space=pltpu.SMEM)
MIB = 1 << 20


def columns(index, width):
    return pl.ds(pl.multiple_of(index * width, HD), width)


def params(mib):
    return pltpu.CompilerParams(vmem_limit_bytes=mib * MIB)


def cost(flops, nbytes):
    return pl.CostEstimate(flops=flops, bytes_accessed=nbytes, transcendentals=0)


def in_vmem(value):
    return pltpu.with_memory_space_constraint(value, pltpu.VMEM)


def in_hbm(value):
    return pltpu.with_memory_space_constraint(value, pltpu.HBM)


def project(size, x_hbm, gain_hbm, wq_hbm, wk_hbm, wv_hbm, *refs):
    outs = refs[:size]
    x, gain, wq, wk, wv, scaled, total, sems = refs[size:]
    depth = x.shape[1]
    steps = depth // CHUNK
    pairs = [(x_hbm, x), (gain_hbm, gain), (wk_hbm, wk), (wv_hbm, wv)]
    small = [pltpu.make_async_copy(a, b, sems.at[steps + i]) for i, (a, b) in enumerate(pairs)]
    large = []
    for step in range(steps):
        part = pl.ds(step * CHUNK, CHUNK)
        large.append(pltpu.make_async_copy(wq_hbm.at[part], wq.at[part], sems.at[step]))
    small[0].start()
    small[1].start()
    for copy in large[:2]:
        copy.start()
    small[2].start()
    small[3].start()
    for copy in large[2:]:
        copy.start()
    small[0].wait()
    small[1].wait()
    wide = x[...].astype(F32)
    scaled[...] = (wide * gain[...]).astype(BF16)
    squares = jnp.sum(wide * wide, 1, keepdims=True)
    width = wq.shape[1]
    dot = functools.partial(jnp.dot, preferred_element_type=F32)
    for step, copy in enumerate(large):
        copy.wait()
        part = slice(step * CHUNK, (step + 1) * CHUNK)
        term = dot(scaled[:, part], wq[part])
        if step == 0:
            total[:, :width] = term
        else:
            total[:, :width] += term
        if step == 1:
            small[2].wait()
            total[:, width : width + HD] = dot(scaled[...], wk[...])
            small[3].wait()
            total[:, width + HD : width + 2 * HD] = dot(scaled[...], wv[...])
            total[:, width + 2 * HD :] = jnp.broadcast_to(squares, (squares.shape[0], HD))
    rows = outs[0].shape[0]
    me = lax.axis_index("gx")
    for mask in range(size):
        start = pl.multiple_of((me ^ mask) * rows, 8)
        outs[mask][...] = total[pl.ds(start, rows), :].astype(outs[mask].dtype)


def fetch_pieces(masks, width, w_hbm, pieces, sems, first):
    me = lax.axis_index("gy")
    copies = []
    for i, mask in enumerate(masks):
        source = w_hbm.at[:, columns(me ^ mask, width)]
        copies.append(pltpu.make_async_copy(source, pieces[i], sems.at[first + i]))
    return copies


def fetch_caches(masks, after, k_hbm, v_hbm, w_hbm, k, v, *refs):
    del after
    *pieces, sems = refs
    copies = [
        pltpu.make_async_copy(k_hbm, k, sems.at[0]),
        pltpu.make_async_copy(v_hbm, v, sems.at[1]),
    ]
    copies += fetch_pieces(masks, pieces[0].shape[1], w_hbm, pieces, sems, 2)
    for copy in copies:
        copy.start()
    for copy in copies:
        copy.wait()


def fetch_weights(masks, after, x_hbm, w_hbm, x, *refs):
    del after
    *pieces, sems = refs
    width = x.shape[1]
    copies = [
        pltpu.make_async_copy(x_hbm.at[:, columns(lax.axis_index("gy"), width)], x, sems.at[0])
    ]
    copies += fetch_pieces(masks, width, w_hbm, pieces, sems, 1)
    for copy in copies:
        copy.start()
    for copy in copies:
        copy.wait()


def attention(size, model, masks, lengths, cosine, sine, k, v, w_hbm, *refs):
    arrived = refs[:size]
    heads = refs[size]
    pieces = refs[size + 1 : size + 1 + len(masks)]
    q_rows, o_rows, sems = refs[size + 1 + len(masks) :]
    copies = fetch_pieces(masks, pieces[0].shape[1], w_hbm, pieces, sems, 0) if masks else []
    for copy in copies:
        copy.start()
    rows, slots = k.shape[0], k.shape[1]
    group = heads.shape[1] // HD
    width = group * HD
    summed = arrived[0][...]
    for item in arrived[1:]:
        summed = summed + item[...].astype(F32)
    scale = lax.rsqrt(summed[:, width + 2 * HD :] / model + EPS)
    cosines, sines = cosine[...], sine[...]

    def turn(value):
        return value * cosines + pltpu.roll(value, HD // 2, 1) * sines

    for head in range(group):
        part = summed[:, head * HD : (head + 1) * HD] * scale
        q_rows[head] = turn(part).astype(BF16).astype(F32)
    new_keys = turn(summed[:, width : width + HD] * scale).astype(BF16).astype(F32)
    new_values = (summed[:, width + HD : width + 2 * HD] * scale).astype(BF16).astype(F32)
    factor = HD ** (-0.5)
    slot = lax.broadcasted_iota(jnp.int32, (group, slots), 1)
    for row in range(rows):
        queries = q_rows[:, row, :]
        scores = (
            lax.dot_general(
                queries.astype(BF16), k[row], (((1,), (1,)), ((), ())), preferred_element_type=F32
            )
            * factor
        )
        own = jnp.sum(queries * new_keys[row : row + 1], 1, keepdims=True) * factor
        scores = jnp.where(slot < lengths[row], scores, -jnp.inf)
        top = jnp.maximum(jnp.max(scores, 1, keepdims=True), own)
        probs = jnp.exp(scores - top)
        own_prob = jnp.exp(own - top)
        share = 1.0 / (jnp.sum(probs, 1, keepdims=True) + own_prob)
        weights = (probs * share).astype(BF16)
        own_weight = (own_prob * share).astype(BF16).astype(F32)
        mixed = jnp.dot(weights, v[row], preferred_element_type=F32)
        o_rows[:, row, :] = mixed + own_weight * new_values[row : row + 1]
    for head in range(group):
        heads[:, head * HD : (head + 1) * HD] = o_rows[head].astype(BF16)
    for copy in copies:
        copy.wait()


def project_out(size, w, *refs):
    blocks, out, gathered = refs[:size], refs[size], refs[size + 1]
    me = lax.axis_index("gx")
    rows = blocks[0].shape[0]
    for mask in range(size):
        gathered[pl.ds(pl.multiple_of((me ^ mask) * rows, 8), rows), :] = blocks[mask][...].astype(F32)
    out[...] = jnp.dot(
        gathered[...].astype(BF16), w[...], preferred_element_type=F32
    ).astype(out.dtype)


def finish(x, own, *refs):
    *arrived, out = refs
    total = own[...]
    for item in arrived:
        total = total + item[...].astype(F32)
    out[...] = (x[...].astype(F32) + total).astype(BF16)


def assemble(size, *refs):
    blocks, out, sems = refs[:size], refs[size], refs[size + 1]
    me = lax.axis_index("gy")
    width = blocks[0].shape[1]
    copies = []
    for mask in range(size):
        target = out.at[:, columns(me ^ mask, width)]
        copies.append(pltpu.make_async_copy(blocks[mask], target, sems.at[mask]))
    for copy in copies:
        copy.start()
    for copy in copies:
        copy.wait()


def swap(value, axis, size, mask):
    return lax.ppermute(value, axis, [(i, i ^ mask) for i in range(size)])


def solution(mesh):
    size_x = mesh.shape["gx"]
    size_y = mesh.shape["gy"]
    struct = jax.ShapeDtypeStruct
    sems = lambda n: pltpu.SemaphoreType.DMA((n,))
    order = list(range(size_y - 1, -1, -1))
    quarter = max(size_y // 4, 1)
    early, middle, late = order[:quarter], order[quarter : 2 * quarter], order[2 * quarter :]

    def shards(inputs, gain, w_query, w_key, w_value, w_output, key_cache, value_cache, lengths):
        batch, depth = inputs.shape
        width = w_query.shape[1]
        rows = key_cache.shape[0]
        packed = width + 3 * HD
        block = w_output.shape[1] // size_y
        piece = pltpu.VMEM((width, block), BF16)
        piece_bytes = 2 * width * block

        sums = pl.pallas_call(
            functools.partial(project, size_x),
            out_shape=[pltpu.VMEM((rows, packed), F32)] * size_x,
            in_specs=[ANY] * 5,
            out_specs=[VMEM] * size_x,
            scratch_shapes=[
                pltpu.VMEM(inputs.shape, BF16),
                pltpu.VMEM((1, depth), F32),
                pltpu.VMEM(w_query.shape, BF16),
                pltpu.VMEM(w_key.shape, BF16),
                pltpu.VMEM(w_value.shape, BF16),
                pltpu.VMEM(inputs.shape, BF16),
                pltpu.VMEM((batch, packed), F32),
                sems(depth // CHUNK + 4),
            ],
            compiler_params=params(28),
            cost_estimate=cost(2 * batch * depth * packed, 2 * depth * packed),
            name="project",
        )(*[in_hbm(a) for a in (inputs, gain.reshape(1, depth), w_query, w_key, w_value)])
        arrived = [sums[0]] + [swap(sums[m], "gx", size_x, m) for m in range(1, size_x)]

        fetched = pl.pallas_call(
            functools.partial(fetch_caches, early),
            out_shape=[pltpu.VMEM(key_cache.shape, BF16), pltpu.VMEM(value_cache.shape, BF16)]
            + [piece] * len(early),
            in_specs=[ANY] * 4,
            out_specs=[VMEM] * (2 + len(early)),
            scratch_shapes=[sems(2 + len(early))],
            compiler_params=params(4),
            cost_estimate=cost(0, 4 * key_cache.size + piece_bytes * len(early)),
            name="fetch_caches",
        )(sums[0], in_hbm(key_cache), in_hbm(value_cache), in_hbm(w_output))
        keys, values, *pieces = fetched

        half = HD // 2
        inverse = ROPE_BASE ** (-(jnp.arange(half, dtype=F32) * 2.0 / HD))
        angles = lengths.astype(F32)[:, None] * inverse[None, :]
        cosine, sine = jnp.cos(angles), jnp.sin(angles)
        heads, *more = pl.pallas_call(
            functools.partial(attention, size_x, depth * size_x, middle),
            out_shape=[pltpu.VMEM((rows, width), BF16)] + [piece] * len(middle),
            in_specs=[SMEM, VMEM, VMEM, VMEM, VMEM, ANY] + [VMEM] * size_x,
            out_specs=[VMEM] * (1 + len(middle)),
            scratch_shapes=[
                pltpu.VMEM((width // HD, rows, HD), F32),
                pltpu.VMEM((width // HD, rows, HD), F32),
                sems(max(len(middle), 1)),
            ],
            compiler_params=params(8),
            cost_estimate=cost(4 * key_cache.size * (width // HD), piece_bytes * len(middle)),
            name="attention",
        )(
            lengths,
            jnp.concatenate([cosine, cosine], 1),
            jnp.concatenate([-sine, sine], 1),
            in_vmem(keys),
            in_vmem(values),
            in_hbm(w_output),
            *[in_vmem(a) for a in arrived],
        )
        pieces += more
        gathered = [heads] + [swap(heads, "gx", size_x, m) for m in range(1, size_x)]

        residual, *more = pl.pallas_call(
            functools.partial(fetch_weights, late),
            out_shape=[pltpu.VMEM((batch, block), BF16)] + [piece] * len(late),
            in_specs=[ANY] * 3,
            out_specs=[VMEM] * (1 + len(late)),
            scratch_shapes=[sems(1 + len(late))],
            compiler_params=params(4),
            cost_estimate=cost(0, piece_bytes * len(late)),
            name="fetch_weights",
        )(heads, in_hbm(inputs), in_hbm(w_output))
        pieces += more

        terms = {}
        for mask, w in zip(order, pieces):
            kind = BF16 if mask else F32
            term = pl.pallas_call(
                functools.partial(project_out, size_x),
                out_shape=pltpu.VMEM((batch, block), kind),
                in_specs=[VMEM] * (1 + size_x),
                out_specs=VMEM,
                scratch_shapes=[pltpu.VMEM((batch, width), F32)],
                compiler_params=params(8),
                cost_estimate=cost(2 * batch * width * block, piece_bytes),
                name="project_out",
            )(in_vmem(w), *[in_vmem(a) for a in gathered])
            terms[mask] = swap(term, "gy", size_y, mask) if mask else term
        done = pl.pallas_call(
            finish,
            out_shape=pltpu.VMEM((batch, block), BF16),
            in_specs=[VMEM] * (1 + size_y),
            out_specs=VMEM,
            compiler_params=params(4),
            name="finish",
        )(in_vmem(residual), *[in_vmem(terms[m]) for m in range(size_y)])
        blocks = [done] + [swap(done, "gy", size_y, m) for m in range(1, size_y)]
        return pl.pallas_call(
            functools.partial(assemble, size_y),
            out_shape=struct((batch, block * size_y), BF16),
            in_specs=[VMEM] * size_y,
            out_specs=ANY,
            scratch_shapes=[sems(size_y)],
            compiler_params=params(4),
            name="assemble",
        )(*[in_vmem(b) for b in blocks])

    placed = (
        P("groups", "gx"),
        P("gx"),
        P("gx", "gy"),
        P("gx", "gy"),
        P("gx", "gy"),
        P("gy", "gx"),
        P(("groups", "gx"), None, "gy"),
        P(("groups", "gx"), None, "gy"),
        P(("groups", "gx")),
    )
    return jax.shard_map(
        shards, mesh=mesh, in_specs=placed, out_specs=P("groups", "gx"), check_vma=False
    )
```

time: 75.5 us -> 49.1 us (0.65)
  matrix products: 27.5 us -> 0 us
  Pallas kernels: 0 us -> 26.1 us
  blocking collectives: 17.7 us -> 0 us
  waiting for transfers between devices: 15 us -> 8.68 us
  starting transfers between devices: 9.74 us -> 14 us
  other arithmetic: 3.98 us -> 0.2 us
  local copies, waits for them, and re-layouts: 0.95 us -> 0.01 us
    dot_general x6 -> x0, matrix products: 27.5 us -> none  [the longest x3 11.7 us: shards(): dot = lambda w: jnp.dot(scaled, w, preferred_element_type=jnp.float32)]
    pallas_call x0 -> x10, Pallas kernels: none -> 26.1 us  [the longest x1 6.98 us: shards(): pl.pallas_call(functools.partial(project, size_x), out_shape=[pltpu.VMEM(...]
    all_to_all x2 -> x0, blocking collectives: 17.7 us -> none  [gather(): arrived = lax.all_to_all(blocks, axis, 0, 0, tiled=True)]
    all_to_all x2 -> x0, waiting for transfers between devices: 15 us -> none  [scatter_sum(): arrived = lax.all_to_all(blocks, axis, 0, 0, tiled=True)]
    ppermute x0 -> x12, starting transfers between devices: none -> 14 us  [swap(): return lax.ppermute(value, axis, [(i, i ^ mask) for i in range(size)])]
    all_to_all x2 -> x0, starting transfers between devices: 9.74 us -> none  [scatter_sum(): arrived = lax.all_to_all(blocks, axis, 0, 0, tiled=True)]
    ppermute x0 -> x12, waiting for transfers between devices: none -> 8.68 us  [swap(): return lax.ppermute(value, axis, [(i, i ^ mask) for i in range(size)])]
    reduce_sum x5 -> x0, other arithmetic: 1.77 us -> none  [the longest x1 1.2 us: shards(): squares = jnp.sum(widened * widened, 1, keepdims=True)]
  transfers between devices with their start and end apart: 2 -> 12, of which waited for: 2 -> 6; matrix products, arithmetic and copies ran while one was open for 0% -> 0% of each run, Pallas kernels for 0% -> 22%
where the time goes in v3:
time: 49.1 us; the launch traced here: 49 us
  Pallas kernels  26.1 us (53%)
  starting transfers between devices  14 us (29%)
  waiting for transfers between devices  8.68 us (18%)
    ppermute x12, starting transfers between devices, swap(): return lax.ppermute(value, axis, [(i, i ^ mask) for i in range(size)])  14 us
    ppermute x12, waiting for transfers between devices, swap(): return lax.ppermute(value, axis, [(i, i ^ mask) for i in range(size)])  8.68 us
    pallas_call x1, Pallas kernels, shards(): pl.pallas_call(functools.partial(project, size_x), out_shape=[pltpu.VMEM(...  6.98 us
    pallas_call x1, Pallas kernels, shards(): pl.pallas_call(functools.partial(attention, size_x, depth * size_x, middl...  6.82 us
    pallas_call x1, Pallas kernels, shards(): pl.pallas_call(functools.partial(fetch_caches, early), out_shape=[pltpu.V...  4.69 us
    pallas_call x1, Pallas kernels, shards(): pl.pallas_call(functools.partial(fetch_weights, late), out_shape=[pltpu.V...  3.53 us
    pallas_call x4, Pallas kernels, shards(): pl.pallas_call(functools.partial(project_out, size_x), out_shape=pltpu.VM...  3.28 us
  transfers between devices with their start and end apart: 12, of which 6 were waited for; matrix products, arithmetic and copies ran while one was open for 0% of the time, Pallas kernels for 22%

profile of v3, /device:TPU:0, one launch (start us, length us, event | category | flops | bytes accessed | tf_op | source)
XLA Modules:
  0.0 49.0 jit_solution(13462338071173807259)
XLA Ops:
  0.0 0.0 copy-start
  0.0 7.0 %project.1 = (f32[8,2432]{1,0:T(8,128)S(1)}, f32[8,2432]{1,0:T(8,128)S(1)}, f32[8,2432]{1,0:T(8,128)S(1)}, f32[8,2432]{1,0:T(8,128)S(1)}) custom-call(bf16[32,4096]{1,0:T(8,128)(2,1)} %x_hbm.3, f32[1,4096]{1,0:T(1,128)} %bitcast.1, bf16[4096,2048]{1,0:T(8,128)(2,1)} %wq_hbm.1, bf16[4096,128]{1,0:T(8,128)(2,1)} %wk_hbm.1, bf16[4096,128]{1,0:T(8,128)(2,1)} %wv_hbm.1), custom_call_target="tpu_custom_call" | custom-call | flops 637534208 | bytes 19922944 | tf_op jit(solution)/shard_map/project/pallas_call | solution.py:233
  7.0 0.5 %collective-permute-start = (f32[8,2432]{1,0:T(8,128)S(1)}, f32[8,2432]{1,0:T(8,128)S(1)}, u32[]{:S(2)}, u32[]{:S(2)}) collective-permute-start(f32[8,2432]{1,0:T(8,128)S(1)} %get-tuple-element.20), channel_id=1, source_target_pairs={{0,4},{4,0},{8,12},{12,8},{1,5},{5,1},{9,13},{13,9},{2,6},{6,2},{1... | collective-permute-start | bytes 233480 | tf_op jit(solution)/shard_map/ppermute | solution.py:212
  7.5 2.6 %collective-permute-start.1 = (f32[8,2432]{1,0:T(8,128)S(1)}, f32[8,2432]{1,0:T(8,128)S(1)}, u32[]{:S(2)}, u32[]{:S(2)}) collective-permute-start(f32[8,2432]{1,0:T(8,128)S(1)} %get-tuple-element.21), channel_id=1, source_target_pairs={{0,8},{4,12},{8,0},{12,4},{1,9},{5,13},{9,1},{13,5},{2,10},{6,14},... | collective-permute-start | bytes 233480 | tf_op jit(solution)/shard_map/ppermute | solution.py:212
  10.1 0.1 collective-permute-start.2
  10.2 0.0 copy-done
  10.2 0.1 fusion
  10.3 4.7 %fetch_caches.1 = (bf16[8,2048,128]{2,1,0:T(8,128)(2,1)S(1)}, bf16[8,2048,128]{2,1,0:T(8,128)(2,1)S(1)}, bf16[2048,1024]{1,0:T(8,128)(2,1)S(1)}) custom-call(f32[8,2432]{1,0:T(8,128)S(1)} %get-tuple-element.17.after.refs_0_, bf16[8,2048,128]{2,1,0:T(8,128)(2,1)} %k_hbm.1, bf16[8,2048,128]{2,1,0:T(8,128)(2,1)} %v_hbm.1, bf16[2048,4096]{1,0:T(8,128)(2,1)} %w_hbm.5), custom_call_target="tpu_custom_call" | custom-call | bytes 12582912 | tf_op jit(solution)/shard_map/fetch_caches/pallas_call | solution.py:254
  15.0 0.1 pad_maximum_fusion
  15.1 0.0 collective-permute-done.refs_1_
  15.1 0.0 collective-permute-done.1.refs_2_
  15.1 0.0 collective-permute-done.2.refs_3_
  15.1 6.8 %attention.1 = (bf16[8,2048]{1,0:T(8,128)(2,1)S(1)}, bf16[2048,1024]{1,0:T(8,128)(2,1)S(1)}) custom-call(s32[8]{0:T(128)S(1)} %copy-done, f32[8,128]{1,0:T(8,128)S(1)} %get-tuple-element.32.cosine, f32[8,128]{1,0:T(8,128)S(1)} %get-tuple-element.33.sine, bf16[8,2048,128]{2,1,0:T(8,128)(2,1)S(1)} %get-tuple-element.18.k, ...), custom_call_target="tpu_custom_call" | custom-call | flops 134217728 | bytes 4194304 | tf_op jit(solution)/shard_map/attention/pallas_call | solution.py:271
  21.9 1.7 %collective-permute-start.5 = (bf16[8,2048]{1,0:T(8,128)(2,1)S(1)}, bf16[8,2048]{1,0:T(8,128)(2,1)S(1)}, u32[]{:S(2)}, u32[]{:S(2)}) collective-permute-start(bf16[8,2048]{1,0:T(8,128)(2,1)S(1)} %get-tuple-element.23.after.refs_0_), channel_id=1, source_target_pairs={{0,12},{4,8},{8,4},{12,0},{1,13},{5,9},{9,5},{13,1},{2,14},{6,10},... | collective-permute-start | bytes 98312 | tf_op jit(solution)/shard_map/ppermute | solution.py:212
  23.6 0.1 collective-permute-start.4
  23.8 0.1 collective-permute-start.3
  23.8 3.5 %fetch_weights.1 = (bf16[32,1024]{1,0:T(8,128)(2,1)S(1)}, bf16[2048,1024]{1,0:T(8,128)(2,1)S(1)}, bf16[2048,1024]{1,0:T(8,128)(2,1)S(1)}) custom-call(bf16[8,2048]{1,0:T(8,128)(2,1)S(1)} %get-tuple-element.23.after.refs_0_, bf16[32,4096]{1,0:T(8,128)(2,1)} %x_hbm.3, bf16[2048,4096]{1,0:T(8,128)(2,1)} %w_hbm.5), custom_call_target="tpu_custom_call" | custom-call | bytes 8388608 | tf_op jit(solution)/shard_map/fetch_weights/pallas_call | solution.py:296
  27.4 0.0 collective-permute-done.5.refs_3_
  27.4 0.2 collective-permute-done.4.refs_2_
  27.6 0.0 collective-permute-done.3.refs_1_
  27.6 0.8 %project_out.6 = bf16[32,1024]{1,0:T(8,128)(2,1)S(1)} custom-call(bf16[2048,1024]{1,0:T(8,128)(2,1)S(1)} %get-tuple-element.27.w, bf16[8,2048]{1,0:T(8,128)(2,1)S(1)} %get-tuple-element.23.after.refs_0_, bf16[8,2048]{1,0:T(8,128)(2,1)S(1)} %collective-permute-done.3.refs_1_, bf16[8,2048]{1,0:T(8,128)(2,1)S(1)} %collective-permute-done.4.refs_2_, ...), custom_call_target="tpu_custom_call" | custom-call | flops 134217728 | bytes 4194304 | tf_op jit(solution)/shard_map/project_out/pallas_call | solution.py:311
  28.4 2.8 %collective-permute-start.7 = (bf16[32,1024]{1,0:T(8,128)(2,1)S(1)}, bf16[32,1024]{1,0:T(8,128)(2,1)S(1)}, u32[]{:S(2)}, u32[]{:S(2)}) collective-permute-start(bf16[32,1024]{1,0:T(8,128)(2,1)S(1)} %project_out.6), channel_id=1, source_target_pairs={{0,2},{1,3},{2,0},{3,1},{4,6},{5,7},{6,4},{7,5},{8,10},{9,11},{10,... | collective-permute-start | bytes 196616 | tf_op jit(solution)/shard_map/ppermute | solution.py:212
  31.2 0.8 %project_out.7 = bf16[32,1024]{1,0:T(8,128)(2,1)S(1)} custom-call(bf16[2048,1024]{1,0:T(8,128)(2,1)S(1)} %get-tuple-element.28.w, bf16[8,2048]{1,0:T(8,128)(2,1)S(1)} %get-tuple-element.23.after.refs_0_, bf16[8,2048]{1,0:T(8,128)(2,1)S(1)} %collective-permute-done.3.refs_1_, bf16[8,2048]{1,0:T(8,128)(2,1)S(1)} %collective-permute-done.4.refs_2_, ...), custom_call_target="tpu_custom_call" | custom-call | flops 134217728 | bytes 4194304 | tf_op jit(solution)/shard_map/project_out/pallas_call | solution.py:311
  32.0 1.4 %collective-permute-start.8 = (bf16[32,1024]{1,0:T(8,128)(2,1)S(1)}, bf16[32,1024]{1,0:T(8,128)(2,1)S(1)}, u32[]{:S(2)}, u32[]{:S(2)}) collective-permute-start(bf16[32,1024]{1,0:T(8,128)(2,1)S(1)} %project_out.7), channel_id=1, source_target_pairs={{0,3},{1,2},{2,1},{3,0},{4,7},{5,6},{6,5},{7,4},{8,11},{9,10},{10,... | collective-permute-start | bytes 196616 | tf_op jit(solution)/shard_map/ppermute | solution.py:212
  33.4 0.8 %project_out.5 = bf16[32,1024]{1,0:T(8,128)(2,1)S(1)} custom-call(bf16[2048,1024]{1,0:T(8,128)(2,1)S(1)} %get-tuple-element.26.w, bf16[8,2048]{1,0:T(8,128)(2,1)S(1)} %get-tuple-element.23.after.refs_0_, bf16[8,2048]{1,0:T(8,128)(2,1)S(1)} %collective-permute-done.3.refs_1_, bf16[8,2048]{1,0:T(8,128)(2,1)S(1)} %collective-permute-done.4.refs_2_, ...), custom_call_target="tpu_custom_call" | custom-call | flops 134217728 | bytes 4194304 | tf_op jit(solution)/shard_map/project_out/pallas_call | solution.py:311
  34.2 0.3 collective-permute-start.6
  34.4 0.8 %project_out.4.own = f32[32,1024]{1,0:T(8,128)S(1)} custom-call(bf16[2048,1024]{1,0:T(8,128)(2,1)S(1)} %get-tuple-element.25.w, bf16[8,2048]{1,0:T(8,128)(2,1)S(1)} %get-tuple-element.23.after.refs_0_, bf16[8,2048]{1,0:T(8,128)(2,1)S(1)} %collective-permute-done.3.refs_1_, bf16[8,2048]{1,0:T(8,128)(2,1)S(1)} %collective-permute-done.4.refs_2_, ...), custom_call_target="tpu_custom_call" | custom-call | flops 134217728 | bytes 4194304 | tf_op jit(solution)/shard_map/project_out/pallas_call | solution.py:311
  35.2 0.1 collective-permute-done.7.refs_1_
  35.3 3.0 %collective-permute-done.8.refs_2_ = bf16[32,1024]{1,0:T(8,128)(2,1)S(1)} collective-permute-done((bf16[32,1024]{1,0:T(8,128)(2,1)S(1)}, bf16[32,1024]{1,0:T(8,128)(2,1)S(1)}, u32[]{:S(2)}, u32[]{:S(2)}) %collective-permute-start.8) | collective-permute-done | bytes 65568 | tf_op jit(solution)/shard_map/ppermute | solution.py:212
  38.4 1.2 %collective-permute-done.6.refs_0_ = bf16[32,1024]{1,0:T(8,128)(2,1)S(1)} collective-permute-done((bf16[32,1024]{1,0:T(8,128)(2,1)S(1)}, bf16[32,1024]{1,0:T(8,128)(2,1)S(1)}, u32[]{:S(2)}, u32[]{:S(2)}) %collective-permute-start.6) | collective-permute-done | bytes 65568 | tf_op jit(solution)/shard_map/ppermute | solution.py:212
  39.6 2.2 %collective-permute-start.11 = (bf16[32,1024]{1,0:T(8,128)(2,1)S(1)}, bf16[32,1024]{1,0:T(8,128)(2,1)S(1)}, u32[]{:S(2)}, u32[]{:S(2)}) collective-permute-start(bf16[32,1024]{1,0:T(8,128)(2,1)S(1)} %finish.1.refs_0_), channel_id=1, source_target_pairs={{0,3},{1,2},{2,1},{3,0},{4,7},{5,6},{6,5},{7,4},{8,11},{9,10},{10,... | collective-permute-start | bytes 196616 | tf_op jit(solution)/shard_map/ppermute | solution.py:212
  41.8 0.0 collective-permute-start.10
  41.8 2.2 %collective-permute-start.9 = (bf16[32,1024]{1,0:T(8,128)(2,1)S(1)}, bf16[32,1024]{1,0:T(8,128)(2,1)S(1)}, u32[]{:S(2)}, u32[]{:S(2)}) collective-permute-start(bf16[32,1024]{1,0:T(8,128)(2,1)S(1)} %finish.1.refs_0_), channel_id=1, source_target_pairs={{0,1},{1,0},{2,3},{3,2},{4,5},{5,4},{6,7},{7,6},{8,9},{9,8},{10,11... | collective-permute-start | bytes 196616 | tf_op jit(solution)/shard_map/ppermute | solution.py:212
  44.0 2.2 %collective-permute-done.11.refs_3_ = bf16[32,1024]{1,0:T(8,128)(2,1)S(1)} collective-permute-done((bf16[32,1024]{1,0:T(8,128)(2,1)S(1)}, bf16[32,1024]{1,0:T(8,128)(2,1)S(1)}, u32[]{:S(2)}, u32[]{:S(2)}) %collective-permute-start.11) | collective-permute-done | bytes 65568 | tf_op jit(solution)/shard_map/ppermute | solution.py:212
  46.3 2.0 %collective-permute-done.10.refs_2_ = bf16[32,1024]{1,0:T(8,128)(2,1)S(1)} collective-permute-done((bf16[32,1024]{1,0:T(8,128)(2,1)S(1)}, bf16[32,1024]{1,0:T(8,128)(2,1)S(1)}, u32[]{:S(2)}, u32[]{:S(2)}) %collective-permute-start.10) | collective-permute-done | bytes 65568 | tf_op jit(solution)/shard_map/ppermute | solution.py:212
  48.3 0.0 collective-permute-done.9.refs_1_
  48.3 0.7 %assemble.1 = bf16[32,4096]{1,0:T(8,128)(2,1)} custom-call(bf16[32,1024]{1,0:T(8,128)(2,1)S(1)} %finish.1.refs_0_, bf16[32,1024]{1,0:T(8,128)(2,1)S(1)} %collective-permute-done.9.refs_1_, bf16[32,1024]{1,0:T(8,128)(2,1)S(1)} %collective-permute-done.10.refs_2_, bf16[32,1024]{1,0:T(8,128)(2,1)S(1)} %collective-permute-done.11.refs_3_), custom_call_target="tpu_custom_call" | custom-call | tf_op jit(solution)/shard_map/assemble/pallas_call | solution.py:331
  (3 shorter events, 0.1 us)
Async XLA Ops:
  0.0 10.2 %copy-start = (s32[8]{0:T(128)S(1)}, s32[8]{0:T(128)}, u32[]{:S(2)}) copy-start(s32[8]{0:T(128)} %lengths.1) | copy-start | bytes 100
  7.0 8.1 %collective-permute-start = (f32[8,2432]{1,0:T(8,128)S(1)}, f32[8,2432]{1,0:T(8,128)S(1)}, u32[]{:S(2)}, u32[]{:S(2)}) collective-permute-start(f32[8,2432]{1,0:T(8,128)S(1)} %get-tuple-element.20), channel_id=1, source_target_pairs={{0,4},{4,0},{8,12},{12,8},{1,5},{5,1},{9,13},{13,9},{2,6},{6,2},{1... | collective-permute-start | bytes 233480 | tf_op jit(solution)/shard_map/ppermute | solution.py:212
  7.5 7.6 %collective-permute-start.1 = (f32[8,2432]{1,0:T(8,128)S(1)}, f32[8,2432]{1,0:T(8,128)S(1)}, u32[]{:S(2)}, u32[]{:S(2)}) collective-permute-start(f32[8,2432]{1,0:T(8,128)S(1)} %get-tuple-element.21), channel_id=1, source_target_pairs={{0,8},{4,12},{8,0},{12,4},{1,9},{5,13},{9,1},{13,5},{2,10},{6,14},... | collective-permute-start | bytes 233480 | tf_op jit(solution)/shard_map/ppermute | solution.py:212
  10.1 5.0 %collective-permute-start.2 = (f32[8,2432]{1,0:T(8,128)S(1)}, f32[8,2432]{1,0:T(8,128)S(1)}, u32[]{:S(2)}, u32[]{:S(2)}) collective-permute-start(f32[8,2432]{1,0:T(8,128)S(1)} %get-tuple-element.22), channel_id=1, source_target_pairs={{0,12},{4,8},{8,4},{12,0},{1,13},{5,9},{9,5},{13,1},{2,14},{6,10},... | collective-permute-start | bytes 233480 | tf_op jit(solution)/shard_map/ppermute | solution.py:212
  21.9 5.5 %collective-permute-start.5 = (bf16[8,2048]{1,0:T(8,128)(2,1)S(1)}, bf16[8,2048]{1,0:T(8,128)(2,1)S(1)}, u32[]{:S(2)}, u32[]{:S(2)}) collective-permute-start(bf16[8,2048]{1,0:T(8,128)(2,1)S(1)} %get-tuple-element.23.after.refs_0_), channel_id=1, source_target_pairs={{0,12},{4,8},{8,4},{12,0},{1,13},{5,9},{9,5},{13,1},{2,14},{6,10},... | collective-permute-start | bytes 98312 | tf_op jit(solution)/shard_map/ppermute | solution.py:212
  23.6 3.9 %collective-permute-start.4 = (bf16[8,2048]{1,0:T(8,128)(2,1)S(1)}, bf16[8,2048]{1,0:T(8,128)(2,1)S(1)}, u32[]{:S(2)}, u32[]{:S(2)}) collective-permute-start(bf16[8,2048]{1,0:T(8,128)(2,1)S(1)} %get-tuple-element.23.after.refs_0_), channel_id=1, source_target_pairs={{0,8},{4,12},{8,0},{12,4},{1,9},{5,13},{9,1},{13,5},{2,10},{6,14},... | collective-permute-start | bytes 98312 | tf_op jit(solution)/shard_map/ppermute | solution.py:212
  23.8 3.8 %collective-permute-start.3 = (bf16[8,2048]{1,0:T(8,128)(2,1)S(1)}, bf16[8,2048]{1,0:T(8,128)(2,1)S(1)}, u32[]{:S(2)}, u32[]{:S(2)}) collective-permute-start(bf16[8,2048]{1,0:T(8,128)(2,1)S(1)} %get-tuple-element.23.after.refs_0_), channel_id=1, source_target_pairs={{0,4},{4,0},{8,12},{12,8},{1,5},{5,1},{9,13},{13,9},{2,6},{6,2},{1... | collective-permute-start | bytes 98312 | tf_op jit(solution)/shard_map/ppermute | solution.py:212
  28.4 7.0 %collective-permute-start.7 = (bf16[32,1024]{1,0:T(8,128)(2,1)S(1)}, bf16[32,1024]{1,0:T(8,128)(2,1)S(1)}, u32[]{:S(2)}, u32[]{:S(2)}) collective-permute-start(bf16[32,1024]{1,0:T(8,128)(2,1)S(1)} %project_out.6), channel_id=1, source_target_pairs={{0,2},{1,3},{2,0},{3,1},{4,6},{5,7},{6,4},{7,5},{8,10},{9,11},{10,... | collective-permute-start | bytes 196616 | tf_op jit(solution)/shard_map/ppermute | solution.py:212
  32.0 6.4 %collective-permute-start.8 = (bf16[32,1024]{1,0:T(8,128)(2,1)S(1)}, bf16[32,1024]{1,0:T(8,128)(2,1)S(1)}, u32[]{:S(2)}, u32[]{:S(2)}) collective-permute-start(bf16[32,1024]{1,0:T(8,128)(2,1)S(1)} %project_out.7), channel_id=1, source_target_pairs={{0,3},{1,2},{2,1},{3,0},{4,7},{5,6},{6,5},{7,4},{8,11},{9,10},{10,... | collective-permute-start | bytes 196616 | tf_op jit(solution)/shard_map/ppermute | solution.py:212
  34.2 5.4 %collective-permute-start.6 = (bf16[32,1024]{1,0:T(8,128)(2,1)S(1)}, bf16[32,1024]{1,0:T(8,128)(2,1)S(1)}, u32[]{:S(2)}, u32[]{:S(2)}) collective-permute-start(bf16[32,1024]{1,0:T(8,128)(2,1)S(1)} %project_out.5), channel_id=1, source_target_pairs={{0,1},{1,0},{2,3},{3,2},{4,5},{5,4},{6,7},{7,6},{8,9},{9,8},{10,11... | collective-permute-start | bytes 196616 | tf_op jit(solution)/shard_map/ppermute | solution.py:212
  39.6 6.7 %collective-permute-start.11 = (bf16[32,1024]{1,0:T(8,128)(2,1)S(1)}, bf16[32,1024]{1,0:T(8,128)(2,1)S(1)}, u32[]{:S(2)}, u32[]{:S(2)}) collective-permute-start(bf16[32,1024]{1,0:T(8,128)(2,1)S(1)} %finish.1.refs_0_), channel_id=1, source_target_pairs={{0,3},{1,2},{2,1},{3,0},{4,7},{5,6},{6,5},{7,4},{8,11},{9,10},{10,... | collective-permute-start | bytes 196616 | tf_op jit(solution)/shard_map/ppermute | solution.py:212
  41.8 6.5 %collective-permute-start.10 = (bf16[32,1024]{1,0:T(8,128)(2,1)S(1)}, bf16[32,1024]{1,0:T(8,128)(2,1)S(1)}, u32[]{:S(2)}, u32[]{:S(2)}) collective-permute-start(bf16[32,1024]{1,0:T(8,128)(2,1)S(1)} %finish.1.refs_0_), channel_id=1, source_target_pairs={{0,2},{1,3},{2,0},{3,1},{4,6},{5,7},{6,4},{7,5},{8,10},{9,11},{10,... | collective-permute-start | bytes 196616 | tf_op jit(solution)/shard_map/ppermute | solution.py:212
  41.8 6.5 %collective-permute-start.9 = (bf16[32,1024]{1,0:T(8,128)(2,1)S(1)}, bf16[32,1024]{1,0:T(8,128)(2,1)S(1)}, u32[]{:S(2)}, u32[]{:S(2)}) collective-permute-start(bf16[32,1024]{1,0:T(8,128)(2,1)S(1)} %finish.1.refs_0_), channel_id=1, source_target_pairs={{0,1},{1,0},{2,3},{3,2},{4,5},{5,4},{6,7},{7,6},{8,9},{9,8},{10,11... | collective-permute-start | bytes 196616 | tf_op jit(solution)/shard_map/ppermute | solution.py:212

commit v4 on v3

--- a/solution.py
+++ b/solution.py
@@ -1,4 +1,5 @@
 import functools
+import math
 
 import jax
 import jax.numpy as jnp
@@ -103,7 +104,8 @@
         pltpu.make_async_copy(k_hbm, k, sems.at[0]),
         pltpu.make_async_copy(v_hbm, v, sems.at[1]),
     ]
-    copies += fetch_pieces(masks, pieces[0].shape[1], w_hbm, pieces, sems, 2)
+    if masks:
+        copies += fetch_pieces(masks, pieces[0].shape[1], w_hbm, pieces, sems, 2)
     for copy in copies:
         copy.start()
     for copy in copies:
@@ -128,7 +130,7 @@
     arrived = refs[:size]
     heads = refs[size]
     pieces = refs[size + 1 : size + 1 + len(masks)]
-    q_rows, o_rows, sems = refs[size + 1 + len(masks) :]
+    q_rows, o_rows, scores, sems = refs[size + 1 + len(masks) :]
     copies = fetch_pieces(masks, pieces[0].shape[1], w_hbm, pieces, sems, 0) if masks else []
     for copy in copies:
         copy.start()
@@ -149,26 +151,36 @@
         q_rows[head] = turn(part).astype(BF16).astype(F32)
     new_keys = turn(summed[:, width : width + HD] * scale).astype(BF16).astype(F32)
     new_values = (summed[:, width + HD : width + 2 * HD] * scale).astype(BF16).astype(F32)
-    factor = HD ** (-0.5)
-    slot = lax.broadcasted_iota(jnp.int32, (group, slots), 1)
+    rate = HD ** (-0.5) * math.log2(math.e)
+    half = slots // 2
+    slot = lax.broadcasted_iota(jnp.int32, (group, half), 1) + half
+    own, top = [], []
     for row in range(rows):
         queries = q_rows[:, row, :]
-        scores = (
-            lax.dot_general(
-                queries.astype(BF16), k[row], (((1,), (1,)), ((), ())), preferred_element_type=F32
-            )
-            * factor
+        mine = slice(row * group, (row + 1) * group)
+        raw = lax.dot_general(
+            queries.astype(BF16), k[row], (((1,), (1,)), ((), ())), preferred_element_type=F32
         )
-        own = jnp.sum(queries * new_keys[row : row + 1], 1, keepdims=True) * factor
-        scores = jnp.where(slot < lengths[row], scores, -jnp.inf)
-        top = jnp.maximum(jnp.max(scores, 1, keepdims=True), own)
-        probs = jnp.exp(scores - top)
-        own_prob = jnp.exp(own - top)
+        low = raw[:, :half]
+        high = jnp.where(slot < lengths[row], raw[:, half:], -jnp.inf)
+        scores[mine, :half] = low
+        scores[mine, half:] = high
+        own.append(jnp.sum(queries * new_keys[row : row + 1], 1, keepdims=True))
+        top.append(jnp.maximum(jnp.max(jnp.maximum(low, high), 1, keepdims=True), own[row]))
+
+    def soften(row):
+        probs = jnp.exp2((scores[row * group : (row + 1) * group] - top[row]) * rate)
+        own_prob = jnp.exp2((own[row] - top[row]) * rate)
         share = 1.0 / (jnp.sum(probs, 1, keepdims=True) + own_prob)
-        weights = (probs * share).astype(BF16)
-        own_weight = (own_prob * share).astype(BF16).astype(F32)
-        mixed = jnp.dot(weights, v[row], preferred_element_type=F32)
-        o_rows[:, row, :] = mixed + own_weight * new_values[row : row + 1]
+        return probs.astype(BF16), own_prob, share
+
+    ready = soften(0)
+    for row in range(rows):
+        probs, own_prob, share = ready
+        if row + 1 < rows:
+            ready = soften(row + 1)
+        mixed = jnp.dot(probs, v[row], preferred_element_type=F32)
+        o_rows[:, row, :] = (mixed + own_prob * new_values[row : row + 1]) * share
     for head in range(group):
         heads[:, head * HD : (head + 1) * HD] = o_rows[head].astype(BF16)
     for copy in copies:
@@ -219,7 +231,7 @@
     sems = lambda n: pltpu.SemaphoreType.DMA((n,))
     order = list(range(size_y - 1, -1, -1))
     quarter = max(size_y // 4, 1)
-    early, middle, late = order[:quarter], order[quarter : 2 * quarter], order[2 * quarter :]
+    early, middle, late = [], order[: 2 * quarter], order[2 * quarter :]
 
     def shards(inputs, gain, w_query, w_key, w_value, w_output, key_cache, value_cache, lengths):
         batch, depth = inputs.shape
@@ -276,6 +288,7 @@
             scratch_shapes=[
                 pltpu.VMEM((width // HD, rows, HD), F32),
                 pltpu.VMEM((width // HD, rows, HD), F32),
+                pltpu.VMEM((rows * (width // HD), key_cache.shape[1]), F32),
                 sems(max(len(middle), 1)),
             ],
             compiler_params=params(8),

time: 49.1 us -> 47.1 us (0.959)
  Pallas kernels: 26.1 us -> 23.9 us
    pallas_call x1, Pallas kernels: 4.69 us -> 3.49 us  [shards(): pl.pallas_call(functools.partial(fetch_caches, early), out_shape=[pltpu.V...]
    pallas_call x1, Pallas kernels: 6.82 us -> 5.81 us  [shards(): pl.pallas_call(functools.partial(attention, size_x, depth * size_x, middl...]
  transfers between devices with their start and end apart: 12 -> 12, of which waited for: 6 -> 5; matrix products, arithmetic and copies ran while one was open for 0% -> 0% of each run, Pallas kernels for 22% -> 20%
where the time goes in v4:
time: 47.1 us; the launch traced here: 46.9 us
  Pallas kernels  23.9 us (51%)
  starting transfers between devices  14.1 us (30%)
  waiting for transfers between devices  8.67 us (18%)
    ppermute x12, starting transfers between devices, swap(): return lax.ppermute(value, axis, [(i, i ^ mask) for i in range(size)])  14.1 us
    ppermute x12, waiting for transfers between devices, swap(): return lax.ppermute(value, axis, [(i, i ^ mask) for i in range(size)])  8.67 us
    pallas_call x1, Pallas kernels, shards(): pl.pallas_call(functools.partial(project, size_x), out_shape=[pltpu.VMEM(...  6.98 us
    pallas_call x1, Pallas kernels, shards(): pl.pallas_call(functools.partial(attention, size_x, depth * size_x, middl...  5.81 us
    pallas_call x1, Pallas kernels, shards(): pl.pallas_call(functools.partial(fetch_weights, late), out_shape=[pltpu.V...  3.53 us
    pallas_call x1, Pallas kernels, shards(): pl.pallas_call(functools.partial(fetch_caches, early), out_shape=[pltpu.V...  3.49 us
    pallas_call x4, Pallas kernels, shards(): pl.pallas_call(functools.partial(project_out, size_x), out_shape=pltpu.VM...  3.27 us
  transfers between devices with their start and end apart: 12, of which 5 were waited for; matrix products, arithmetic and copies ran while one was open for 0% of the time, Pallas kernels for 20%

profile of v4, /device:TPU:0, one launch (start us, length us, event | category | flops | bytes accessed | tf_op | source)
XLA Modules:
  0.0 46.9 jit_solution(12665538260061265911)
XLA Ops:
  0.0 0.0 copy-start
  0.0 7.0 %project.1 = (f32[8,2432]{1,0:T(8,128)S(1)}, f32[8,2432]{1,0:T(8,128)S(1)}, f32[8,2432]{1,0:T(8,128)S(1)}, f32[8,2432]{1,0:T(8,128)S(1)}) custom-call(bf16[32,4096]{1,0:T(8,128)(2,1)} %x_hbm.3, f32[1,4096]{1,0:T(1,128)} %bitcast.1, bf16[4096,2048]{1,0:T(8,128)(2,1)} %wq_hbm.1, bf16[4096,128]{1,0:T(8,128)(2,1)} %wk_hbm.1, bf16[4096,128]{1,0:T(8,128)(2,1)} %wv_hbm.1), custom_call_target="tpu_custom_call" | custom-call | flops 637534208 | bytes 19922944 | tf_op jit(solution)/shard_map/project/pallas_call | solution.py:245
  7.0 0.5 %collective-permute-start = (f32[8,2432]{1,0:T(8,128)S(1)}, f32[8,2432]{1,0:T(8,128)S(1)}, u32[]{:S(2)}, u32[]{:S(2)}) collective-permute-start(f32[8,2432]{1,0:T(8,128)S(1)} %get-tuple-element.20), channel_id=1, source_target_pairs={{0,4},{4,0},{8,12},{12,8},{1,5},{5,1},{9,13},{13,9},{2,6},{6,2},{1... | collective-permute-start | bytes 233480 | tf_op jit(solution)/shard_map/ppermute | solution.py:224
  7.5 2.6 %collective-permute-start.1 = (f32[8,2432]{1,0:T(8,128)S(1)}, f32[8,2432]{1,0:T(8,128)S(1)}, u32[]{:S(2)}, u32[]{:S(2)}) collective-permute-start(f32[8,2432]{1,0:T(8,128)S(1)} %get-tuple-element.21), channel_id=1, source_target_pairs={{0,8},{4,12},{8,0},{12,4},{1,9},{5,13},{9,1},{13,5},{2,10},{6,14},... | collective-permute-start | bytes 233480 | tf_op jit(solution)/shard_map/ppermute | solution.py:224
  10.1 0.1 collective-permute-start.2
  10.2 0.0 copy-done
  10.2 0.1 fusion
  10.3 3.5 %fetch_caches.1 = (bf16[8,2048,128]{2,1,0:T(8,128)(2,1)S(1)}, bf16[8,2048,128]{2,1,0:T(8,128)(2,1)S(1)}) custom-call(f32[8,2432]{1,0:T(8,128)S(1)} %get-tuple-element.17.after.refs_0_, bf16[8,2048,128]{2,1,0:T(8,128)(2,1)} %k_hbm.1, bf16[8,2048,128]{2,1,0:T(8,128)(2,1)} %v_hbm.1, bf16[2048,4096]{1,0:T(8,128)(2,1)} %w_hbm.5), custom_call_target="tpu_custom_call" | custom-call | bytes 8388608 | tf_op jit(solution)/shard_map/fetch_caches/pallas_call | solution.py:266
  13.8 0.1 pad_maximum_fusion
  13.9 0.0 collective-permute-done.refs_1_
  13.9 0.0 collective-permute-done.1.refs_2_
  13.9 0.5 %collective-permute-done.2.refs_3_ = f32[8,2432]{1,0:T(8,128)S(1)} collective-permute-done((f32[8,2432]{1,0:T(8,128)S(1)}, f32[8,2432]{1,0:T(8,128)S(1)}, u32[]{:S(2)}, u32[]{:S(2)}) %collective-permute-start.2) | collective-permute-done | bytes 77856 | tf_op jit(solution)/shard_map/ppermute | solution.py:224
  14.4 5.8 %attention.1 = (bf16[8,2048]{1,0:T(8,128)(2,1)S(1)}, bf16[2048,1024]{1,0:T(8,128)(2,1)S(1)}, bf16[2048,1024]{1,0:T(8,128)(2,1)S(1)}) custom-call(s32[8]{0:T(128)S(1)} %copy-done, f32[8,128]{1,0:T(8,128)S(1)} %get-tuple-element.32.cosine, f32[8,128]{1,0:T(8,128)S(1)} %get-tuple-element.33.sine, bf16[8,2048,128]{2,1,0:T(8,128)(2,1)S(1)} %get-tuple-element.18.k, ...), custom_call_target="tpu_custom_call" | custom-call | flops 134217728 | bytes 8388608 | tf_op jit(solution)/shard_map/attention/pallas_call | solution.py:283
  20.2 1.6 %collective-permute-start.5 = (bf16[8,2048]{1,0:T(8,128)(2,1)S(1)}, bf16[8,2048]{1,0:T(8,128)(2,1)S(1)}, u32[]{:S(2)}, u32[]{:S(2)}) collective-permute-start(bf16[8,2048]{1,0:T(8,128)(2,1)S(1)} %get-tuple-element.23.after.refs_0_), channel_id=1, source_target_pairs={{0,12},{4,8},{8,4},{12,0},{1,13},{5,9},{9,5},{13,1},{2,14},{6,10},... | collective-permute-start | bytes 98312 | tf_op jit(solution)/shard_map/ppermute | solution.py:224
  21.8 0.3 collective-permute-start.4
  22.1 0.1 collective-permute-start.3
  22.1 3.5 %fetch_weights.1 = (bf16[32,1024]{1,0:T(8,128)(2,1)S(1)}, bf16[2048,1024]{1,0:T(8,128)(2,1)S(1)}, bf16[2048,1024]{1,0:T(8,128)(2,1)S(1)}) custom-call(bf16[8,2048]{1,0:T(8,128)(2,1)S(1)} %get-tuple-element.23.after.refs_0_, bf16[32,4096]{1,0:T(8,128)(2,1)} %x_hbm.3, bf16[2048,4096]{1,0:T(8,128)(2,1)} %w_hbm.5), custom_call_target="tpu_custom_call" | custom-call | bytes 8388608 | tf_op jit(solution)/shard_map/fetch_weights/pallas_call | solution.py:309
  25.7 0.0 collective-permute-done.5.refs_3_
  25.7 0.0 collective-permute-done.4.refs_2_
  25.7 0.0 collective-permute-done.3.refs_1_
  25.7 0.8 %project_out.6 = bf16[32,1024]{1,0:T(8,128)(2,1)S(1)} custom-call(bf16[2048,1024]{1,0:T(8,128)(2,1)S(1)} %get-tuple-element.27.w, bf16[8,2048]{1,0:T(8,128)(2,1)S(1)} %get-tuple-element.23.after.refs_0_, bf16[8,2048]{1,0:T(8,128)(2,1)S(1)} %collective-permute-done.3.refs_1_, bf16[8,2048]{1,0:T(8,128)(2,1)S(1)} %collective-permute-done.4.refs_2_, ...), custom_call_target="tpu_custom_call" | custom-call | flops 134217728 | bytes 4194304 | tf_op jit(solution)/shard_map/project_out/pallas_call | solution.py:324
  26.5 3.0 %collective-permute-start.7 = (bf16[32,1024]{1,0:T(8,128)(2,1)S(1)}, bf16[32,1024]{1,0:T(8,128)(2,1)S(1)}, u32[]{:S(2)}, u32[]{:S(2)}) collective-permute-start(bf16[32,1024]{1,0:T(8,128)(2,1)S(1)} %project_out.6), channel_id=1, source_target_pairs={{0,2},{1,3},{2,0},{3,1},{4,6},{5,7},{6,4},{7,5},{8,10},{9,11},{10,... | collective-permute-start | bytes 196616 | tf_op jit(solution)/shard_map/ppermute | solution.py:224
  29.5 0.8 %project_out.7 = bf16[32,1024]{1,0:T(8,128)(2,1)S(1)} custom-call(bf16[2048,1024]{1,0:T(8,128)(2,1)S(1)} %get-tuple-element.28.w, bf16[8,2048]{1,0:T(8,128)(2,1)S(1)} %get-tuple-element.23.after.refs_0_, bf16[8,2048]{1,0:T(8,128)(2,1)S(1)} %collective-permute-done.3.refs_1_, bf16[8,2048]{1,0:T(8,128)(2,1)S(1)} %collective-permute-done.4.refs_2_, ...), custom_call_target="tpu_custom_call" | custom-call | flops 134217728 | bytes 4194304 | tf_op jit(solution)/shard_map/project_out/pallas_call | solution.py:324
  30.3 1.4 %collective-permute-start.8 = (bf16[32,1024]{1,0:T(8,128)(2,1)S(1)}, bf16[32,1024]{1,0:T(8,128)(2,1)S(1)}, u32[]{:S(2)}, u32[]{:S(2)}) collective-permute-start(bf16[32,1024]{1,0:T(8,128)(2,1)S(1)} %project_out.7), channel_id=1, source_target_pairs={{0,3},{1,2},{2,1},{3,0},{4,7},{5,6},{6,5},{7,4},{8,11},{9,10},{10,... | collective-permute-start | bytes 196616 | tf_op jit(solution)/shard_map/ppermute | solution.py:224
  31.7 0.8 %project_out.5 = bf16[32,1024]{1,0:T(8,128)(2,1)S(1)} custom-call(bf16[2048,1024]{1,0:T(8,128)(2,1)S(1)} %get-tuple-element.26.w, bf16[8,2048]{1,0:T(8,128)(2,1)S(1)} %get-tuple-element.23.after.refs_0_, bf16[8,2048]{1,0:T(8,128)(2,1)S(1)} %collective-permute-done.3.refs_1_, bf16[8,2048]{1,0:T(8,128)(2,1)S(1)} %collective-permute-done.4.refs_2_, ...), custom_call_target="tpu_custom_call" | custom-call | flops 134217728 | bytes 4194304 | tf_op jit(solution)/shard_map/project_out/pallas_call | solution.py:324
  32.5 0.2 collective-permute-start.6
  32.8 0.8 %project_out.4.own = f32[32,1024]{1,0:T(8,128)S(1)} custom-call(bf16[2048,1024]{1,0:T(8,128)(2,1)S(1)} %get-tuple-element.25.w, bf16[8,2048]{1,0:T(8,128)(2,1)S(1)} %get-tuple-element.23.after.refs_0_, bf16[8,2048]{1,0:T(8,128)(2,1)S(1)} %collective-permute-done.3.refs_1_, bf16[8,2048]{1,0:T(8,128)(2,1)S(1)} %collective-permute-done.4.refs_2_, ...), custom_call_target="tpu_custom_call" | custom-call | flops 134217728 | bytes 4194304 | tf_op jit(solution)/shard_map/project_out/pallas_call | solution.py:324
  33.6 0.0 collective-permute-done.7.refs_1_
  33.6 3.2 %collective-permute-done.8.refs_2_ = bf16[32,1024]{1,0:T(8,128)(2,1)S(1)} collective-permute-done((bf16[32,1024]{1,0:T(8,128)(2,1)S(1)}, bf16[32,1024]{1,0:T(8,128)(2,1)S(1)}, u32[]{:S(2)}, u32[]{:S(2)}) %collective-permute-start.8) | collective-permute-done | bytes 65568 | tf_op jit(solution)/shard_map/ppermute | solution.py:224
  36.8 0.8 %collective-permute-done.6.refs_0_ = bf16[32,1024]{1,0:T(8,128)(2,1)S(1)} collective-permute-done((bf16[32,1024]{1,0:T(8,128)(2,1)S(1)}, bf16[32,1024]{1,0:T(8,128)(2,1)S(1)}, u32[]{:S(2)}, u32[]{:S(2)}) %collective-permute-start.6) | collective-permute-done | bytes 65568 | tf_op jit(solution)/shard_map/ppermute | solution.py:224
  37.7 2.3 %collective-permute-start.11 = (bf16[32,1024]{1,0:T(8,128)(2,1)S(1)}, bf16[32,1024]{1,0:T(8,128)(2,1)S(1)}, u32[]{:S(2)}, u32[]{:S(2)}) collective-permute-start(bf16[32,1024]{1,0:T(8,128)(2,1)S(1)} %finish.1.refs_0_), channel_id=1, source_target_pairs={{0,3},{1,2},{2,1},{3,0},{4,7},{5,6},{6,5},{7,4},{8,11},{9,10},{10,... | collective-permute-start | bytes 196616 | tf_op jit(solution)/shard_map/ppermute | solution.py:224
  40.0 0.0 collective-permute-start.10
  40.0 2.1 %collective-permute-start.9 = (bf16[32,1024]{1,0:T(8,128)(2,1)S(1)}, bf16[32,1024]{1,0:T(8,128)(2,1)S(1)}, u32[]{:S(2)}, u32[]{:S(2)}) collective-permute-start(bf16[32,1024]{1,0:T(8,128)(2,1)S(1)} %finish.1.refs_0_), channel_id=1, source_target_pairs={{0,1},{1,0},{2,3},{3,2},{4,5},{5,4},{6,7},{7,6},{8,9},{9,8},{10,11... | collective-permute-start | bytes 196616 | tf_op jit(solution)/shard_map/ppermute | solution.py:224
  42.1 2.1 %collective-permute-done.11.refs_3_ = bf16[32,1024]{1,0:T(8,128)(2,1)S(1)} collective-permute-done((bf16[32,1024]{1,0:T(8,128)(2,1)S(1)}, bf16[32,1024]{1,0:T(8,128)(2,1)S(1)}, u32[]{:S(2)}, u32[]{:S(2)}) %collective-permute-start.11) | collective-permute-done | bytes 65568 | tf_op jit(solution)/shard_map/ppermute | solution.py:224
  44.3 2.0 %collective-permute-done.10.refs_2_ = bf16[32,1024]{1,0:T(8,128)(2,1)S(1)} collective-permute-done((bf16[32,1024]{1,0:T(8,128)(2,1)S(1)}, bf16[32,1024]{1,0:T(8,128)(2,1)S(1)}, u32[]{:S(2)}, u32[]{:S(2)}) %collective-permute-start.10) | collective-permute-done | bytes 65568 | tf_op jit(solution)/shard_map/ppermute | solution.py:224
  46.2 0.0 collective-permute-done.9.refs_1_
  46.2 0.7 %assemble.1 = bf16[32,4096]{1,0:T(8,128)(2,1)} custom-call(bf16[32,1024]{1,0:T(8,128)(2,1)S(1)} %finish.1.refs_0_, bf16[32,1024]{1,0:T(8,128)(2,1)S(1)} %collective-permute-done.9.refs_1_, bf16[32,1024]{1,0:T(8,128)(2,1)S(1)} %collective-permute-done.10.refs_2_, bf16[32,1024]{1,0:T(8,128)(2,1)S(1)} %collective-permute-done.11.refs_3_), custom_call_target="tpu_custom_call" | custom-call | tf_op jit(solution)/shard_map/assemble/pallas_call | solution.py:344
  (3 shorter events, 0.1 us)
Async XLA Ops:
  0.0 10.2 %copy-start = (s32[8]{0:T(128)S(1)}, s32[8]{0:T(128)}, u32[]{:S(2)}) copy-start(s32[8]{0:T(128)} %lengths.1) | copy-start | bytes 100
  7.0 6.9 %collective-permute-start = (f32[8,2432]{1,0:T(8,128)S(1)}, f32[8,2432]{1,0:T(8,128)S(1)}, u32[]{:S(2)}, u32[]{:S(2)}) collective-permute-start(f32[8,2432]{1,0:T(8,128)S(1)} %get-tuple-element.20), channel_id=1, source_target_pairs={{0,4},{4,0},{8,12},{12,8},{1,5},{5,1},{9,13},{13,9},{2,6},{6,2},{1... | collective-permute-start | bytes 233480 | tf_op jit(solution)/shard_map/ppermute | solution.py:224
  7.5 6.3 %collective-permute-start.1 = (f32[8,2432]{1,0:T(8,128)S(1)}, f32[8,2432]{1,0:T(8,128)S(1)}, u32[]{:S(2)}, u32[]{:S(2)}) collective-permute-start(f32[8,2432]{1,0:T(8,128)S(1)} %get-tuple-element.21), channel_id=1, source_target_pairs={{0,8},{4,12},{8,0},{12,4},{1,9},{5,13},{9,1},{13,5},{2,10},{6,14},... | collective-permute-start | bytes 233480 | tf_op jit(solution)/shard_map/ppermute | solution.py:224
  10.1 4.3 %collective-permute-start.2 = (f32[8,2432]{1,0:T(8,128)S(1)}, f32[8,2432]{1,0:T(8,128)S(1)}, u32[]{:S(2)}, u32[]{:S(2)}) collective-permute-start(f32[8,2432]{1,0:T(8,128)S(1)} %get-tuple-element.22), channel_id=1, source_target_pairs={{0,12},{4,8},{8,4},{12,0},{1,13},{5,9},{9,5},{13,1},{2,14},{6,10},... | collective-permute-start | bytes 233480 | tf_op jit(solution)/shard_map/ppermute | solution.py:224
  20.2 5.5 %collective-permute-start.5 = (bf16[8,2048]{1,0:T(8,128)(2,1)S(1)}, bf16[8,2048]{1,0:T(8,128)(2,1)S(1)}, u32[]{:S(2)}, u32[]{:S(2)}) collective-permute-start(bf16[8,2048]{1,0:T(8,128)(2,1)S(1)} %get-tuple-element.23.after.refs_0_), channel_id=1, source_target_pairs={{0,12},{4,8},{8,4},{12,0},{1,13},{5,9},{9,5},{13,1},{2,14},{6,10},... | collective-permute-start | bytes 98312 | tf_op jit(solution)/shard_map/ppermute | solution.py:224
  21.8 3.9 %collective-permute-start.4 = (bf16[8,2048]{1,0:T(8,128)(2,1)S(1)}, bf16[8,2048]{1,0:T(8,128)(2,1)S(1)}, u32[]{:S(2)}, u32[]{:S(2)}) collective-permute-start(bf16[8,2048]{1,0:T(8,128)(2,1)S(1)} %get-tuple-element.23.after.refs_0_), channel_id=1, source_target_pairs={{0,8},{4,12},{8,0},{12,4},{1,9},{5,13},{9,1},{13,5},{2,10},{6,14},... | collective-permute-start | bytes 98312 | tf_op jit(solution)/shard_map/ppermute | solution.py:224
  22.1 3.6 %collective-permute-start.3 = (bf16[8,2048]{1,0:T(8,128)(2,1)S(1)}, bf16[8,2048]{1,0:T(8,128)(2,1)S(1)}, u32[]{:S(2)}, u32[]{:S(2)}) collective-permute-start(bf16[8,2048]{1,0:T(8,128)(2,1)S(1)} %get-tuple-element.23.after.refs_0_), channel_id=1, source_target_pairs={{0,4},{4,0},{8,12},{12,8},{1,5},{5,1},{9,13},{13,9},{2,6},{6,2},{1... | collective-permute-start | bytes 98312 | tf_op jit(solution)/shard_map/ppermute | solution.py:224
  26.5 7.1 %collective-permute-start.7 = (bf16[32,1024]{1,0:T(8,128)(2,1)S(1)}, bf16[32,1024]{1,0:T(8,128)(2,1)S(1)}, u32[]{:S(2)}, u32[]{:S(2)}) collective-permute-start(bf16[32,1024]{1,0:T(8,128)(2,1)S(1)} %project_out.6), channel_id=1, source_target_pairs={{0,2},{1,3},{2,0},{3,1},{4,6},{5,7},{6,4},{7,5},{8,10},{9,11},{10,... | collective-permute-start | bytes 196616 | tf_op jit(solution)/shard_map/ppermute | solution.py:224
  30.3 6.5 %collective-permute-start.8 = (bf16[32,1024]{1,0:T(8,128)(2,1)S(1)}, bf16[32,1024]{1,0:T(8,128)(2,1)S(1)}, u32[]{:S(2)}, u32[]{:S(2)}) collective-permute-start(bf16[32,1024]{1,0:T(8,128)(2,1)S(1)} %project_out.7), channel_id=1, source_target_pairs={{0,3},{1,2},{2,1},{3,0},{4,7},{5,6},{6,5},{7,4},{8,11},{9,10},{10,... | collective-permute-start | bytes 196616 | tf_op jit(solution)/shard_map/ppermute | solution.py:224
  32.5 5.1 %collective-permute-start.6 = (bf16[32,1024]{1,0:T(8,128)(2,1)S(1)}, bf16[32,1024]{1,0:T(8,128)(2,1)S(1)}, u32[]{:S(2)}, u32[]{:S(2)}) collective-permute-start(bf16[32,1024]{1,0:T(8,128)(2,1)S(1)} %project_out.5), channel_id=1, source_target_pairs={{0,1},{1,0},{2,3},{3,2},{4,5},{5,4},{6,7},{7,6},{8,9},{9,8},{10,11... | collective-permute-start | bytes 196616 | tf_op jit(solution)/shard_map/ppermute | solution.py:224
  37.7 6.6 %collective-permute-start.11 = (bf16[32,1024]{1,0:T(8,128)(2,1)S(1)}, bf16[32,1024]{1,0:T(8,128)(2,1)S(1)}, u32[]{:S(2)}, u32[]{:S(2)}) collective-permute-start(bf16[32,1024]{1,0:T(8,128)(2,1)S(1)} %finish.1.refs_0_), channel_id=1, source_target_pairs={{0,3},{1,2},{2,1},{3,0},{4,7},{5,6},{6,5},{7,4},{8,11},{9,10},{10,... | collective-permute-start | bytes 196616 | tf_op jit(solution)/shard_map/ppermute | solution.py:224
  40.0 6.2 %collective-permute-start.10 = (bf16[32,1024]{1,0:T(8,128)(2,1)S(1)}, bf16[32,1024]{1,0:T(8,128)(2,1)S(1)}, u32[]{:S(2)}, u32[]{:S(2)}) collective-permute-start(bf16[32,1024]{1,0:T(8,128)(2,1)S(1)} %finish.1.refs_0_), channel_id=1, source_target_pairs={{0,2},{1,3},{2,0},{3,1},{4,6},{5,7},{6,4},{7,5},{8,10},{9,11},{10,... | collective-permute-start | bytes 196616 | tf_op jit(solution)/shard_map/ppermute | solution.py:224
  40.0 6.2 %collective-permute-start.9 = (bf16[32,1024]{1,0:T(8,128)(2,1)S(1)}, bf16[32,1024]{1,0:T(8,128)(2,1)S(1)}, u32[]{:S(2)}, u32[]{:S(2)}) collective-permute-start(bf16[32,1024]{1,0:T(8,128)(2,1)S(1)} %finish.1.refs_0_), channel_id=1, source_target_pairs={{0,1},{1,0},{2,3},{3,2},{4,5},{5,4},{6,7},{7,6},{8,9},{9,8},{10,11... | collective-permute-start | bytes 196616 | tf_op jit(solution)/shard_map/ppermute | solution.py:224

commit v5 on v3

--- a/solution.py
+++ b/solution.py
@@ -1,4 +1,5 @@
 import functools
+import math
 
 import jax
 import jax.numpy as jnp
@@ -103,7 +104,8 @@
         pltpu.make_async_copy(k_hbm, k, sems.at[0]),
         pltpu.make_async_copy(v_hbm, v, sems.at[1]),
     ]
-    copies += fetch_pieces(masks, pieces[0].shape[1], w_hbm, pieces, sems, 2)
+    if masks:
+        copies += fetch_pieces(masks, pieces[0].shape[1], w_hbm, pieces, sems, 2)
     for copy in copies:
         copy.start()
     for copy in copies:
@@ -128,13 +130,14 @@
     arrived = refs[:size]
     heads = refs[size]
     pieces = refs[size + 1 : size + 1 + len(masks)]
-    q_rows, o_rows, sems = refs[size + 1 + len(masks) :]
+    q_rows, o_rows, blocks, scores, weights, sems = refs[size + 1 + len(masks) :]
     copies = fetch_pieces(masks, pieces[0].shape[1], w_hbm, pieces, sems, 0) if masks else []
     for copy in copies:
         copy.start()
     rows, slots = k.shape[0], k.shape[1]
     group = heads.shape[1] // HD
     width = group * HD
+    lanes = rows * group
     summed = arrived[0][...]
     for item in arrived[1:]:
         summed = summed + item[...].astype(F32)
@@ -146,29 +149,53 @@
 
     for head in range(group):
         part = summed[:, head * HD : (head + 1) * HD] * scale
-        q_rows[head] = turn(part).astype(BF16).astype(F32)
-    new_keys = turn(summed[:, width : width + HD] * scale).astype(BF16).astype(F32)
+        q_rows[head] = turn(part)
+    new_keys = turn(summed[:, width : width + HD] * scale).astype(BF16)
     new_values = (summed[:, width + HD : width + 2 * HD] * scale).astype(BF16).astype(F32)
-    factor = HD ** (-0.5)
-    slot = lax.broadcasted_iota(jnp.int32, (group, slots), 1)
+    queries = jnp.concatenate([q_rows[:, row, :] for row in range(rows)], 0).T.astype(BF16)
+
+    owner = lax.broadcasted_iota(jnp.int32, (1, lanes), 1) // group
+    limits = jnp.zeros((1, lanes), jnp.int32)
     for row in range(rows):
-        queries = q_rows[:, row, :]
-        scores = (
-            lax.dot_general(
-                queries.astype(BF16), k[row], (((1,), (1,)), ((), ())), preferred_element_type=F32
-            )
-            * factor
-        )
-        own = jnp.sum(queries * new_keys[row : row + 1], 1, keepdims=True) * factor
-        scores = jnp.where(slot < lengths[row], scores, -jnp.inf)
-        top = jnp.maximum(jnp.max(scores, 1, keepdims=True), own)
-        probs = jnp.exp(scores - top)
-        own_prob = jnp.exp(own - top)
-        share = 1.0 / (jnp.sum(probs, 1, keepdims=True) + own_prob)
-        weights = (probs * share).astype(BF16)
-        own_weight = (own_prob * share).astype(BF16).astype(F32)
-        mixed = jnp.dot(weights, v[row], preferred_element_type=F32)
-        o_rows[:, row, :] = mixed + own_weight * new_values[row : row + 1]
+        limits = jnp.where(owner == row, lengths[row], limits)
+        blocks[row * HD : (row + 1) * HD] = jnp.where(owner == row, queries, 0).astype(BF16)
+    flat = jnp.concatenate([new_keys[row : row + 1] for row in range(rows)], 1)
+    own = jnp.dot(
+        jnp.broadcast_to(flat.astype(F32), (16, rows * HD)).astype(BF16),
+        blocks[...],
+        preferred_element_type=F32,
+    )[:1]
+
+    rate = HD ** (-0.5) * math.log2(math.e)
+    top = jnp.full((8, lanes), -jnp.inf, F32)
+    slot = lax.broadcasted_iota(jnp.int32, (CHUNK, lanes), 0)
+    for start in range(0, slots, CHUNK):
+        part = slice(start, start + CHUNK)
+        keys = jnp.concatenate([k[row, part] for row in range(rows)], 1)
+        raw = jnp.dot(keys, blocks[...], preferred_element_type=F32)
+        if start + CHUNK > slots // 2:
+            raw = jnp.where(slot + start < limits, raw, -jnp.inf)
+        scores[part] = raw
+        top = jnp.maximum(top, jnp.max(raw.reshape(CHUNK // 8, 8, lanes), 0))
+    top = jnp.maximum(jnp.max(top, 0, keepdims=True), own)
+    total = jnp.zeros((8, lanes), F32)
+    for start in range(0, slots, CHUNK):
+        part = slice(start, start + CHUNK)
+        probs = jnp.exp2((scores[part] - top) * rate)
+        total = total + jnp.sum(probs.reshape(CHUNK // 8, 8, lanes), 0)
+        weights[:, part] = probs.T.astype(BF16)
+    own_prob = jnp.exp2((own - top) * rate)
+    share = 1.0 / (jnp.sum(total, 0, keepdims=True) + own_prob)
+    tall = jnp.concatenate([share, own_prob * share, jnp.zeros((6, lanes), F32)], 0).T
+    for row in range(0, rows, 2):
+        pair = slice(row * group, (row + 2) * group)
+        both = jnp.concatenate([v[row], v[row + 1]], 1)
+        mixed = jnp.dot(weights[pair], both, preferred_element_type=F32)
+        for side in range(2):
+            mine = slice((row + side) * group, (row + side + 1) * group)
+            value = mixed[side * group : (side + 1) * group, side * HD : (side + 1) * HD]
+            extra = tall[mine, 1:2] * new_values[row + side : row + side + 1]
+            o_rows[:, row + side, :] = value * tall[mine, :1] + extra
     for head in range(group):
         heads[:, head * HD : (head + 1) * HD] = o_rows[head].astype(BF16)
     for copy in copies:
@@ -219,12 +246,13 @@
     sems = lambda n: pltpu.SemaphoreType.DMA((n,))
     order = list(range(size_y - 1, -1, -1))
     quarter = max(size_y // 4, 1)
-    early, middle, late = order[:quarter], order[quarter : 2 * quarter], order[2 * quarter :]
+    early, middle, late = [], order[: 2 * quarter], order[2 * quarter :]
 
     def shards(inputs, gain, w_query, w_key, w_value, w_output, key_cache, value_cache, lengths):
         batch, depth = inputs.shape
         width = w_query.shape[1]
         rows = key_cache.shape[0]
+        lanes = rows * (width // HD)
         packed = width + 3 * HD
         block = w_output.shape[1] // size_y
         piece = pltpu.VMEM((width, block), BF16)
@@ -276,6 +304,9 @@
             scratch_shapes=[
                 pltpu.VMEM((width // HD, rows, HD), F32),
                 pltpu.VMEM((width // HD, rows, HD), F32),
+                pltpu.VMEM((rows * HD, lanes), BF16),
+                pltpu.VMEM((key_cache.shape[1], lanes), F32),
+                pltpu.VMEM((lanes, key_cache.shape[1]), BF16),
                 sems(max(len(middle), 1)),
             ],
             compiler_params=params(8),

time: 49.1 us -> 47.7 us (0.971)
  Pallas kernels: 26.1 us -> 24.4 us
    pallas_call x1, Pallas kernels: 4.69 us -> 3.49 us  [shards(): pl.pallas_call(functools.partial(fetch_caches, early), out_shape=[pltpu.V...]
  transfers between devices with their start and end apart: 12 -> 12, of which waited for: 6 -> 5; matrix products, arithmetic and copies ran while one was open for 0% -> 0% of each run, Pallas kernels for 22% -> 20%
where the time goes in v5:
time: 47.7 us; the launch traced here: 47.6 us
  Pallas kernels  24.4 us (51%)
  starting transfers between devices  14.1 us (30%)
  waiting for transfers between devices  8.81 us (18%)
    ppermute x12, starting transfers between devices, swap(): return lax.ppermute(value, axis, [(i, i ^ mask) for i in range(size)])  14.1 us
    ppermute x12, waiting for transfers between devices, swap(): return lax.ppermute(value, axis, [(i, i ^ mask) for i in range(size)])  8.81 us
    pallas_call x1, Pallas kernels, shards(): pl.pallas_call(functools.partial(project, size_x), out_shape=[pltpu.VMEM(...  6.98 us
    pallas_call x1, Pallas kernels, shards(): pl.pallas_call(functools.partial(attention, size_x, depth * size_x, middl...  6.33 us
    pallas_call x1, Pallas kernels, shards(): pl.pallas_call(functools.partial(fetch_weights, late), out_shape=[pltpu.V...  3.53 us
    pallas_call x1, Pallas kernels, shards(): pl.pallas_call(functools.partial(fetch_caches, early), out_shape=[pltpu.V...  3.49 us
    pallas_call x4, Pallas kernels, shards(): pl.pallas_call(functools.partial(project_out, size_x), out_shape=pltpu.VM...  3.27 us
  transfers between devices with their start and end apart: 12, of which 5 were waited for; matrix products, arithmetic and copies ran while one was open for 0% of the time, Pallas kernels for 20%

profile of v5, /device:TPU:0, one launch (start us, length us, event | category | flops | bytes accessed | tf_op | source)
XLA Modules:
  0.0 47.6 jit_solution(1773585148816200290)
XLA Ops:
  0.0 0.0 copy-start
  0.0 7.0 %project.1 = (f32[8,2432]{1,0:T(8,128)S(1)}, f32[8,2432]{1,0:T(8,128)S(1)}, f32[8,2432]{1,0:T(8,128)S(1)}, f32[8,2432]{1,0:T(8,128)S(1)}) custom-call(bf16[32,4096]{1,0:T(8,128)(2,1)} %x_hbm.3, f32[1,4096]{1,0:T(1,128)} %bitcast.1, bf16[4096,2048]{1,0:T(8,128)(2,1)} %wq_hbm.1, bf16[4096,128]{1,0:T(8,128)(2,1)} %wk_hbm.1, bf16[4096,128]{1,0:T(8,128)(2,1)} %wv_hbm.1), custom_call_target="tpu_custom_call" | custom-call | flops 637534208 | bytes 19922944 | tf_op jit(solution)/shard_map/project/pallas_call | solution.py:261
  7.0 0.5 %collective-permute-start = (f32[8,2432]{1,0:T(8,128)S(1)}, f32[8,2432]{1,0:T(8,128)S(1)}, u32[]{:S(2)}, u32[]{:S(2)}) collective-permute-start(f32[8,2432]{1,0:T(8,128)S(1)} %get-tuple-element.20), channel_id=1, source_target_pairs={{0,4},{4,0},{8,12},{12,8},{1,5},{5,1},{9,13},{13,9},{2,6},{6,2},{1... | collective-permute-start | bytes 233480 | tf_op jit(solution)/shard_map/ppermute | solution.py:239
  7.5 2.6 %collective-permute-start.1 = (f32[8,2432]{1,0:T(8,128)S(1)}, f32[8,2432]{1,0:T(8,128)S(1)}, u32[]{:S(2)}, u32[]{:S(2)}) collective-permute-start(f32[8,2432]{1,0:T(8,128)S(1)} %get-tuple-element.21), channel_id=1, source_target_pairs={{0,8},{4,12},{8,0},{12,4},{1,9},{5,13},{9,1},{13,5},{2,10},{6,14},... | collective-permute-start | bytes 233480 | tf_op jit(solution)/shard_map/ppermute | solution.py:239
  10.1 0.1 collective-permute-start.2
  10.2 0.0 copy-done
  10.2 0.1 fusion
  10.3 3.5 %fetch_caches.1 = (bf16[8,2048,128]{2,1,0:T(8,128)(2,1)S(1)}, bf16[8,2048,128]{2,1,0:T(8,128)(2,1)S(1)}) custom-call(f32[8,2432]{1,0:T(8,128)S(1)} %get-tuple-element.17.after.refs_0_, bf16[8,2048,128]{2,1,0:T(8,128)(2,1)} %k_hbm.1, bf16[8,2048,128]{2,1,0:T(8,128)(2,1)} %v_hbm.1, bf16[2048,4096]{1,0:T(8,128)(2,1)} %w_hbm.5), custom_call_target="tpu_custom_call" | custom-call | bytes 8388608 | tf_op jit(solution)/shard_map/fetch_caches/pallas_call | solution.py:282
  13.8 0.1 pad_maximum_fusion
  13.9 0.0 collective-permute-done.refs_1_
  13.9 0.0 collective-permute-done.1.refs_2_
  13.9 0.5 %collective-permute-done.2.refs_3_ = f32[8,2432]{1,0:T(8,128)S(1)} collective-permute-done((f32[8,2432]{1,0:T(8,128)S(1)}, f32[8,2432]{1,0:T(8,128)S(1)}, u32[]{:S(2)}, u32[]{:S(2)}) %collective-permute-start.2) | collective-permute-done | bytes 77856 | tf_op jit(solution)/shard_map/ppermute | solution.py:239
  14.4 6.3 %attention.1 = (bf16[8,2048]{1,0:T(8,128)(2,1)S(1)}, bf16[2048,1024]{1,0:T(8,128)(2,1)S(1)}, bf16[2048,1024]{1,0:T(8,128)(2,1)S(1)}) custom-call(s32[8]{0:T(128)S(1)} %copy-done, f32[8,128]{1,0:T(8,128)S(1)} %get-tuple-element.32.cosine, f32[8,128]{1,0:T(8,128)S(1)} %get-tuple-element.33.sine, bf16[8,2048,128]{2,1,0:T(8,128)(2,1)S(1)} %get-tuple-element.18.k, ...), custom_call_target="tpu_custom_call" | custom-call | flops 134217728 | bytes 8388608 | tf_op jit(solution)/shard_map/attention/pallas_call | solution.py:299
  20.7 1.6 %collective-permute-start.5 = (bf16[8,2048]{1,0:T(8,128)(2,1)S(1)}, bf16[8,2048]{1,0:T(8,128)(2,1)S(1)}, u32[]{:S(2)}, u32[]{:S(2)}) collective-permute-start(bf16[8,2048]{1,0:T(8,128)(2,1)S(1)} %get-tuple-element.23.after.refs_0_), channel_id=1, source_target_pairs={{0,12},{4,8},{8,4},{12,0},{1,13},{5,9},{9,5},{13,1},{2,14},{6,10},... | collective-permute-start | bytes 98312 | tf_op jit(solution)/shard_map/ppermute | solution.py:239
  22.3 0.3 collective-permute-start.4
  22.6 0.1 collective-permute-start.3
  22.7 3.5 %fetch_weights.1 = (bf16[32,1024]{1,0:T(8,128)(2,1)S(1)}, bf16[2048,1024]{1,0:T(8,128)(2,1)S(1)}, bf16[2048,1024]{1,0:T(8,128)(2,1)S(1)}) custom-call(bf16[8,2048]{1,0:T(8,128)(2,1)S(1)} %get-tuple-element.23.after.refs_0_, bf16[32,4096]{1,0:T(8,128)(2,1)} %x_hbm.3, bf16[2048,4096]{1,0:T(8,128)(2,1)} %w_hbm.5), custom_call_target="tpu_custom_call" | custom-call | bytes 8388608 | tf_op jit(solution)/shard_map/fetch_weights/pallas_call | solution.py:327
  26.2 0.0 collective-permute-done.5.refs_3_
  26.2 0.0 collective-permute-done.4.refs_2_
  26.2 0.0 collective-permute-done.3.refs_1_
  26.2 0.8 %project_out.6 = bf16[32,1024]{1,0:T(8,128)(2,1)S(1)} custom-call(bf16[2048,1024]{1,0:T(8,128)(2,1)S(1)} %get-tuple-element.27.w, bf16[8,2048]{1,0:T(8,128)(2,1)S(1)} %get-tuple-element.23.after.refs_0_, bf16[8,2048]{1,0:T(8,128)(2,1)S(1)} %collective-permute-done.3.refs_1_, bf16[8,2048]{1,0:T(8,128)(2,1)S(1)} %collective-permute-done.4.refs_2_, ...), custom_call_target="tpu_custom_call" | custom-call | flops 134217728 | bytes 4194304 | tf_op jit(solution)/shard_map/project_out/pallas_call | solution.py:342
  27.0 2.9 %collective-permute-start.7 = (bf16[32,1024]{1,0:T(8,128)(2,1)S(1)}, bf16[32,1024]{1,0:T(8,128)(2,1)S(1)}, u32[]{:S(2)}, u32[]{:S(2)}) collective-permute-start(bf16[32,1024]{1,0:T(8,128)(2,1)S(1)} %project_out.6), channel_id=1, source_target_pairs={{0,2},{1,3},{2,0},{3,1},{4,6},{5,7},{6,4},{7,5},{8,10},{9,11},{10,... | collective-permute-start | bytes 196616 | tf_op jit(solution)/shard_map/ppermute | solution.py:239
  30.0 0.8 %project_out.7 = bf16[32,1024]{1,0:T(8,128)(2,1)S(1)} custom-call(bf16[2048,1024]{1,0:T(8,128)(2,1)S(1)} %get-tuple-element.28.w, bf16[8,2048]{1,0:T(8,128)(2,1)S(1)} %get-tuple-element.23.after.refs_0_, bf16[8,2048]{1,0:T(8,128)(2,1)S(1)} %collective-permute-done.3.refs_1_, bf16[8,2048]{1,0:T(8,128)(2,1)S(1)} %collective-permute-done.4.refs_2_, ...), custom_call_target="tpu_custom_call" | custom-call | flops 134217728 | bytes 4194304 | tf_op jit(solution)/shard_map/project_out/pallas_call | solution.py:342
  30.8 1.4 %collective-permute-start.8 = (bf16[32,1024]{1,0:T(8,128)(2,1)S(1)}, bf16[32,1024]{1,0:T(8,128)(2,1)S(1)}, u32[]{:S(2)}, u32[]{:S(2)}) collective-permute-start(bf16[32,1024]{1,0:T(8,128)(2,1)S(1)} %project_out.7), channel_id=1, source_target_pairs={{0,3},{1,2},{2,1},{3,0},{4,7},{5,6},{6,5},{7,4},{8,11},{9,10},{10,... | collective-permute-start | bytes 196616 | tf_op jit(solution)/shard_map/ppermute | solution.py:239
  32.2 0.8 %project_out.5 = bf16[32,1024]{1,0:T(8,128)(2,1)S(1)} custom-call(bf16[2048,1024]{1,0:T(8,128)(2,1)S(1)} %get-tuple-element.26.w, bf16[8,2048]{1,0:T(8,128)(2,1)S(1)} %get-tuple-element.23.after.refs_0_, bf16[8,2048]{1,0:T(8,128)(2,1)S(1)} %collective-permute-done.3.refs_1_, bf16[8,2048]{1,0:T(8,128)(2,1)S(1)} %collective-permute-done.4.refs_2_, ...), custom_call_target="tpu_custom_call" | custom-call | flops 134217728 | bytes 4194304 | tf_op jit(solution)/shard_map/project_out/pallas_call | solution.py:342
  33.0 0.3 collective-permute-start.6
  33.3 0.8 %project_out.4.own = f32[32,1024]{1,0:T(8,128)S(1)} custom-call(bf16[2048,1024]{1,0:T(8,128)(2,1)S(1)} %get-tuple-element.25.w, bf16[8,2048]{1,0:T(8,128)(2,1)S(1)} %get-tuple-element.23.after.refs_0_, bf16[8,2048]{1,0:T(8,128)(2,1)S(1)} %collective-permute-done.3.refs_1_, bf16[8,2048]{1,0:T(8,128)(2,1)S(1)} %collective-permute-done.4.refs_2_, ...), custom_call_target="tpu_custom_call" | custom-call | flops 134217728 | bytes 4194304 | tf_op jit(solution)/shard_map/project_out/pallas_call | solution.py:342
  34.1 0.0 collective-permute-done.7.refs_1_
  34.1 3.2 %collective-permute-done.8.refs_2_ = bf16[32,1024]{1,0:T(8,128)(2,1)S(1)} collective-permute-done((bf16[32,1024]{1,0:T(8,128)(2,1)S(1)}, bf16[32,1024]{1,0:T(8,128)(2,1)S(1)}, u32[]{:S(2)}, u32[]{:S(2)}) %collective-permute-start.8) | collective-permute-done | bytes 65568 | tf_op jit(solution)/shard_map/ppermute | solution.py:239
  37.3 0.9 %collective-permute-done.6.refs_0_ = bf16[32,1024]{1,0:T(8,128)(2,1)S(1)} collective-permute-done((bf16[32,1024]{1,0:T(8,128)(2,1)S(1)}, bf16[32,1024]{1,0:T(8,128)(2,1)S(1)}, u32[]{:S(2)}, u32[]{:S(2)}) %collective-permute-start.6) | collective-permute-done | bytes 65568 | tf_op jit(solution)/shard_map/ppermute | solution.py:239
  38.2 2.3 %collective-permute-start.11 = (bf16[32,1024]{1,0:T(8,128)(2,1)S(1)}, bf16[32,1024]{1,0:T(8,128)(2,1)S(1)}, u32[]{:S(2)}, u32[]{:S(2)}) collective-permute-start(bf16[32,1024]{1,0:T(8,128)(2,1)S(1)} %finish.1.refs_0_), channel_id=1, source_target_pairs={{0,3},{1,2},{2,1},{3,0},{4,7},{5,6},{6,5},{7,4},{8,11},{9,10},{10,... | collective-permute-start | bytes 196616 | tf_op jit(solution)/shard_map/ppermute | solution.py:239
  40.5 0.0 collective-permute-start.10
  40.6 2.1 %collective-permute-start.9 = (bf16[32,1024]{1,0:T(8,128)(2,1)S(1)}, bf16[32,1024]{1,0:T(8,128)(2,1)S(1)}, u32[]{:S(2)}, u32[]{:S(2)}) collective-permute-start(bf16[32,1024]{1,0:T(8,128)(2,1)S(1)} %finish.1.refs_0_), channel_id=1, source_target_pairs={{0,1},{1,0},{2,3},{3,2},{4,5},{5,4},{6,7},{7,6},{8,9},{9,8},{10,11... | collective-permute-start | bytes 196616 | tf_op jit(solution)/shard_map/ppermute | solution.py:239
  42.7 2.2 %collective-permute-done.11.refs_3_ = bf16[32,1024]{1,0:T(8,128)(2,1)S(1)} collective-permute-done((bf16[32,1024]{1,0:T(8,128)(2,1)S(1)}, bf16[32,1024]{1,0:T(8,128)(2,1)S(1)}, u32[]{:S(2)}, u32[]{:S(2)}) %collective-permute-start.11) | collective-permute-done | bytes 65568 | tf_op jit(solution)/shard_map/ppermute | solution.py:239
  44.9 2.0 %collective-permute-done.10.refs_2_ = bf16[32,1024]{1,0:T(8,128)(2,1)S(1)} collective-permute-done((bf16[32,1024]{1,0:T(8,128)(2,1)S(1)}, bf16[32,1024]{1,0:T(8,128)(2,1)S(1)}, u32[]{:S(2)}, u32[]{:S(2)}) %collective-permute-start.10) | collective-permute-done | bytes 65568 | tf_op jit(solution)/shard_map/ppermute | solution.py:239
  46.9 0.0 collective-permute-done.9.refs_1_
  46.9 0.7 %assemble.1 = bf16[32,4096]{1,0:T(8,128)(2,1)} custom-call(bf16[32,1024]{1,0:T(8,128)(2,1)S(1)} %finish.1.refs_0_, bf16[32,1024]{1,0:T(8,128)(2,1)S(1)} %collective-permute-done.9.refs_1_, bf16[32,1024]{1,0:T(8,128)(2,1)S(1)} %collective-permute-done.10.refs_2_, bf16[32,1024]{1,0:T(8,128)(2,1)S(1)} %collective-permute-done.11.refs_3_), custom_call_target="tpu_custom_call" | custom-call | tf_op jit(solution)/shard_map/assemble/pallas_call | solution.py:362
  (3 shorter events, 0.1 us)
Async XLA Ops:
  0.0 10.2 %copy-start = (s32[8]{0:T(128)S(1)}, s32[8]{0:T(128)}, u32[]{:S(2)}) copy-start(s32[8]{0:T(128)} %lengths.1) | copy-start | bytes 100
  7.0 6.9 %collective-permute-start = (f32[8,2432]{1,0:T(8,128)S(1)}, f32[8,2432]{1,0:T(8,128)S(1)}, u32[]{:S(2)}, u32[]{:S(2)}) collective-permute-start(f32[8,2432]{1,0:T(8,128)S(1)} %get-tuple-element.20), channel_id=1, source_target_pairs={{0,4},{4,0},{8,12},{12,8},{1,5},{5,1},{9,13},{13,9},{2,6},{6,2},{1... | collective-permute-start | bytes 233480 | tf_op jit(solution)/shard_map/ppermute | solution.py:239
  7.5 6.3 %collective-permute-start.1 = (f32[8,2432]{1,0:T(8,128)S(1)}, f32[8,2432]{1,0:T(8,128)S(1)}, u32[]{:S(2)}, u32[]{:S(2)}) collective-permute-start(f32[8,2432]{1,0:T(8,128)S(1)} %get-tuple-element.21), channel_id=1, source_target_pairs={{0,8},{4,12},{8,0},{12,4},{1,9},{5,13},{9,1},{13,5},{2,10},{6,14},... | collective-permute-start | bytes 233480 | tf_op jit(solution)/shard_map/ppermute | solution.py:239
  10.1 4.3 %collective-permute-start.2 = (f32[8,2432]{1,0:T(8,128)S(1)}, f32[8,2432]{1,0:T(8,128)S(1)}, u32[]{:S(2)}, u32[]{:S(2)}) collective-permute-start(f32[8,2432]{1,0:T(8,128)S(1)} %get-tuple-element.22), channel_id=1, source_target_pairs={{0,12},{4,8},{8,4},{12,0},{1,13},{5,9},{9,5},{13,1},{2,14},{6,10},... | collective-permute-start | bytes 233480 | tf_op jit(solution)/shard_map/ppermute | solution.py:239
  20.7 5.5 %collective-permute-start.5 = (bf16[8,2048]{1,0:T(8,128)(2,1)S(1)}, bf16[8,2048]{1,0:T(8,128)(2,1)S(1)}, u32[]{:S(2)}, u32[]{:S(2)}) collective-permute-start(bf16[8,2048]{1,0:T(8,128)(2,1)S(1)} %get-tuple-element.23.after.refs_0_), channel_id=1, source_target_pairs={{0,12},{4,8},{8,4},{12,0},{1,13},{5,9},{9,5},{13,1},{2,14},{6,10},... | collective-permute-start | bytes 98312 | tf_op jit(solution)/shard_map/ppermute | solution.py:239
  22.3 3.9 %collective-permute-start.4 = (bf16[8,2048]{1,0:T(8,128)(2,1)S(1)}, bf16[8,2048]{1,0:T(8,128)(2,1)S(1)}, u32[]{:S(2)}, u32[]{:S(2)}) collective-permute-start(bf16[8,2048]{1,0:T(8,128)(2,1)S(1)} %get-tuple-element.23.after.refs_0_), channel_id=1, source_target_pairs={{0,8},{4,12},{8,0},{12,4},{1,9},{5,13},{9,1},{13,5},{2,10},{6,14},... | collective-permute-start | bytes 98312 | tf_op jit(solution)/shard_map/ppermute | solution.py:239
  22.6 3.6 %collective-permute-start.3 = (bf16[8,2048]{1,0:T(8,128)(2,1)S(1)}, bf16[8,2048]{1,0:T(8,128)(2,1)S(1)}, u32[]{:S(2)}, u32[]{:S(2)}) collective-permute-start(bf16[8,2048]{1,0:T(8,128)(2,1)S(1)} %get-tuple-element.23.after.refs_0_), channel_id=1, source_target_pairs={{0,4},{4,0},{8,12},{12,8},{1,5},{5,1},{9,13},{13,9},{2,6},{6,2},{1... | collective-permute-start | bytes 98312 | tf_op jit(solution)/shard_map/ppermute | solution.py:239
  27.0 7.1 %collective-permute-start.7 = (bf16[32,1024]{1,0:T(8,128)(2,1)S(1)}, bf16[32,1024]{1,0:T(8,128)(2,1)S(1)}, u32[]{:S(2)}, u32[]{:S(2)}) collective-permute-start(bf16[32,1024]{1,0:T(8,128)(2,1)S(1)} %project_out.6), channel_id=1, source_target_pairs={{0,2},{1,3},{2,0},{3,1},{4,6},{5,7},{6,4},{7,5},{8,10},{9,11},{10,... | collective-permute-start | bytes 196616 | tf_op jit(solution)/shard_map/ppermute | solution.py:239
  30.8 6.5 %collective-permute-start.8 = (bf16[32,1024]{1,0:T(8,128)(2,1)S(1)}, bf16[32,1024]{1,0:T(8,128)(2,1)S(1)}, u32[]{:S(2)}, u32[]{:S(2)}) collective-permute-start(bf16[32,1024]{1,0:T(8,128)(2,1)S(1)} %project_out.7), channel_id=1, source_target_pairs={{0,3},{1,2},{2,1},{3,0},{4,7},{5,6},{6,5},{7,4},{8,11},{9,10},{10,... | collective-permute-start | bytes 196616 | tf_op jit(solution)/shard_map/ppermute | solution.py:239
  33.0 5.2 %collective-permute-start.6 = (bf16[32,1024]{1,0:T(8,128)(2,1)S(1)}, bf16[32,1024]{1,0:T(8,128)(2,1)S(1)}, u32[]{:S(2)}, u32[]{:S(2)}) collective-permute-start(bf16[32,1024]{1,0:T(8,128)(2,1)S(1)} %project_out.5), channel_id=1, source_target_pairs={{0,1},{1,0},{2,3},{3,2},{4,5},{5,4},{6,7},{7,6},{8,9},{9,8},{10,11... | collective-permute-start | bytes 196616 | tf_op jit(solution)/shard_map/ppermute | solution.py:239
  38.2 6.7 %collective-permute-start.11 = (bf16[32,1024]{1,0:T(8,128)(2,1)S(1)}, bf16[32,1024]{1,0:T(8,128)(2,1)S(1)}, u32[]{:S(2)}, u32[]{:S(2)}) collective-permute-start(bf16[32,1024]{1,0:T(8,128)(2,1)S(1)} %finish.1.refs_0_), channel_id=1, source_target_pairs={{0,3},{1,2},{2,1},{3,0},{4,7},{5,6},{6,5},{7,4},{8,11},{9,10},{10,... | collective-permute-start | bytes 196616 | tf_op jit(solution)/shard_map/ppermute | solution.py:239
  40.5 6.3 %collective-permute-start.10 = (bf16[32,1024]{1,0:T(8,128)(2,1)S(1)}, bf16[32,1024]{1,0:T(8,128)(2,1)S(1)}, u32[]{:S(2)}, u32[]{:S(2)}) collective-permute-start(bf16[32,1024]{1,0:T(8,128)(2,1)S(1)} %finish.1.refs_0_), channel_id=1, source_target_pairs={{0,2},{1,3},{2,0},{3,1},{4,6},{5,7},{6,4},{7,5},{8,10},{9,11},{10,... | collective-permute-start | bytes 196616 | tf_op jit(solution)/shard_map/ppermute | solution.py:239
  40.6 6.3 %collective-permute-start.9 = (bf16[32,1024]{1,0:T(8,128)(2,1)S(1)}, bf16[32,1024]{1,0:T(8,128)(2,1)S(1)}, u32[]{:S(2)}, u32[]{:S(2)}) collective-permute-start(bf16[32,1024]{1,0:T(8,128)(2,1)S(1)} %finish.1.refs_0_), channel_id=1, source_target_pairs={{0,1},{1,0},{2,3},{3,2},{4,5},{5,4},{6,7},{7,6},{8,9},{9,8},{10,11... | collective-permute-start | bytes 196616 | tf_op jit(solution)/shard_map/ppermute | solution.py:239

commit v6 on v4

--- a/solution.py
+++ b/solution.py
@@ -42,8 +42,7 @@
 
 
 def project(size, x_hbm, gain_hbm, wq_hbm, wk_hbm, wv_hbm, *refs):
-    outs = refs[:size]
-    x, gain, wq, wk, wv, scaled, total, sems = refs[size:]
+    kept, given, x, gain, wq, wk, wv, scaled, total, sems = refs
     depth = x.shape[1]
     steps = depth // CHUNK
     pairs = [(x_hbm, x), (gain_hbm, gain), (wk_hbm, wk), (wv_hbm, wv)]
@@ -81,11 +80,17 @@
             small[3].wait()
             total[:, width + HD : width + 2 * HD] = dot(scaled[...], wv[...])
             total[:, width + 2 * HD :] = jnp.broadcast_to(squares, (squares.shape[0], HD))
-    rows = outs[0].shape[0]
+    rows = kept.shape[1]
     me = lax.axis_index("gx")
     for mask in range(size):
+        out = given if mask % 2 else kept
         start = pl.multiple_of((me ^ mask) * rows, 8)
-        outs[mask][...] = total[pl.ds(start, rows), :].astype(outs[mask].dtype)
+        out[mask // 2] = total[pl.ds(start, rows), :]
+
+
+def merge(kept, arrived, *outs):
+    for index, out in enumerate(outs):
+        out[...] = kept[index] + arrived[index]
 
 
 def fetch_pieces(masks, width, w_hbm, pieces, sems, first):
@@ -112,14 +117,10 @@
         copy.wait()
 
 
-def fetch_weights(masks, after, x_hbm, w_hbm, x, *refs):
+def fetch_weights(masks, after, w_hbm, *refs):
     del after
     *pieces, sems = refs
-    width = x.shape[1]
-    copies = [
-        pltpu.make_async_copy(x_hbm.at[:, columns(lax.axis_index("gy"), width)], x, sems.at[0])
-    ]
-    copies += fetch_pieces(masks, width, w_hbm, pieces, sems, 1)
+    copies = fetch_pieces(masks, pieces[0].shape[1], w_hbm, pieces, sems, 0)
     for copy in copies:
         copy.start()
     for copy in copies:
@@ -153,57 +154,107 @@
     new_values = (summed[:, width + HD : width + 2 * HD] * scale).astype(BF16).astype(F32)
     rate = HD ** (-0.5) * math.log2(math.e)
     half = slots // 2
-    slot = lax.broadcasted_iota(jnp.int32, (group, half), 1) + half
+    slot = lax.broadcasted_iota(jnp.int32, (2 * group, half), 1) + half
+    second = lax.broadcasted_iota(jnp.int32, (2 * group, 1), 0) >= group
+    empty = jnp.zeros((group, HD), F32)
     own, top = [], []
-    for row in range(rows):
-        queries = q_rows[:, row, :]
-        mine = slice(row * group, (row + 1) * group)
+    for row in range(0, rows, 2):
+        first, other = q_rows[:, row, :], q_rows[:, row + 1, :]
+        queries = jnp.concatenate(
+            [jnp.concatenate([first, empty], 1), jnp.concatenate([empty, other], 1)], 0
+        )
+        keys = jnp.concatenate([k[row], k[row + 1]], 1)
         raw = lax.dot_general(
-            queries.astype(BF16), k[row], (((1,), (1,)), ((), ())), preferred_element_type=F32
+            queries.astype(BF16), keys, (((1,), (1,)), ((), ())), preferred_element_type=F32
         )
         low = raw[:, :half]
-        high = jnp.where(slot < lengths[row], raw[:, half:], -jnp.inf)
+        limit = jnp.where(second, lengths[row + 1], lengths[row])
+        high = jnp.where(slot < limit, raw[:, half:], -jnp.inf)
+        mine = slice(row * group, (row + 2) * group)
         scores[mine, :half] = low
         scores[mine, half:] = high
-        own.append(jnp.sum(queries * new_keys[row : row + 1], 1, keepdims=True))
-        top.append(jnp.maximum(jnp.max(jnp.maximum(low, high), 1, keepdims=True), own[row]))
-
-    def soften(row):
-        probs = jnp.exp2((scores[row * group : (row + 1) * group] - top[row]) * rate)
-        own_prob = jnp.exp2((own[row] - top[row]) * rate)
+        both = jnp.concatenate(
+            [first * new_keys[row : row + 1], other * new_keys[row + 1 : row + 2]], 0
+        )
+        own.append(jnp.sum(both, 1, keepdims=True))
+        top.append(jnp.maximum(jnp.max(jnp.maximum(low, high), 1, keepdims=True), own[-1]))
+
+    def soften(pair):
+        mine = slice(2 * pair * group, (2 * pair + 2) * group)
+        probs = jnp.exp2((scores[mine] - top[pair]) * rate)
+        own_prob = jnp.exp2((own[pair] - top[pair]) * rate)
         share = 1.0 / (jnp.sum(probs, 1, keepdims=True) + own_prob)
         return probs.astype(BF16), own_prob, share
 
     ready = soften(0)
-    for row in range(rows):
+    for pair in range(rows // 2):
         probs, own_prob, share = ready
-        if row + 1 < rows:
-            ready = soften(row + 1)
-        mixed = jnp.dot(probs, v[row], preferred_element_type=F32)
-        o_rows[:, row, :] = (mixed + own_prob * new_values[row : row + 1]) * share
+        if pair + 1 < rows // 2:
+            ready = soften(pair + 1)
+        sides = jnp.concatenate([v[2 * pair], v[2 * pair + 1]], 1)
+        mixed = jnp.dot(probs, sides, preferred_element_type=F32)
+        for side in range(2):
+            row = 2 * pair + side
+            mine = slice(side * group, (side + 1) * group)
+            value = mixed[mine, side * HD : (side + 1) * HD]
+            extra = own_prob[mine] * new_values[row : row + 1]
+            o_rows[:, row, :] = (value + extra) * share[mine]
     for head in range(group):
         heads[:, head * HD : (head + 1) * HD] = o_rows[head].astype(BF16)
     for copy in copies:
         copy.wait()
 
 
-def project_out(size, w, *refs):
-    blocks, out, gathered = refs[:size], refs[size], refs[size + 1]
+def gather_rows(blocks, gathered):
     me = lax.axis_index("gx")
     rows = blocks[0].shape[0]
-    for mask in range(size):
-        gathered[pl.ds(pl.multiple_of((me ^ mask) * rows, 8), rows), :] = blocks[mask][...].astype(F32)
-    out[...] = jnp.dot(
-        gathered[...].astype(BF16), w[...], preferred_element_type=F32
-    ).astype(out.dtype)
-
-
-def finish(x, own, *refs):
+    for mask, block in enumerate(blocks):
+        start = pl.multiple_of((me ^ mask) * rows, 8)
+        gathered[pl.ds(start, rows), :] = block[...].astype(F32)
+    return gathered[...].astype(BF16)
+
+
+def project_out(size, w, *refs):
+    blocks, out, gathered = refs[:size], refs[-2], refs[-1]
+    heads = gather_rows(blocks, gathered)
+    out[...] = jnp.dot(heads, w[...], preferred_element_type=F32).astype(out.dtype)
+
+
+def stream_out(size, mask, w_hbm, x_hbm, *refs):
+    blocks = refs[:size]
+    out, gathered, w, x, sems = refs[-5:]
+    width = out.shape[1]
+    me = lax.axis_index("gy")
+    steps = w.shape[0] // (2 * CHUNK)
+    copies = []
+    for step in range(steps):
+        part = pl.ds(step * 2 * CHUNK, 2 * CHUNK)
+        source = w_hbm.at[part, columns(me ^ mask, width)]
+        copies.append(pltpu.make_async_copy(source, w.at[part], sems.at[step]))
+    if not mask:
+        source = x_hbm.at[:, columns(me, width)]
+        copies.append(pltpu.make_async_copy(source, x, sems.at[steps]))
+    for copy in copies:
+        copy.start()
+    heads = gather_rows(blocks, gathered)
+    total = None
+    for step in range(steps):
+        copies[step].wait()
+        part = slice(step * 2 * CHUNK, (step + 1) * 2 * CHUNK)
+        term = jnp.dot(heads[:, part], w[part], preferred_element_type=F32)
+        total = term if total is None else total + term
+    if not mask:
+        copies[steps].wait()
+        total = total + x[...].astype(F32)
+    out[...] = total.astype(out.dtype)
+
+
+def finish(own, *refs):
     *arrived, out = refs
     total = own[...]
     for item in arrived:
         total = total + item[...].astype(F32)
-    out[...] = (x[...].astype(F32) + total).astype(BF16)
+    out[...] = total.astype(BF16)
 
 
 def assemble(size, *refs):
@@ -231,7 +282,7 @@
     sems = lambda n: pltpu.SemaphoreType.DMA((n,))
     order = list(range(size_y - 1, -1, -1))
     quarter = max(size_y // 4, 1)
-    early, middle, late = [], order[: 2 * quarter], order[2 * quarter :]
+    early, middle, late = [], order[: 2 * quarter], order[2 * quarter : -1]
 
     def shards(inputs, gain, w_query, w_key, w_value, w_output, key_cache, value_cache, lengths):
         batch, depth = inputs.shape
@@ -242,11 +293,12 @@
         piece = pltpu.VMEM((width, block), BF16)
         piece_bytes = 2 * width * block
 
-        sums = pl.pallas_call(
+        levels = size_x // 2
+        kept, given = pl.pallas_call(
             functools.partial(project, size_x),
-            out_shape=[pltpu.VMEM((rows, packed), F32)] * size_x,
+            out_shape=[pltpu.VMEM((levels, rows, packed), F32)] * 2,
             in_specs=[ANY] * 5,
-            out_specs=[VMEM] * size_x,
+            out_specs=[VMEM] * 2,
             scratch_shapes=[
                 pltpu.VMEM(inputs.shape, BF16),
                 pltpu.VMEM((1, depth), F32),
@@ -261,7 +313,15 @@
             cost_estimate=cost(2 * batch * depth * packed, 2 * depth * packed),
             name="project",
         )(*[in_hbm(a) for a in (inputs, gain.reshape(1, depth), w_query, w_key, w_value)])
-        arrived = [sums[0]] + [swap(sums[m], "gx", size_x, m) for m in range(1, size_x)]
+        sums = pl.pallas_call(
+            merge,
+            out_shape=[pltpu.VMEM((rows, packed), F32)] * levels,
+            in_specs=[VMEM] * 2,
+            out_specs=[VMEM] * levels,
+            compiler_params=params(4),
+            name="merge",
+        )(in_vmem(kept), in_vmem(swap(given, "gx", size_x, 1)))
+        arrived = [sums[0]] + [swap(sums[j], "gx", size_x, 2 * j) for j in range(1, levels)]
 
         fetched = pl.pallas_call(
             functools.partial(fetch_caches, early),
@@ -281,9 +341,9 @@
         angles = lengths.astype(F32)[:, None] * inverse[None, :]
         cosine, sine = jnp.cos(angles), jnp.sin(angles)
         heads, *more = pl.pallas_call(
-            functools.partial(attention, size_x, depth * size_x, middle),
+            functools.partial(attention, levels, depth * size_x, middle),
             out_shape=[pltpu.VMEM((rows, width), BF16)] + [piece] * len(middle),
-            in_specs=[SMEM, VMEM, VMEM, VMEM, VMEM, ANY] + [VMEM] * size_x,
+            in_specs=[SMEM, VMEM, VMEM, VMEM, VMEM, ANY] + [VMEM] * levels,
             out_specs=[VMEM] * (1 + len(middle)),
             scratch_shapes=[
                 pltpu.VMEM((width // HD, rows, HD), F32),
@@ -306,40 +366,59 @@
         pieces += more
         gathered = [heads] + [swap(heads, "gx", size_x, m) for m in range(1, size_x)]
 
-        residual, *more = pl.pallas_call(
+        pieces += pl.pallas_call(
             functools.partial(fetch_weights, late),
-            out_shape=[pltpu.VMEM((batch, block), BF16)] + [piece] * len(late),
-            in_specs=[ANY] * 3,
-            out_specs=[VMEM] * (1 + len(late)),
-            scratch_shapes=[sems(1 + len(late))],
+            out_shape=[piece] * len(late),
+            in_specs=[ANY] * 2,
+            out_specs=[VMEM] * len(late),
+            scratch_shapes=[sems(len(late))],
             compiler_params=params(4),
             cost_estimate=cost(0, piece_bytes * len(late)),
             name="fetch_weights",
-        )(heads, in_hbm(inputs), in_hbm(w_output))
-        pieces += more
+        )(heads, in_hbm(w_output))
 
         terms = {}
-        for mask, w in zip(order, pieces):
+        for index, mask in enumerate(order):
             kind = BF16 if mask else F32
-            term = pl.pallas_call(
-                functools.partial(project_out, size_x),
+            ready = index < len(pieces)
+            shared = dict(
                 out_shape=pltpu.VMEM((batch, block), kind),
-                in_specs=[VMEM] * (1 + size_x),
                 out_specs=VMEM,
-                scratch_shapes=[pltpu.VMEM((batch, width), F32)],
-                compiler_params=params(8),
+                compiler_params=params(12),
                 cost_estimate=cost(2 * batch * width * block, piece_bytes),
-                name="project_out",
-            )(in_vmem(w), *[in_vmem(a) for a in gathered])
+            )
+            rows_in = [in_vmem(a) for a in gathered]
+            scratch = [pltpu.VMEM((batch, width), F32)]
+            if ready:
+                term = pl.pallas_call(
+                    functools.partial(project_out, size_x),
+                    in_specs=[VMEM] * (1 + size_x),
+                    scratch_shapes=scratch,
+                    name="project_out",
+                    **shared,
+                )(in_vmem(pieces[index]), *rows_in)
+            else:
+                scratch += [
+                    pltpu.VMEM((width, block), BF16),
+                    pltpu.VMEM((batch, block), BF16),
+                    sems(width // (2 * CHUNK) + 1),
+                ]
+                term = pl.pallas_call(
+                    functools.partial(stream_out, size_x, mask),
+                    in_specs=[ANY] * 2 + [VMEM] * size_x,
+                    scratch_shapes=scratch,
+                    name="stream_out",
+                    **shared,
+                )(in_hbm(w_output), in_hbm(inputs), *rows_in)
             terms[mask] = swap(term, "gy", size_y, mask) if mask else term
         done = pl.pallas_call(
             finish,
             out_shape=pltpu.VMEM((batch, block), BF16),
-            in_specs=[VMEM] * (1 + size_y),
+            in_specs=[VMEM] * size_y,
             out_specs=VMEM,
             compiler_params=params(4),
             name="finish",
-        )(in_vmem(residual), *[in_vmem(terms[m]) for m in range(size_y)])
+        )(*[in_vmem(terms[m]) for m in range(size_y)])
         blocks = [done] + [swap(done, "gy", size_y, m) for m in range(1, size_y)]
         return pl.pallas_call(
             functools.partial(assemble, size_y),

time: 47.1 us -> 45.8 us (0.972)
  waiting for transfers between devices: 8.67 us -> 6.83 us
  Pallas kernels: 23.9 us -> 24.5 us
    ppermute x12 -> x11, waiting for transfers between devices: 8.67 us -> 6.83 us  [swap(): return lax.ppermute(value, axis, [(i, i ^ mask) for i in range(size)])]
    pallas_call x6 -> x7, Pallas kernels: 12.6 us -> 13.3 us  [the longest x1 6.09 us: shards(): pl.pallas_call(functools.partial(attention, levels, depth * size_x, middl...]
    ppermute x12 -> x11, starting transfers between devices: 14.1 us -> 14 us  [swap(): return lax.ppermute(value, axis, [(i, i ^ mask) for i in range(size)])]
  transfers between devices with their start and end apart: 12 -> 11, of which waited for: 5 -> 6; matrix products, arithmetic and copies ran while one was open for 0% -> 0% of each run, Pallas kernels for 20% -> 22%
where the time goes in v6:
time: 45.8 us; the launch traced here: 45.7 us
  Pallas kernels  24.5 us (53%)
  starting transfers between devices  14 us (31%)
  waiting for transfers between devices  6.83 us (15%)
    ppermute x11, starting transfers between devices, swap(): return lax.ppermute(value, axis, [(i, i ^ mask) for i in range(size)])  14 us
    pallas_call x1, Pallas kernels, shards(): pl.pallas_call(functools.partial(project, size_x), out_shape=[pltpu.VMEM(...  6.98 us
    ppermute x11, waiting for transfers between devices, swap(): return lax.ppermute(value, axis, [(i, i ^ mask) for i in range(size)])  6.83 us
    pallas_call x1, Pallas kernels, shards(): pl.pallas_call(functools.partial(attention, levels, depth * size_x, middl...  6.09 us
    pallas_call x1, Pallas kernels, shards(): pl.pallas_call(functools.partial(fetch_caches, early), out_shape=[pltpu.V...  3.48 us
    pallas_call x1, Pallas kernels, shards(): pl.pallas_call(functools.partial(stream_out, size_x, mask), in_specs=[ANY...  2.53 us
    pallas_call x3, Pallas kernels, shards(): pl.pallas_call(functools.partial(project_out, size_x), in_specs=[VMEM] *...  2.45 us
    pallas_call x1, Pallas kernels, shards(): pl.pallas_call(functools.partial(fetch_weights, late), out_shape=[piece]...  2.2 us
  transfers between devices with their start and end apart: 11, of which 6 were waited for; matrix products, arithmetic and copies ran while one was open for 0% of the time, Pallas kernels for 22%

profile of v6, /device:TPU:0, one launch (start us, length us, event | category | flops | bytes accessed | tf_op | source)
XLA Modules:
  0.0 45.7 jit_solution(18310428322521206748)
XLA Ops:
  0.0 0.0 copy-start
  0.0 7.0 %project.1 = (f32[2,8,2432]{2,1,0:T(8,128)S(1)}, f32[2,8,2432]{2,1,0:T(8,128)S(1)}) custom-call(bf16[32,4096]{1,0:T(8,128)(2,1)} %x_hbm.3, f32[1,4096]{1,0:T(1,128)} %bitcast.1, bf16[4096,2048]{1,0:T(8,128)(2,1)} %wq_hbm.1, bf16[4096,128]{1,0:T(8,128)(2,1)} %wk_hbm.1, bf16[4096,128]{1,0:T(8,128)(2,1)} %wv_hbm.1), custom_call_target="tpu_custom_call" | custom-call | flops 637534208 | bytes 19922944 | tf_op jit(solution)/shard_map/project/pallas_call | solution.py:297
  7.0 0.5 %collective-permute-start = (f32[2,8,2432]{2,1,0:T(8,128)S(1)}, f32[2,8,2432]{2,1,0:T(8,128)S(1)}, u32[]{:S(2)}, u32[]{:S(2)}) collective-permute-start(f32[2,8,2432]{2,1,0:T(8,128)S(1)} %get-tuple-element.15), channel_id=1, source_target_pairs={{0,4},{4,0},{8,12},{12,8},{1,5},{5,1},{9,13},{13,9},{2,6},{6,2},{1... | collective-permute-start | bytes 466952 | tf_op jit(solution)/shard_map/ppermute | solution.py:275
  7.5 0.0 copy-done
  7.5 0.1 fusion
  7.6 0.9 %collective-permute-done.arrived = f32[2,8,2432]{2,1,0:T(8,128)S(1)} collective-permute-done((f32[2,8,2432]{2,1,0:T(8,128)S(1)}, f32[2,8,2432]{2,1,0:T(8,128)S(1)}, u32[]{:S(2)}, u32[]{:S(2)}) %collective-permute-start) | collective-permute-done | bytes 155680 | tf_op jit(solution)/shard_map/ppermute | solution.py:275
  8.6 2.9 %collective-permute-start.1 = (f32[8,2432]{1,0:T(8,128)S(1)}, f32[8,2432]{1,0:T(8,128)S(1)}, u32[]{:S(2)}, u32[]{:S(2)}) collective-permute-start(f32[8,2432]{1,0:T(8,128)S(1)} %get-tuple-element.19), channel_id=1, source_target_pairs={{0,8},{4,12},{8,0},{12,4},{1,9},{5,13},{9,1},{13,5},{2,10},{6,14},... | collective-permute-start | bytes 233480 | tf_op jit(solution)/shard_map/ppermute | solution.py:275
  11.5 0.1 pad_maximum_fusion
  11.5 3.5 %fetch_caches.1 = (bf16[8,2048,128]{2,1,0:T(8,128)(2,1)S(1)}, bf16[8,2048,128]{2,1,0:T(8,128)(2,1)S(1)}) custom-call(f32[8,2432]{1,0:T(8,128)S(1)} %get-tuple-element.16.after.refs_0_, bf16[8,2048,128]{2,1,0:T(8,128)(2,1)} %k_hbm.1, bf16[8,2048,128]{2,1,0:T(8,128)(2,1)} %v_hbm.1, bf16[2048,4096]{1,0:T(8,128)(2,1)} %w_hbm.7), custom_call_target="tpu_custom_call" | custom-call | bytes 8388608 | tf_op jit(solution)/shard_map/fetch_caches/pallas_call | solution.py:326
  15.0 0.0 collective-permute-done.1.refs_1_
  15.0 6.1 %attention.1 = (bf16[8,2048]{1,0:T(8,128)(2,1)S(1)}, bf16[2048,1024]{1,0:T(8,128)(2,1)S(1)}, bf16[2048,1024]{1,0:T(8,128)(2,1)S(1)}) custom-call(s32[8]{0:T(128)S(1)} %copy-done, f32[8,128]{1,0:T(8,128)S(1)} %get-tuple-element.26.cosine, f32[8,128]{1,0:T(8,128)S(1)} %get-tuple-element.27.sine, bf16[8,2048,128]{2,1,0:T(8,128)(2,1)S(1)} %get-tuple-element.17.k, ...), custom_call_target="tpu_custom_call" | custom-call | flops 134217728 | bytes 8388608 | tf_op jit(solution)/shard_map/attention/pallas_call | solution.py:343
  21.1 0.1 collective-permute-start.4
  21.2 1.5 %collective-permute-start.3 = (bf16[8,2048]{1,0:T(8,128)(2,1)S(1)}, bf16[8,2048]{1,0:T(8,128)(2,1)S(1)}, u32[]{:S(2)}, u32[]{:S(2)}) collective-permute-start(bf16[8,2048]{1,0:T(8,128)(2,1)S(1)} %get-tuple-element.20.refs_0_.after), channel_id=1, source_target_pairs={{0,8},{4,12},{8,0},{12,4},{1,9},{5,13},{9,1},{13,5},{2,10},{6,14},... | collective-permute-start | bytes 98312 | tf_op jit(solution)/shard_map/ppermute | solution.py:275
  22.7 0.4 collective-permute-start.2
  23.1 2.2 %fetch_weights.1.w = bf16[2048,1024]{1,0:T(8,128)(2,1)S(1)} custom-call(bf16[8,2048]{1,0:T(8,128)(2,1)S(1)} %get-tuple-element.20.refs_0_.after, bf16[2048,4096]{1,0:T(8,128)(2,1)} %w_hbm.7), custom_call_target="tpu_custom_call" | custom-call | bytes 4194304 | tf_op jit(solution)/shard_map/fetch_weights/pallas_call | solution.py:369
  25.3 0.0 collective-permute-done.4.refs_3_
  25.3 0.3 collective-permute-done.3.refs_2_
  25.6 0.0 collective-permute-done.2.refs_1_
  25.6 0.8 %project_out.4 = bf16[32,1024]{1,0:T(8,128)(2,1)S(1)} custom-call(bf16[2048,1024]{1,0:T(8,128)(2,1)S(1)} %get-tuple-element.21.w, bf16[8,2048]{1,0:T(8,128)(2,1)S(1)} %get-tuple-element.20.refs_0_.after, bf16[8,2048]{1,0:T(8,128)(2,1)S(1)} %collective-permute-done.2.refs_1_, bf16[8,2048]{1,0:T(8,128)(2,1)S(1)} %collective-permute-done.3.refs_2_, ...), custom_call_target="tpu_custom_call" | custom-call | flops 134217728 | bytes 4194304 | tf_op jit(solution)/shard_map/project_out/pallas_call | solution.py:393
  26.4 2.6 %collective-permute-start.6 = (bf16[32,1024]{1,0:T(8,128)(2,1)S(1)}, bf16[32,1024]{1,0:T(8,128)(2,1)S(1)}, u32[]{:S(2)}, u32[]{:S(2)}) collective-permute-start(bf16[32,1024]{1,0:T(8,128)(2,1)S(1)} %project_out.4), channel_id=1, source_target_pairs={{0,2},{1,3},{2,0},{3,1},{4,6},{5,7},{6,4},{7,5},{8,10},{9,11},{10,... | collective-permute-start | bytes 196616 | tf_op jit(solution)/shard_map/ppermute | solution.py:275
  29.0 0.8 %project_out.5 = bf16[32,1024]{1,0:T(8,128)(2,1)S(1)} custom-call(bf16[2048,1024]{1,0:T(8,128)(2,1)S(1)} %get-tuple-element.22.w, bf16[8,2048]{1,0:T(8,128)(2,1)S(1)} %get-tuple-element.20.refs_0_.after, bf16[8,2048]{1,0:T(8,128)(2,1)S(1)} %collective-permute-done.2.refs_1_, bf16[8,2048]{1,0:T(8,128)(2,1)S(1)} %collective-permute-done.3.refs_2_, ...), custom_call_target="tpu_custom_call" | custom-call | flops 134217728 | bytes 4194304 | tf_op jit(solution)/shard_map/project_out/pallas_call | solution.py:393
  29.9 1.4 %collective-permute-start.7 = (bf16[32,1024]{1,0:T(8,128)(2,1)S(1)}, bf16[32,1024]{1,0:T(8,128)(2,1)S(1)}, u32[]{:S(2)}, u32[]{:S(2)}) collective-permute-start(bf16[32,1024]{1,0:T(8,128)(2,1)S(1)} %project_out.5), channel_id=1, source_target_pairs={{0,3},{1,2},{2,1},{3,0},{4,7},{5,6},{6,5},{7,4},{8,11},{9,10},{10,... | collective-permute-start | bytes 196616 | tf_op jit(solution)/shard_map/ppermute | solution.py:275
  31.2 0.8 %project_out.3 = bf16[32,1024]{1,0:T(8,128)(2,1)S(1)} custom-call(bf16[2048,1024]{1,0:T(8,128)(2,1)S(1)} %fetch_weights.1.w, bf16[8,2048]{1,0:T(8,128)(2,1)S(1)} %get-tuple-element.20.refs_0_.after, bf16[8,2048]{1,0:T(8,128)(2,1)S(1)} %collective-permute-done.2.refs_1_, bf16[8,2048]{1,0:T(8,128)(2,1)S(1)} %collective-permute-done.3.refs_2_, ...), custom_call_target="tpu_custom_call" | custom-call | flops 134217728 | bytes 4194304 | tf_op jit(solution)/shard_map/project_out/pallas_call | solution.py:393
  32.0 0.3 collective-permute-start.5
  32.3 2.5 %stream_out.1.own = f32[32,1024]{1,0:T(8,128)S(1)} custom-call(bf16[2048,4096]{1,0:T(8,128)(2,1)} %w_hbm.7, bf16[32,4096]{1,0:T(8,128)(2,1)} %x_hbm.3, bf16[8,2048]{1,0:T(8,128)(2,1)S(1)} %get-tuple-element.20.refs_0_.after, bf16[8,2048]{1,0:T(8,128)(2,1)S(1)} %collective-permute-done.2.refs_1_, bf16[8,2048]{1,0:T(8,128)(2,1)S(1)} %collective-permute-done.3.refs_2_, ...), custom_call_target="tpu_custom_call" | custom-call | flops 134217728 | bytes 4194304 | tf_op jit(solution)/shard_map/stream_out/pallas_call | solution.py:406
  34.8 0.0 collective-permute-done.6.refs_1_
  34.8 1.7 %collective-permute-done.7.refs_2_ = bf16[32,1024]{1,0:T(8,128)(2,1)S(1)} collective-permute-done((bf16[32,1024]{1,0:T(8,128)(2,1)S(1)}, bf16[32,1024]{1,0:T(8,128)(2,1)S(1)}, u32[]{:S(2)}, u32[]{:S(2)}) %collective-permute-start.7) | collective-permute-done | bytes 65568 | tf_op jit(solution)/shard_map/ppermute | solution.py:275
  36.6 0.3 collective-permute-done.5.refs_0_
  36.9 2.3 %collective-permute-start.10 = (bf16[32,1024]{1,0:T(8,128)(2,1)S(1)}, bf16[32,1024]{1,0:T(8,128)(2,1)S(1)}, u32[]{:S(2)}, u32[]{:S(2)}) collective-permute-start(bf16[32,1024]{1,0:T(8,128)(2,1)S(1)} %finish.1.refs_0_), channel_id=1, source_target_pairs={{0,3},{1,2},{2,1},{3,0},{4,7},{5,6},{6,5},{7,4},{8,11},{9,10},{10,... | collective-permute-start | bytes 196616 | tf_op jit(solution)/shard_map/ppermute | solution.py:275
  39.2 0.0 collective-permute-start.9
  39.2 2.1 %collective-permute-start.8 = (bf16[32,1024]{1,0:T(8,128)(2,1)S(1)}, bf16[32,1024]{1,0:T(8,128)(2,1)S(1)}, u32[]{:S(2)}, u32[]{:S(2)}) collective-permute-start(bf16[32,1024]{1,0:T(8,128)(2,1)S(1)} %finish.1.refs_0_), channel_id=1, source_target_pairs={{0,1},{1,0},{2,3},{3,2},{4,5},{5,4},{6,7},{7,6},{8,9},{9,8},{10,11... | collective-permute-start | bytes 196616 | tf_op jit(solution)/shard_map/ppermute | solution.py:275
  41.4 1.7 %collective-permute-done.10.refs_3_ = bf16[32,1024]{1,0:T(8,128)(2,1)S(1)} collective-permute-done((bf16[32,1024]{1,0:T(8,128)(2,1)S(1)}, bf16[32,1024]{1,0:T(8,128)(2,1)S(1)}, u32[]{:S(2)}, u32[]{:S(2)}) %collective-permute-start.10) | collective-permute-done | bytes 65568 | tf_op jit(solution)/shard_map/ppermute | solution.py:275
  43.0 1.9 %collective-permute-done.9.refs_2_ = bf16[32,1024]{1,0:T(8,128)(2,1)S(1)} collective-permute-done((bf16[32,1024]{1,0:T(8,128)(2,1)S(1)}, bf16[32,1024]{1,0:T(8,128)(2,1)S(1)}, u32[]{:S(2)}, u32[]{:S(2)}) %collective-permute-start.9) | collective-permute-done | bytes 65568 | tf_op jit(solution)/shard_map/ppermute | solution.py:275
  45.0 0.0 collective-permute-done.8.refs_1_
  45.0 0.7 %assemble.1 = bf16[32,4096]{1,0:T(8,128)(2,1)} custom-call(bf16[32,1024]{1,0:T(8,128)(2,1)S(1)} %finish.1.refs_0_, bf16[32,1024]{1,0:T(8,128)(2,1)S(1)} %collective-permute-done.8.refs_1_, bf16[32,1024]{1,0:T(8,128)(2,1)S(1)} %collective-permute-done.9.refs_2_, bf16[32,1024]{1,0:T(8,128)(2,1)S(1)} %collective-permute-done.10.refs_3_), custom_call_target="tpu_custom_call" | custom-call | tf_op jit(solution)/shard_map/assemble/pallas_call | solution.py:423
  (4 shorter events, 0.1 us)
Async XLA Ops:
  0.0 7.5 %copy-start = (s32[8]{0:T(128)S(1)}, s32[8]{0:T(128)}, u32[]{:S(2)}) copy-start(s32[8]{0:T(128)} %lengths.1) | copy-start | bytes 100
  7.0 1.5 %collective-permute-start = (f32[2,8,2432]{2,1,0:T(8,128)S(1)}, f32[2,8,2432]{2,1,0:T(8,128)S(1)}, u32[]{:S(2)}, u32[]{:S(2)}) collective-permute-start(f32[2,8,2432]{2,1,0:T(8,128)S(1)} %get-tuple-element.15), channel_id=1, source_target_pairs={{0,4},{4,0},{8,12},{12,8},{1,5},{5,1},{9,13},{13,9},{2,6},{6,2},{1... | collective-permute-start | bytes 466952 | tf_op jit(solution)/shard_map/ppermute | solution.py:275
  8.6 6.5 %collective-permute-start.1 = (f32[8,2432]{1,0:T(8,128)S(1)}, f32[8,2432]{1,0:T(8,128)S(1)}, u32[]{:S(2)}, u32[]{:S(2)}) collective-permute-start(f32[8,2432]{1,0:T(8,128)S(1)} %get-tuple-element.19), channel_id=1, source_target_pairs={{0,8},{4,12},{8,0},{12,4},{1,9},{5,13},{9,1},{13,5},{2,10},{6,14},... | collective-permute-start | bytes 233480 | tf_op jit(solution)/shard_map/ppermute | solution.py:275
  21.1 4.1 %collective-permute-start.4 = (bf16[8,2048]{1,0:T(8,128)(2,1)S(1)}, bf16[8,2048]{1,0:T(8,128)(2,1)S(1)}, u32[]{:S(2)}, u32[]{:S(2)}) collective-permute-start(bf16[8,2048]{1,0:T(8,128)(2,1)S(1)} %get-tuple-element.20.refs_0_.after), channel_id=1, source_target_pairs={{0,12},{4,8},{8,4},{12,0},{1,13},{5,9},{9,5},{13,1},{2,14},{6,10},... | collective-permute-start | bytes 98312 | tf_op jit(solution)/shard_map/ppermute | solution.py:275
  21.2 4.4 %collective-permute-start.3 = (bf16[8,2048]{1,0:T(8,128)(2,1)S(1)}, bf16[8,2048]{1,0:T(8,128)(2,1)S(1)}, u32[]{:S(2)}, u32[]{:S(2)}) collective-permute-start(bf16[8,2048]{1,0:T(8,128)(2,1)S(1)} %get-tuple-element.20.refs_0_.after), channel_id=1, source_target_pairs={{0,8},{4,12},{8,0},{12,4},{1,9},{5,13},{9,1},{13,5},{2,10},{6,14},... | collective-permute-start | bytes 98312 | tf_op jit(solution)/shard_map/ppermute | solution.py:275
  22.7 2.9 %collective-permute-start.2 = (bf16[8,2048]{1,0:T(8,128)(2,1)S(1)}, bf16[8,2048]{1,0:T(8,128)(2,1)S(1)}, u32[]{:S(2)}, u32[]{:S(2)}) collective-permute-start(bf16[8,2048]{1,0:T(8,128)(2,1)S(1)} %get-tuple-element.20.refs_0_.after), channel_id=1, source_target_pairs={{0,4},{4,0},{8,12},{12,8},{1,5},{5,1},{9,13},{13,9},{2,6},{6,2},{1... | collective-permute-start | bytes 98312 | tf_op jit(solution)/shard_map/ppermute | solution.py:275
  26.4 8.4 %collective-permute-start.6 = (bf16[32,1024]{1,0:T(8,128)(2,1)S(1)}, bf16[32,1024]{1,0:T(8,128)(2,1)S(1)}, u32[]{:S(2)}, u32[]{:S(2)}) collective-permute-start(bf16[32,1024]{1,0:T(8,128)(2,1)S(1)} %project_out.4), channel_id=1, source_target_pairs={{0,2},{1,3},{2,0},{3,1},{4,6},{5,7},{6,4},{7,5},{8,10},{9,11},{10,... | collective-permute-start | bytes 196616 | tf_op jit(solution)/shard_map/ppermute | solution.py:275
  29.9 6.7 %collective-permute-start.7 = (bf16[32,1024]{1,0:T(8,128)(2,1)S(1)}, bf16[32,1024]{1,0:T(8,128)(2,1)S(1)}, u32[]{:S(2)}, u32[]{:S(2)}) collective-permute-start(bf16[32,1024]{1,0:T(8,128)(2,1)S(1)} %project_out.5), channel_id=1, source_target_pairs={{0,3},{1,2},{2,1},{3,0},{4,7},{5,6},{6,5},{7,4},{8,11},{9,10},{10,... | collective-permute-start | bytes 196616 | tf_op jit(solution)/shard_map/ppermute | solution.py:275
  32.0 4.8 %collective-permute-start.5 = (bf16[32,1024]{1,0:T(8,128)(2,1)S(1)}, bf16[32,1024]{1,0:T(8,128)(2,1)S(1)}, u32[]{:S(2)}, u32[]{:S(2)}) collective-permute-start(bf16[32,1024]{1,0:T(8,128)(2,1)S(1)} %project_out.3), channel_id=1, source_target_pairs={{0,1},{1,0},{2,3},{3,2},{4,5},{5,4},{6,7},{7,6},{8,9},{9,8},{10,11... | collective-permute-start | bytes 196616 | tf_op jit(solution)/shard_map/ppermute | solution.py:275
  36.9 6.1 %collective-permute-start.10 = (bf16[32,1024]{1,0:T(8,128)(2,1)S(1)}, bf16[32,1024]{1,0:T(8,128)(2,1)S(1)}, u32[]{:S(2)}, u32[]{:S(2)}) collective-permute-start(bf16[32,1024]{1,0:T(8,128)(2,1)S(1)} %finish.1.refs_0_), channel_id=1, source_target_pairs={{0,3},{1,2},{2,1},{3,0},{4,7},{5,6},{6,5},{7,4},{8,11},{9,10},{10,... | collective-permute-start | bytes 196616 | tf_op jit(solution)/shard_map/ppermute | solution.py:275
  39.2 5.7 %collective-permute-start.9 = (bf16[32,1024]{1,0:T(8,128)(2,1)S(1)}, bf16[32,1024]{1,0:T(8,128)(2,1)S(1)}, u32[]{:S(2)}, u32[]{:S(2)}) collective-permute-start(bf16[32,1024]{1,0:T(8,128)(2,1)S(1)} %finish.1.refs_0_), channel_id=1, source_target_pairs={{0,2},{1,3},{2,0},{3,1},{4,6},{5,7},{6,4},{7,5},{8,10},{9,11},{10,... | collective-permute-start | bytes 196616 | tf_op jit(solution)/shard_map/ppermute | solution.py:275
  39.2 5.7 %collective-permute-start.8 = (bf16[32,1024]{1,0:T(8,128)(2,1)S(1)}, bf16[32,1024]{1,0:T(8,128)(2,1)S(1)}, u32[]{:S(2)}, u32[]{:S(2)}) collective-permute-start(bf16[32,1024]{1,0:T(8,128)(2,1)S(1)} %finish.1.refs_0_), channel_id=1, source_target_pairs={{0,1},{1,0},{2,3},{3,2},{4,5},{5,4},{6,7},{7,6},{8,9},{9,8},{10,11... | collective-permute-start | bytes 196616 | tf_op jit(solution)/shard_map/ppermute | solution.py:275

commit v7 on v6

--- a/solution.py
+++ b/solution.py
@@ -102,41 +102,25 @@
     return copies
 
 
-def fetch_caches(masks, after, k_hbm, v_hbm, w_hbm, k, v, *refs):
+def fetch(after, source, target, sem):
     del after
-    *pieces, sems = refs
-    copies = [
-        pltpu.make_async_copy(k_hbm, k, sems.at[0]),
-        pltpu.make_async_copy(v_hbm, v, sems.at[1]),
-    ]
+    copy = pltpu.make_async_copy(source, target, sem)
+    copy.start()
+    copy.wait()
+
+
+def weigh(size, model, masks, lengths, cosine, sine, k, v_hbm, w_hbm, *refs):
+    arrived = refs[:size]
+    probs_out, own_out, share_out, new_out, v = refs[size : size + 5]
+    pieces = refs[size + 5 : size + 5 + len(masks)]
+    q_rows, scores, sems = refs[size + 5 + len(masks) :]
+    copies = [pltpu.make_async_copy(v_hbm, v, sems.at[0])]
     if masks:
-        copies += fetch_pieces(masks, pieces[0].shape[1], w_hbm, pieces, sems, 2)
-    for copy in copies:
-        copy.start()
-    for copy in copies:
-        copy.wait()
-
-
-def fetch_weights(masks, after, w_hbm, *refs):
-    del after
-    *pieces, sems = refs
-    copies = fetch_pieces(masks, pieces[0].shape[1], w_hbm, pieces, sems, 0)
-    for copy in copies:
-        copy.start()
-    for copy in copies:
-        copy.wait()
-
-
-def attention(size, model, masks, lengths, cosine, sine, k, v, w_hbm, *refs):
-    arrived = refs[:size]
-    heads = refs[size]
-    pieces = refs[size + 1 : size + 1 + len(masks)]
-    q_rows, o_rows, scores, sems = refs[size + 1 + len(masks) :]
-    copies = fetch_pieces(masks, pieces[0].shape[1], w_hbm, pieces, sems, 0) if masks else []
+        copies += fetch_pieces(masks, pieces[0].shape[1], w_hbm, pieces, sems, 1)
     for copy in copies:
         copy.start()
     rows, slots = k.shape[0], k.shape[1]
-    group = heads.shape[1] // HD
+    group = probs_out.shape[0] // rows
     width = group * HD
     summed = arrived[0][...]
     for item in arrived[1:]:
@@ -151,7 +135,7 @@
         part = summed[:, head * HD : (head + 1) * HD] * scale
         q_rows[head] = turn(part).astype(BF16).astype(F32)
     new_keys = turn(summed[:, width : width + HD] * scale).astype(BF16).astype(F32)
-    new_values = (summed[:, width + HD : width + 2 * HD] * scale).astype(BF16).astype(F32)
+    new_out[...] = (summed[:, width + HD : width + 2 * HD] * scale).astype(BF16).astype(F32)
     rate = HD ** (-0.5) * math.log2(math.e)
     half = slots // 2
     slot = lax.broadcasted_iota(jnp.int32, (2 * group, half), 1) + half
@@ -178,27 +162,35 @@
         )
         own.append(jnp.sum(both, 1, keepdims=True))
         top.append(jnp.maximum(jnp.max(jnp.maximum(low, high), 1, keepdims=True), own[-1]))
-
-    def soften(pair):
+    for pair in range(rows // 2):
         mine = slice(2 * pair * group, (2 * pair + 2) * group)
         probs = jnp.exp2((scores[mine] - top[pair]) * rate)
         own_prob = jnp.exp2((own[pair] - top[pair]) * rate)
         share = 1.0 / (jnp.sum(probs, 1, keepdims=True) + own_prob)
-        return probs.astype(BF16), own_prob, share
-
-    ready = soften(0)
-    for pair in range(rows // 2):
-        probs, own_prob, share = ready
-        if pair + 1 < rows // 2:
-            ready = soften(pair + 1)
-        sides = jnp.concatenate([v[2 * pair], v[2 * pair + 1]], 1)
-        mixed = jnp.dot(probs, sides, preferred_element_type=F32)
+        probs_out[mine] = probs.astype(BF16)
+        own_out[mine] = jnp.broadcast_to(own_prob, (2 * group, HD))
+        share_out[mine] = jnp.broadcast_to(share, (2 * group, HD))
+    for copy in copies:
+        copy.wait()
+
+
+def mix(masks, probs, own, share, new, v, w_hbm, heads, *refs):
+    *pieces, o_rows, sems = refs
+    copies = fetch_pieces(masks, pieces[0].shape[1], w_hbm, pieces, sems, 0) if masks else []
+    for copy in copies:
+        copy.start()
+    rows = v.shape[0]
+    group = probs.shape[0] // rows
+    for row in range(0, rows, 2):
+        sides = jnp.concatenate([v[row], v[row + 1]], 1)
+        pair = slice(row * group, (row + 2) * group)
+        mixed = jnp.dot(probs[pair], sides, preferred_element_type=F32)
         for side in range(2):
-            row = 2 * pair + side
-            mine = slice(side * group, (side + 1) * group)
-            value = mixed[mine, side * HD : (side + 1) * HD]
-            extra = own_prob[mine] * new_values[row : row + 1]
-            o_rows[:, row, :] = (value + extra) * share[mine]
+            part = slice(side * group, (side + 1) * group)
+            mine = slice((row + side) * group, (row + side + 1) * group)
+            value = mixed[part, side * HD : (side + 1) * HD]
+            extra = own[mine] * new[row + side : row + side + 1]
+            o_rows[:, row + side, :] = (value + extra) * share[mine]
     for head in range(group):
         heads[:, head * HD : (head + 1) * HD] = o_rows[head].astype(BF16)
     for copy in copies:
@@ -282,7 +274,7 @@
     sems = lambda n: pltpu.SemaphoreType.DMA((n,))
     order = list(range(size_y - 1, -1, -1))
     quarter = max(size_y // 4, 1)
-    early, middle, late = [], order[: 2 * quarter], order[2 * quarter : -1]
+    early, middle = order[:quarter], order[quarter:-1]
 
     def shards(inputs, gain, w_query, w_key, w_value, w_output, key_cache, value_cache, lengths):
         batch, depth = inputs.shape
@@ -323,59 +315,70 @@
         )(in_vmem(kept), in_vmem(swap(given, "gx", size_x, 1)))
         arrived = [sums[0]] + [swap(sums[j], "gx", size_x, 2 * j) for j in range(1, levels)]
 
-        fetched = pl.pallas_call(
-            functools.partial(fetch_caches, early),
-            out_shape=[pltpu.VMEM(key_cache.shape, BF16), pltpu.VMEM(value_cache.shape, BF16)]
-            + [piece] * len(early),
-            in_specs=[ANY] * 4,
-            out_specs=[VMEM] * (2 + len(early)),
-            scratch_shapes=[sems(2 + len(early))],
+        keys = pl.pallas_call(
+            fetch,
+            out_shape=pltpu.VMEM(key_cache.shape, BF16),
+            in_specs=[ANY] * 2,
+            out_specs=VMEM,
+            scratch_shapes=[pltpu.SemaphoreType.DMA],
             compiler_params=params(4),
-            cost_estimate=cost(0, 4 * key_cache.size + piece_bytes * len(early)),
-            name="fetch_caches",
-        )(sums[0], in_hbm(key_cache), in_hbm(value_cache), in_hbm(w_output))
-        keys, values, *pieces = fetched
+            cost_estimate=cost(0, 2 * key_cache.size),
+            name="fetch",
+        )(sums[0], in_hbm(key_cache))
 
         half = HD // 2
         inverse = ROPE_BASE ** (-(jnp.arange(half, dtype=F32) * 2.0 / HD))
         angles = lengths.astype(F32)[:, None] * inverse[None, :]
         cosine, sine = jnp.cos(angles), jnp.sin(angles)
-        heads, *more = pl.pallas_call(
-            functools.partial(attention, levels, depth * size_x, middle),
-            out_shape=[pltpu.VMEM((rows, width), BF16)] + [piece] * len(middle),
-            in_specs=[SMEM, VMEM, VMEM, VMEM, VMEM, ANY] + [VMEM] * levels,
-            out_specs=[VMEM] * (1 + len(middle)),
+        lanes = rows * (width // HD)
+        stat = pltpu.VMEM((lanes, HD), F32)
+        probs, own, share, new_values, values, *pieces = pl.pallas_call(
+            functools.partial(weigh, levels, depth * size_x, early),
+            out_shape=[
+                pltpu.VMEM((lanes, key_cache.shape[1]), BF16),
+                stat,
+                stat,
+                pltpu.VMEM((rows, HD), F32),
+                pltpu.VMEM(value_cache.shape, BF16),
+            ]
+            + [piece] * len(early),
+            in_specs=[SMEM, VMEM, VMEM, VMEM, ANY, ANY] + [VMEM] * levels,
+            out_specs=[VMEM] * (5 + len(early)),
             scratch_shapes=[
                 pltpu.VMEM((width // HD, rows, HD), F32),
-                pltpu.VMEM((width // HD, rows, HD), F32),
-                pltpu.VMEM((rows * (width // HD), key_cache.shape[1]), F32),
-                sems(max(len(middle), 1)),
+                pltpu.VMEM((lanes, key_cache.shape[1]), F32),
+                sems(1 + len(early)),
             ],
             compiler_params=params(8),
-            cost_estimate=cost(4 * key_cache.size * (width // HD), piece_bytes * len(middle)),
-            name="attention",
+            cost_estimate=cost(2 * key_cache.size * (width // HD), 2 * value_cache.size),
+            name="weigh",
         )(
             lengths,
             jnp.concatenate([cosine, cosine], 1),
             jnp.concatenate([-sine, sine], 1),
             in_vmem(keys),
-            in_vmem(values),
+            in_hbm(value_cache),
             in_hbm(w_output),
             *[in_vmem(a) for a in arrived],
         )
+        heads, *more = pl.pallas_call(
+            functools.partial(mix, middle),
+            out_shape=[pltpu.VMEM((rows, width), BF16)] + [piece] * len(middle),
+            in_specs=[VMEM] * 5 + [ANY],
+            out_specs=[VMEM] * (1 + len(middle)),
+            scratch_shapes=[
+                pltpu.VMEM((width // HD, rows, HD), F32),
+                sems(max(len(middle), 1)),
+            ],
+            compiler_params=params(8),
+            cost_estimate=cost(2 * key_cache.size * (width // HD), piece_bytes * len(middle)),
+            name="mix",
+        )(*[in_vmem(a) for a in (probs, own, share, new_values, values)], in_hbm(w_output))
         pieces += more
-        gathered = [heads] + [swap(heads, "gx", size_x, m) for m in range(1, size_x)]
-
-        pieces += pl.pallas_call(
-            functools.partial(fetch_weights, late),
-            out_shape=[piece] * len(late),
-            in_specs=[ANY] * 2,
-            out_specs=[VMEM] * len(late),
-            scratch_shapes=[sems(len(late))],
-            compiler_params=params(4),
-            cost_estimate=cost(0, piece_bytes * len(late)),
-            name="fetch_weights",
-        )(heads, in_hbm(w_output))
+        gathered = [heads]
+        for mask in range(2, size_x, 2):
+            gathered.append(swap(heads, "gx", size_x, mask))
+        gathered = [g for even in gathered for g in (even, swap(even, "gx", size_x, 1))]
 
         terms = {}
         for index, mask in enumerate(order):

time: 45.8 us -> 50 us (1.092)
  waiting for transfers between devices: 6.83 us -> 11.6 us
  Pallas kernels: 24.5 us -> 23.8 us
    ppermute x11, waiting for transfers between devices: 6.83 us -> 11.6 us  [swap(): return lax.ppermute(value, axis, [(i, i ^ mask) for i in range(size)])]
    pallas_call x3, Pallas kernels: 11.8 us -> 11.1 us  [the longest x1 4.72 us: shards(): pl.pallas_call(functools.partial(weigh, levels, depth * size_x, early), o...]
  transfers between devices with their start and end apart: 11 -> 11, of which waited for: 6 -> 8; matrix products, arithmetic and copies ran while one was open for 0% -> 0% of each run, Pallas kernels for 22% -> 13%
where the time goes in v7:
time: 50 us; the launch traced here: 49.8 us
  Pallas kernels  23.8 us (48%)
  starting transfers between devices  14.2 us (28%)
  waiting for transfers between devices  11.6 us (23%)
    ppermute x11, starting transfers between devices, swap(): return lax.ppermute(value, axis, [(i, i ^ mask) for i in range(size)])  14.2 us
    ppermute x11, waiting for transfers between devices, swap(): return lax.ppermute(value, axis, [(i, i ^ mask) for i in range(size)])  11.6 us
    pallas_call x1, Pallas kernels, shards(): pl.pallas_call(functools.partial(project, size_x), out_shape=[pltpu.VMEM(...  6.98 us
    pallas_call x1, Pallas kernels, shards(): pl.pallas_call(functools.partial(weigh, levels, depth * size_x, early), o...  4.72 us
    pallas_call x1, Pallas kernels, shards(): pl.pallas_call(functools.partial(mix, middle), out_shape=[pltpu.VMEM((row...  4.17 us
    pallas_call x1, Pallas kernels, shards(): pl.pallas_call(functools.partial(stream_out, size_x, mask), in_specs=[ANY...  2.54 us
    pallas_call x3, Pallas kernels, shards(): pl.pallas_call(functools.partial(project_out, size_x), in_specs=[VMEM] *...  2.45 us
    pallas_call x1, Pallas kernels, shards(): pl.pallas_call(fetch, out_shape=pltpu.VMEM(key_cache.shape, BF16), in_spe...  2.2 us
  transfers between devices with their start and end apart: 11, of which 8 were waited for; matrix products, arithmetic and copies ran while one was open for 0% of the time, Pallas kernels for 13%

profile of v7, /device:TPU:0, one launch (start us, length us, event | category | flops | bytes accessed | tf_op | source)
XLA Modules:
  0.0 49.8 jit_solution(2871658714381334469)
XLA Ops:
  0.0 0.0 copy-start
  0.0 7.0 %project.1 = (f32[2,8,2432]{2,1,0:T(8,128)S(1)}, f32[2,8,2432]{2,1,0:T(8,128)S(1)}) custom-call(bf16[32,4096]{1,0:T(8,128)(2,1)} %x_hbm.3, f32[1,4096]{1,0:T(1,128)} %bitcast.1, bf16[4096,2048]{1,0:T(8,128)(2,1)} %wq_hbm.1, bf16[4096,128]{1,0:T(8,128)(2,1)} %wk_hbm.1, bf16[4096,128]{1,0:T(8,128)(2,1)} %wv_hbm.1), custom_call_target="tpu_custom_call" | custom-call | flops 637534208 | bytes 19922944 | tf_op jit(solution)/shard_map/project/pallas_call | solution.py:289
  7.0 0.5 %collective-permute-start = (f32[2,8,2432]{2,1,0:T(8,128)S(1)}, f32[2,8,2432]{2,1,0:T(8,128)S(1)}, u32[]{:S(2)}, u32[]{:S(2)}) collective-permute-start(f32[2,8,2432]{2,1,0:T(8,128)S(1)} %get-tuple-element.19), channel_id=1, source_target_pairs={{0,4},{4,0},{8,12},{12,8},{1,5},{5,1},{9,13},{13,9},{2,6},{6,2},{1... | collective-permute-start | bytes 466952 | tf_op jit(solution)/shard_map/ppermute | solution.py:267
  7.5 0.0 copy-done
  7.5 0.1 fusion
  7.6 0.9 %collective-permute-done.arrived = f32[2,8,2432]{2,1,0:T(8,128)S(1)} collective-permute-done((f32[2,8,2432]{2,1,0:T(8,128)S(1)}, f32[2,8,2432]{2,1,0:T(8,128)S(1)}, u32[]{:S(2)}, u32[]{:S(2)}) %collective-permute-start) | collective-permute-done | bytes 155680 | tf_op jit(solution)/shard_map/ppermute | solution.py:267
  8.5 2.9 %collective-permute-start.1 = (f32[8,2432]{1,0:T(8,128)S(1)}, f32[8,2432]{1,0:T(8,128)S(1)}, u32[]{:S(2)}, u32[]{:S(2)}) collective-permute-start(f32[8,2432]{1,0:T(8,128)S(1)} %get-tuple-element.21), channel_id=1, source_target_pairs={{0,8},{4,12},{8,0},{12,4},{1,9},{5,13},{9,1},{13,5},{2,10},{6,14},... | collective-permute-start | bytes 233480 | tf_op jit(solution)/shard_map/ppermute | solution.py:267
  11.5 0.1 pad_maximum_fusion
  11.5 2.2 %fetch.1.k = bf16[8,2048,128]{2,1,0:T(8,128)(2,1)S(1)} custom-call(f32[8,2432]{1,0:T(8,128)S(1)} %get-tuple-element.20.after.refs_0_, bf16[8,2048,128]{2,1,0:T(8,128)(2,1)} %source.1), custom_call_target="tpu_custom_call" | custom-call | bytes 4194304 | tf_op jit(solution)/shard_map/fetch/pallas_call | solution.py:318
  13.7 0.4 collective-permute-done.1.refs_1_
  14.1 4.7 %weigh.1 = (bf16[128,2048]{1,0:T(8,128)(2,1)S(1)}, f32[128,128]{1,0:T(8,128)S(1)}, f32[128,128]{1,0:T(8,128)S(1)}, f32[8,128]{1,0:T(8,128)S(1)}, bf16[8,2048,128...) custom-call(s32[8]{0:T(128)S(1)} %copy-done, f32[8,128]{1,0:T(8,128)S(1)} %get-tuple-element.34.cosine, ...), custom_call_target="tpu_custom_call" | custom-call | flops 67108864 | bytes 4194304 | tf_op jit(solution)/shard_map/weigh/pallas_call | solution.py:335
  18.9 4.2 %mix.1 = (bf16[8,2048]{1,0:T(8,128)(2,1)S(1)}, bf16[2048,1024]{1,0:T(8,128)(2,1)S(1)}, bf16[2048,1024]{1,0:T(8,128)(2,1)S(1)}) custom-call(bf16[128,2048]{1,0:T(8,128)(2,1)S(1)} %get-tuple-element.22.probs, f32[128,128]{1,0:T(8,128)S(1)} %get-tuple-element.23.own, f32[128,128]{1,0:T(8,128)S(1)} %get-tuple-element.24.share, ...), custom_call_target="tpu_custom_call" | custom-call | flops 67108864 | bytes 8388608 | tf_op jit(solution)/shard_map/mix/pallas_call | solution.py:364
  23.0 1.8 %collective-permute-start.3 = (bf16[8,2048]{1,0:T(8,128)(2,1)S(1)}, bf16[8,2048]{1,0:T(8,128)(2,1)S(1)}, u32[]{:S(2)}, u32[]{:S(2)}) collective-permute-start(bf16[8,2048]{1,0:T(8,128)(2,1)S(1)} %get-tuple-element.27.refs_0_), channel_id=1, source_target_pairs={{0,8},{4,12},{8,0},{12,4},{1,9},{5,13},{9,1},{13,5},{2,10},{6,14},... | collective-permute-start | bytes 98312 | tf_op jit(solution)/shard_map/ppermute | solution.py:267
  24.8 0.0 collective-permute-start.2
  24.8 2.2 %collective-permute-done.3.refs_2_ = bf16[8,2048]{1,0:T(8,128)(2,1)S(1)} collective-permute-done((bf16[8,2048]{1,0:T(8,128)(2,1)S(1)}, bf16[8,2048]{1,0:T(8,128)(2,1)S(1)}, u32[]{:S(2)}, u32[]{:S(2)}) %collective-permute-start.3) | collective-permute-done | bytes 32800 | tf_op jit(solution)/shard_map/ppermute | solution.py:267
  27.0 0.0 collective-permute-start.4
  27.0 0.0 collective-permute-done.2.refs_1_
  27.0 1.2 %collective-permute-done.4.refs_3_ = bf16[8,2048]{1,0:T(8,128)(2,1)S(1)} collective-permute-done((bf16[8,2048]{1,0:T(8,128)(2,1)S(1)}, bf16[8,2048]{1,0:T(8,128)(2,1)S(1)}, u32[]{:S(2)}, u32[]{:S(2)}) %collective-permute-start.4) | collective-permute-done | bytes 32800 | tf_op jit(solution)/shard_map/ppermute | solution.py:267
  28.2 0.8 %project_out.3 = bf16[32,1024]{1,0:T(8,128)(2,1)S(1)} custom-call(bf16[2048,1024]{1,0:T(8,128)(2,1)S(1)} %get-tuple-element.28.w, bf16[8,2048]{1,0:T(8,128)(2,1)S(1)} %get-tuple-element.27.refs_0_, bf16[8,2048]{1,0:T(8,128)(2,1)S(1)} %collective-permute-done.2.refs_1_, bf16[8,2048]{1,0:T(8,128)(2,1)S(1)} %collective-permute-done.3.refs_2_, ...), custom_call_target="tpu_custom_call" | custom-call | flops 134217728 | bytes 4194304 | tf_op jit(solution)/shard_map/project_out/pallas_call | solution.py:396
  29.0 1.8 %collective-permute-start.5 = (bf16[32,1024]{1,0:T(8,128)(2,1)S(1)}, bf16[32,1024]{1,0:T(8,128)(2,1)S(1)}, u32[]{:S(2)}, u32[]{:S(2)}) collective-permute-start(bf16[32,1024]{1,0:T(8,128)(2,1)S(1)} %project_out.3), channel_id=1, source_target_pairs={{0,1},{1,0},{2,3},{3,2},{4,5},{5,4},{6,7},{7,6},{8,9},{9,8},{10,11... | collective-permute-start | bytes 196616 | tf_op jit(solution)/shard_map/ppermute | solution.py:267
  30.9 0.8 %project_out.4 = bf16[32,1024]{1,0:T(8,128)(2,1)S(1)} custom-call(bf16[2048,1024]{1,0:T(8,128)(2,1)S(1)} %get-tuple-element.29.w, bf16[8,2048]{1,0:T(8,128)(2,1)S(1)} %get-tuple-element.27.refs_0_, bf16[8,2048]{1,0:T(8,128)(2,1)S(1)} %collective-permute-done.2.refs_1_, bf16[8,2048]{1,0:T(8,128)(2,1)S(1)} %collective-permute-done.3.refs_2_, ...), custom_call_target="tpu_custom_call" | custom-call | flops 134217728 | bytes 4194304 | tf_op jit(solution)/shard_map/project_out/pallas_call | solution.py:396
  31.7 2.6 %collective-permute-start.6 = (bf16[32,1024]{1,0:T(8,128)(2,1)S(1)}, bf16[32,1024]{1,0:T(8,128)(2,1)S(1)}, u32[]{:S(2)}, u32[]{:S(2)}) collective-permute-start(bf16[32,1024]{1,0:T(8,128)(2,1)S(1)} %project_out.4), channel_id=1, source_target_pairs={{0,2},{1,3},{2,0},{3,1},{4,6},{5,7},{6,4},{7,5},{8,10},{9,11},{10,... | collective-permute-start | bytes 196616 | tf_op jit(solution)/shard_map/ppermute | solution.py:267
  34.3 0.8 %project_out.5 = bf16[32,1024]{1,0:T(8,128)(2,1)S(1)} custom-call(bf16[2048,1024]{1,0:T(8,128)(2,1)S(1)} %get-tuple-element.30.w, bf16[8,2048]{1,0:T(8,128)(2,1)S(1)} %get-tuple-element.27.refs_0_, bf16[8,2048]{1,0:T(8,128)(2,1)S(1)} %collective-permute-done.2.refs_1_, bf16[8,2048]{1,0:T(8,128)(2,1)S(1)} %collective-permute-done.3.refs_2_, ...), custom_call_target="tpu_custom_call" | custom-call | flops 134217728 | bytes 4194304 | tf_op jit(solution)/shard_map/project_out/pallas_call | solution.py:396
  35.1 0.0 collective-permute-start.7
  35.1 2.5 %stream_out.1.own = f32[32,1024]{1,0:T(8,128)S(1)} custom-call(bf16[2048,4096]{1,0:T(8,128)(2,1)} %w_hbm.5, bf16[32,4096]{1,0:T(8,128)(2,1)} %x_hbm.3, bf16[8,2048]{1,0:T(8,128)(2,1)S(1)} %get-tuple-element.27.refs_0_, bf16[8,2048]{1,0:T(8,128)(2,1)S(1)} %collective-permute-done.2.refs_1_, bf16[8,2048]{1,0:T(8,128)(2,1)S(1)} %collective-permute-done.3.refs_2_, ...), custom_call_target="tpu_custom_call" | custom-call | flops 134217728 | bytes 4194304 | tf_op jit(solution)/shard_map/stream_out/pallas_call | solution.py:409
  37.7 0.0 collective-permute-done.5.refs_0_
  37.7 0.7 %collective-permute-done.6.refs_1_ = bf16[32,1024]{1,0:T(8,128)(2,1)S(1)} collective-permute-done((bf16[32,1024]{1,0:T(8,128)(2,1)S(1)}, bf16[32,1024]{1,0:T(8,128)(2,1)S(1)}, u32[]{:S(2)}, u32[]{:S(2)}) %collective-permute-start.6) | collective-permute-done | bytes 65568 | tf_op jit(solution)/shard_map/ppermute | solution.py:267
  38.4 2.8 %collective-permute-done.7.refs_2_ = bf16[32,1024]{1,0:T(8,128)(2,1)S(1)} collective-permute-done((bf16[32,1024]{1,0:T(8,128)(2,1)S(1)}, bf16[32,1024]{1,0:T(8,128)(2,1)S(1)}, u32[]{:S(2)}, u32[]{:S(2)}) %collective-permute-start.7) | collective-permute-done | bytes 65568 | tf_op jit(solution)/shard_map/ppermute | solution.py:267
  41.2 1.6 %collective-permute-start.10 = (bf16[32,1024]{1,0:T(8,128)(2,1)S(1)}, bf16[32,1024]{1,0:T(8,128)(2,1)S(1)}, u32[]{:S(2)}, u32[]{:S(2)}) collective-permute-start(bf16[32,1024]{1,0:T(8,128)(2,1)S(1)} %finish.1.refs_0_), channel_id=1, source_target_pairs={{0,3},{1,2},{2,1},{3,0},{4,7},{5,6},{6,5},{7,4},{8,11},{9,10},{10,... | collective-permute-start | bytes 196616 | tf_op jit(solution)/shard_map/ppermute | solution.py:267
  42.9 0.0 collective-permute-start.9
  42.9 2.8 %collective-permute-start.8 = (bf16[32,1024]{1,0:T(8,128)(2,1)S(1)}, bf16[32,1024]{1,0:T(8,128)(2,1)S(1)}, u32[]{:S(2)}, u32[]{:S(2)}) collective-permute-start(bf16[32,1024]{1,0:T(8,128)(2,1)S(1)} %finish.1.refs_0_), channel_id=1, source_target_pairs={{0,1},{1,0},{2,3},{3,2},{4,5},{5,4},{6,7},{7,6},{8,9},{9,8},{10,11... | collective-permute-start | bytes 196616 | tf_op jit(solution)/shard_map/ppermute | solution.py:267
  45.7 1.8 %collective-permute-done.10.refs_3_ = bf16[32,1024]{1,0:T(8,128)(2,1)S(1)} collective-permute-done((bf16[32,1024]{1,0:T(8,128)(2,1)S(1)}, bf16[32,1024]{1,0:T(8,128)(2,1)S(1)}, u32[]{:S(2)}, u32[]{:S(2)}) %collective-permute-start.10) | collective-permute-done | bytes 65568 | tf_op jit(solution)/shard_map/ppermute | solution.py:267
  47.5 1.6 %collective-permute-done.9.refs_2_ = bf16[32,1024]{1,0:T(8,128)(2,1)S(1)} collective-permute-done((bf16[32,1024]{1,0:T(8,128)(2,1)S(1)}, bf16[32,1024]{1,0:T(8,128)(2,1)S(1)}, u32[]{:S(2)}, u32[]{:S(2)}) %collective-permute-start.9) | collective-permute-done | bytes 65568 | tf_op jit(solution)/shard_map/ppermute | solution.py:267
  49.1 0.0 collective-permute-done.8.refs_1_
  49.1 0.7 %assemble.1 = bf16[32,4096]{1,0:T(8,128)(2,1)} custom-call(bf16[32,1024]{1,0:T(8,128)(2,1)S(1)} %finish.1.refs_0_, bf16[32,1024]{1,0:T(8,128)(2,1)S(1)} %collective-permute-done.8.refs_1_, bf16[32,1024]{1,0:T(8,128)(2,1)S(1)} %collective-permute-done.9.refs_2_, bf16[32,1024]{1,0:T(8,128)(2,1)S(1)} %collective-permute-done.10.refs_3_), custom_call_target="tpu_custom_call" | custom-call | tf_op jit(solution)/shard_map/assemble/pallas_call | solution.py:426
  (4 shorter events, 0.1 us)
Async XLA Ops:
  0.0 7.5 %copy-start = (s32[8]{0:T(128)S(1)}, s32[8]{0:T(128)}, u32[]{:S(2)}) copy-start(s32[8]{0:T(128)} %lengths.1) | copy-start | bytes 100
  7.0 1.5 %collective-permute-start = (f32[2,8,2432]{2,1,0:T(8,128)S(1)}, f32[2,8,2432]{2,1,0:T(8,128)S(1)}, u32[]{:S(2)}, u32[]{:S(2)}) collective-permute-start(f32[2,8,2432]{2,1,0:T(8,128)S(1)} %get-tuple-element.19), channel_id=1, source_target_pairs={{0,4},{4,0},{8,12},{12,8},{1,5},{5,1},{9,13},{13,9},{2,6},{6,2},{1... | collective-permute-start | bytes 466952 | tf_op jit(solution)/shard_map/ppermute | solution.py:267
  8.5 5.6 %collective-permute-start.1 = (f32[8,2432]{1,0:T(8,128)S(1)}, f32[8,2432]{1,0:T(8,128)S(1)}, u32[]{:S(2)}, u32[]{:S(2)}) collective-permute-start(f32[8,2432]{1,0:T(8,128)S(1)} %get-tuple-element.21), channel_id=1, source_target_pairs={{0,8},{4,12},{8,0},{12,4},{1,9},{5,13},{9,1},{13,5},{2,10},{6,14},... | collective-permute-start | bytes 233480 | tf_op jit(solution)/shard_map/ppermute | solution.py:267
  23.0 4.0 %collective-permute-start.3 = (bf16[8,2048]{1,0:T(8,128)(2,1)S(1)}, bf16[8,2048]{1,0:T(8,128)(2,1)S(1)}, u32[]{:S(2)}, u32[]{:S(2)}) collective-permute-start(bf16[8,2048]{1,0:T(8,128)(2,1)S(1)} %get-tuple-element.27.refs_0_), channel_id=1, source_target_pairs={{0,8},{4,12},{8,0},{12,4},{1,9},{5,13},{9,1},{13,5},{2,10},{6,14},... | collective-permute-start | bytes 98312 | tf_op jit(solution)/shard_map/ppermute | solution.py:267
  24.8 2.2 %collective-permute-start.2 = (bf16[8,2048]{1,0:T(8,128)(2,1)S(1)}, bf16[8,2048]{1,0:T(8,128)(2,1)S(1)}, u32[]{:S(2)}, u32[]{:S(2)}) collective-permute-start(bf16[8,2048]{1,0:T(8,128)(2,1)S(1)} %get-tuple-element.27.refs_0_), channel_id=1, source_target_pairs={{0,4},{4,0},{8,12},{12,8},{1,5},{5,1},{9,13},{13,9},{2,6},{6,2},{1... | collective-permute-start | bytes 98312 | tf_op jit(solution)/shard_map/ppermute | solution.py:267
  27.0 1.2 %collective-permute-start.4 = (bf16[8,2048]{1,0:T(8,128)(2,1)S(1)}, bf16[8,2048]{1,0:T(8,128)(2,1)S(1)}, u32[]{:S(2)}, u32[]{:S(2)}) collective-permute-start(bf16[8,2048]{1,0:T(8,128)(2,1)S(1)} %collective-permute-done.3.refs_2_), channel_id=1, source_target_pairs={{0,4},{4,0},{8,12},{12,8},{1,5},{5,1},{9,13},{13,9},{2,6},{6,2},{1... | collective-permute-start | bytes 98312 | tf_op jit(solution)/shard_map/ppermute | solution.py:267
  29.0 8.7 %collective-permute-start.5 = (bf16[32,1024]{1,0:T(8,128)(2,1)S(1)}, bf16[32,1024]{1,0:T(8,128)(2,1)S(1)}, u32[]{:S(2)}, u32[]{:S(2)}) collective-permute-start(bf16[32,1024]{1,0:T(8,128)(2,1)S(1)} %project_out.3), channel_id=1, source_target_pairs={{0,1},{1,0},{2,3},{3,2},{4,5},{5,4},{6,7},{7,6},{8,9},{9,8},{10,11... | collective-permute-start | bytes 196616 | tf_op jit(solution)/shard_map/ppermute | solution.py:267
  31.7 6.7 %collective-permute-start.6 = (bf16[32,1024]{1,0:T(8,128)(2,1)S(1)}, bf16[32,1024]{1,0:T(8,128)(2,1)S(1)}, u32[]{:S(2)}, u32[]{:S(2)}) collective-permute-start(bf16[32,1024]{1,0:T(8,128)(2,1)S(1)} %project_out.4), channel_id=1, source_target_pairs={{0,2},{1,3},{2,0},{3,1},{4,6},{5,7},{6,4},{7,5},{8,10},{9,11},{10,... | collective-permute-start | bytes 196616 | tf_op jit(solution)/shard_map/ppermute | solution.py:267
  35.1 6.1 %collective-permute-start.7 = (bf16[32,1024]{1,0:T(8,128)(2,1)S(1)}, bf16[32,1024]{1,0:T(8,128)(2,1)S(1)}, u32[]{:S(2)}, u32[]{:S(2)}) collective-permute-start(bf16[32,1024]{1,0:T(8,128)(2,1)S(1)} %project_out.5), channel_id=1, source_target_pairs={{0,3},{1,2},{2,1},{3,0},{4,7},{5,6},{6,5},{7,4},{8,11},{9,10},{10,... | collective-permute-start | bytes 196616 | tf_op jit(solution)/shard_map/ppermute | solution.py:267
  41.2 6.3 %collective-permute-start.10 = (bf16[32,1024]{1,0:T(8,128)(2,1)S(1)}, bf16[32,1024]{1,0:T(8,128)(2,1)S(1)}, u32[]{:S(2)}, u32[]{:S(2)}) collective-permute-start(bf16[32,1024]{1,0:T(8,128)(2,1)S(1)} %finish.1.refs_0_), channel_id=1, source_target_pairs={{0,3},{1,2},{2,1},{3,0},{4,7},{5,6},{6,5},{7,4},{8,11},{9,10},{10,... | collective-permute-start | bytes 196616 | tf_op jit(solution)/shard_map/ppermute | solution.py:267
  42.9 6.2 %collective-permute-start.9 = (bf16[32,1024]{1,0:T(8,128)(2,1)S(1)}, bf16[32,1024]{1,0:T(8,128)(2,1)S(1)}, u32[]{:S(2)}, u32[]{:S(2)}) collective-permute-start(bf16[32,1024]{1,0:T(8,128)(2,1)S(1)} %finish.1.refs_0_), channel_id=1, source_target_pairs={{0,2},{1,3},{2,0},{3,1},{4,6},{5,7},{6,4},{7,5},{8,10},{9,11},{10,... | collective-permute-start | bytes 196616 | tf_op jit(solution)/shard_map/ppermute | solution.py:267
  42.9 6.2 %collective-permute-start.8 = (bf16[32,1024]{1,0:T(8,128)(2,1)S(1)}, bf16[32,1024]{1,0:T(8,128)(2,1)S(1)}, u32[]{:S(2)}, u32[]{:S(2)}) collective-permute-start(bf16[32,1024]{1,0:T(8,128)(2,1)S(1)} %finish.1.refs_0_), channel_id=1, source_target_pairs={{0,1},{1,0},{2,3},{3,2},{4,5},{5,4},{6,7},{7,6},{8,9},{9,8},{10,11... | collective-permute-start | bytes 196616 | tf_op jit(solution)/shard_map/ppermute | solution.py:267

commit v8 on v6

--- a/solution.py
+++ b/solution.py
@@ -17,7 +17,6 @@
 
 ANY = pl.BlockSpec(memory_space=pl.ANY)
 VMEM = pl.BlockSpec(memory_space=pltpu.VMEM)
-SMEM = pl.BlockSpec(memory_space=pltpu.SMEM)
 MIB = 1 << 20
 
 
@@ -102,19 +101,19 @@
     return copies
 
 
-def fetch_caches(masks, after, k_hbm, v_hbm, w_hbm, k, v, *refs):
+def fetch_caches(after, k_hbm, v_hbm, k_turned, v, k, sems):
     del after
-    *pieces, sems = refs
-    copies = [
-        pltpu.make_async_copy(k_hbm, k, sems.at[0]),
-        pltpu.make_async_copy(v_hbm, v, sems.at[1]),
-    ]
-    if masks:
-        copies += fetch_pieces(masks, pieces[0].shape[1], w_hbm, pieces, sems, 2)
-    for copy in copies:
-        copy.start()
-    for copy in copies:
-        copy.wait()
+    rows, slots = k.shape[0], k.shape[1]
+    copies = [pltpu.make_async_copy(k_hbm.at[r], k.at[r], sems.at[r]) for r in range(rows)]
+    copies.append(pltpu.make_async_copy(v_hbm, v, sems.at[rows]))
+    for copy in copies:
+        copy.start()
+    for row in range(rows):
+        copies[row].wait()
+        for start in range(0, slots, CHUNK):
+            part = slice(start, start + CHUNK)
+            k_turned[row, :, part] = k[row, part, :].T
+    copies[rows].wait()
 
 
 def fetch_weights(masks, after, w_hbm, *refs):
@@ -135,7 +134,7 @@
     copies = fetch_pieces(masks, pieces[0].shape[1], w_hbm, pieces, sems, 0) if masks else []
     for copy in copies:
         copy.start()
-    rows, slots = k.shape[0], k.shape[1]
+    rows, slots = k.shape[0], k.shape[2]
     group = heads.shape[1] // HD
     width = group * HD
     summed = arrived[0][...]
@@ -163,12 +162,10 @@
         queries = jnp.concatenate(
             [jnp.concatenate([first, empty], 1), jnp.concatenate([empty, other], 1)], 0
         )
-        keys = jnp.concatenate([k[row], k[row + 1]], 1)
-        raw = lax.dot_general(
-            queries.astype(BF16), keys, (((1,), (1,)), ((), ())), preferred_element_type=F32
-        )
+        keys = jnp.concatenate([k[row], k[row + 1]], 0)
+        raw = jnp.dot(queries.astype(BF16), keys, preferred_element_type=F32)
         low = raw[:, :half]
-        limit = jnp.where(second, lengths[row + 1], lengths[row])
+        limit = jnp.where(second, lengths[row + 1 : row + 2, :1], lengths[row : row + 1, :1])
         high = jnp.where(slot < limit, raw[:, half:], -jnp.inf)
         mine = slice(row * group, (row + 2) * group)
         scores[mine, :half] = low
@@ -282,7 +279,7 @@
     sems = lambda n: pltpu.SemaphoreType.DMA((n,))
     order = list(range(size_y - 1, -1, -1))
     quarter = max(size_y // 4, 1)
-    early, middle, late = [], order[: 2 * quarter], order[2 * quarter : -1]
+    middle, late = order[: 2 * quarter], order[2 * quarter : -1]
 
     def shards(inputs, gain, w_query, w_key, w_value, w_output, key_cache, value_cache, lengths):
         batch, depth = inputs.shape
@@ -323,18 +320,20 @@
         )(in_vmem(kept), in_vmem(swap(given, "gx", size_x, 1)))
         arrived = [sums[0]] + [swap(sums[j], "gx", size_x, 2 * j) for j in range(1, levels)]
 
-        fetched = pl.pallas_call(
-            functools.partial(fetch_caches, early),
-            out_shape=[pltpu.VMEM(key_cache.shape, BF16), pltpu.VMEM(value_cache.shape, BF16)]
-            + [piece] * len(early),
-            in_specs=[ANY] * 4,
-            out_specs=[VMEM] * (2 + len(early)),
-            scratch_shapes=[sems(2 + len(early))],
-            compiler_params=params(4),
-            cost_estimate=cost(0, 4 * key_cache.size + piece_bytes * len(early)),
+        keys, values = pl.pallas_call(
+            fetch_caches,
+            out_shape=[
+                pltpu.VMEM((rows, HD, key_cache.shape[1]), BF16),
+                pltpu.VMEM(value_cache.shape, BF16),
+            ],
+            in_specs=[ANY] * 3,
+            out_specs=[VMEM] * 2,
+            scratch_shapes=[pltpu.VMEM(key_cache.shape, BF16), sems(rows + 1)],
+            compiler_params=params(12),
+            cost_estimate=cost(0, 4 * key_cache.size),
             name="fetch_caches",
-        )(sums[0], in_hbm(key_cache), in_hbm(value_cache), in_hbm(w_output))
-        keys, values, *pieces = fetched
+        )(sums[0], in_hbm(key_cache), in_hbm(value_cache))
+        pieces = []
 
         half = HD // 2
         inverse = ROPE_BASE ** (-(jnp.arange(half, dtype=F32) * 2.0 / HD))
@@ -343,7 +342,7 @@
         heads, *more = pl.pallas_call(
             functools.partial(attention, levels, depth * size_x, middle),
             out_shape=[pltpu.VMEM((rows, width), BF16)] + [piece] * len(middle),
-            in_specs=[SMEM, VMEM, VMEM, VMEM, VMEM, ANY] + [VMEM] * levels,
+            in_specs=[VMEM, VMEM, VMEM, VMEM, VMEM, ANY] + [VMEM] * levels,
             out_specs=[VMEM] * (1 + len(middle)),
             scratch_shapes=[
                 pltpu.VMEM((width // HD, rows, HD), F32),
@@ -355,7 +354,7 @@
             cost_estimate=cost(4 * key_cache.size * (width // HD), piece_bytes * len(middle)),
             name="attention",
         )(
-            lengths,
+            jnp.broadcast_to(lengths[:, None], (rows, HD)),
             jnp.concatenate([cosine, cosine], 1),
             jnp.concatenate([-sine, sine], 1),
             in_vmem(keys),

time: 45.8 us -> 45 us (0.983)
  Pallas kernels: 24.5 us -> 23.6 us
    pallas_call x1, Pallas kernels: 6.09 us -> 5.1 us  [shards(): pl.pallas_call(functools.partial(attention, levels, depth * size_x, middl...]
where the time goes in v8:
time: 45 us; the launch traced here: 44.8 us
  Pallas kernels  23.6 us (52%)
  starting transfers between devices  14 us (31%)
  waiting for transfers between devices  6.83 us (15%)
    ppermute x11, starting transfers between devices, swap(): return lax.ppermute(value, axis, [(i, i ^ mask) for i in range(size)])  14 us
    pallas_call x1, Pallas kernels, shards(): pl.pallas_call(functools.partial(project, size_x), out_shape=[pltpu.VMEM(...  6.98 us
    ppermute x11, waiting for transfers between devices, swap(): return lax.ppermute(value, axis, [(i, i ^ mask) for i in range(size)])  6.83 us
    pallas_call x1, Pallas kernels, shards(): pl.pallas_call(functools.partial(attention, levels, depth * size_x, middl...  5.1 us
    pallas_call x1, Pallas kernels, shards(): pl.pallas_call(fetch_caches, out_shape=[pltpu.VMEM((rows, HD, key_cache.s...  3.56 us
    pallas_call x1, Pallas kernels, shards(): pl.pallas_call(functools.partial(stream_out, size_x, mask), in_specs=[ANY...  2.53 us
    pallas_call x3, Pallas kernels, shards(): pl.pallas_call(functools.partial(project_out, size_x), in_specs=[VMEM] *...  2.45 us
    pallas_call x1, Pallas kernels, shards(): pl.pallas_call(functools.partial(fetch_weights, late), out_shape=[piece]...  2.2 us
  transfers between devices with their start and end apart: 11, of which 6 were waited for; matrix products, arithmetic and copies ran while one was open for 0% of the time, Pallas kernels for 22%

profile of v8, /device:TPU:0, one launch (start us, length us, event | category | flops | bytes accessed | tf_op | source)
XLA Modules:
  0.0 44.8 jit_solution(18127930860934802454)
XLA Ops:
  0.0 0.0 copy-start
  0.0 7.0 %project.1 = (f32[2,8,2432]{2,1,0:T(8,128)S(1)}, f32[2,8,2432]{2,1,0:T(8,128)S(1)}) custom-call(bf16[32,4096]{1,0:T(8,128)(2,1)} %x_hbm.3, f32[1,4096]{1,0:T(1,128)} %bitcast.1, bf16[4096,2048]{1,0:T(8,128)(2,1)} %wq_hbm.1, bf16[4096,128]{1,0:T(8,128)(2,1)} %wk_hbm.1, bf16[4096,128]{1,0:T(8,128)(2,1)} %wv_hbm.1), custom_call_target="tpu_custom_call" | custom-call | flops 637534208 | bytes 19922944 | tf_op jit(solution)/shard_map/project/pallas_call | solution.py:294
  7.0 0.5 %collective-permute-start = (f32[2,8,2432]{2,1,0:T(8,128)S(1)}, f32[2,8,2432]{2,1,0:T(8,128)S(1)}, u32[]{:S(2)}, u32[]{:S(2)}) collective-permute-start(f32[2,8,2432]{2,1,0:T(8,128)S(1)} %get-tuple-element.15), channel_id=1, source_target_pairs={{0,4},{4,0},{8,12},{12,8},{1,5},{5,1},{9,13},{13,9},{2,6},{6,2},{1... | collective-permute-start | bytes 466952 | tf_op jit(solution)/shard_map/ppermute | solution.py:272
  7.5 0.0 copy-done
  7.5 0.1 fusion
  7.6 0.9 %collective-permute-done.arrived = f32[2,8,2432]{2,1,0:T(8,128)S(1)} collective-permute-done((f32[2,8,2432]{2,1,0:T(8,128)S(1)}, f32[2,8,2432]{2,1,0:T(8,128)S(1)}, u32[]{:S(2)}, u32[]{:S(2)}) %collective-permute-start) | collective-permute-done | bytes 155680 | tf_op jit(solution)/shard_map/ppermute | solution.py:272
  8.6 2.9 %collective-permute-start.1 = (f32[8,2432]{1,0:T(8,128)S(1)}, f32[8,2432]{1,0:T(8,128)S(1)}, u32[]{:S(2)}, u32[]{:S(2)}) collective-permute-start(f32[8,2432]{1,0:T(8,128)S(1)} %get-tuple-element.19), channel_id=1, source_target_pairs={{0,8},{4,12},{8,0},{12,4},{1,9},{5,13},{9,1},{13,5},{2,10},{6,14},... | collective-permute-start | bytes 233480 | tf_op jit(solution)/shard_map/ppermute | solution.py:272
  11.5 0.1 pad_maximum_fusion
  11.5 3.6 %fetch_caches.1 = (bf16[8,128,2048]{2,1,0:T(8,128)(2,1)S(1)}, bf16[8,2048,128]{2,1,0:T(8,128)(2,1)S(1)}) custom-call(f32[8,2432]{1,0:T(8,128)S(1)} %get-tuple-element.16.after.refs_0_, bf16[8,2048,128]{2,1,0:T(8,128)(2,1)} %k_hbm.1, bf16[8,2048,128]{2,1,0:T(8,128)(2,1)} %v_hbm.1), custom_call_target="tpu_custom_call" | custom-call | bytes 8388608 | tf_op jit(solution)/shard_map/fetch_caches/pallas_call | solution.py:323
  15.1 0.0 collective-permute-done.1.refs_1_
  15.1 0.1 broadcast_in_dim.2.lengths
  15.2 5.1 %attention.1 = (bf16[8,2048]{1,0:T(8,128)(2,1)S(1)}, bf16[2048,1024]{1,0:T(8,128)(2,1)S(1)}, bf16[2048,1024]{1,0:T(8,128)(2,1)S(1)}) custom-call(s32[8,128]{1,0:T(8,128)S(1)} %broadcast_in_dim.2.lengths, f32[8,128]{1,0:T(8,128)S(1)} %get-tuple-element.26.cosine, f32[8,128]{1,0:T(8,128)S(1)} %get-tuple-element.27.sine, ...), custom_call_target="tpu_custom_call" | custom-call | flops 134217728 | bytes 8388608 | tf_op jit(solution)/shard_map/attention/pallas_call | solution.py:342
  20.3 0.1 collective-permute-start.4
  20.4 1.5 %collective-permute-start.3 = (bf16[8,2048]{1,0:T(8,128)(2,1)S(1)}, bf16[8,2048]{1,0:T(8,128)(2,1)S(1)}, u32[]{:S(2)}, u32[]{:S(2)}) collective-permute-start(bf16[8,2048]{1,0:T(8,128)(2,1)S(1)} %get-tuple-element.20.refs_0_.after), channel_id=1, source_target_pairs={{0,8},{4,12},{8,0},{12,4},{1,9},{5,13},{9,1},{13,5},{2,10},{6,14},... | collective-permute-start | bytes 98312 | tf_op jit(solution)/shard_map/ppermute | solution.py:272
  21.9 0.4 collective-permute-start.2
  22.2 2.2 %fetch_weights.1.w = bf16[2048,1024]{1,0:T(8,128)(2,1)S(1)} custom-call(bf16[8,2048]{1,0:T(8,128)(2,1)S(1)} %get-tuple-element.20.refs_0_.after, bf16[2048,4096]{1,0:T(8,128)(2,1)} %w_hbm.5), custom_call_target="tpu_custom_call" | custom-call | bytes 4194304 | tf_op jit(solution)/shard_map/fetch_weights/pallas_call | solution.py:368
  24.4 0.0 collective-permute-done.4.refs_3_
  24.4 0.3 collective-permute-done.3.refs_2_
  24.8 0.0 collective-permute-done.2.refs_1_
  24.8 0.8 %project_out.4 = bf16[32,1024]{1,0:T(8,128)(2,1)S(1)} custom-call(bf16[2048,1024]{1,0:T(8,128)(2,1)S(1)} %get-tuple-element.21.w, bf16[8,2048]{1,0:T(8,128)(2,1)S(1)} %get-tuple-element.20.refs_0_.after, bf16[8,2048]{1,0:T(8,128)(2,1)S(1)} %collective-permute-done.2.refs_1_, bf16[8,2048]{1,0:T(8,128)(2,1)S(1)} %collective-permute-done.3.refs_2_, ...), custom_call_target="tpu_custom_call" | custom-call | flops 134217728 | bytes 4194304 | tf_op jit(solution)/shard_map/project_out/pallas_call | solution.py:392
  25.6 2.6 %collective-permute-start.6 = (bf16[32,1024]{1,0:T(8,128)(2,1)S(1)}, bf16[32,1024]{1,0:T(8,128)(2,1)S(1)}, u32[]{:S(2)}, u32[]{:S(2)}) collective-permute-start(bf16[32,1024]{1,0:T(8,128)(2,1)S(1)} %project_out.4), channel_id=1, source_target_pairs={{0,2},{1,3},{2,0},{3,1},{4,6},{5,7},{6,4},{7,5},{8,10},{9,11},{10,... | collective-permute-start | bytes 196616 | tf_op jit(solution)/shard_map/ppermute | solution.py:272
  28.2 0.8 %project_out.5 = bf16[32,1024]{1,0:T(8,128)(2,1)S(1)} custom-call(bf16[2048,1024]{1,0:T(8,128)(2,1)S(1)} %get-tuple-element.22.w, bf16[8,2048]{1,0:T(8,128)(2,1)S(1)} %get-tuple-element.20.refs_0_.after, bf16[8,2048]{1,0:T(8,128)(2,1)S(1)} %collective-permute-done.2.refs_1_, bf16[8,2048]{1,0:T(8,128)(2,1)S(1)} %collective-permute-done.3.refs_2_, ...), custom_call_target="tpu_custom_call" | custom-call | flops 134217728 | bytes 4194304 | tf_op jit(solution)/shard_map/project_out/pallas_call | solution.py:392
  29.0 1.4 %collective-permute-start.7 = (bf16[32,1024]{1,0:T(8,128)(2,1)S(1)}, bf16[32,1024]{1,0:T(8,128)(2,1)S(1)}, u32[]{:S(2)}, u32[]{:S(2)}) collective-permute-start(bf16[32,1024]{1,0:T(8,128)(2,1)S(1)} %project_out.5), channel_id=1, source_target_pairs={{0,3},{1,2},{2,1},{3,0},{4,7},{5,6},{6,5},{7,4},{8,11},{9,10},{10,... | collective-permute-start | bytes 196616 | tf_op jit(solution)/shard_map/ppermute | solution.py:272
  30.4 0.8 %project_out.3 = bf16[32,1024]{1,0:T(8,128)(2,1)S(1)} custom-call(bf16[2048,1024]{1,0:T(8,128)(2,1)S(1)} %fetch_weights.1.w, bf16[8,2048]{1,0:T(8,128)(2,1)S(1)} %get-tuple-element.20.refs_0_.after, bf16[8,2048]{1,0:T(8,128)(2,1)S(1)} %collective-permute-done.2.refs_1_, bf16[8,2048]{1,0:T(8,128)(2,1)S(1)} %collective-permute-done.3.refs_2_, ...), custom_call_target="tpu_custom_call" | custom-call | flops 134217728 | bytes 4194304 | tf_op jit(solution)/shard_map/project_out/pallas_call | solution.py:392
  31.2 0.3 collective-permute-start.5
  31.4 2.5 %stream_out.1.own = f32[32,1024]{1,0:T(8,128)S(1)} custom-call(bf16[2048,4096]{1,0:T(8,128)(2,1)} %w_hbm.5, bf16[32,4096]{1,0:T(8,128)(2,1)} %x_hbm.3, bf16[8,2048]{1,0:T(8,128)(2,1)S(1)} %get-tuple-element.20.refs_0_.after, bf16[8,2048]{1,0:T(8,128)(2,1)S(1)} %collective-permute-done.2.refs_1_, bf16[8,2048]{1,0:T(8,128)(2,1)S(1)} %collective-permute-done.3.refs_2_, ...), custom_call_target="tpu_custom_call" | custom-call | flops 134217728 | bytes 4194304 | tf_op jit(solution)/shard_map/stream_out/pallas_call | solution.py:405
  34.0 0.0 collective-permute-done.6.refs_1_
  34.0 1.7 %collective-permute-done.7.refs_2_ = bf16[32,1024]{1,0:T(8,128)(2,1)S(1)} collective-permute-done((bf16[32,1024]{1,0:T(8,128)(2,1)S(1)}, bf16[32,1024]{1,0:T(8,128)(2,1)S(1)}, u32[]{:S(2)}, u32[]{:S(2)}) %collective-permute-start.7) | collective-permute-done | bytes 65568 | tf_op jit(solution)/shard_map/ppermute | solution.py:272
  35.7 0.3 collective-permute-done.5.refs_0_
  36.0 2.3 %collective-permute-start.10 = (bf16[32,1024]{1,0:T(8,128)(2,1)S(1)}, bf16[32,1024]{1,0:T(8,128)(2,1)S(1)}, u32[]{:S(2)}, u32[]{:S(2)}) collective-permute-start(bf16[32,1024]{1,0:T(8,128)(2,1)S(1)} %finish.1.refs_0_), channel_id=1, source_target_pairs={{0,3},{1,2},{2,1},{3,0},{4,7},{5,6},{6,5},{7,4},{8,11},{9,10},{10,... | collective-permute-start | bytes 196616 | tf_op jit(solution)/shard_map/ppermute | solution.py:272
  38.4 0.0 collective-permute-start.9
  38.4 2.1 %collective-permute-start.8 = (bf16[32,1024]{1,0:T(8,128)(2,1)S(1)}, bf16[32,1024]{1,0:T(8,128)(2,1)S(1)}, u32[]{:S(2)}, u32[]{:S(2)}) collective-permute-start(bf16[32,1024]{1,0:T(8,128)(2,1)S(1)} %finish.1.refs_0_), channel_id=1, source_target_pairs={{0,1},{1,0},{2,3},{3,2},{4,5},{5,4},{6,7},{7,6},{8,9},{9,8},{10,11... | collective-permute-start | bytes 196616 | tf_op jit(solution)/shard_map/ppermute | solution.py:272
  40.5 1.7 %collective-permute-done.10.refs_3_ = bf16[32,1024]{1,0:T(8,128)(2,1)S(1)} collective-permute-done((bf16[32,1024]{1,0:T(8,128)(2,1)S(1)}, bf16[32,1024]{1,0:T(8,128)(2,1)S(1)}, u32[]{:S(2)}, u32[]{:S(2)}) %collective-permute-start.10) | collective-permute-done | bytes 65568 | tf_op jit(solution)/shard_map/ppermute | solution.py:272
  42.2 1.9 %collective-permute-done.9.refs_2_ = bf16[32,1024]{1,0:T(8,128)(2,1)S(1)} collective-permute-done((bf16[32,1024]{1,0:T(8,128)(2,1)S(1)}, bf16[32,1024]{1,0:T(8,128)(2,1)S(1)}, u32[]{:S(2)}, u32[]{:S(2)}) %collective-permute-start.9) | collective-permute-done | bytes 65568 | tf_op jit(solution)/shard_map/ppermute | solution.py:272
  44.1 0.0 collective-permute-done.8.refs_1_
  44.1 0.7 %assemble.1 = bf16[32,4096]{1,0:T(8,128)(2,1)} custom-call(bf16[32,1024]{1,0:T(8,128)(2,1)S(1)} %finish.1.refs_0_, bf16[32,1024]{1,0:T(8,128)(2,1)S(1)} %collective-permute-done.8.refs_1_, bf16[32,1024]{1,0:T(8,128)(2,1)S(1)} %collective-permute-done.9.refs_2_, bf16[32,1024]{1,0:T(8,128)(2,1)S(1)} %collective-permute-done.10.refs_3_), custom_call_target="tpu_custom_call" | custom-call | tf_op jit(solution)/shard_map/assemble/pallas_call | solution.py:422
  (4 shorter events, 0.1 us)
Async XLA Ops:
  0.0 7.5 %copy-start = (s32[8]{0:T(128)S(1)}, s32[8]{0:T(128)}, u32[]{:S(2)}) copy-start(s32[8]{0:T(128)} %param.17) | copy-start | bytes 100
  7.0 1.5 %collective-permute-start = (f32[2,8,2432]{2,1,0:T(8,128)S(1)}, f32[2,8,2432]{2,1,0:T(8,128)S(1)}, u32[]{:S(2)}, u32[]{:S(2)}) collective-permute-start(f32[2,8,2432]{2,1,0:T(8,128)S(1)} %get-tuple-element.15), channel_id=1, source_target_pairs={{0,4},{4,0},{8,12},{12,8},{1,5},{5,1},{9,13},{13,9},{2,6},{6,2},{1... | collective-permute-start | bytes 466952 | tf_op jit(solution)/shard_map/ppermute | solution.py:272
  8.6 6.6 %collective-permute-start.1 = (f32[8,2432]{1,0:T(8,128)S(1)}, f32[8,2432]{1,0:T(8,128)S(1)}, u32[]{:S(2)}, u32[]{:S(2)}) collective-permute-start(f32[8,2432]{1,0:T(8,128)S(1)} %get-tuple-element.19), channel_id=1, source_target_pairs={{0,8},{4,12},{8,0},{12,4},{1,9},{5,13},{9,1},{13,5},{2,10},{6,14},... | collective-permute-start | bytes 233480 | tf_op jit(solution)/shard_map/ppermute | solution.py:272
  20.3 4.1 %collective-permute-start.4 = (bf16[8,2048]{1,0:T(8,128)(2,1)S(1)}, bf16[8,2048]{1,0:T(8,128)(2,1)S(1)}, u32[]{:S(2)}, u32[]{:S(2)}) collective-permute-start(bf16[8,2048]{1,0:T(8,128)(2,1)S(1)} %get-tuple-element.20.refs_0_.after), channel_id=1, source_target_pairs={{0,12},{4,8},{8,4},{12,0},{1,13},{5,9},{9,5},{13,1},{2,14},{6,10},... | collective-permute-start | bytes 98312 | tf_op jit(solution)/shard_map/ppermute | solution.py:272
  20.4 4.4 %collective-permute-start.3 = (bf16[8,2048]{1,0:T(8,128)(2,1)S(1)}, bf16[8,2048]{1,0:T(8,128)(2,1)S(1)}, u32[]{:S(2)}, u32[]{:S(2)}) collective-permute-start(bf16[8,2048]{1,0:T(8,128)(2,1)S(1)} %get-tuple-element.20.refs_0_.after), channel_id=1, source_target_pairs={{0,8},{4,12},{8,0},{12,4},{1,9},{5,13},{9,1},{13,5},{2,10},{6,14},... | collective-permute-start | bytes 98312 | tf_op jit(solution)/shard_map/ppermute | solution.py:272
  21.9 2.9 %collective-permute-start.2 = (bf16[8,2048]{1,0:T(8,128)(2,1)S(1)}, bf16[8,2048]{1,0:T(8,128)(2,1)S(1)}, u32[]{:S(2)}, u32[]{:S(2)}) collective-permute-start(bf16[8,2048]{1,0:T(8,128)(2,1)S(1)} %get-tuple-element.20.refs_0_.after), channel_id=1, source_target_pairs={{0,4},{4,0},{8,12},{12,8},{1,5},{5,1},{9,13},{13,9},{2,6},{6,2},{1... | collective-permute-start | bytes 98312 | tf_op jit(solution)/shard_map/ppermute | solution.py:272
  25.6 8.4 %collective-permute-start.6 = (bf16[32,1024]{1,0:T(8,128)(2,1)S(1)}, bf16[32,1024]{1,0:T(8,128)(2,1)S(1)}, u32[]{:S(2)}, u32[]{:S(2)}) collective-permute-start(bf16[32,1024]{1,0:T(8,128)(2,1)S(1)} %project_out.4), channel_id=1, source_target_pairs={{0,2},{1,3},{2,0},{3,1},{4,6},{5,7},{6,4},{7,5},{8,10},{9,11},{10,... | collective-permute-start | bytes 196616 | tf_op jit(solution)/shard_map/ppermute | solution.py:272
  29.0 6.7 %collective-permute-start.7 = (bf16[32,1024]{1,0:T(8,128)(2,1)S(1)}, bf16[32,1024]{1,0:T(8,128)(2,1)S(1)}, u32[]{:S(2)}, u32[]{:S(2)}) collective-permute-start(bf16[32,1024]{1,0:T(8,128)(2,1)S(1)} %project_out.5), channel_id=1, source_target_pairs={{0,3},{1,2},{2,1},{3,0},{4,7},{5,6},{6,5},{7,4},{8,11},{9,10},{10,... | collective-permute-start | bytes 196616 | tf_op jit(solution)/shard_map/ppermute | solution.py:272
  31.2 4.8 %collective-permute-start.5 = (bf16[32,1024]{1,0:T(8,128)(2,1)S(1)}, bf16[32,1024]{1,0:T(8,128)(2,1)S(1)}, u32[]{:S(2)}, u32[]{:S(2)}) collective-permute-start(bf16[32,1024]{1,0:T(8,128)(2,1)S(1)} %project_out.3), channel_id=1, source_target_pairs={{0,1},{1,0},{2,3},{3,2},{4,5},{5,4},{6,7},{7,6},{8,9},{9,8},{10,11... | collective-permute-start | bytes 196616 | tf_op jit(solution)/shard_map/ppermute | solution.py:272
  36.0 6.1 %collective-permute-start.10 = (bf16[32,1024]{1,0:T(8,128)(2,1)S(1)}, bf16[32,1024]{1,0:T(8,128)(2,1)S(1)}, u32[]{:S(2)}, u32[]{:S(2)}) collective-permute-start(bf16[32,1024]{1,0:T(8,128)(2,1)S(1)} %finish.1.refs_0_), channel_id=1, source_target_pairs={{0,3},{1,2},{2,1},{3,0},{4,7},{5,6},{6,5},{7,4},{8,11},{9,10},{10,... | collective-permute-start | bytes 196616 | tf_op jit(solution)/shard_map/ppermute | solution.py:272
  38.4 5.7 %collective-permute-start.9 = (bf16[32,1024]{1,0:T(8,128)(2,1)S(1)}, bf16[32,1024]{1,0:T(8,128)(2,1)S(1)}, u32[]{:S(2)}, u32[]{:S(2)}) collective-permute-start(bf16[32,1024]{1,0:T(8,128)(2,1)S(1)} %finish.1.refs_0_), channel_id=1, source_target_pairs={{0,2},{1,3},{2,0},{3,1},{4,6},{5,7},{6,4},{7,5},{8,10},{9,11},{10,... | collective-permute-start | bytes 196616 | tf_op jit(solution)/shard_map/ppermute | solution.py:272
  38.4 5.7 %collective-permute-start.8 = (bf16[32,1024]{1,0:T(8,128)(2,1)S(1)}, bf16[32,1024]{1,0:T(8,128)(2,1)S(1)}, u32[]{:S(2)}, u32[]{:S(2)}) collective-permute-start(bf16[32,1024]{1,0:T(8,128)(2,1)S(1)} %finish.1.refs_0_), channel_id=1, source_target_pairs={{0,1},{1,0},{2,3},{3,2},{4,5},{5,4},{6,7},{7,6},{8,9},{9,8},{10,11... | collective-permute-start | bytes 196616 | tf_op jit(solution)/shard_map/ppermute | solution.py:272

commit v9 on v8

--- a/solution.py
+++ b/solution.py
@@ -14,6 +14,8 @@
 CHUNK = 256
 F32 = jnp.float32
 BF16 = jnp.bfloat16
+F16 = jnp.float16
+SQUARES = 2.0**-8
 
 ANY = pl.BlockSpec(memory_space=pl.ANY)
 VMEM = pl.BlockSpec(memory_space=pltpu.VMEM)
@@ -41,7 +43,8 @@
 
 
 def project(size, x_hbm, gain_hbm, wq_hbm, wk_hbm, wv_hbm, *refs):
-    kept, given, x, gain, wq, wk, wv, scaled, total, sems = refs
+    outs = refs[:size]
+    x, gain, wq, wk, wv, scaled, total, sems = refs[size:]
     depth = x.shape[1]
     steps = depth // CHUNK
     pairs = [(x_hbm, x), (gain_hbm, gain), (wk_hbm, wk), (wv_hbm, wv)]
@@ -79,17 +82,19 @@
             small[3].wait()
             total[:, width + HD : width + 2 * HD] = dot(scaled[...], wv[...])
             total[:, width + 2 * HD :] = jnp.broadcast_to(squares, (squares.shape[0], HD))
-    rows = kept.shape[1]
+    rows = outs[0].shape[0]
     me = lax.axis_index("gx")
-    for mask in range(size):
-        out = given if mask % 2 else kept
+    first = lax.broadcasted_iota(jnp.int32, (rows, HD), 1) < HD // 2
+    for mask, out in enumerate(outs):
         start = pl.multiple_of((me ^ mask) * rows, 8)
-        out[mask // 2] = total[pl.ds(start, rows), :]
-
-
-def merge(kept, arrived, *outs):
-    for index, out in enumerate(outs):
-        out[...] = kept[index] + arrived[index]
+        part = total[pl.ds(start, rows), :]
+        if mask:
+            whole = part[:, width + 2 * HD :] * SQUARES
+            high = whole.astype(BF16).astype(F32)
+            out[:, : width + 2 * HD] = part[:, : width + 2 * HD]
+            out[:, width + 2 * HD :] = jnp.where(first, high, whole - high)
+        else:
+            out[...] = part
 
 
 def fetch_pieces(masks, width, w_hbm, pieces, sems, first):
@@ -101,11 +106,10 @@
     return copies
 
 
-def fetch_caches(after, k_hbm, v_hbm, k_turned, v, k, sems):
+def fetch_keys(after, k_hbm, k_turned, k, sems):
     del after
     rows, slots = k.shape[0], k.shape[1]
     copies = [pltpu.make_async_copy(k_hbm.at[r], k.at[r], sems.at[r]) for r in range(rows)]
-    copies.append(pltpu.make_async_copy(v_hbm, v, sems.at[rows]))
     for copy in copies:
         copy.start()
     for row in range(rows):
@@ -113,7 +117,6 @@
         for start in range(0, slots, CHUNK):
             part = slice(start, start + CHUNK)
             k_turned[row, :, part] = k[row, part, :].T
-    copies[rows].wait()
 
 
 def fetch_weights(masks, after, w_hbm, *refs):
@@ -126,21 +129,26 @@
         copy.wait()
 
 
-def attention(size, model, masks, lengths, cosine, sine, k, v, w_hbm, *refs):
+def attention(size, model, masks, lengths, cosine, sine, k, v_hbm, w_hbm, *refs):
     arrived = refs[:size]
     heads = refs[size]
     pieces = refs[size + 1 : size + 1 + len(masks)]
-    q_rows, o_rows, scores, sems = refs[size + 1 + len(masks) :]
-    copies = fetch_pieces(masks, pieces[0].shape[1], w_hbm, pieces, sems, 0) if masks else []
+    q_rows, o_rows, scores, v, sems = refs[size + 1 + len(masks) :]
+    copies = [pltpu.make_async_copy(v_hbm, v, sems.at[0])]
+    if masks:
+        copies += fetch_pieces(masks, pieces[0].shape[1], w_hbm, pieces, sems, 1)
     for copy in copies:
         copy.start()
     rows, slots = k.shape[0], k.shape[2]
     group = heads.shape[1] // HD
     width = group * HD
-    summed = arrived[0][...]
+    summed = arrived[0][:, : width + 2 * HD]
+    squares = arrived[0][:, width + 2 * HD :]
     for item in arrived[1:]:
-        summed = summed + item[...].astype(F32)
-    scale = lax.rsqrt(summed[:, width + 2 * HD :] / model + EPS)
+        summed = summed + item[:, : width + 2 * HD].astype(F32)
+        parts = item[:, width + 2 * HD :].astype(F32)
+        squares = squares + (parts + pltpu.roll(parts, HD // 2, 1)) * (1.0 / SQUARES)
+    scale = lax.rsqrt(squares / model + EPS)
     cosines, sines = cosine[...], sine[...]
 
     def turn(value):
@@ -148,7 +156,7 @@
 
     for head in range(group):
         part = summed[:, head * HD : (head + 1) * HD] * scale
-        q_rows[head] = turn(part).astype(BF16).astype(F32)
+        q_rows[head * rows : (head + 1) * rows] = turn(part).astype(BF16).astype(F32)
     new_keys = turn(summed[:, width : width + HD] * scale).astype(BF16).astype(F32)
     new_values = (summed[:, width + HD : width + 2 * HD] * scale).astype(BF16).astype(F32)
     rate = HD ** (-0.5) * math.log2(math.e)
@@ -158,7 +166,8 @@
     empty = jnp.zeros((group, HD), F32)
     own, top = [], []
     for row in range(0, rows, 2):
-        first, other = q_rows[:, row, :], q_rows[:, row + 1, :]
+        first = q_rows[pl.ds(row, group, stride=rows), :]
+        other = q_rows[pl.ds(row + 1, group, stride=rows), :]
         queries = jnp.concatenate(
             [jnp.concatenate([first, empty], 1), jnp.concatenate([empty, other], 1)], 0
         )
@@ -181,24 +190,26 @@
         probs = jnp.exp2((scores[mine] - top[pair]) * rate)
         own_prob = jnp.exp2((own[pair] - top[pair]) * rate)
         share = 1.0 / (jnp.sum(probs, 1, keepdims=True) + own_prob)
-        return probs.astype(BF16), own_prob, share
+        return (probs * share).astype(BF16), (own_prob * share).astype(BF16).astype(F32)
 
     ready = soften(0)
     for pair in range(rows // 2):
-        probs, own_prob, share = ready
+        weights, own_weight = ready
         if pair + 1 < rows // 2:
             ready = soften(pair + 1)
+        if not pair:
+            copies[0].wait()
         sides = jnp.concatenate([v[2 * pair], v[2 * pair + 1]], 1)
-        mixed = jnp.dot(probs, sides, preferred_element_type=F32)
+        mixed = jnp.dot(weights, sides, preferred_element_type=F32)
         for side in range(2):
             row = 2 * pair + side
             mine = slice(side * group, (side + 1) * group)
             value = mixed[mine, side * HD : (side + 1) * HD]
-            extra = own_prob[mine] * new_values[row : row + 1]
-            o_rows[:, row, :] = (value + extra) * share[mine]
+            extra = own_weight[mine] * new_values[row : row + 1]
+            o_rows[pl.ds(row, group, stride=rows), :] = value + extra
     for head in range(group):
-        heads[:, head * HD : (head + 1) * HD] = o_rows[head].astype(BF16)
-    for copy in copies:
+        heads[:, head * HD : (head + 1) * HD] = o_rows[head * rows : (head + 1) * rows].astype(BF16)
+    for copy in copies[1:]:
         copy.wait()
 
 
@@ -290,12 +301,11 @@
         piece = pltpu.VMEM((width, block), BF16)
         piece_bytes = 2 * width * block
 
-        levels = size_x // 2
-        kept, given = pl.pallas_call(
+        sums = pl.pallas_call(
             functools.partial(project, size_x),
-            out_shape=[pltpu.VMEM((levels, rows, packed), F32)] * 2,
+            out_shape=[pltpu.VMEM((rows, packed), F32)] * size_x,
             in_specs=[ANY] * 5,
-            out_specs=[VMEM] * 2,
+            out_specs=[VMEM] * size_x,
             scratch_shapes=[
                 pltpu.VMEM(inputs.shape, BF16),
                 pltpu.VMEM((1, depth), F32),
@@ -310,29 +320,19 @@
             cost_estimate=cost(2 * batch * depth * packed, 2 * depth * packed),
             name="project",
         )(*[in_hbm(a) for a in (inputs, gain.reshape(1, depth), w_query, w_key, w_value)])
-        sums = pl.pallas_call(
-            merge,
-            out_shape=[pltpu.VMEM((rows, packed), F32)] * levels,
-            in_specs=[VMEM] * 2,
-            out_specs=[VMEM] * levels,
-            compiler_params=params(4),
-            name="merge",
-        )(in_vmem(kept), in_vmem(swap(given, "gx", size_x, 1)))
-        arrived = [sums[0]] + [swap(sums[j], "gx", size_x, 2 * j) for j in range(1, levels)]
-
-        keys, values = pl.pallas_call(
-            fetch_caches,
-            out_shape=[
-                pltpu.VMEM((rows, HD, key_cache.shape[1]), BF16),
-                pltpu.VMEM(value_cache.shape, BF16),
-            ],
-            in_specs=[ANY] * 3,
-            out_specs=[VMEM] * 2,
-            scratch_shapes=[pltpu.VMEM(key_cache.shape, BF16), sems(rows + 1)],
+        arrived = [sums[0]]
+        for mask in range(1, size_x):
+            arrived.append(swap(sums[mask].astype(F16), "gx", size_x, mask).astype(F32))
+        keys = pl.pallas_call(
+            fetch_keys,
+            out_shape=pltpu.VMEM((rows, HD, key_cache.shape[1]), BF16),
+            in_specs=[ANY] * 2,
+            out_specs=VMEM,
+            scratch_shapes=[pltpu.VMEM(key_cache.shape, BF16), sems(rows)],
             compiler_params=params(12),
-            cost_estimate=cost(0, 4 * key_cache.size),
-            name="fetch_caches",
-        )(sums[0], in_hbm(key_cache), in_hbm(value_cache))
+            cost_estimate=cost(0, 2 * key_cache.size),
+            name="fetch_keys",
+        )(sums[0], in_hbm(key_cache))
         pieces = []
 
         half = HD // 2
@@ -340,17 +340,18 @@
         angles = lengths.astype(F32)[:, None] * inverse[None, :]
         cosine, sine = jnp.cos(angles), jnp.sin(angles)
         heads, *more = pl.pallas_call(
-            functools.partial(attention, levels, depth * size_x, middle),
+            functools.partial(attention, size_x, depth * size_x, middle),
             out_shape=[pltpu.VMEM((rows, width), BF16)] + [piece] * len(middle),
-            in_specs=[VMEM, VMEM, VMEM, VMEM, VMEM, ANY] + [VMEM] * levels,
+            in_specs=[VMEM, VMEM, VMEM, VMEM, ANY, ANY] + [VMEM] * size_x,
             out_specs=[VMEM] * (1 + len(middle)),
             scratch_shapes=[
-                pltpu.VMEM((width // HD, rows, HD), F32),
-                pltpu.VMEM((width // HD, rows, HD), F32),
+                pltpu.VMEM((rows * (width // HD), HD), F32),
+                pltpu.VMEM((rows * (width // HD), HD), F32),
                 pltpu.VMEM((rows * (width // HD), key_cache.shape[1]), F32),
-                sems(max(len(middle), 1)),
+                pltpu.VMEM(value_cache.shape, BF16),
+                sems(1 + len(middle)),
             ],
-            compiler_params=params(8),
+            compiler_params=params(12),
             cost_estimate=cost(4 * key_cache.size * (width // HD), piece_bytes * len(middle)),
             name="attention",
         )(
@@ -358,7 +359,7 @@
             jnp.concatenate([cosine, cosine], 1),
             jnp.concatenate([-sine, sine], 1),
             in_vmem(keys),
-            in_vmem(values),
+            in_hbm(value_cache),
             in_hbm(w_output),
             *[in_vmem(a) for a in arrived],
         )

time: 45 us -> 43.8 us (0.973)
  Pallas kernels: 23.6 us -> 22.5 us
    pallas_call x3 -> x2, Pallas kernels: 8.68 us -> 7.58 us  [the longest x1 4.94 us: shards(): pl.pallas_call(functools.partial(attention, size_x, depth * size_x, middl...]
    ppermute x11 -> x12, starting transfers between devices: 14 us -> 13.9 us  [swap(): return lax.ppermute(value, axis, [(i, i ^ mask) for i in range(size)])]
    ppermute x11 -> x12, waiting for transfers between devices: 6.83 us -> 6.76 us  [swap(): return lax.ppermute(value, axis, [(i, i ^ mask) for i in range(size)])]
  transfers between devices with their start and end apart: 11 -> 12, of which waited for: 6 -> 6; matrix products, arithmetic and copies ran while one was open for 0% -> 1% of each run, Pallas kernels for 22% -> 21%
where the time goes in v9:
time: 43.8 us; the launch traced here: 43.6 us
  Pallas kernels  22.5 us (51%)
  starting transfers between devices  13.9 us (32%)
  waiting for transfers between devices  6.76 us (15%)
    ppermute x12, starting transfers between devices, swap(): return lax.ppermute(value, axis, [(i, i ^ mask) for i in range(size)])  13.9 us
    pallas_call x1, Pallas kernels, shards(): pl.pallas_call(functools.partial(project, size_x), out_shape=[pltpu.VMEM(...  6.98 us
    ppermute x12, waiting for transfers between devices, swap(): return lax.ppermute(value, axis, [(i, i ^ mask) for i in range(size)])  6.76 us
    pallas_call x1, Pallas kernels, shards(): pl.pallas_call(functools.partial(attention, size_x, depth * size_x, middl...  4.94 us
    pallas_call x1, Pallas kernels, shards(): pl.pallas_call(fetch_keys, out_shape=pltpu.VMEM((rows, HD, key_cache.shap...  2.64 us
    pallas_call x1, Pallas kernels, shards(): pl.pallas_call(functools.partial(stream_out, size_x, mask), in_specs=[ANY...  2.53 us
    pallas_call x3, Pallas kernels, shards(): pl.pallas_call(functools.partial(project_out, size_x), in_specs=[VMEM] *...  2.45 us
    pallas_call x1, Pallas kernels, shards(): pl.pallas_call(functools.partial(fetch_weights, late), out_shape=[piece]...  2.2 us
  transfers between devices with their start and end apart: 12, of which 6 were waited for; matrix products, arithmetic and copies ran while one was open for 1% of the time, Pallas kernels for 21%

profile of v9, /device:TPU:0, one launch (start us, length us, event | category | flops | bytes accessed | tf_op | source)
XLA Modules:
  0.0 43.6 jit_solution(7081397008047282734)
XLA Ops:
  0.0 0.0 copy-start
  0.0 7.0 %project.1 = (f32[8,2432]{1,0:T(8,128)S(1)}, f32[8,2432]{1,0:T(8,128)S(1)}, f32[8,2432]{1,0:T(8,128)S(1)}, f32[8,2432]{1,0:T(8,128)S(1)}) custom-call(bf16[32,4096]{1,0:T(8,128)(2,1)} %x_hbm.3, f32[1,4096]{1,0:T(1,128)} %bitcast.1, bf16[4096,2048]{1,0:T(8,128)(2,1)} %wq_hbm.1, bf16[4096,128]{1,0:T(8,128)(2,1)} %wk_hbm.1, bf16[4096,128]{1,0:T(8,128)(2,1)} %wv_hbm.1), custom_call_target="tpu_custom_call" | custom-call | flops 637534208 | bytes 19922944 | tf_op jit(solution)/shard_map/project/pallas_call | solution.py:304
  7.0 2.4 %collective-permute-start.2 = (f16[8,2432]{1,0:T(8,128)(2,1)S(1)}, f16[8,2432]{1,0:T(8,128)(2,1)S(1)}, u32[]{:S(2)}, u32[]{:S(2)}) collective-permute-start(f16[8,2432]{1,0:T(8,128)(2,1)S(1)} %convert_element_type.26), channel_id=1, source_target_pairs={{0,12},{4,8},{8,4},{12,0},{1,13},{5,9},{9,5},{13,1},{2,14},{6,10},... | collective-permute-start | bytes 116744 | tf_op jit(solution)/shard_map/ppermute | solution.py:283
  9.5 0.6 %collective-permute-start.1 = (f16[8,2432]{1,0:T(8,128)(2,1)S(1)}, f16[8,2432]{1,0:T(8,128)(2,1)S(1)}, u32[]{:S(2)}, u32[]{:S(2)}) collective-permute-start(f16[8,2432]{1,0:T(8,128)(2,1)S(1)} %convert_element_type.24), channel_id=1, source_target_pairs={{0,8},{4,12},{8,0},{12,4},{1,9},{5,13},{9,1},{13,5},{2,10},{6,14},... | collective-permute-start | bytes 116744 | tf_op jit(solution)/shard_map/ppermute | solution.py:283
  10.1 0.2 collective-permute-start
  10.3 0.0 copy-done
  10.3 0.1 fusion
  10.4 0.1 pad_maximum_fusion
  10.5 2.6 %fetch_keys.1.k = bf16[8,128,2048]{2,1,0:T(8,128)(2,1)S(1)} custom-call(f32[8,2432]{1,0:T(8,128)S(1)} %get-tuple-element.12.after.refs_0_, bf16[8,2048,128]{2,1,0:T(8,128)(2,1)} %k_hbm.1), custom_call_target="tpu_custom_call" | custom-call | bytes 4194304 | tf_op jit(solution)/shard_map/fetch_keys/pallas_call | solution.py:326
  13.2 0.0 collective-permute-done.2
  13.2 0.4 %collective-permute-done.1 = f16[8,2432]{1,0:T(8,128)(2,1)S(1)} collective-permute-done((f16[8,2432]{1,0:T(8,128)(2,1)S(1)}, f16[8,2432]{1,0:T(8,128)(2,1)S(1)}, u32[]{:S(2)}, u32[]{:S(2)}) %collective-permute-start.1) | collective-permute-done | bytes 38944 | tf_op jit(solution)/shard_map/ppermute | solution.py:283
  13.6 0.0 collective-permute-done
  13.7 0.1 broadcast_in_dim.2.lengths
  13.7 4.9 %attention.1 = (bf16[8,2048]{1,0:T(8,128)(2,1)S(1)}, bf16[2048,1024]{1,0:T(8,128)(2,1)S(1)}, bf16[2048,1024]{1,0:T(8,128)(2,1)S(1)}) custom-call(s32[8,128]{1,0:T(8,128)S(1)} %broadcast_in_dim.2.lengths, f32[8,128]{1,0:T(8,128)S(1)} %get-tuple-element.22.cosine, f32[8,128]{1,0:T(8,128)S(1)} %get-tuple-element.23.sine, ...), custom_call_target="tpu_custom_call" | custom-call | flops 134217728 | bytes 8388608 | tf_op jit(solution)/shard_map/attention/pallas_call | solution.py:342
  18.7 1.1 %collective-permute-start.5 = (bf16[8,2048]{1,0:T(8,128)(2,1)S(1)}, bf16[8,2048]{1,0:T(8,128)(2,1)S(1)}, u32[]{:S(2)}, u32[]{:S(2)}) collective-permute-start(bf16[8,2048]{1,0:T(8,128)(2,1)S(1)} %get-tuple-element.16.refs_0_.after), channel_id=1, source_target_pairs={{0,12},{4,8},{8,4},{12,0},{1,13},{5,9},{9,5},{13,1},{2,14},{6,10},... | collective-permute-start | bytes 98312 | tf_op jit(solution)/shard_map/ppermute | solution.py:283
  19.8 0.6 %collective-permute-start.4 = (bf16[8,2048]{1,0:T(8,128)(2,1)S(1)}, bf16[8,2048]{1,0:T(8,128)(2,1)S(1)}, u32[]{:S(2)}, u32[]{:S(2)}) collective-permute-start(bf16[8,2048]{1,0:T(8,128)(2,1)S(1)} %get-tuple-element.16.refs_0_.after), channel_id=1, source_target_pairs={{0,8},{4,12},{8,0},{12,4},{1,9},{5,13},{9,1},{13,5},{2,10},{6,14},... | collective-permute-start | bytes 98312 | tf_op jit(solution)/shard_map/ppermute | solution.py:283
  20.3 0.3 collective-permute-start.3
  20.6 2.2 %fetch_weights.1.w = bf16[2048,1024]{1,0:T(8,128)(2,1)S(1)} custom-call(bf16[8,2048]{1,0:T(8,128)(2,1)S(1)} %get-tuple-element.16.refs_0_.after, bf16[2048,4096]{1,0:T(8,128)(2,1)} %w_hbm.5), custom_call_target="tpu_custom_call" | custom-call | bytes 4194304 | tf_op jit(solution)/shard_map/fetch_weights/pallas_call | solution.py:369
  22.8 0.0 collective-permute-done.5.refs_3_
  22.8 0.8 %collective-permute-done.4.refs_2_ = bf16[8,2048]{1,0:T(8,128)(2,1)S(1)} collective-permute-done((bf16[8,2048]{1,0:T(8,128)(2,1)S(1)}, bf16[8,2048]{1,0:T(8,128)(2,1)S(1)}, u32[]{:S(2)}, u32[]{:S(2)}) %collective-permute-start.4) | collective-permute-done | bytes 32800 | tf_op jit(solution)/shard_map/ppermute | solution.py:283
  23.7 0.0 collective-permute-done.3.refs_1_
  23.7 0.8 %project_out.4 = bf16[32,1024]{1,0:T(8,128)(2,1)S(1)} custom-call(bf16[2048,1024]{1,0:T(8,128)(2,1)S(1)} %get-tuple-element.17.w, bf16[8,2048]{1,0:T(8,128)(2,1)S(1)} %get-tuple-element.16.refs_0_.after, bf16[8,2048]{1,0:T(8,128)(2,1)S(1)} %collective-permute-done.3.refs_1_, bf16[8,2048]{1,0:T(8,128)(2,1)S(1)} %collective-permute-done.4.refs_2_, ...), custom_call_target="tpu_custom_call" | custom-call | flops 134217728 | bytes 4194304 | tf_op jit(solution)/shard_map/project_out/pallas_call | solution.py:393
  24.5 2.6 %collective-permute-start.7 = (bf16[32,1024]{1,0:T(8,128)(2,1)S(1)}, bf16[32,1024]{1,0:T(8,128)(2,1)S(1)}, u32[]{:S(2)}, u32[]{:S(2)}) collective-permute-start(bf16[32,1024]{1,0:T(8,128)(2,1)S(1)} %project_out.4), channel_id=1, source_target_pairs={{0,2},{1,3},{2,0},{3,1},{4,6},{5,7},{6,4},{7,5},{8,10},{9,11},{10,... | collective-permute-start | bytes 196616 | tf_op jit(solution)/shard_map/ppermute | solution.py:283
  27.1 0.8 %project_out.5 = bf16[32,1024]{1,0:T(8,128)(2,1)S(1)} custom-call(bf16[2048,1024]{1,0:T(8,128)(2,1)S(1)} %get-tuple-element.18.w, bf16[8,2048]{1,0:T(8,128)(2,1)S(1)} %get-tuple-element.16.refs_0_.after, bf16[8,2048]{1,0:T(8,128)(2,1)S(1)} %collective-permute-done.3.refs_1_, bf16[8,2048]{1,0:T(8,128)(2,1)S(1)} %collective-permute-done.4.refs_2_, ...), custom_call_target="tpu_custom_call" | custom-call | flops 134217728 | bytes 4194304 | tf_op jit(solution)/shard_map/project_out/pallas_call | solution.py:393
  27.9 1.4 %collective-permute-start.8 = (bf16[32,1024]{1,0:T(8,128)(2,1)S(1)}, bf16[32,1024]{1,0:T(8,128)(2,1)S(1)}, u32[]{:S(2)}, u32[]{:S(2)}) collective-permute-start(bf16[32,1024]{1,0:T(8,128)(2,1)S(1)} %project_out.5), channel_id=1, source_target_pairs={{0,3},{1,2},{2,1},{3,0},{4,7},{5,6},{6,5},{7,4},{8,11},{9,10},{10,... | collective-permute-start | bytes 196616 | tf_op jit(solution)/shard_map/ppermute | solution.py:283
  29.3 0.8 %project_out.3 = bf16[32,1024]{1,0:T(8,128)(2,1)S(1)} custom-call(bf16[2048,1024]{1,0:T(8,128)(2,1)S(1)} %fetch_weights.1.w, bf16[8,2048]{1,0:T(8,128)(2,1)S(1)} %get-tuple-element.16.refs_0_.after, bf16[8,2048]{1,0:T(8,128)(2,1)S(1)} %collective-permute-done.3.refs_1_, bf16[8,2048]{1,0:T(8,128)(2,1)S(1)} %collective-permute-done.4.refs_2_, ...), custom_call_target="tpu_custom_call" | custom-call | flops 134217728 | bytes 4194304 | tf_op jit(solution)/shard_map/project_out/pallas_call | solution.py:393
  30.1 0.3 collective-permute-start.6
  30.4 2.5 %stream_out.1.own = f32[32,1024]{1,0:T(8,128)S(1)} custom-call(bf16[2048,4096]{1,0:T(8,128)(2,1)} %w_hbm.5, bf16[32,4096]{1,0:T(8,128)(2,1)} %x_hbm.3, bf16[8,2048]{1,0:T(8,128)(2,1)S(1)} %get-tuple-element.16.refs_0_.after, bf16[8,2048]{1,0:T(8,128)(2,1)S(1)} %collective-permute-done.3.refs_1_, bf16[8,2048]{1,0:T(8,128)(2,1)S(1)} %collective-permute-done.4.refs_2_, ...), custom_call_target="tpu_custom_call" | custom-call | flops 134217728 | bytes 4194304 | tf_op jit(solution)/shard_map/stream_out/pallas_call | solution.py:406
  32.9 0.0 collective-permute-done.7.refs_1_
  32.9 1.2 %collective-permute-done.8.refs_2_ = bf16[32,1024]{1,0:T(8,128)(2,1)S(1)} collective-permute-done((bf16[32,1024]{1,0:T(8,128)(2,1)S(1)}, bf16[32,1024]{1,0:T(8,128)(2,1)S(1)}, u32[]{:S(2)}, u32[]{:S(2)}) %collective-permute-start.8) | collective-permute-done | bytes 65568 | tf_op jit(solution)/shard_map/ppermute | solution.py:283
  34.1 0.7 %collective-permute-done.6.refs_0_ = bf16[32,1024]{1,0:T(8,128)(2,1)S(1)} collective-permute-done((bf16[32,1024]{1,0:T(8,128)(2,1)S(1)}, bf16[32,1024]{1,0:T(8,128)(2,1)S(1)}, u32[]{:S(2)}, u32[]{:S(2)}) %collective-permute-start.6) | collective-permute-done | bytes 65568 | tf_op jit(solution)/shard_map/ppermute | solution.py:283
  34.8 2.1 %collective-permute-start.11 = (bf16[32,1024]{1,0:T(8,128)(2,1)S(1)}, bf16[32,1024]{1,0:T(8,128)(2,1)S(1)}, u32[]{:S(2)}, u32[]{:S(2)}) collective-permute-start(bf16[32,1024]{1,0:T(8,128)(2,1)S(1)} %finish.1.refs_0_), channel_id=1, source_target_pairs={{0,3},{1,2},{2,1},{3,0},{4,7},{5,6},{6,5},{7,4},{8,11},{9,10},{10,... | collective-permute-start | bytes 196616 | tf_op jit(solution)/shard_map/ppermute | solution.py:283
  37.0 0.0 collective-permute-start.10
  37.0 2.3 %collective-permute-start.9 = (bf16[32,1024]{1,0:T(8,128)(2,1)S(1)}, bf16[32,1024]{1,0:T(8,128)(2,1)S(1)}, u32[]{:S(2)}, u32[]{:S(2)}) collective-permute-start(bf16[32,1024]{1,0:T(8,128)(2,1)S(1)} %finish.1.refs_0_), channel_id=1, source_target_pairs={{0,1},{1,0},{2,3},{3,2},{4,5},{5,4},{6,7},{7,6},{8,9},{9,8},{10,11... | collective-permute-start | bytes 196616 | tf_op jit(solution)/shard_map/ppermute | solution.py:283
  39.3 2.3 %collective-permute-done.11.refs_3_ = bf16[32,1024]{1,0:T(8,128)(2,1)S(1)} collective-permute-done((bf16[32,1024]{1,0:T(8,128)(2,1)S(1)}, bf16[32,1024]{1,0:T(8,128)(2,1)S(1)}, u32[]{:S(2)}, u32[]{:S(2)}) %collective-permute-start.11) | collective-permute-done | bytes 65568 | tf_op jit(solution)/shard_map/ppermute | solution.py:283
  41.6 1.3 %collective-permute-done.10.refs_2_ = bf16[32,1024]{1,0:T(8,128)(2,1)S(1)} collective-permute-done((bf16[32,1024]{1,0:T(8,128)(2,1)S(1)}, bf16[32,1024]{1,0:T(8,128)(2,1)S(1)}, u32[]{:S(2)}, u32[]{:S(2)}) %collective-permute-start.10) | collective-permute-done | bytes 65568 | tf_op jit(solution)/shard_map/ppermute | solution.py:283
  42.9 0.0 collective-permute-done.9.refs_1_
  42.9 0.7 %assemble.1 = bf16[32,4096]{1,0:T(8,128)(2,1)} custom-call(bf16[32,1024]{1,0:T(8,128)(2,1)S(1)} %finish.1.refs_0_, bf16[32,1024]{1,0:T(8,128)(2,1)S(1)} %collective-permute-done.9.refs_1_, bf16[32,1024]{1,0:T(8,128)(2,1)S(1)} %collective-permute-done.10.refs_2_, bf16[32,1024]{1,0:T(8,128)(2,1)S(1)} %collective-permute-done.11.refs_3_), custom_call_target="tpu_custom_call" | custom-call | tf_op jit(solution)/shard_map/assemble/pallas_call | solution.py:423
  (9 shorter events, 0.1 us)
Async XLA Ops:
  0.0 10.3 %copy-start = (s32[8]{0:T(128)S(1)}, s32[8]{0:T(128)}, u32[]{:S(2)}) copy-start(s32[8]{0:T(128)} %param.17) | copy-start | bytes 100
  7.0 6.2 %collective-permute-start.2 = (f16[8,2432]{1,0:T(8,128)(2,1)S(1)}, f16[8,2432]{1,0:T(8,128)(2,1)S(1)}, u32[]{:S(2)}, u32[]{:S(2)}) collective-permute-start(f16[8,2432]{1,0:T(8,128)(2,1)S(1)} %convert_element_type.26), channel_id=1, source_target_pairs={{0,12},{4,8},{8,4},{12,0},{1,13},{5,9},{9,5},{13,1},{2,14},{6,10},... | collective-permute-start | bytes 116744 | tf_op jit(solution)/shard_map/ppermute | solution.py:283
  9.5 4.2 %collective-permute-start.1 = (f16[8,2432]{1,0:T(8,128)(2,1)S(1)}, f16[8,2432]{1,0:T(8,128)(2,1)S(1)}, u32[]{:S(2)}, u32[]{:S(2)}) collective-permute-start(f16[8,2432]{1,0:T(8,128)(2,1)S(1)} %convert_element_type.24), channel_id=1, source_target_pairs={{0,8},{4,12},{8,0},{12,4},{1,9},{5,13},{9,1},{13,5},{2,10},{6,14},... | collective-permute-start | bytes 116744 | tf_op jit(solution)/shard_map/ppermute | solution.py:283
  10.1 3.5 %collective-permute-start = (f16[8,2432]{1,0:T(8,128)(2,1)S(1)}, f16[8,2432]{1,0:T(8,128)(2,1)S(1)}, u32[]{:S(2)}, u32[]{:S(2)}) collective-permute-start(f16[8,2432]{1,0:T(8,128)(2,1)S(1)} %convert_element_type.22), channel_id=1, source_target_pairs={{0,4},{4,0},{8,12},{12,8},{1,5},{5,1},{9,13},{13,9},{2,6},{6,2},{1... | collective-permute-start | bytes 116744 | tf_op jit(solution)/shard_map/ppermute | solution.py:283
  18.7 4.1 %collective-permute-start.5 = (bf16[8,2048]{1,0:T(8,128)(2,1)S(1)}, bf16[8,2048]{1,0:T(8,128)(2,1)S(1)}, u32[]{:S(2)}, u32[]{:S(2)}) collective-permute-start(bf16[8,2048]{1,0:T(8,128)(2,1)S(1)} %get-tuple-element.16.refs_0_.after), channel_id=1, source_target_pairs={{0,12},{4,8},{8,4},{12,0},{1,13},{5,9},{9,5},{13,1},{2,14},{6,10},... | collective-permute-start | bytes 98312 | tf_op jit(solution)/shard_map/ppermute | solution.py:283
  19.8 3.9 %collective-permute-start.4 = (bf16[8,2048]{1,0:T(8,128)(2,1)S(1)}, bf16[8,2048]{1,0:T(8,128)(2,1)S(1)}, u32[]{:S(2)}, u32[]{:S(2)}) collective-permute-start(bf16[8,2048]{1,0:T(8,128)(2,1)S(1)} %get-tuple-element.16.refs_0_.after), channel_id=1, source_target_pairs={{0,8},{4,12},{8,0},{12,4},{1,9},{5,13},{9,1},{13,5},{2,10},{6,14},... | collective-permute-start | bytes 98312 | tf_op jit(solution)/shard_map/ppermute | solution.py:283
  20.3 3.3 %collective-permute-start.3 = (bf16[8,2048]{1,0:T(8,128)(2,1)S(1)}, bf16[8,2048]{1,0:T(8,128)(2,1)S(1)}, u32[]{:S(2)}, u32[]{:S(2)}) collective-permute-start(bf16[8,2048]{1,0:T(8,128)(2,1)S(1)} %get-tuple-element.16.refs_0_.after), channel_id=1, source_target_pairs={{0,4},{4,0},{8,12},{12,8},{1,5},{5,1},{9,13},{13,9},{2,6},{6,2},{1... | collective-permute-start | bytes 98312 | tf_op jit(solution)/shard_map/ppermute | solution.py:283
  24.5 8.4 %collective-permute-start.7 = (bf16[32,1024]{1,0:T(8,128)(2,1)S(1)}, bf16[32,1024]{1,0:T(8,128)(2,1)S(1)}, u32[]{:S(2)}, u32[]{:S(2)}) collective-permute-start(bf16[32,1024]{1,0:T(8,128)(2,1)S(1)} %project_out.4), channel_id=1, source_target_pairs={{0,2},{1,3},{2,0},{3,1},{4,6},{5,7},{6,4},{7,5},{8,10},{9,11},{10,... | collective-permute-start | bytes 196616 | tf_op jit(solution)/shard_map/ppermute | solution.py:283
  27.9 6.2 %collective-permute-start.8 = (bf16[32,1024]{1,0:T(8,128)(2,1)S(1)}, bf16[32,1024]{1,0:T(8,128)(2,1)S(1)}, u32[]{:S(2)}, u32[]{:S(2)}) collective-permute-start(bf16[32,1024]{1,0:T(8,128)(2,1)S(1)} %project_out.5), channel_id=1, source_target_pairs={{0,3},{1,2},{2,1},{3,0},{4,7},{5,6},{6,5},{7,4},{8,11},{9,10},{10,... | collective-permute-start | bytes 196616 | tf_op jit(solution)/shard_map/ppermute | solution.py:283
  30.1 4.7 %collective-permute-start.6 = (bf16[32,1024]{1,0:T(8,128)(2,1)S(1)}, bf16[32,1024]{1,0:T(8,128)(2,1)S(1)}, u32[]{:S(2)}, u32[]{:S(2)}) collective-permute-start(bf16[32,1024]{1,0:T(8,128)(2,1)S(1)} %project_out.3), channel_id=1, source_target_pairs={{0,1},{1,0},{2,3},{3,2},{4,5},{5,4},{6,7},{7,6},{8,9},{9,8},{10,11... | collective-permute-start | bytes 196616 | tf_op jit(solution)/shard_map/ppermute | solution.py:283
  34.8 6.7 %collective-permute-start.11 = (bf16[32,1024]{1,0:T(8,128)(2,1)S(1)}, bf16[32,1024]{1,0:T(8,128)(2,1)S(1)}, u32[]{:S(2)}, u32[]{:S(2)}) collective-permute-start(bf16[32,1024]{1,0:T(8,128)(2,1)S(1)} %finish.1.refs_0_), channel_id=1, source_target_pairs={{0,3},{1,2},{2,1},{3,0},{4,7},{5,6},{6,5},{7,4},{8,11},{9,10},{10,... | collective-permute-start | bytes 196616 | tf_op jit(solution)/shard_map/ppermute | solution.py:283
  37.0 5.9 %collective-permute-start.10 = (bf16[32,1024]{1,0:T(8,128)(2,1)S(1)}, bf16[32,1024]{1,0:T(8,128)(2,1)S(1)}, u32[]{:S(2)}, u32[]{:S(2)}) collective-permute-start(bf16[32,1024]{1,0:T(8,128)(2,1)S(1)} %finish.1.refs_0_), channel_id=1, source_target_pairs={{0,2},{1,3},{2,0},{3,1},{4,6},{5,7},{6,4},{7,5},{8,10},{9,11},{10,... | collective-permute-start | bytes 196616 | tf_op jit(solution)/shard_map/ppermute | solution.py:283
  37.0 5.9 %collective-permute-start.9 = (bf16[32,1024]{1,0:T(8,128)(2,1)S(1)}, bf16[32,1024]{1,0:T(8,128)(2,1)S(1)}, u32[]{:S(2)}, u32[]{:S(2)}) collective-permute-start(bf16[32,1024]{1,0:T(8,128)(2,1)S(1)} %finish.1.refs_0_), channel_id=1, source_target_pairs={{0,1},{1,0},{2,3},{3,2},{4,5},{5,4},{6,7},{7,6},{8,9},{9,8},{10,11... | collective-permute-start | bytes 196616 | tf_op jit(solution)/shard_map/ppermute | solution.py:283

commit v10 on v9

--- a/solution.py
+++ b/solution.py
@@ -42,9 +42,8 @@
     return pltpu.with_memory_space_constraint(value, pltpu.HBM)
 
 
-def project(size, x_hbm, gain_hbm, wq_hbm, wk_hbm, wv_hbm, *refs):
-    outs = refs[:size]
-    x, gain, wq, wk, wv, scaled, total, sems = refs[size:]
+def project(x_hbm, gain_hbm, wq_hbm, wk_hbm, wv_hbm, *refs):
+    total, x, gain, wq, wk, wv, scaled, sems = refs
     depth = x.shape[1]
     steps = depth // CHUNK
     pairs = [(x_hbm, x), (gain_hbm, gain), (wk_hbm, wk), (wv_hbm, wv)]
@@ -82,6 +81,11 @@
             small[3].wait()
             total[:, width + HD : width + 2 * HD] = dot(scaled[...], wv[...])
             total[:, width + 2 * HD :] = jnp.broadcast_to(squares, (squares.shape[0], HD))
+
+
+def split(total, weights, *outs):
+    del weights
+    width = total.shape[1] - 3 * HD
     rows = outs[0].shape[0]
     me = lax.axis_index("gx")
     first = lax.broadcasted_iota(jnp.int32, (rows, HD), 1) < HD // 2
@@ -97,48 +101,19 @@
             out[...] = part
 
 
-def fetch_pieces(masks, width, w_hbm, pieces, sems, first):
-    me = lax.axis_index("gy")
-    copies = []
-    for i, mask in enumerate(masks):
-        source = w_hbm.at[:, columns(me ^ mask, width)]
-        copies.append(pltpu.make_async_copy(source, pieces[i], sems.at[first + i]))
-    return copies
-
-
-def fetch_keys(after, k_hbm, k_turned, k, sems):
-    del after
+def turn_keys(after, k, v, k_turned):
+    del after, v
     rows, slots = k.shape[0], k.shape[1]
-    copies = [pltpu.make_async_copy(k_hbm.at[r], k.at[r], sems.at[r]) for r in range(rows)]
-    for copy in copies:
-        copy.start()
     for row in range(rows):
-        copies[row].wait()
         for start in range(0, slots, CHUNK):
             part = slice(start, start + CHUNK)
             k_turned[row, :, part] = k[row, part, :].T
 
 
-def fetch_weights(masks, after, w_hbm, *refs):
-    del after
-    *pieces, sems = refs
-    copies = fetch_pieces(masks, pieces[0].shape[1], w_hbm, pieces, sems, 0)
-    for copy in copies:
-        copy.start()
-    for copy in copies:
-        copy.wait()
-
-
-def attention(size, model, masks, lengths, cosine, sine, k, v_hbm, w_hbm, *refs):
+def attention(size, model, weights, lengths, cosine, sine, k, v, *refs):
+    del weights
     arrived = refs[:size]
-    heads = refs[size]
-    pieces = refs[size + 1 : size + 1 + len(masks)]
-    q_rows, o_rows, scores, v, sems = refs[size + 1 + len(masks) :]
-    copies = [pltpu.make_async_copy(v_hbm, v, sems.at[0])]
-    if masks:
-        copies += fetch_pieces(masks, pieces[0].shape[1], w_hbm, pieces, sems, 1)
-    for copy in copies:
-        copy.start()
+    heads, q_rows, o_rows, scores = refs[size:]
     rows, slots = k.shape[0], k.shape[2]
     group = heads.shape[1] // HD
     width = group * HD
@@ -197,8 +172,6 @@
         weights, own_weight = ready
         if pair + 1 < rows // 2:
             ready = soften(pair + 1)
-        if not pair:
-            copies[0].wait()
         sides = jnp.concatenate([v[2 * pair], v[2 * pair + 1]], 1)
         mixed = jnp.dot(weights, sides, preferred_element_type=F32)
         for side in range(2):
@@ -209,8 +182,6 @@
             o_rows[pl.ds(row, group, stride=rows), :] = value + extra
     for head in range(group):
         heads[:, head * HD : (head + 1) * HD] = o_rows[head * rows : (head + 1) * rows].astype(BF16)
-    for copy in copies[1:]:
-        copy.wait()
 
 
 def gather_rows(blocks, gathered):
@@ -222,38 +193,13 @@
     return gathered[...].astype(BF16)
 
 
-def project_out(size, w, *refs):
+def project_out(size, mask, w, x, *refs):
     blocks, out, gathered = refs[:size], refs[-2], refs[-1]
+    part = columns(lax.axis_index("gy") ^ mask, out.shape[1])
     heads = gather_rows(blocks, gathered)
-    out[...] = jnp.dot(heads, w[...], preferred_element_type=F32).astype(out.dtype)
-
-
-def stream_out(size, mask, w_hbm, x_hbm, *refs):
-    blocks = refs[:size]
-    out, gathered, w, x, sems = refs[-5:]
-    width = out.shape[1]
-    me = lax.axis_index("gy")
-    steps = w.shape[0] // (2 * CHUNK)
-    copies = []
-    for step in range(steps):
-        part = pl.ds(step * 2 * CHUNK, 2 * CHUNK)
-        source = w_hbm.at[part, columns(me ^ mask, width)]
-        copies.append(pltpu.make_async_copy(source, w.at[part], sems.at[step]))
+    total = jnp.dot(heads, w[:, part], preferred_element_type=F32)
     if not mask:
-        source = x_hbm.at[:, columns(me, width)]
-        copies.append(pltpu.make_async_copy(source, x, sems.at[steps]))
-    for copy in copies:
-        copy.start()
-    heads = gather_rows(blocks, gathered)
-    total = None
-    for step in range(steps):
-        copies[step].wait()
-        part = slice(step * 2 * CHUNK, (step + 1) * 2 * CHUNK)
-        term = jnp.dot(heads[:, part], w[part], preferred_element_type=F32)
-        total = term if total is None else total + term
-    if not mask:
-        copies[steps].wait()
-        total = total + x[...].astype(F32)
+        total = total + x[:, part].astype(F32)
     out[...] = total.astype(out.dtype)
 
 
@@ -289,8 +235,6 @@
     struct = jax.ShapeDtypeStruct
     sems = lambda n: pltpu.SemaphoreType.DMA((n,))
     order = list(range(size_y - 1, -1, -1))
-    quarter = max(size_y // 4, 1)
-    middle, late = order[: 2 * quarter], order[2 * quarter : -1]
 
     def shards(inputs, gain, w_query, w_key, w_value, w_output, key_cache, value_cache, lengths):
         batch, depth = inputs.shape
@@ -298,14 +242,12 @@
         rows = key_cache.shape[0]
         packed = width + 3 * HD
         block = w_output.shape[1] // size_y
-        piece = pltpu.VMEM((width, block), BF16)
-        piece_bytes = 2 * width * block
-
-        sums = pl.pallas_call(
-            functools.partial(project, size_x),
-            out_shape=[pltpu.VMEM((rows, packed), F32)] * size_x,
+
+        total = pl.pallas_call(
+            project,
+            out_shape=pltpu.VMEM((batch, packed), F32),
             in_specs=[ANY] * 5,
-            out_specs=[VMEM] * size_x,
+            out_specs=VMEM,
             scratch_shapes=[
                 pltpu.VMEM(inputs.shape, BF16),
                 pltpu.VMEM((1, depth), F32),
@@ -313,103 +255,76 @@
                 pltpu.VMEM(w_key.shape, BF16),
                 pltpu.VMEM(w_value.shape, BF16),
                 pltpu.VMEM(inputs.shape, BF16),
-                pltpu.VMEM((batch, packed), F32),
                 sems(depth // CHUNK + 4),
             ],
             compiler_params=params(28),
             cost_estimate=cost(2 * batch * depth * packed, 2 * depth * packed),
             name="project",
         )(*[in_hbm(a) for a in (inputs, gain.reshape(1, depth), w_query, w_key, w_value)])
+        sums = pl.pallas_call(
+            split,
+            out_shape=[pltpu.VMEM((rows, packed), F32)] * size_x,
+            in_specs=[VMEM, ANY],
+            out_specs=[VMEM] * size_x,
+            compiler_params=params(4),
+            name="split",
+        )(in_vmem(total), in_hbm(w_query))
         arrived = [sums[0]]
         for mask in range(1, size_x):
             arrived.append(swap(sums[mask].astype(F16), "gx", size_x, mask).astype(F32))
+
+        values = in_vmem(value_cache)
         keys = pl.pallas_call(
-            fetch_keys,
+            turn_keys,
             out_shape=pltpu.VMEM((rows, HD, key_cache.shape[1]), BF16),
-            in_specs=[ANY] * 2,
+            in_specs=[ANY, VMEM, ANY],
             out_specs=VMEM,
-            scratch_shapes=[pltpu.VMEM(key_cache.shape, BF16), sems(rows)],
-            compiler_params=params(12),
+            compiler_params=params(4),
             cost_estimate=cost(0, 2 * key_cache.size),
-            name="fetch_keys",
-        )(sums[0], in_hbm(key_cache))
-        pieces = []
+            name="turn_keys",
+        )(sums[0], in_vmem(key_cache), values)
 
         half = HD // 2
         inverse = ROPE_BASE ** (-(jnp.arange(half, dtype=F32) * 2.0 / HD))
         angles = lengths.astype(F32)[:, None] * inverse[None, :]
         cosine, sine = jnp.cos(angles), jnp.sin(angles)
-        heads, *more = pl.pallas_call(
-            functools.partial(attention, size_x, depth * size_x, middle),
-            out_shape=[pltpu.VMEM((rows, width), BF16)] + [piece] * len(middle),
-            in_specs=[VMEM, VMEM, VMEM, VMEM, ANY, ANY] + [VMEM] * size_x,
-            out_specs=[VMEM] * (1 + len(middle)),
+        lanes = rows * (width // HD)
+        heads = pl.pallas_call(
+            functools.partial(attention, size_x, depth * size_x),
+            out_shape=pltpu.VMEM((rows, width), BF16),
+            in_specs=[ANY] + [VMEM] * (5 + size_x),
+            out_specs=VMEM,
             scratch_shapes=[
-                pltpu.VMEM((rows * (width // HD), HD), F32),
-                pltpu.VMEM((rows * (width // HD), HD), F32),
-                pltpu.VMEM((rows * (width // HD), key_cache.shape[1]), F32),
-                pltpu.VMEM(value_cache.shape, BF16),
-                sems(1 + len(middle)),
+                pltpu.VMEM((lanes, HD), F32),
+                pltpu.VMEM((lanes, HD), F32),
+                pltpu.VMEM((lanes, key_cache.shape[1]), F32),
             ],
-            compiler_params=params(12),
-            cost_estimate=cost(4 * key_cache.size * (width // HD), piece_bytes * len(middle)),
+            compiler_params=params(8),
+            cost_estimate=cost(4 * key_cache.size * (width // HD), 4 * key_cache.size),
             name="attention",
         )(
+            in_hbm(w_query),
             jnp.broadcast_to(lengths[:, None], (rows, HD)),
             jnp.concatenate([cosine, cosine], 1),
             jnp.concatenate([-sine, sine], 1),
             in_vmem(keys),
-            in_hbm(value_cache),
-            in_hbm(w_output),
+            values,
             *[in_vmem(a) for a in arrived],
         )
-        pieces += more
         gathered = [heads] + [swap(heads, "gx", size_x, m) for m in range(1, size_x)]
 
-        pieces += pl.pallas_call(
-            functools.partial(fetch_weights, late),
-            out_shape=[piece] * len(late),
-            in_specs=[ANY] * 2,
-            out_specs=[VMEM] * len(late),
-            scratch_shapes=[sems(len(late))],
-            compiler_params=params(4),
-            cost_estimate=cost(0, piece_bytes * len(late)),
-            name="fetch_weights",
-        )(heads, in_hbm(w_output))
-
         terms = {}
-        for index, mask in enumerate(order):
-            kind = BF16 if mask else F32
-            ready = index < len(pieces)
-            shared = dict(
-                out_shape=pltpu.VMEM((batch, block), kind),
+        for mask in order:
+            term = pl.pallas_call(
+                functools.partial(project_out, size_x, mask),
+                out_shape=pltpu.VMEM((batch, block), BF16 if mask else F32),
+                in_specs=[VMEM] * (2 + size_x),
                 out_specs=VMEM,
-                compiler_params=params(12),
-                cost_estimate=cost(2 * batch * width * block, piece_bytes),
-            )
-            rows_in = [in_vmem(a) for a in gathered]
-            scratch = [pltpu.VMEM((batch, width), F32)]
-            if ready:
-                term = pl.pallas_call(
-                    functools.partial(project_out, size_x),
-                    in_specs=[VMEM] * (1 + size_x),
-                    scratch_shapes=scratch,
-                    name="project_out",
-                    **shared,
-                )(in_vmem(pieces[index]), *rows_in)
-            else:
-                scratch += [
-                    pltpu.VMEM((width, block), BF16),
-                    pltpu.VMEM((batch, block), BF16),
-                    sems(width // (2 * CHUNK) + 1),
-                ]
-                term = pl.pallas_call(
-                    functools.partial(stream_out, size_x, mask),
-                    in_specs=[ANY] * 2 + [VMEM] * size_x,
-                    scratch_shapes=scratch,
-                    name="stream_out",
-                    **shared,
-                )(in_hbm(w_output), in_hbm(inputs), *rows_in)
+                scratch_shapes=[pltpu.VMEM((batch, width), F32)],
+                compiler_params=params(8),
+                cost_estimate=cost(2 * batch * width * block, 2 * width * block),
+                name="project_out",
+            )(in_vmem(w_output), in_vmem(inputs), *[in_vmem(a) for a in gathered])
             terms[mask] = swap(term, "gy", size_y, mask) if mask else term
         done = pl.pallas_call(
             finish,

time: 43.8 us -> 41.4 us (0.945)
  Pallas kernels: 22.5 us -> 14 us
  waiting for transfers between devices: 6.76 us -> 12.6 us
    pallas_call x8, Pallas kernels: 21.7 us -> 13.3 us  [the longest x1 6.95 us: shards(): pl.pallas_call(project, out_shape=pltpu.VMEM((batch, packed), F32), in_sp...]
    ppermute x12, waiting for transfers between devices: 6.76 us -> 12.6 us  [swap(): return lax.ppermute(value, axis, [(i, i ^ mask) for i in range(size)])]
  transfers between devices with their start and end apart: 12 -> 12, of which waited for: 6 -> 7; matrix products, arithmetic and copies ran while one was open for 1% -> 1% of each run, Pallas kernels for 21% -> 9%
where the time goes in v10:
time: 41.4 us; the launch traced here: 41.3 us
  starting transfers between devices  14.1 us (34%)
  Pallas kernels  14 us (34%)
  waiting for transfers between devices  12.6 us (30%)
    ppermute x12, starting transfers between devices, swap(): return lax.ppermute(value, axis, [(i, i ^ mask) for i in range(size)])  14.1 us
    ppermute x12, waiting for transfers between devices, swap(): return lax.ppermute(value, axis, [(i, i ^ mask) for i in range(size)])  12.6 us
    pallas_call x1, Pallas kernels, shards(): pl.pallas_call(project, out_shape=pltpu.VMEM((batch, packed), F32), in_sp...  6.95 us
    pallas_call x4, Pallas kernels, shards(): pl.pallas_call(functools.partial(project_out, size_x, mask), out_shape=pl...  3.34 us
    pallas_call x1, Pallas kernels, shards(): pl.pallas_call(functools.partial(attention, size_x, depth * size_x), out_...  1.82 us
    pallas_call x1, Pallas kernels, shards(): pl.pallas_call(turn_keys, out_shape=pltpu.VMEM((rows, HD, key_cache.shape...  1.13 us
  transfers between devices with their start and end apart: 12, of which 7 were waited for; matrix products, arithmetic and copies ran while one was open for 1% of the time, Pallas kernels for 9%

profile of v10, /device:TPU:0, one launch (start us, length us, event | category | flops | bytes accessed | tf_op | source)
XLA Modules:
  0.0 41.3 jit_solution(3754816082207153684)
XLA Ops:
  0.0 7.0 %project.1.total = f32[32,2432]{1,0:T(8,128)S(1)} custom-call(bf16[32,4096]{1,0:T(8,128)(2,1)} %x.7, f32[1,4096]{1,0:T(1,128)} %bitcast.3, bf16[4096,2048]{1,0:T(8,128)(2,1)} %weights.3, bf16[4096,128]{1,0:T(8,128)(2,1)} %wk_hbm.1, bf16[4096,128]{1,0:T(8,128)(2,1)} %wv_hbm.1), custom_call_target="tpu_custom_call" | custom-call | flops 637534208 | bytes 19922944 | tf_op jit(solution)/shard_map/project/pallas_call | solution.py:246
  7.0 0.0 copy-start.3
  7.0 0.0 copy-start
  7.0 0.0 copy-start.2
  7.1 2.4 %collective-permute-start.2 = (f16[8,2432]{1,0:T(8,128)(2,1)S(1)}, f16[8,2432]{1,0:T(8,128)(2,1)S(1)}, u32[]{:S(2)}, u32[]{:S(2)}) collective-permute-start(f16[8,2432]{1,0:T(8,128)(2,1)S(1)} %convert_element_type.26), channel_id=1, source_target_pairs={{0,12},{4,8},{8,4},{12,0},{1,13},{5,9},{9,5},{13,1},{2,14},{6,10},... | collective-permute-start | bytes 116744 | tf_op jit(solution)/shard_map/ppermute | solution.py:229
  9.5 0.6 %collective-permute-start.1 = (f16[8,2432]{1,0:T(8,128)(2,1)S(1)}, f16[8,2432]{1,0:T(8,128)(2,1)S(1)}, u32[]{:S(2)}, u32[]{:S(2)}) collective-permute-start(f16[8,2432]{1,0:T(8,128)(2,1)S(1)} %convert_element_type.24), channel_id=1, source_target_pairs={{0,8},{4,12},{8,0},{12,4},{1,9},{5,13},{9,1},{13,5},{2,10},{6,14},... | collective-permute-start | bytes 116744 | tf_op jit(solution)/shard_map/ppermute | solution.py:229
  10.2 0.2 collective-permute-start
  10.4 0.0 copy-done.3
  10.4 0.1 fusion
  10.5 0.1 pad_maximum_fusion
  10.6 0.0 copy-done
  10.6 0.0 copy-done.2
  10.6 0.0 slice-start
  10.6 0.0 slice-start.1
  10.6 1.1 %turn_keys.1.k = bf16[8,128,2048]{2,1,0:T(8,128)(2,1)S(1)} custom-call(f32[8,2432]{1,0:T(8,128)S(1)} %get-tuple-element.9.after.refs_0_, bf16[8,2048,128]{2,1,0:T(8,128)(2,1)S(1)} %copy-done.2, bf16[8,2048,128]{2,1,0:T(8,128)(2,1)S(1)} %copy-done), custom_call_target="tpu_custom_call" | custom-call | bytes 4194304 | tf_op jit(solution)/shard_map/turn_keys/pallas_call | solution.py:277
  11.7 0.0 collective-permute-done.2
  11.7 1.9 %collective-permute-done.1 = f16[8,2432]{1,0:T(8,128)(2,1)S(1)} collective-permute-done((f16[8,2432]{1,0:T(8,128)(2,1)S(1)}, f16[8,2432]{1,0:T(8,128)(2,1)S(1)}, u32[]{:S(2)}, u32[]{:S(2)}) %collective-permute-start.1) | collective-permute-done | bytes 38944 | tf_op jit(solution)/shard_map/ppermute | solution.py:229
  13.7 0.0 collective-permute-done
  13.7 0.1 broadcast_in_dim.2.lengths
  13.8 1.8 %attention.1.refs_0_ = bf16[8,2048]{1,0:T(8,128)(2,1)S(1)} custom-call(bf16[4096,2048]{1,0:T(8,128)(2,1)} %weights.3, s32[8,128]{1,0:T(8,128)S(1)} %broadcast_in_dim.2.lengths, f32[8,128]{1,0:T(8,128)S(1)} %get-tuple-element.16.cosine, f32[8,128]{1,0:T(8,128)S(1)} %get-tuple-element.17.sine, bf16[8,128,2048]{2,1,0:T(8,128)(2,1)S(1)} %turn_keys.1.k, ...), custom_call_target="tpu_custom_call" | custom-call | flops 134217728 | bytes 8388608 | tf_op jit(solution)/shard_map/attention/pallas_call | solution.py:292
  15.6 0.8 %collective-permute-start.5 = (bf16[8,2048]{1,0:T(8,128)(2,1)S(1)}, bf16[8,2048]{1,0:T(8,128)(2,1)S(1)}, u32[]{:S(2)}, u32[]{:S(2)}) collective-permute-start(bf16[8,2048]{1,0:T(8,128)(2,1)S(1)} %attention.1.refs_0_), channel_id=1, source_target_pairs={{0,12},{4,8},{8,4},{12,0},{1,13},{5,9},{9,5},{13,1},{2,14},{6,10},... | collective-permute-start | bytes 98312 | tf_op jit(solution)/shard_map/ppermute | solution.py:229
  16.4 0.7 %collective-permute-start.4 = (bf16[8,2048]{1,0:T(8,128)(2,1)S(1)}, bf16[8,2048]{1,0:T(8,128)(2,1)S(1)}, u32[]{:S(2)}, u32[]{:S(2)}) collective-permute-start(bf16[8,2048]{1,0:T(8,128)(2,1)S(1)} %attention.1.refs_0_), channel_id=1, source_target_pairs={{0,8},{4,12},{8,0},{12,4},{1,9},{5,13},{9,1},{13,5},{2,10},{6,14},... | collective-permute-start | bytes 98312 | tf_op jit(solution)/shard_map/ppermute | solution.py:229
  17.1 0.4 collective-permute-start.3
  17.5 1.8 %collective-permute-done.5.refs_3_ = bf16[8,2048]{1,0:T(8,128)(2,1)S(1)} collective-permute-done((bf16[8,2048]{1,0:T(8,128)(2,1)S(1)}, bf16[8,2048]{1,0:T(8,128)(2,1)S(1)}, u32[]{:S(2)}, u32[]{:S(2)}) %collective-permute-start.5) | collective-permute-done | bytes 32800 | tf_op jit(solution)/shard_map/ppermute | solution.py:229
  19.4 1.0 %collective-permute-done.4.refs_2_ = bf16[8,2048]{1,0:T(8,128)(2,1)S(1)} collective-permute-done((bf16[8,2048]{1,0:T(8,128)(2,1)S(1)}, bf16[8,2048]{1,0:T(8,128)(2,1)S(1)}, u32[]{:S(2)}, u32[]{:S(2)}) %collective-permute-start.4) | collective-permute-done | bytes 32800 | tf_op jit(solution)/shard_map/ppermute | solution.py:229
  20.4 0.0 collective-permute-done.3.refs_1_
  20.4 0.0 slice-done
  20.4 0.0 slice-done.1
  20.4 0.0 slice-done.2
  20.4 0.0 slice-done.3
  20.4 0.0 copy-done.1
  20.4 0.8 %project_out.5 = bf16[32,1024]{1,0:T(8,128)(2,1)S(1)} custom-call(bf16[2048,4096]{1,0:T(8,128)(2,1)S(1)} %bitcast.2, bf16[32,4096]{1,0:T(8,128)(2,1)S(1)} %copy-done.1, bf16[8,2048]{1,0:T(8,128)(2,1)S(1)} %attention.1.refs_0_, bf16[8,2048]{1,0:T(8,128)(2,1)S(1)} %collective-permute-done.3.refs_1_, bf16[8,2048]{1,0:T(8,128)(2,1)S(1)} %collective-permute-done.4.refs_2_, ...), custom_call_target="tpu_custom_call" | custom-call | flops 134217728 | bytes 4194304 | tf_op jit(solution)/shard_map/project_out/pallas_call | solution.py:318
  21.2 1.6 %collective-permute-start.6 = (bf16[32,1024]{1,0:T(8,128)(2,1)S(1)}, bf16[32,1024]{1,0:T(8,128)(2,1)S(1)}, u32[]{:S(2)}, u32[]{:S(2)}) collective-permute-start(bf16[32,1024]{1,0:T(8,128)(2,1)S(1)} %project_out.5), channel_id=1, source_target_pairs={{0,1},{1,0},{2,3},{3,2},{4,5},{5,4},{6,7},{7,6},{8,9},{9,8},{10,11... | collective-permute-start | bytes 196616 | tf_op jit(solution)/shard_map/ppermute | solution.py:229
  22.8 0.8 %project_out.6 = bf16[32,1024]{1,0:T(8,128)(2,1)S(1)} custom-call(bf16[2048,4096]{1,0:T(8,128)(2,1)S(1)} %bitcast.2, bf16[32,4096]{1,0:T(8,128)(2,1)S(1)} %copy-done.1, bf16[8,2048]{1,0:T(8,128)(2,1)S(1)} %attention.1.refs_0_, bf16[8,2048]{1,0:T(8,128)(2,1)S(1)} %collective-permute-done.3.refs_1_, bf16[8,2048]{1,0:T(8,128)(2,1)S(1)} %collective-permute-done.4.refs_2_, ...), custom_call_target="tpu_custom_call" | custom-call | flops 134217728 | bytes 4194304 | tf_op jit(solution)/shard_map/project_out/pallas_call | solution.py:318
  23.7 2.6 %collective-permute-start.7 = (bf16[32,1024]{1,0:T(8,128)(2,1)S(1)}, bf16[32,1024]{1,0:T(8,128)(2,1)S(1)}, u32[]{:S(2)}, u32[]{:S(2)}) collective-permute-start(bf16[32,1024]{1,0:T(8,128)(2,1)S(1)} %project_out.6), channel_id=1, source_target_pairs={{0,2},{1,3},{2,0},{3,1},{4,6},{5,7},{6,4},{7,5},{8,10},{9,11},{10,... | collective-permute-start | bytes 196616 | tf_op jit(solution)/shard_map/ppermute | solution.py:229
  26.3 0.8 %project_out.7 = bf16[32,1024]{1,0:T(8,128)(2,1)S(1)} custom-call(bf16[2048,4096]{1,0:T(8,128)(2,1)S(1)} %bitcast.2, bf16[32,4096]{1,0:T(8,128)(2,1)S(1)} %copy-done.1, bf16[8,2048]{1,0:T(8,128)(2,1)S(1)} %attention.1.refs_0_, bf16[8,2048]{1,0:T(8,128)(2,1)S(1)} %collective-permute-done.3.refs_1_, bf16[8,2048]{1,0:T(8,128)(2,1)S(1)} %collective-permute-done.4.refs_2_, ...), custom_call_target="tpu_custom_call" | custom-call | flops 134217728 | bytes 4194304 | tf_op jit(solution)/shard_map/project_out/pallas_call | solution.py:318
  27.1 0.2 collective-permute-start.8
  27.4 0.8 %project_out.4.own = f32[32,1024]{1,0:T(8,128)S(1)} custom-call(bf16[2048,4096]{1,0:T(8,128)(2,1)S(1)} %bitcast.2, bf16[32,4096]{1,0:T(8,128)(2,1)S(1)} %copy-done.1, bf16[8,2048]{1,0:T(8,128)(2,1)S(1)} %attention.1.refs_0_, bf16[8,2048]{1,0:T(8,128)(2,1)S(1)} %collective-permute-done.3.refs_1_, bf16[8,2048]{1,0:T(8,128)(2,1)S(1)} %collective-permute-done.4.refs_2_, ...), custom_call_target="tpu_custom_call" | custom-call | flops 134217728 | bytes 4194304 | tf_op jit(solution)/shard_map/project_out/pallas_call | solution.py:318
  28.2 0.0 collective-permute-done.6.refs_0_
  28.2 1.9 %collective-permute-done.7.refs_1_ = bf16[32,1024]{1,0:T(8,128)(2,1)S(1)} collective-permute-done((bf16[32,1024]{1,0:T(8,128)(2,1)S(1)}, bf16[32,1024]{1,0:T(8,128)(2,1)S(1)}, u32[]{:S(2)}, u32[]{:S(2)}) %collective-permute-start.7) | collective-permute-done | bytes 65568 | tf_op jit(solution)/shard_map/ppermute | solution.py:229
  30.1 3.1 %collective-permute-done.8.refs_2_ = bf16[32,1024]{1,0:T(8,128)(2,1)S(1)} collective-permute-done((bf16[32,1024]{1,0:T(8,128)(2,1)S(1)}, bf16[32,1024]{1,0:T(8,128)(2,1)S(1)}, u32[]{:S(2)}, u32[]{:S(2)}) %collective-permute-start.8) | collective-permute-done | bytes 65568 | tf_op jit(solution)/shard_map/ppermute | solution.py:229
  33.2 0.8 %collective-permute-start.11 = (bf16[32,1024]{1,0:T(8,128)(2,1)S(1)}, bf16[32,1024]{1,0:T(8,128)(2,1)S(1)}, u32[]{:S(2)}, u32[]{:S(2)}) collective-permute-start(bf16[32,1024]{1,0:T(8,128)(2,1)S(1)} %finish.1.refs_0_), channel_id=1, source_target_pairs={{0,3},{1,2},{2,1},{3,0},{4,7},{5,6},{6,5},{7,4},{8,11},{9,10},{10,... | collective-permute-start | bytes 196616 | tf_op jit(solution)/shard_map/ppermute | solution.py:229
  34.0 0.0 collective-permute-start.10
  34.0 3.7 %collective-permute-start.9 = (bf16[32,1024]{1,0:T(8,128)(2,1)S(1)}, bf16[32,1024]{1,0:T(8,128)(2,1)S(1)}, u32[]{:S(2)}, u32[]{:S(2)}) collective-permute-start(bf16[32,1024]{1,0:T(8,128)(2,1)S(1)} %finish.1.refs_0_), channel_id=1, source_target_pairs={{0,1},{1,0},{2,3},{3,2},{4,5},{5,4},{6,7},{7,6},{8,9},{9,8},{10,11... | collective-permute-start | bytes 196616 | tf_op jit(solution)/shard_map/ppermute | solution.py:229
  37.7 1.8 %collective-permute-done.11.refs_3_ = bf16[32,1024]{1,0:T(8,128)(2,1)S(1)} collective-permute-done((bf16[32,1024]{1,0:T(8,128)(2,1)S(1)}, bf16[32,1024]{1,0:T(8,128)(2,1)S(1)}, u32[]{:S(2)}, u32[]{:S(2)}) %collective-permute-start.11) | collective-permute-done | bytes 65568 | tf_op jit(solution)/shard_map/ppermute | solution.py:229
  39.5 1.1 %collective-permute-done.10.refs_2_ = bf16[32,1024]{1,0:T(8,128)(2,1)S(1)} collective-permute-done((bf16[32,1024]{1,0:T(8,128)(2,1)S(1)}, bf16[32,1024]{1,0:T(8,128)(2,1)S(1)}, u32[]{:S(2)}, u32[]{:S(2)}) %collective-permute-start.10) | collective-permute-done | bytes 65568 | tf_op jit(solution)/shard_map/ppermute | solution.py:229
  40.6 0.0 collective-permute-done.9.refs_1_
  40.6 0.7 %assemble.1 = bf16[32,4096]{1,0:T(8,128)(2,1)} custom-call(bf16[32,1024]{1,0:T(8,128)(2,1)S(1)} %finish.1.refs_0_, bf16[32,1024]{1,0:T(8,128)(2,1)S(1)} %collective-permute-done.9.refs_1_, bf16[32,1024]{1,0:T(8,128)(2,1)S(1)} %collective-permute-done.10.refs_2_, bf16[32,1024]{1,0:T(8,128)(2,1)S(1)} %collective-permute-done.11.refs_3_), custom_call_target="tpu_custom_call" | custom-call | tf_op jit(solution)/shard_map/assemble/pallas_call | solution.py:338
  (14 shorter events, 0.1 us)
Async XLA Ops:
  7.0 3.4 %copy-start.3 = (s32[8]{0:T(128)S(1)}, s32[8]{0:T(128)}, u32[]{:S(2)}) copy-start(s32[8]{0:T(128)} %param.17) | copy-start | bytes 100
  7.0 3.6 %copy-start = (bf16[8,2048,128]{2,1,0:T(8,128)(2,1)S(1)}, bf16[8,2048,128]{2,1,0:T(8,128)(2,1)}, u32[]{:S(2)}) copy-start(bf16[8,2048,128]{2,1,0:T(8,128)(2,1)} %v.3) | copy-start | bytes 12582916
  7.0 3.6 %copy-start.2 = (bf16[8,2048,128]{2,1,0:T(8,128)(2,1)S(1)}, bf16[8,2048,128]{2,1,0:T(8,128)(2,1)}, u32[]{:S(2)}) copy-start(bf16[8,2048,128]{2,1,0:T(8,128)(2,1)} %k.1) | copy-start | bytes 12582916
  7.1 4.7 %collective-permute-start.2 = (f16[8,2432]{1,0:T(8,128)(2,1)S(1)}, f16[8,2432]{1,0:T(8,128)(2,1)S(1)}, u32[]{:S(2)}, u32[]{:S(2)}) collective-permute-start(f16[8,2432]{1,0:T(8,128)(2,1)S(1)} %convert_element_type.26), channel_id=1, source_target_pairs={{0,12},{4,8},{8,4},{12,0},{1,13},{5,9},{9,5},{13,1},{2,14},{6,10},... | collective-permute-start | bytes 116744 | tf_op jit(solution)/shard_map/ppermute | solution.py:229
  9.5 4.2 %collective-permute-start.1 = (f16[8,2432]{1,0:T(8,128)(2,1)S(1)}, f16[8,2432]{1,0:T(8,128)(2,1)S(1)}, u32[]{:S(2)}, u32[]{:S(2)}) collective-permute-start(f16[8,2432]{1,0:T(8,128)(2,1)S(1)} %convert_element_type.24), channel_id=1, source_target_pairs={{0,8},{4,12},{8,0},{12,4},{1,9},{5,13},{9,1},{13,5},{2,10},{6,14},... | collective-permute-start | bytes 116744 | tf_op jit(solution)/shard_map/ppermute | solution.py:229
  10.2 3.5 %collective-permute-start = (f16[8,2432]{1,0:T(8,128)(2,1)S(1)}, f16[8,2432]{1,0:T(8,128)(2,1)S(1)}, u32[]{:S(2)}, u32[]{:S(2)}) collective-permute-start(f16[8,2432]{1,0:T(8,128)(2,1)S(1)} %convert_element_type.22), channel_id=1, source_target_pairs={{0,4},{4,0},{8,12},{12,8},{1,5},{5,1},{9,13},{13,9},{2,6},{6,2},{1... | collective-permute-start | bytes 116744 | tf_op jit(solution)/shard_map/ppermute | solution.py:229
  10.6 9.8 %slice-start = ((s8[16777216]{0:T(1024)(128)(4,1)}), s8[4194304]{0:T(1024)(128)(4,1)S(1)}, s32[]{:S(2)}) async-start(s8[16777216]{0:T(1024)(128)(4,1)} %bitcast.1), calls=%async_computation | async-start | bytes 8388608
  10.6 9.8 %slice-start.1 = ((s8[16777216]{0:T(1024)(128)(4,1)}), s8[4194304]{0:T(1024)(128)(4,1)S(1)}, s32[]{:S(2)}) async-start(s8[16777216]{0:T(1024)(128)(4,1)} %bitcast.1), calls=%async_computation.1 | async-start | bytes 8388608
  13.8 6.6 %slice-start.2 = ((s8[16777216]{0:T(1024)(128)(4,1)}), s8[4194304]{0:T(1024)(128)(4,1)S(1)}, s32[]{:S(2)}) async-start(s8[16777216]{0:T(1024)(128)(4,1)} %bitcast.1), calls=%async_computation.2 | async-start | bytes 8388608
  13.8 6.6 %slice-start.3 = ((s8[16777216]{0:T(1024)(128)(4,1)}), s8[4194304]{0:T(1024)(128)(4,1)S(1)}, s32[]{:S(2)}) async-start(s8[16777216]{0:T(1024)(128)(4,1)} %bitcast.1), calls=%async_computation.3 | async-start | bytes 8388608
  13.8 6.6 %copy-start.1 = (bf16[32,4096]{1,0:T(8,128)(2,1)S(1)}, bf16[32,4096]{1,0:T(8,128)(2,1)}, u32[]{:S(2)}) copy-start(bf16[32,4096]{1,0:T(8,128)(2,1)} %x.7) | copy-start | bytes 786436
  15.6 3.8 %collective-permute-start.5 = (bf16[8,2048]{1,0:T(8,128)(2,1)S(1)}, bf16[8,2048]{1,0:T(8,128)(2,1)S(1)}, u32[]{:S(2)}, u32[]{:S(2)}) collective-permute-start(bf16[8,2048]{1,0:T(8,128)(2,1)S(1)} %attention.1.refs_0_), channel_id=1, source_target_pairs={{0,12},{4,8},{8,4},{12,0},{1,13},{5,9},{9,5},{13,1},{2,14},{6,10},... | collective-permute-start | bytes 98312 | tf_op jit(solution)/shard_map/ppermute | solution.py:229
  16.4 3.9 %collective-permute-start.4 = (bf16[8,2048]{1,0:T(8,128)(2,1)S(1)}, bf16[8,2048]{1,0:T(8,128)(2,1)S(1)}, u32[]{:S(2)}, u32[]{:S(2)}) collective-permute-start(bf16[8,2048]{1,0:T(8,128)(2,1)S(1)} %attention.1.refs_0_), channel_id=1, source_target_pairs={{0,8},{4,12},{8,0},{12,4},{1,9},{5,13},{9,1},{13,5},{2,10},{6,14},... | collective-permute-start | bytes 98312 | tf_op jit(solution)/shard_map/ppermute | solution.py:229
  17.1 3.2 %collective-permute-start.3 = (bf16[8,2048]{1,0:T(8,128)(2,1)S(1)}, bf16[8,2048]{1,0:T(8,128)(2,1)S(1)}, u32[]{:S(2)}, u32[]{:S(2)}) collective-permute-start(bf16[8,2048]{1,0:T(8,128)(2,1)S(1)} %attention.1.refs_0_), channel_id=1, source_target_pairs={{0,4},{4,0},{8,12},{12,8},{1,5},{5,1},{9,13},{13,9},{2,6},{6,2},{1... | collective-permute-start | bytes 98312 | tf_op jit(solution)/shard_map/ppermute | solution.py:229
  21.2 7.0 %collective-permute-start.6 = (bf16[32,1024]{1,0:T(8,128)(2,1)S(1)}, bf16[32,1024]{1,0:T(8,128)(2,1)S(1)}, u32[]{:S(2)}, u32[]{:S(2)}) collective-permute-start(bf16[32,1024]{1,0:T(8,128)(2,1)S(1)} %project_out.5), channel_id=1, source_target_pairs={{0,1},{1,0},{2,3},{3,2},{4,5},{5,4},{6,7},{7,6},{8,9},{9,8},{10,11... | collective-permute-start | bytes 196616 | tf_op jit(solution)/shard_map/ppermute | solution.py:229
  23.7 6.5 %collective-permute-start.7 = (bf16[32,1024]{1,0:T(8,128)(2,1)S(1)}, bf16[32,1024]{1,0:T(8,128)(2,1)S(1)}, u32[]{:S(2)}, u32[]{:S(2)}) collective-permute-start(bf16[32,1024]{1,0:T(8,128)(2,1)S(1)} %project_out.6), channel_id=1, source_target_pairs={{0,2},{1,3},{2,0},{3,1},{4,6},{5,7},{6,4},{7,5},{8,10},{9,11},{10,... | collective-permute-start | bytes 196616 | tf_op jit(solution)/shard_map/ppermute | solution.py:229
  27.1 6.1 %collective-permute-start.8 = (bf16[32,1024]{1,0:T(8,128)(2,1)S(1)}, bf16[32,1024]{1,0:T(8,128)(2,1)S(1)}, u32[]{:S(2)}, u32[]{:S(2)}) collective-permute-start(bf16[32,1024]{1,0:T(8,128)(2,1)S(1)} %project_out.7), channel_id=1, source_target_pairs={{0,3},{1,2},{2,1},{3,0},{4,7},{5,6},{6,5},{7,4},{8,11},{9,10},{10,... | collective-permute-start | bytes 196616 | tf_op jit(solution)/shard_map/ppermute | solution.py:229
  33.2 6.3 %collective-permute-start.11 = (bf16[32,1024]{1,0:T(8,128)(2,1)S(1)}, bf16[32,1024]{1,0:T(8,128)(2,1)S(1)}, u32[]{:S(2)}, u32[]{:S(2)}) collective-permute-start(bf16[32,1024]{1,0:T(8,128)(2,1)S(1)} %finish.1.refs_0_), channel_id=1, source_target_pairs={{0,3},{1,2},{2,1},{3,0},{4,7},{5,6},{6,5},{7,4},{8,11},{9,10},{10,... | collective-permute-start | bytes 196616 | tf_op jit(solution)/shard_map/ppermute | solution.py:229
  34.0 6.6 %collective-permute-start.10 = (bf16[32,1024]{1,0:T(8,128)(2,1)S(1)}, bf16[32,1024]{1,0:T(8,128)(2,1)S(1)}, u32[]{:S(2)}, u32[]{:S(2)}) collective-permute-start(bf16[32,1024]{1,0:T(8,128)(2,1)S(1)} %finish.1.refs_0_), channel_id=1, source_target_pairs={{0,2},{1,3},{2,0},{3,1},{4,6},{5,7},{6,4},{7,5},{8,10},{9,11},{10,... | collective-permute-start | bytes 196616 | tf_op jit(solution)/shard_map/ppermute | solution.py:229
  34.0 6.6 %collective-permute-start.9 = (bf16[32,1024]{1,0:T(8,128)(2,1)S(1)}, bf16[32,1024]{1,0:T(8,128)(2,1)S(1)}, u32[]{:S(2)}, u32[]{:S(2)}) collective-permute-start(bf16[32,1024]{1,0:T(8,128)(2,1)S(1)} %finish.1.refs_0_), channel_id=1, source_target_pairs={{0,1},{1,0},{2,3},{3,2},{4,5},{5,4},{6,7},{7,6},{8,9},{9,8},{10,11... | collective-permute-start | bytes 196616 | tf_op jit(solution)/shard_map/ppermute | solution.py:229

commit v11 on v10

--- a/solution.py
+++ b/solution.py
@@ -193,14 +193,16 @@
     return gathered[...].astype(BF16)
 
 
-def project_out(size, mask, w, x, *refs):
-    blocks, out, gathered = refs[:size], refs[-2], refs[-1]
-    part = columns(lax.axis_index("gy") ^ mask, out.shape[1])
+def project_out(size_x, size_y, w, x, *refs):
+    blocks, outs, gathered = refs[:size_x], refs[size_x : size_x + size_y], refs[-1]
     heads = gather_rows(blocks, gathered)
-    total = jnp.dot(heads, w[:, part], preferred_element_type=F32)
-    if not mask:
-        total = total + x[:, part].astype(F32)
-    out[...] = total.astype(out.dtype)
+    for mask in reversed(range(size_y)):
+        out = outs[mask]
+        part = columns(lax.axis_index("gy") ^ mask, out.shape[1])
+        total = jnp.dot(heads, w[:, part], preferred_element_type=F32)
+        if not mask:
+            total = total + x[:, part].astype(F32)
+        out[...] = total.astype(out.dtype)
 
 
 def finish(own, *refs):
@@ -234,7 +236,7 @@
     size_y = mesh.shape["gy"]
     struct = jax.ShapeDtypeStruct
     sems = lambda n: pltpu.SemaphoreType.DMA((n,))
-    order = list(range(size_y - 1, -1, -1))
+    order = [*range(size_y // 2, size_y), *range(1, size_y // 2)]
 
     def shards(inputs, gain, w_query, w_key, w_value, w_output, key_cache, value_cache, lengths):
         batch, depth = inputs.shape
@@ -313,19 +315,17 @@
         )
         gathered = [heads] + [swap(heads, "gx", size_x, m) for m in range(1, size_x)]
 
-        terms = {}
-        for mask in order:
-            term = pl.pallas_call(
-                functools.partial(project_out, size_x, mask),
-                out_shape=pltpu.VMEM((batch, block), BF16 if mask else F32),
-                in_specs=[VMEM] * (2 + size_x),
-                out_specs=VMEM,
-                scratch_shapes=[pltpu.VMEM((batch, width), F32)],
-                compiler_params=params(8),
-                cost_estimate=cost(2 * batch * width * block, 2 * width * block),
-                name="project_out",
-            )(in_vmem(w_output), in_vmem(inputs), *[in_vmem(a) for a in gathered])
-            terms[mask] = swap(term, "gy", size_y, mask) if mask else term
+        terms = pl.pallas_call(
+            functools.partial(project_out, size_x, size_y),
+            out_shape=[pltpu.VMEM((batch, block), BF16 if m else F32) for m in range(size_y)],
+            in_specs=[VMEM] * (2 + size_x),
+            out_specs=[VMEM] * size_y,
+            scratch_shapes=[pltpu.VMEM((batch, width), F32)],
+            compiler_params=params(8),
+            cost_estimate=cost(2 * batch * w_output.size, 2 * w_output.size),
+            name="project_out",
+        )(in_vmem(w_output), in_vmem(inputs), *[in_vmem(a) for a in gathered])
+        landed = [swap(terms[m], "gy", size_y, m) for m in order]
         done = pl.pallas_call(
             finish,
             out_shape=pltpu.VMEM((batch, block), BF16),
@@ -333,8 +333,9 @@
             out_specs=VMEM,
             compiler_params=params(4),
             name="finish",
-        )(*[in_vmem(terms[m]) for m in range(size_y)])
-        blocks = [done] + [swap(done, "gy", size_y, m) for m in range(1, size_y)]
+        )(*[in_vmem(a) for a in (terms[0], *landed)])
+        blocks = {0: done} | {m: swap(done, "gy", size_y, m) for m in order}
+        blocks = [blocks[m] for m in range(size_y)]
         return pl.pallas_call(
             functools.partial(assemble, size_y),
             out_shape=struct((batch, block * size_y), BF16),

time: 41.4 us -> 41.5 us (level)
  waiting for transfers between devices: 12.6 us -> 13.3 us
    ppermute x12, waiting for transfers between devices: 12.6 us -> 13.3 us  [swap(): return lax.ppermute(value, axis, [(i, i ^ mask) for i in range(size)])]
    pallas_call x4 -> x1, Pallas kernels: 3.34 us -> 2.98 us  [shards(): pl.pallas_call(functools.partial(project_out, size_x, size_y), out_shape=...]
  transfers between devices with their start and end apart: 12 -> 12, of which waited for: 7 -> 8; matrix products, arithmetic and copies ran while one was open for 1% -> 1% of each run, Pallas kernels for 9% -> 3%
where the time goes in v11:
time: 41.5 us; the launch traced here: 41.3 us
  starting transfers between devices  13.8 us (33%)
  Pallas kernels  13.7 us (33%)
  waiting for transfers between devices  13.3 us (32%)
    ppermute x12, starting transfers between devices, swap(): return lax.ppermute(value, axis, [(i, i ^ mask) for i in range(size)])  13.8 us
    ppermute x12, waiting for transfers between devices, swap(): return lax.ppermute(value, axis, [(i, i ^ mask) for i in range(size)])  13.3 us
    pallas_call x1, Pallas kernels, shards(): pl.pallas_call(project, out_shape=pltpu.VMEM((batch, packed), F32), in_sp...  6.95 us
    pallas_call x1, Pallas kernels, shards(): pl.pallas_call(functools.partial(project_out, size_x, size_y), out_shape=...  2.98 us
    pallas_call x1, Pallas kernels, shards(): pl.pallas_call(functools.partial(attention, size_x, depth * size_x), out_...  1.82 us
    pallas_call x1, Pallas kernels, shards(): pl.pallas_call(turn_keys, out_shape=pltpu.VMEM((rows, HD, key_cache.shape...  1.13 us
  transfers between devices with their start and end apart: 12, of which 8 were waited for; matrix products, arithmetic and copies ran while one was open for 1% of the time, Pallas kernels for 3%

profile of v11, /device:TPU:0, one launch (start us, length us, event | category | flops | bytes accessed | tf_op | source)
XLA Modules:
  0.0 41.3 jit_solution(6935734835271281913)
XLA Ops:
  0.0 7.0 %project.1.total = f32[32,2432]{1,0:T(8,128)S(1)} custom-call(bf16[32,4096]{1,0:T(8,128)(2,1)} %x.1, f32[1,4096]{1,0:T(1,128)} %bitcast.3, bf16[4096,2048]{1,0:T(8,128)(2,1)} %weights.3, bf16[4096,128]{1,0:T(8,128)(2,1)} %wk_hbm.1, bf16[4096,128]{1,0:T(8,128)(2,1)} %wv_hbm.1), custom_call_target="tpu_custom_call" | custom-call | flops 637534208 | bytes 19922944 | tf_op jit(solution)/shard_map/project/pallas_call | solution.py:248
  7.0 0.0 copy-start.3
  7.0 0.0 copy-start
  7.0 0.0 copy-start.1
  7.1 2.4 %collective-permute-start.2 = (f16[8,2432]{1,0:T(8,128)(2,1)S(1)}, f16[8,2432]{1,0:T(8,128)(2,1)S(1)}, u32[]{:S(2)}, u32[]{:S(2)}) collective-permute-start(f16[8,2432]{1,0:T(8,128)(2,1)S(1)} %convert_element_type.26), channel_id=1, source_target_pairs={{0,12},{4,8},{8,4},{12,0},{1,13},{5,9},{9,5},{13,1},{2,14},{6,10},... | collective-permute-start | bytes 116744 | tf_op jit(solution)/shard_map/ppermute | solution.py:231
  9.5 0.6 %collective-permute-start.1 = (f16[8,2432]{1,0:T(8,128)(2,1)S(1)}, f16[8,2432]{1,0:T(8,128)(2,1)S(1)}, u32[]{:S(2)}, u32[]{:S(2)}) collective-permute-start(f16[8,2432]{1,0:T(8,128)(2,1)S(1)} %convert_element_type.24), channel_id=1, source_target_pairs={{0,8},{4,12},{8,0},{12,4},{1,9},{5,13},{9,1},{13,5},{2,10},{6,14},... | collective-permute-start | bytes 116744 | tf_op jit(solution)/shard_map/ppermute | solution.py:231
  10.2 0.2 collective-permute-start
  10.4 0.0 copy-done.3
  10.4 0.1 fusion
  10.5 0.1 pad_maximum_fusion
  10.6 0.0 copy-done
  10.6 0.0 copy-done.1
  10.6 0.0 slice-start
  10.6 0.0 slice-start.1
  10.6 1.1 %turn_keys.1.k = bf16[8,128,2048]{2,1,0:T(8,128)(2,1)S(1)} custom-call(f32[8,2432]{1,0:T(8,128)S(1)} %get-tuple-element.13.after.refs_0_, bf16[8,2048,128]{2,1,0:T(8,128)(2,1)S(1)} %copy-done.1, bf16[8,2048,128]{2,1,0:T(8,128)(2,1)S(1)} %copy-done), custom_call_target="tpu_custom_call" | custom-call | bytes 4194304 | tf_op jit(solution)/shard_map/turn_keys/pallas_call | solution.py:279
  11.7 0.0 collective-permute-done.2
  11.7 1.9 %collective-permute-done.1 = f16[8,2432]{1,0:T(8,128)(2,1)S(1)} collective-permute-done((f16[8,2432]{1,0:T(8,128)(2,1)S(1)}, f16[8,2432]{1,0:T(8,128)(2,1)S(1)}, u32[]{:S(2)}, u32[]{:S(2)}) %collective-permute-start.1) | collective-permute-done | bytes 38944 | tf_op jit(solution)/shard_map/ppermute | solution.py:231
  13.7 0.0 collective-permute-done
  13.7 0.1 broadcast_in_dim.2.lengths
  13.8 0.0 slice-start.2
  13.8 0.0 slice-start.3
  13.8 0.0 copy-start.2
  13.8 1.8 %attention.1.refs_0_ = bf16[8,2048]{1,0:T(8,128)(2,1)S(1)} custom-call(bf16[4096,2048]{1,0:T(8,128)(2,1)} %weights.3, s32[8,128]{1,0:T(8,128)S(1)} %broadcast_in_dim.2.lengths, f32[8,128]{1,0:T(8,128)S(1)} %get-tuple-element.24.cosine, f32[8,128]{1,0:T(8,128)S(1)} %get-tuple-element.25.sine, bf16[8,128,2048]{2,1,0:T(8,128)(2,1)S(1)} %turn_keys.1.k, ...), custom_call_target="tpu_custom_call" | custom-call | flops 134217728 | bytes 8388608 | tf_op jit(solution)/shard_map/attention/pallas_call | solution.py:294
  15.6 0.8 %collective-permute-start.5 = (bf16[8,2048]{1,0:T(8,128)(2,1)S(1)}, bf16[8,2048]{1,0:T(8,128)(2,1)S(1)}, u32[]{:S(2)}, u32[]{:S(2)}) collective-permute-start(bf16[8,2048]{1,0:T(8,128)(2,1)S(1)} %attention.1.refs_0_), channel_id=1, source_target_pairs={{0,12},{4,8},{8,4},{12,0},{1,13},{5,9},{9,5},{13,1},{2,14},{6,10},... | collective-permute-start | bytes 98312 | tf_op jit(solution)/shard_map/ppermute | solution.py:231
  16.4 0.7 %collective-permute-start.4 = (bf16[8,2048]{1,0:T(8,128)(2,1)S(1)}, bf16[8,2048]{1,0:T(8,128)(2,1)S(1)}, u32[]{:S(2)}, u32[]{:S(2)}) collective-permute-start(bf16[8,2048]{1,0:T(8,128)(2,1)S(1)} %attention.1.refs_0_), channel_id=1, source_target_pairs={{0,8},{4,12},{8,0},{12,4},{1,9},{5,13},{9,1},{13,5},{2,10},{6,14},... | collective-permute-start | bytes 98312 | tf_op jit(solution)/shard_map/ppermute | solution.py:231
  17.1 0.4 collective-permute-start.3
  17.5 1.8 %collective-permute-done.5.refs_3_ = bf16[8,2048]{1,0:T(8,128)(2,1)S(1)} collective-permute-done((bf16[8,2048]{1,0:T(8,128)(2,1)S(1)}, bf16[8,2048]{1,0:T(8,128)(2,1)S(1)}, u32[]{:S(2)}, u32[]{:S(2)}) %collective-permute-start.5) | collective-permute-done | bytes 32800 | tf_op jit(solution)/shard_map/ppermute | solution.py:231
  19.4 1.0 %collective-permute-done.4.refs_2_ = bf16[8,2048]{1,0:T(8,128)(2,1)S(1)} collective-permute-done((bf16[8,2048]{1,0:T(8,128)(2,1)S(1)}, bf16[8,2048]{1,0:T(8,128)(2,1)S(1)}, u32[]{:S(2)}, u32[]{:S(2)}) %collective-permute-start.4) | collective-permute-done | bytes 32800 | tf_op jit(solution)/shard_map/ppermute | solution.py:231
  20.4 0.0 collective-permute-done.3.refs_1_
  20.4 0.0 slice-done
  20.4 0.0 slice-done.1
  20.4 0.0 slice-done.2
  20.4 0.0 slice-done.3
  20.4 0.0 copy-done.2
  20.4 3.0 %project_out.1 = (f32[32,1024]{1,0:T(8,128)S(1)}, bf16[32,1024]{1,0:T(8,128)(2,1)S(1)}, bf16[32,1024]{1,0:T(8,128)(2,1)S(1)}, bf16[32,1024]{1,0:T(8,128)(2,1)S(1)}) custom-call(bf16[2048,4096]{1,0:T(8,128)(2,1)S(1)} %bitcast.2, bf16[32,4096]{1,0:T(8,128)(2,1)S(1)} %copy-done.2, bf16[8,2048]{1,0:T(8,128)(2,1)S(1)} %attention.1.refs_0_, ...), custom_call_target="tpu_custom_call" | custom-call | flops 536870912 | bytes 16777216 | tf_op jit(solution)/shard_map/project_out/pallas_call | solution.py:318
  23.4 2.6 %collective-permute-start.6 = (bf16[32,1024]{1,0:T(8,128)(2,1)S(1)}, bf16[32,1024]{1,0:T(8,128)(2,1)S(1)}, u32[]{:S(2)}, u32[]{:S(2)}) collective-permute-start(bf16[32,1024]{1,0:T(8,128)(2,1)S(1)} %get-tuple-element.18), channel_id=1, source_target_pairs={{0,2},{1,3},{2,0},{3,1},{4,6},{5,7},{6,4},{7,5},{8,10},{9,11},{10,... | collective-permute-start | bytes 196616 | tf_op jit(solution)/shard_map/ppermute | solution.py:231
  26.0 1.3 %collective-permute-start.7 = (bf16[32,1024]{1,0:T(8,128)(2,1)S(1)}, bf16[32,1024]{1,0:T(8,128)(2,1)S(1)}, u32[]{:S(2)}, u32[]{:S(2)}) collective-permute-start(bf16[32,1024]{1,0:T(8,128)(2,1)S(1)} %get-tuple-element.19), channel_id=1, source_target_pairs={{0,3},{1,2},{2,1},{3,0},{4,7},{5,6},{6,5},{7,4},{8,11},{9,10},{10,... | collective-permute-start | bytes 196616 | tf_op jit(solution)/shard_map/ppermute | solution.py:231
  27.3 0.2 collective-permute-start.8
  27.6 1.0 %collective-permute-done.6.refs_0_ = bf16[32,1024]{1,0:T(8,128)(2,1)S(1)} collective-permute-done((bf16[32,1024]{1,0:T(8,128)(2,1)S(1)}, bf16[32,1024]{1,0:T(8,128)(2,1)S(1)}, u32[]{:S(2)}, u32[]{:S(2)}) %collective-permute-start.6) | collective-permute-done | bytes 65568 | tf_op jit(solution)/shard_map/ppermute | solution.py:231
  28.6 3.6 %collective-permute-done.7.refs_1_ = bf16[32,1024]{1,0:T(8,128)(2,1)S(1)} collective-permute-done((bf16[32,1024]{1,0:T(8,128)(2,1)S(1)}, bf16[32,1024]{1,0:T(8,128)(2,1)S(1)}, u32[]{:S(2)}, u32[]{:S(2)}) %collective-permute-start.7) | collective-permute-done | bytes 65568 | tf_op jit(solution)/shard_map/ppermute | solution.py:231
  32.2 0.1 collective-permute-done.8.refs_2_
  32.3 2.4 %collective-permute-start.11 = (bf16[32,1024]{1,0:T(8,128)(2,1)S(1)}, bf16[32,1024]{1,0:T(8,128)(2,1)S(1)}, u32[]{:S(2)}, u32[]{:S(2)}) collective-permute-start(bf16[32,1024]{1,0:T(8,128)(2,1)S(1)} %finish.1.refs_0_), channel_id=1, source_target_pairs={{0,3},{1,2},{2,1},{3,0},{4,7},{5,6},{6,5},{7,4},{8,11},{9,10},{10,... | collective-permute-start | bytes 196616 | tf_op jit(solution)/shard_map/ppermute | solution.py:231
  34.7 0.0 collective-permute-start.10
  34.8 2.0 %collective-permute-start.9 = (bf16[32,1024]{1,0:T(8,128)(2,1)S(1)}, bf16[32,1024]{1,0:T(8,128)(2,1)S(1)}, u32[]{:S(2)}, u32[]{:S(2)}) collective-permute-start(bf16[32,1024]{1,0:T(8,128)(2,1)S(1)} %finish.1.refs_0_), channel_id=1, source_target_pairs={{0,1},{1,0},{2,3},{3,2},{4,5},{5,4},{6,7},{7,6},{8,9},{9,8},{10,11... | collective-permute-start | bytes 196616 | tf_op jit(solution)/shard_map/ppermute | solution.py:231
  36.8 2.3 %collective-permute-done.11.refs_3_ = bf16[32,1024]{1,0:T(8,128)(2,1)S(1)} collective-permute-done((bf16[32,1024]{1,0:T(8,128)(2,1)S(1)}, bf16[32,1024]{1,0:T(8,128)(2,1)S(1)}, u32[]{:S(2)}, u32[]{:S(2)}) %collective-permute-start.11) | collective-permute-done | bytes 65568 | tf_op jit(solution)/shard_map/ppermute | solution.py:231
  39.1 1.4 %collective-permute-done.10.refs_2_ = bf16[32,1024]{1,0:T(8,128)(2,1)S(1)} collective-permute-done((bf16[32,1024]{1,0:T(8,128)(2,1)S(1)}, bf16[32,1024]{1,0:T(8,128)(2,1)S(1)}, u32[]{:S(2)}, u32[]{:S(2)}) %collective-permute-start.10) | collective-permute-done | bytes 65568 | tf_op jit(solution)/shard_map/ppermute | solution.py:231
  40.6 0.0 collective-permute-done.9.refs_1_
  40.6 0.7 %assemble.1 = bf16[32,4096]{1,0:T(8,128)(2,1)} custom-call(bf16[32,1024]{1,0:T(8,128)(2,1)S(1)} %finish.1.refs_0_, bf16[32,1024]{1,0:T(8,128)(2,1)S(1)} %collective-permute-done.9.refs_1_, bf16[32,1024]{1,0:T(8,128)(2,1)S(1)} %collective-permute-done.10.refs_2_, bf16[32,1024]{1,0:T(8,128)(2,1)S(1)} %collective-permute-done.11.refs_3_), custom_call_target="tpu_custom_call" | custom-call | tf_op jit(solution)/shard_map/assemble/pallas_call | solution.py:339
  (11 shorter events, 0.1 us)
Async XLA Ops:
  7.0 3.4 %copy-start.3 = (s32[8]{0:T(128)S(1)}, s32[8]{0:T(128)}, u32[]{:S(2)}) copy-start(s32[8]{0:T(128)} %param.17) | copy-start | bytes 100
  7.0 3.6 %copy-start = (bf16[8,2048,128]{2,1,0:T(8,128)(2,1)S(1)}, bf16[8,2048,128]{2,1,0:T(8,128)(2,1)}, u32[]{:S(2)}) copy-start(bf16[8,2048,128]{2,1,0:T(8,128)(2,1)} %v.3) | copy-start | bytes 12582916
  7.0 3.6 %copy-start.1 = (bf16[8,2048,128]{2,1,0:T(8,128)(2,1)S(1)}, bf16[8,2048,128]{2,1,0:T(8,128)(2,1)}, u32[]{:S(2)}) copy-start(bf16[8,2048,128]{2,1,0:T(8,128)(2,1)} %k.1) | copy-start | bytes 12582916
  7.1 4.7 %collective-permute-start.2 = (f16[8,2432]{1,0:T(8,128)(2,1)S(1)}, f16[8,2432]{1,0:T(8,128)(2,1)S(1)}, u32[]{:S(2)}, u32[]{:S(2)}) collective-permute-start(f16[8,2432]{1,0:T(8,128)(2,1)S(1)} %convert_element_type.26), channel_id=1, source_target_pairs={{0,12},{4,8},{8,4},{12,0},{1,13},{5,9},{9,5},{13,1},{2,14},{6,10},... | collective-permute-start | bytes 116744 | tf_op jit(solution)/shard_map/ppermute | solution.py:231
  9.5 4.2 %collective-permute-start.1 = (f16[8,2432]{1,0:T(8,128)(2,1)S(1)}, f16[8,2432]{1,0:T(8,128)(2,1)S(1)}, u32[]{:S(2)}, u32[]{:S(2)}) collective-permute-start(f16[8,2432]{1,0:T(8,128)(2,1)S(1)} %convert_element_type.24), channel_id=1, source_target_pairs={{0,8},{4,12},{8,0},{12,4},{1,9},{5,13},{9,1},{13,5},{2,10},{6,14},... | collective-permute-start | bytes 116744 | tf_op jit(solution)/shard_map/ppermute | solution.py:231
  10.2 3.5 %collective-permute-start = (f16[8,2432]{1,0:T(8,128)(2,1)S(1)}, f16[8,2432]{1,0:T(8,128)(2,1)S(1)}, u32[]{:S(2)}, u32[]{:S(2)}) collective-permute-start(f16[8,2432]{1,0:T(8,128)(2,1)S(1)} %convert_element_type.22), channel_id=1, source_target_pairs={{0,4},{4,0},{8,12},{12,8},{1,5},{5,1},{9,13},{13,9},{2,6},{6,2},{1... | collective-permute-start | bytes 116744 | tf_op jit(solution)/shard_map/ppermute | solution.py:231
  10.6 9.8 %slice-start = ((s8[16777216]{0:T(1024)(128)(4,1)}), s8[4194304]{0:T(1024)(128)(4,1)S(1)}, s32[]{:S(2)}) async-start(s8[16777216]{0:T(1024)(128)(4,1)} %bitcast.1), calls=%async_computation | async-start | bytes 8388608
  10.6 9.8 %slice-start.1 = ((s8[16777216]{0:T(1024)(128)(4,1)}), s8[4194304]{0:T(1024)(128)(4,1)S(1)}, s32[]{:S(2)}) async-start(s8[16777216]{0:T(1024)(128)(4,1)} %bitcast.1), calls=%async_computation.1 | async-start | bytes 8388608
  13.8 6.6 %slice-start.2 = ((s8[16777216]{0:T(1024)(128)(4,1)}), s8[4194304]{0:T(1024)(128)(4,1)S(1)}, s32[]{:S(2)}) async-start(s8[16777216]{0:T(1024)(128)(4,1)} %bitcast.1), calls=%async_computation.2 | async-start | bytes 8388608
  13.8 6.6 %slice-start.3 = ((s8[16777216]{0:T(1024)(128)(4,1)}), s8[4194304]{0:T(1024)(128)(4,1)S(1)}, s32[]{:S(2)}) async-start(s8[16777216]{0:T(1024)(128)(4,1)} %bitcast.1), calls=%async_computation.3 | async-start | bytes 8388608
  13.8 6.6 %copy-start.2 = (bf16[32,4096]{1,0:T(8,128)(2,1)S(1)}, bf16[32,4096]{1,0:T(8,128)(2,1)}, u32[]{:S(2)}) copy-start(bf16[32,4096]{1,0:T(8,128)(2,1)} %x.1) | copy-start | bytes 786436
  15.6 3.8 %collective-permute-start.5 = (bf16[8,2048]{1,0:T(8,128)(2,1)S(1)}, bf16[8,2048]{1,0:T(8,128)(2,1)S(1)}, u32[]{:S(2)}, u32[]{:S(2)}) collective-permute-start(bf16[8,2048]{1,0:T(8,128)(2,1)S(1)} %attention.1.refs_0_), channel_id=1, source_target_pairs={{0,12},{4,8},{8,4},{12,0},{1,13},{5,9},{9,5},{13,1},{2,14},{6,10},... | collective-permute-start | bytes 98312 | tf_op jit(solution)/shard_map/ppermute | solution.py:231
  16.4 3.9 %collective-permute-start.4 = (bf16[8,2048]{1,0:T(8,128)(2,1)S(1)}, bf16[8,2048]{1,0:T(8,128)(2,1)S(1)}, u32[]{:S(2)}, u32[]{:S(2)}) collective-permute-start(bf16[8,2048]{1,0:T(8,128)(2,1)S(1)} %attention.1.refs_0_), channel_id=1, source_target_pairs={{0,8},{4,12},{8,0},{12,4},{1,9},{5,13},{9,1},{13,5},{2,10},{6,14},... | collective-permute-start | bytes 98312 | tf_op jit(solution)/shard_map/ppermute | solution.py:231
  17.1 3.2 %collective-permute-start.3 = (bf16[8,2048]{1,0:T(8,128)(2,1)S(1)}, bf16[8,2048]{1,0:T(8,128)(2,1)S(1)}, u32[]{:S(2)}, u32[]{:S(2)}) collective-permute-start(bf16[8,2048]{1,0:T(8,128)(2,1)S(1)} %attention.1.refs_0_), channel_id=1, source_target_pairs={{0,4},{4,0},{8,12},{12,8},{1,5},{5,1},{9,13},{13,9},{2,6},{6,2},{1... | collective-permute-start | bytes 98312 | tf_op jit(solution)/shard_map/ppermute | solution.py:231
  23.4 5.2 %collective-permute-start.6 = (bf16[32,1024]{1,0:T(8,128)(2,1)S(1)}, bf16[32,1024]{1,0:T(8,128)(2,1)S(1)}, u32[]{:S(2)}, u32[]{:S(2)}) collective-permute-start(bf16[32,1024]{1,0:T(8,128)(2,1)S(1)} %get-tuple-element.18), channel_id=1, source_target_pairs={{0,2},{1,3},{2,0},{3,1},{4,6},{5,7},{6,4},{7,5},{8,10},{9,11},{10,... | collective-permute-start | bytes 196616 | tf_op jit(solution)/shard_map/ppermute | solution.py:231
  26.0 6.2 %collective-permute-start.7 = (bf16[32,1024]{1,0:T(8,128)(2,1)S(1)}, bf16[32,1024]{1,0:T(8,128)(2,1)S(1)}, u32[]{:S(2)}, u32[]{:S(2)}) collective-permute-start(bf16[32,1024]{1,0:T(8,128)(2,1)S(1)} %get-tuple-element.19), channel_id=1, source_target_pairs={{0,3},{1,2},{2,1},{3,0},{4,7},{5,6},{6,5},{7,4},{8,11},{9,10},{10,... | collective-permute-start | bytes 196616 | tf_op jit(solution)/shard_map/ppermute | solution.py:231
  27.3 5.0 %collective-permute-start.8 = (bf16[32,1024]{1,0:T(8,128)(2,1)S(1)}, bf16[32,1024]{1,0:T(8,128)(2,1)S(1)}, u32[]{:S(2)}, u32[]{:S(2)}) collective-permute-start(bf16[32,1024]{1,0:T(8,128)(2,1)S(1)} %get-tuple-element.20), channel_id=1, source_target_pairs={{0,1},{1,0},{2,3},{3,2},{4,5},{5,4},{6,7},{7,6},{8,9},{9,8},{10,11... | collective-permute-start | bytes 196616 | tf_op jit(solution)/shard_map/ppermute | solution.py:231
  32.3 6.8 %collective-permute-start.11 = (bf16[32,1024]{1,0:T(8,128)(2,1)S(1)}, bf16[32,1024]{1,0:T(8,128)(2,1)S(1)}, u32[]{:S(2)}, u32[]{:S(2)}) collective-permute-start(bf16[32,1024]{1,0:T(8,128)(2,1)S(1)} %finish.1.refs_0_), channel_id=1, source_target_pairs={{0,3},{1,2},{2,1},{3,0},{4,7},{5,6},{6,5},{7,4},{8,11},{9,10},{10,... | collective-permute-start | bytes 196616 | tf_op jit(solution)/shard_map/ppermute | solution.py:231
  34.7 5.8 %collective-permute-start.10 = (bf16[32,1024]{1,0:T(8,128)(2,1)S(1)}, bf16[32,1024]{1,0:T(8,128)(2,1)S(1)}, u32[]{:S(2)}, u32[]{:S(2)}) collective-permute-start(bf16[32,1024]{1,0:T(8,128)(2,1)S(1)} %finish.1.refs_0_), channel_id=1, source_target_pairs={{0,2},{1,3},{2,0},{3,1},{4,6},{5,7},{6,4},{7,5},{8,10},{9,11},{10,... | collective-permute-start | bytes 196616 | tf_op jit(solution)/shard_map/ppermute | solution.py:231
  34.8 5.8 %collective-permute-start.9 = (bf16[32,1024]{1,0:T(8,128)(2,1)S(1)}, bf16[32,1024]{1,0:T(8,128)(2,1)S(1)}, u32[]{:S(2)}, u32[]{:S(2)}) collective-permute-start(bf16[32,1024]{1,0:T(8,128)(2,1)S(1)} %finish.1.refs_0_), channel_id=1, source_target_pairs={{0,1},{1,0},{2,3},{3,2},{4,5},{5,4},{6,7},{7,6},{8,9},{9,8},{10,11... | collective-permute-start | bytes 196616 | tf_op jit(solution)/shard_map/ppermute | solution.py:231

commit v12 on v10

--- a/solution.py
+++ b/solution.py
@@ -45,12 +45,14 @@
 def project(x_hbm, gain_hbm, wq_hbm, wk_hbm, wv_hbm, *refs):
     total, x, gain, wq, wk, wv, scaled, sems = refs
     depth = x.shape[1]
-    steps = depth // CHUNK
+    cuts = [*range(0, depth, 2 * CHUNK), depth - CHUNK, depth]
+    spans = [slice(a, b) for a, b in zip(cuts, cuts[1:])]
+    steps = len(spans)
     pairs = [(x_hbm, x), (gain_hbm, gain), (wk_hbm, wk), (wv_hbm, wv)]
     small = [pltpu.make_async_copy(a, b, sems.at[steps + i]) for i, (a, b) in enumerate(pairs)]
     large = []
-    for step in range(steps):
-        part = pl.ds(step * CHUNK, CHUNK)
+    for step, span in enumerate(spans):
+        part = pl.ds(span.start, span.stop - span.start)
         large.append(pltpu.make_async_copy(wq_hbm.at[part], wq.at[part], sems.at[step]))
     small[0].start()
     small[1].start()
@@ -69,7 +71,7 @@
     dot = functools.partial(jnp.dot, preferred_element_type=F32)
     for step, copy in enumerate(large):
         copy.wait()
-        part = slice(step * CHUNK, (step + 1) * CHUNK)
+        part = spans[step]
         term = dot(scaled[:, part], wq[part])
         if step == 0:
             total[:, :width] = term
@@ -234,7 +236,7 @@
     size_y = mesh.shape["gy"]
     struct = jax.ShapeDtypeStruct
     sems = lambda n: pltpu.SemaphoreType.DMA((n,))
-    order = list(range(size_y - 1, -1, -1))
+    order = [0, *range(size_y // 2, size_y), *range(1, size_y // 2)]
 
     def shards(inputs, gain, w_query, w_key, w_value, w_output, key_cache, value_cache, lengths):
         batch, depth = inputs.shape
@@ -255,7 +257,7 @@
                 pltpu.VMEM(w_key.shape, BF16),
                 pltpu.VMEM(w_value.shape, BF16),
                 pltpu.VMEM(inputs.shape, BF16),
-                sems(depth // CHUNK + 4),
+                sems(depth // (2 * CHUNK) + 5),
             ],
             compiler_params=params(28),
             cost_estimate=cost(2 * batch * depth * packed, 2 * depth * packed),
@@ -333,7 +335,7 @@
             out_specs=VMEM,
             compiler_params=params(4),
             name="finish",
-        )(*[in_vmem(terms[m]) for m in range(size_y)])
+        )(*[in_vmem(terms[m]) for m in order])
         blocks = [done] + [swap(done, "gy", size_y, m) for m in range(1, size_y)]
         return pl.pallas_call(
             functools.partial(assemble, size_y),

time: 41.4 us -> 40.4 us (0.976)
  waiting for transfers between devices: 12.6 us -> 11.8 us
    ppermute x12, waiting for transfers between devices: 12.6 us -> 11.8 us  [swap(): return lax.ppermute(value, axis, [(i, i ^ mask) for i in range(size)])]
where the time goes in v12:
time: 40.4 us; the launch traced here: 40.3 us
  Pallas kernels  14 us (35%)
  starting transfers between devices  13.9 us (34%)
  waiting for transfers between devices  11.8 us (29%)
    ppermute x12, starting transfers between devices, swap(): return lax.ppermute(value, axis, [(i, i ^ mask) for i in range(size)])  13.9 us
    ppermute x12, waiting for transfers between devices, swap(): return lax.ppermute(value, axis, [(i, i ^ mask) for i in range(size)])  11.8 us
    pallas_call x1, Pallas kernels, shards(): pl.pallas_call(project, out_shape=pltpu.VMEM((batch, packed), F32), in_sp...  6.92 us
    pallas_call x4, Pallas kernels, shards(): pl.pallas_call(functools.partial(project_out, size_x, mask), out_shape=pl...  3.34 us
    pallas_call x1, Pallas kernels, shards(): pl.pallas_call(functools.partial(attention, size_x, depth * size_x), out_...  1.83 us
    pallas_call x1, Pallas kernels, shards(): pl.pallas_call(turn_keys, out_shape=pltpu.VMEM((rows, HD, key_cache.shape...  1.13 us
  transfers between devices with their start and end apart: 12, of which 7 were waited for; matrix products, arithmetic and copies ran while one was open for 1% of the time, Pallas kernels for 9%

profile of v12, /device:TPU:0, one launch (start us, length us, event | category | flops | bytes accessed | tf_op | source)
XLA Modules:
  0.0 40.3 jit_solution(13814107210989083219)
XLA Ops:
  0.0 6.9 %project.1.total = f32[32,2432]{1,0:T(8,128)S(1)} custom-call(bf16[32,4096]{1,0:T(8,128)(2,1)} %x.7, f32[1,4096]{1,0:T(1,128)} %bitcast.3, bf16[4096,2048]{1,0:T(8,128)(2,1)} %weights.3, bf16[4096,128]{1,0:T(8,128)(2,1)} %wk_hbm.1, bf16[4096,128]{1,0:T(8,128)(2,1)} %wv_hbm.1), custom_call_target="tpu_custom_call" | custom-call | flops 637534208 | bytes 19922944 | tf_op jit(solution)/shard_map/project/pallas_call | solution.py:248
  6.9 0.0 copy-start.3
  6.9 0.0 copy-start
  7.0 0.0 copy-start.2
  7.0 2.4 %collective-permute-start.2 = (f16[8,2432]{1,0:T(8,128)(2,1)S(1)}, f16[8,2432]{1,0:T(8,128)(2,1)S(1)}, u32[]{:S(2)}, u32[]{:S(2)}) collective-permute-start(f16[8,2432]{1,0:T(8,128)(2,1)S(1)} %convert_element_type.26), channel_id=1, source_target_pairs={{0,12},{4,8},{8,4},{12,0},{1,13},{5,9},{9,5},{13,1},{2,14},{6,10},... | collective-permute-start | bytes 116744 | tf_op jit(solution)/shard_map/ppermute | solution.py:231
  9.5 0.6 %collective-permute-start.1 = (f16[8,2432]{1,0:T(8,128)(2,1)S(1)}, f16[8,2432]{1,0:T(8,128)(2,1)S(1)}, u32[]{:S(2)}, u32[]{:S(2)}) collective-permute-start(f16[8,2432]{1,0:T(8,128)(2,1)S(1)} %convert_element_type.24), channel_id=1, source_target_pairs={{0,8},{4,12},{8,0},{12,4},{1,9},{5,13},{9,1},{13,5},{2,10},{6,14},... | collective-permute-start | bytes 116744 | tf_op jit(solution)/shard_map/ppermute | solution.py:231
  10.1 0.2 collective-permute-start
  10.3 0.0 copy-done.3
  10.3 0.1 fusion
  10.4 0.1 pad_maximum_fusion
  10.5 0.0 copy-done
  10.5 0.0 copy-done.2
  10.5 0.0 slice-start
  10.5 0.0 slice-start.1
  10.5 1.1 %turn_keys.1.k = bf16[8,128,2048]{2,1,0:T(8,128)(2,1)S(1)} custom-call(f32[8,2432]{1,0:T(8,128)S(1)} %get-tuple-element.9.after.refs_0_, bf16[8,2048,128]{2,1,0:T(8,128)(2,1)S(1)} %copy-done.2, bf16[8,2048,128]{2,1,0:T(8,128)(2,1)S(1)} %copy-done), custom_call_target="tpu_custom_call" | custom-call | bytes 4194304 | tf_op jit(solution)/shard_map/turn_keys/pallas_call | solution.py:279
  11.7 0.0 collective-permute-done.2
  11.7 1.9 %collective-permute-done.1 = f16[8,2432]{1,0:T(8,128)(2,1)S(1)} collective-permute-done((f16[8,2432]{1,0:T(8,128)(2,1)S(1)}, f16[8,2432]{1,0:T(8,128)(2,1)S(1)}, u32[]{:S(2)}, u32[]{:S(2)}) %collective-permute-start.1) | collective-permute-done | bytes 38944 | tf_op jit(solution)/shard_map/ppermute | solution.py:231
  13.7 0.0 collective-permute-done
  13.7 0.1 broadcast_in_dim.2.lengths
  13.8 1.8 %attention.1.refs_0_ = bf16[8,2048]{1,0:T(8,128)(2,1)S(1)} custom-call(bf16[4096,2048]{1,0:T(8,128)(2,1)} %weights.3, s32[8,128]{1,0:T(8,128)S(1)} %broadcast_in_dim.2.lengths, f32[8,128]{1,0:T(8,128)S(1)} %get-tuple-element.16.cosine, f32[8,128]{1,0:T(8,128)S(1)} %get-tuple-element.17.sine, bf16[8,128,2048]{2,1,0:T(8,128)(2,1)S(1)} %turn_keys.1.k, ...), custom_call_target="tpu_custom_call" | custom-call | flops 134217728 | bytes 8388608 | tf_op jit(solution)/shard_map/attention/pallas_call | solution.py:294
  15.6 0.8 %collective-permute-start.5 = (bf16[8,2048]{1,0:T(8,128)(2,1)S(1)}, bf16[8,2048]{1,0:T(8,128)(2,1)S(1)}, u32[]{:S(2)}, u32[]{:S(2)}) collective-permute-start(bf16[8,2048]{1,0:T(8,128)(2,1)S(1)} %attention.1.refs_0_), channel_id=1, source_target_pairs={{0,12},{4,8},{8,4},{12,0},{1,13},{5,9},{9,5},{13,1},{2,14},{6,10},... | collective-permute-start | bytes 98312 | tf_op jit(solution)/shard_map/ppermute | solution.py:231
  16.4 0.7 %collective-permute-start.4 = (bf16[8,2048]{1,0:T(8,128)(2,1)S(1)}, bf16[8,2048]{1,0:T(8,128)(2,1)S(1)}, u32[]{:S(2)}, u32[]{:S(2)}) collective-permute-start(bf16[8,2048]{1,0:T(8,128)(2,1)S(1)} %attention.1.refs_0_), channel_id=1, source_target_pairs={{0,8},{4,12},{8,0},{12,4},{1,9},{5,13},{9,1},{13,5},{2,10},{6,14},... | collective-permute-start | bytes 98312 | tf_op jit(solution)/shard_map/ppermute | solution.py:231
  17.1 0.4 %collective-permute-start.3 = (bf16[8,2048]{1,0:T(8,128)(2,1)S(1)}, bf16[8,2048]{1,0:T(8,128)(2,1)S(1)}, u32[]{:S(2)}, u32[]{:S(2)}) collective-permute-start(bf16[8,2048]{1,0:T(8,128)(2,1)S(1)} %attention.1.refs_0_), channel_id=1, source_target_pairs={{0,4},{4,0},{8,12},{12,8},{1,5},{5,1},{9,13},{13,9},{2,6},{6,2},{1... | collective-permute-start | bytes 98312 | tf_op jit(solution)/shard_map/ppermute | solution.py:231
  17.5 1.8 %collective-permute-done.5.refs_3_ = bf16[8,2048]{1,0:T(8,128)(2,1)S(1)} collective-permute-done((bf16[8,2048]{1,0:T(8,128)(2,1)S(1)}, bf16[8,2048]{1,0:T(8,128)(2,1)S(1)}, u32[]{:S(2)}, u32[]{:S(2)}) %collective-permute-start.5) | collective-permute-done | bytes 32800 | tf_op jit(solution)/shard_map/ppermute | solution.py:231
  19.3 1.0 %collective-permute-done.4.refs_2_ = bf16[8,2048]{1,0:T(8,128)(2,1)S(1)} collective-permute-done((bf16[8,2048]{1,0:T(8,128)(2,1)S(1)}, bf16[8,2048]{1,0:T(8,128)(2,1)S(1)}, u32[]{:S(2)}, u32[]{:S(2)}) %collective-permute-start.4) | collective-permute-done | bytes 32800 | tf_op jit(solution)/shard_map/ppermute | solution.py:231
  20.3 0.0 collective-permute-done.3.refs_1_
  20.3 0.0 slice-done
  20.3 0.0 slice-done.1
  20.3 0.0 slice-done.2
  20.3 0.0 slice-done.3
  20.4 0.0 copy-done.1
  20.4 0.8 %project_out.5 = bf16[32,1024]{1,0:T(8,128)(2,1)S(1)} custom-call(bf16[2048,4096]{1,0:T(8,128)(2,1)S(1)} %bitcast.2, bf16[32,4096]{1,0:T(8,128)(2,1)S(1)} %copy-done.1, bf16[8,2048]{1,0:T(8,128)(2,1)S(1)} %attention.1.refs_0_, bf16[8,2048]{1,0:T(8,128)(2,1)S(1)} %collective-permute-done.3.refs_1_, bf16[8,2048]{1,0:T(8,128)(2,1)S(1)} %collective-permute-done.4.refs_2_, ...), custom_call_target="tpu_custom_call" | custom-call | flops 134217728 | bytes 4194304 | tf_op jit(solution)/shard_map/project_out/pallas_call | solution.py:320
  21.2 2.6 %collective-permute-start.6 = (bf16[32,1024]{1,0:T(8,128)(2,1)S(1)}, bf16[32,1024]{1,0:T(8,128)(2,1)S(1)}, u32[]{:S(2)}, u32[]{:S(2)}) collective-permute-start(bf16[32,1024]{1,0:T(8,128)(2,1)S(1)} %project_out.5), channel_id=1, source_target_pairs={{0,2},{1,3},{2,0},{3,1},{4,6},{5,7},{6,4},{7,5},{8,10},{9,11},{10,... | collective-permute-start | bytes 196616 | tf_op jit(solution)/shard_map/ppermute | solution.py:231
  23.8 0.8 %project_out.6 = bf16[32,1024]{1,0:T(8,128)(2,1)S(1)} custom-call(bf16[2048,4096]{1,0:T(8,128)(2,1)S(1)} %bitcast.2, bf16[32,4096]{1,0:T(8,128)(2,1)S(1)} %copy-done.1, bf16[8,2048]{1,0:T(8,128)(2,1)S(1)} %attention.1.refs_0_, bf16[8,2048]{1,0:T(8,128)(2,1)S(1)} %collective-permute-done.3.refs_1_, bf16[8,2048]{1,0:T(8,128)(2,1)S(1)} %collective-permute-done.4.refs_2_, ...), custom_call_target="tpu_custom_call" | custom-call | flops 134217728 | bytes 4194304 | tf_op jit(solution)/shard_map/project_out/pallas_call | solution.py:320
  24.7 1.4 %collective-permute-start.7 = (bf16[32,1024]{1,0:T(8,128)(2,1)S(1)}, bf16[32,1024]{1,0:T(8,128)(2,1)S(1)}, u32[]{:S(2)}, u32[]{:S(2)}) collective-permute-start(bf16[32,1024]{1,0:T(8,128)(2,1)S(1)} %project_out.6), channel_id=1, source_target_pairs={{0,3},{1,2},{2,1},{3,0},{4,7},{5,6},{6,5},{7,4},{8,11},{9,10},{10,... | collective-permute-start | bytes 196616 | tf_op jit(solution)/shard_map/ppermute | solution.py:231
  26.0 0.8 %project_out.7 = bf16[32,1024]{1,0:T(8,128)(2,1)S(1)} custom-call(bf16[2048,4096]{1,0:T(8,128)(2,1)S(1)} %bitcast.2, bf16[32,4096]{1,0:T(8,128)(2,1)S(1)} %copy-done.1, bf16[8,2048]{1,0:T(8,128)(2,1)S(1)} %attention.1.refs_0_, bf16[8,2048]{1,0:T(8,128)(2,1)S(1)} %collective-permute-done.3.refs_1_, bf16[8,2048]{1,0:T(8,128)(2,1)S(1)} %collective-permute-done.4.refs_2_, ...), custom_call_target="tpu_custom_call" | custom-call | flops 134217728 | bytes 4194304 | tf_op jit(solution)/shard_map/project_out/pallas_call | solution.py:320
  26.9 0.3 collective-permute-start.8
  27.1 0.8 %project_out.4.own = f32[32,1024]{1,0:T(8,128)S(1)} custom-call(bf16[2048,4096]{1,0:T(8,128)(2,1)S(1)} %bitcast.2, bf16[32,4096]{1,0:T(8,128)(2,1)S(1)} %copy-done.1, bf16[8,2048]{1,0:T(8,128)(2,1)S(1)} %attention.1.refs_0_, bf16[8,2048]{1,0:T(8,128)(2,1)S(1)} %collective-permute-done.3.refs_1_, bf16[8,2048]{1,0:T(8,128)(2,1)S(1)} %collective-permute-done.4.refs_2_, ...), custom_call_target="tpu_custom_call" | custom-call | flops 134217728 | bytes 4194304 | tf_op jit(solution)/shard_map/project_out/pallas_call | solution.py:320
  28.0 0.0 collective-permute-done.6.refs_0_
  28.0 2.8 %collective-permute-done.7.refs_1_ = bf16[32,1024]{1,0:T(8,128)(2,1)S(1)} collective-permute-done((bf16[32,1024]{1,0:T(8,128)(2,1)S(1)}, bf16[32,1024]{1,0:T(8,128)(2,1)S(1)}, u32[]{:S(2)}, u32[]{:S(2)}) %collective-permute-start.7) | collective-permute-done | bytes 65568 | tf_op jit(solution)/shard_map/ppermute | solution.py:231
  30.8 0.7 %collective-permute-done.8.refs_2_ = bf16[32,1024]{1,0:T(8,128)(2,1)S(1)} collective-permute-done((bf16[32,1024]{1,0:T(8,128)(2,1)S(1)}, bf16[32,1024]{1,0:T(8,128)(2,1)S(1)}, u32[]{:S(2)}, u32[]{:S(2)}) %collective-permute-start.8) | collective-permute-done | bytes 65568 | tf_op jit(solution)/shard_map/ppermute | solution.py:231
  31.5 2.2 %collective-permute-start.11 = (bf16[32,1024]{1,0:T(8,128)(2,1)S(1)}, bf16[32,1024]{1,0:T(8,128)(2,1)S(1)}, u32[]{:S(2)}, u32[]{:S(2)}) collective-permute-start(bf16[32,1024]{1,0:T(8,128)(2,1)S(1)} %finish.1.refs_0_), channel_id=1, source_target_pairs={{0,3},{1,2},{2,1},{3,0},{4,7},{5,6},{6,5},{7,4},{8,11},{9,10},{10,... | collective-permute-start | bytes 196616 | tf_op jit(solution)/shard_map/ppermute | solution.py:231
  33.7 0.0 collective-permute-start.10
  33.7 2.2 %collective-permute-start.9 = (bf16[32,1024]{1,0:T(8,128)(2,1)S(1)}, bf16[32,1024]{1,0:T(8,128)(2,1)S(1)}, u32[]{:S(2)}, u32[]{:S(2)}) collective-permute-start(bf16[32,1024]{1,0:T(8,128)(2,1)S(1)} %finish.1.refs_0_), channel_id=1, source_target_pairs={{0,1},{1,0},{2,3},{3,2},{4,5},{5,4},{6,7},{7,6},{8,9},{9,8},{10,11... | collective-permute-start | bytes 196616 | tf_op jit(solution)/shard_map/ppermute | solution.py:231
  35.9 2.2 %collective-permute-done.11.refs_3_ = bf16[32,1024]{1,0:T(8,128)(2,1)S(1)} collective-permute-done((bf16[32,1024]{1,0:T(8,128)(2,1)S(1)}, bf16[32,1024]{1,0:T(8,128)(2,1)S(1)}, u32[]{:S(2)}, u32[]{:S(2)}) %collective-permute-start.11) | collective-permute-done | bytes 65568 | tf_op jit(solution)/shard_map/ppermute | solution.py:231
  38.1 1.4 %collective-permute-done.10.refs_2_ = bf16[32,1024]{1,0:T(8,128)(2,1)S(1)} collective-permute-done((bf16[32,1024]{1,0:T(8,128)(2,1)S(1)}, bf16[32,1024]{1,0:T(8,128)(2,1)S(1)}, u32[]{:S(2)}, u32[]{:S(2)}) %collective-permute-start.10) | collective-permute-done | bytes 65568 | tf_op jit(solution)/shard_map/ppermute | solution.py:231
  39.5 0.0 collective-permute-done.9.refs_1_
  39.5 0.7 %assemble.1 = bf16[32,4096]{1,0:T(8,128)(2,1)} custom-call(bf16[32,1024]{1,0:T(8,128)(2,1)S(1)} %finish.1.refs_0_, bf16[32,1024]{1,0:T(8,128)(2,1)S(1)} %collective-permute-done.9.refs_1_, bf16[32,1024]{1,0:T(8,128)(2,1)S(1)} %collective-permute-done.10.refs_2_, bf16[32,1024]{1,0:T(8,128)(2,1)S(1)} %collective-permute-done.11.refs_3_), custom_call_target="tpu_custom_call" | custom-call | tf_op jit(solution)/shard_map/assemble/pallas_call | solution.py:340
  (14 shorter events, 0.1 us)
Async XLA Ops:
  6.9 3.4 %copy-start.3 = (s32[8]{0:T(128)S(1)}, s32[8]{0:T(128)}, u32[]{:S(2)}) copy-start(s32[8]{0:T(128)} %param.17) | copy-start | bytes 100
  6.9 3.6 %copy-start = (bf16[8,2048,128]{2,1,0:T(8,128)(2,1)S(1)}, bf16[8,2048,128]{2,1,0:T(8,128)(2,1)}, u32[]{:S(2)}) copy-start(bf16[8,2048,128]{2,1,0:T(8,128)(2,1)} %v.3) | copy-start | bytes 12582916
  7.0 3.6 %copy-start.2 = (bf16[8,2048,128]{2,1,0:T(8,128)(2,1)S(1)}, bf16[8,2048,128]{2,1,0:T(8,128)(2,1)}, u32[]{:S(2)}) copy-start(bf16[8,2048,128]{2,1,0:T(8,128)(2,1)} %k.1) | copy-start | bytes 12582916
  7.0 4.7 %collective-permute-start.2 = (f16[8,2432]{1,0:T(8,128)(2,1)S(1)}, f16[8,2432]{1,0:T(8,128)(2,1)S(1)}, u32[]{:S(2)}, u32[]{:S(2)}) collective-permute-start(f16[8,2432]{1,0:T(8,128)(2,1)S(1)} %convert_element_type.26), channel_id=1, source_target_pairs={{0,12},{4,8},{8,4},{12,0},{1,13},{5,9},{9,5},{13,1},{2,14},{6,10},... | collective-permute-start | bytes 116744 | tf_op jit(solution)/shard_map/ppermute | solution.py:231
  9.5 4.2 %collective-permute-start.1 = (f16[8,2432]{1,0:T(8,128)(2,1)S(1)}, f16[8,2432]{1,0:T(8,128)(2,1)S(1)}, u32[]{:S(2)}, u32[]{:S(2)}) collective-permute-start(f16[8,2432]{1,0:T(8,128)(2,1)S(1)} %convert_element_type.24), channel_id=1, source_target_pairs={{0,8},{4,12},{8,0},{12,4},{1,9},{5,13},{9,1},{13,5},{2,10},{6,14},... | collective-permute-start | bytes 116744 | tf_op jit(solution)/shard_map/ppermute | solution.py:231
  10.1 3.5 %collective-permute-start = (f16[8,2432]{1,0:T(8,128)(2,1)S(1)}, f16[8,2432]{1,0:T(8,128)(2,1)S(1)}, u32[]{:S(2)}, u32[]{:S(2)}) collective-permute-start(f16[8,2432]{1,0:T(8,128)(2,1)S(1)} %convert_element_type.22), channel_id=1, source_target_pairs={{0,4},{4,0},{8,12},{12,8},{1,5},{5,1},{9,13},{13,9},{2,6},{6,2},{1... | collective-permute-start | bytes 116744 | tf_op jit(solution)/shard_map/ppermute | solution.py:231
  10.5 9.8 %slice-start = ((s8[16777216]{0:T(1024)(128)(4,1)}), s8[4194304]{0:T(1024)(128)(4,1)S(1)}, s32[]{:S(2)}) async-start(s8[16777216]{0:T(1024)(128)(4,1)} %bitcast.1), calls=%async_computation | async-start | bytes 8388608
  10.5 9.8 %slice-start.1 = ((s8[16777216]{0:T(1024)(128)(4,1)}), s8[4194304]{0:T(1024)(128)(4,1)S(1)}, s32[]{:S(2)}) async-start(s8[16777216]{0:T(1024)(128)(4,1)} %bitcast.1), calls=%async_computation.1 | async-start | bytes 8388608
  13.7 6.6 %slice-start.2 = ((s8[16777216]{0:T(1024)(128)(4,1)}), s8[4194304]{0:T(1024)(128)(4,1)S(1)}, s32[]{:S(2)}) async-start(s8[16777216]{0:T(1024)(128)(4,1)} %bitcast.1), calls=%async_computation.2 | async-start | bytes 8388608
  13.8 6.6 %slice-start.3 = ((s8[16777216]{0:T(1024)(128)(4,1)}), s8[4194304]{0:T(1024)(128)(4,1)S(1)}, s32[]{:S(2)}) async-start(s8[16777216]{0:T(1024)(128)(4,1)} %bitcast.1), calls=%async_computation.3 | async-start | bytes 8388608
  13.8 6.6 %copy-start.1 = (bf16[32,4096]{1,0:T(8,128)(2,1)S(1)}, bf16[32,4096]{1,0:T(8,128)(2,1)}, u32[]{:S(2)}) copy-start(bf16[32,4096]{1,0:T(8,128)(2,1)} %x.7) | copy-start | bytes 786436
  15.6 3.8 %collective-permute-start.5 = (bf16[8,2048]{1,0:T(8,128)(2,1)S(1)}, bf16[8,2048]{1,0:T(8,128)(2,1)S(1)}, u32[]{:S(2)}, u32[]{:S(2)}) collective-permute-start(bf16[8,2048]{1,0:T(8,128)(2,1)S(1)} %attention.1.refs_0_), channel_id=1, source_target_pairs={{0,12},{4,8},{8,4},{12,0},{1,13},{5,9},{9,5},{13,1},{2,14},{6,10},... | collective-permute-start | bytes 98312 | tf_op jit(solution)/shard_map/ppermute | solution.py:231
  16.4 3.9 %collective-permute-start.4 = (bf16[8,2048]{1,0:T(8,128)(2,1)S(1)}, bf16[8,2048]{1,0:T(8,128)(2,1)S(1)}, u32[]{:S(2)}, u32[]{:S(2)}) collective-permute-start(bf16[8,2048]{1,0:T(8,128)(2,1)S(1)} %attention.1.refs_0_), channel_id=1, source_target_pairs={{0,8},{4,12},{8,0},{12,4},{1,9},{5,13},{9,1},{13,5},{2,10},{6,14},... | collective-permute-start | bytes 98312 | tf_op jit(solution)/shard_map/ppermute | solution.py:231
  17.1 3.2 %collective-permute-start.3 = (bf16[8,2048]{1,0:T(8,128)(2,1)S(1)}, bf16[8,2048]{1,0:T(8,128)(2,1)S(1)}, u32[]{:S(2)}, u32[]{:S(2)}) collective-permute-start(bf16[8,2048]{1,0:T(8,128)(2,1)S(1)} %attention.1.refs_0_), channel_id=1, source_target_pairs={{0,4},{4,0},{8,12},{12,8},{1,5},{5,1},{9,13},{13,9},{2,6},{6,2},{1... | collective-permute-start | bytes 98312 | tf_op jit(solution)/shard_map/ppermute | solution.py:231
  21.2 6.7 %collective-permute-start.6 = (bf16[32,1024]{1,0:T(8,128)(2,1)S(1)}, bf16[32,1024]{1,0:T(8,128)(2,1)S(1)}, u32[]{:S(2)}, u32[]{:S(2)}) collective-permute-start(bf16[32,1024]{1,0:T(8,128)(2,1)S(1)} %project_out.5), channel_id=1, source_target_pairs={{0,2},{1,3},{2,0},{3,1},{4,6},{5,7},{6,4},{7,5},{8,10},{9,11},{10,... | collective-permute-start | bytes 196616 | tf_op jit(solution)/shard_map/ppermute | solution.py:231
  24.7 6.1 %collective-permute-start.7 = (bf16[32,1024]{1,0:T(8,128)(2,1)S(1)}, bf16[32,1024]{1,0:T(8,128)(2,1)S(1)}, u32[]{:S(2)}, u32[]{:S(2)}) collective-permute-start(bf16[32,1024]{1,0:T(8,128)(2,1)S(1)} %project_out.6), channel_id=1, source_target_pairs={{0,3},{1,2},{2,1},{3,0},{4,7},{5,6},{6,5},{7,4},{8,11},{9,10},{10,... | collective-permute-start | bytes 196616 | tf_op jit(solution)/shard_map/ppermute | solution.py:231
  26.9 4.6 %collective-permute-start.8 = (bf16[32,1024]{1,0:T(8,128)(2,1)S(1)}, bf16[32,1024]{1,0:T(8,128)(2,1)S(1)}, u32[]{:S(2)}, u32[]{:S(2)}) collective-permute-start(bf16[32,1024]{1,0:T(8,128)(2,1)S(1)} %project_out.7), channel_id=1, source_target_pairs={{0,1},{1,0},{2,3},{3,2},{4,5},{5,4},{6,7},{7,6},{8,9},{9,8},{10,11... | collective-permute-start | bytes 196616 | tf_op jit(solution)/shard_map/ppermute | solution.py:231
  31.5 6.6 %collective-permute-start.11 = (bf16[32,1024]{1,0:T(8,128)(2,1)S(1)}, bf16[32,1024]{1,0:T(8,128)(2,1)S(1)}, u32[]{:S(2)}, u32[]{:S(2)}) collective-permute-start(bf16[32,1024]{1,0:T(8,128)(2,1)S(1)} %finish.1.refs_0_), channel_id=1, source_target_pairs={{0,3},{1,2},{2,1},{3,0},{4,7},{5,6},{6,5},{7,4},{8,11},{9,10},{10,... | collective-permute-start | bytes 196616 | tf_op jit(solution)/shard_map/ppermute | solution.py:231
  33.7 5.8 %collective-permute-start.10 = (bf16[32,1024]{1,0:T(8,128)(2,1)S(1)}, bf16[32,1024]{1,0:T(8,128)(2,1)S(1)}, u32[]{:S(2)}, u32[]{:S(2)}) collective-permute-start(bf16[32,1024]{1,0:T(8,128)(2,1)S(1)} %finish.1.refs_0_), channel_id=1, source_target_pairs={{0,2},{1,3},{2,0},{3,1},{4,6},{5,7},{6,4},{7,5},{8,10},{9,11},{10,... | collective-permute-start | bytes 196616 | tf_op jit(solution)/shard_map/ppermute | solution.py:231
  33.7 5.8 %collective-permute-start.9 = (bf16[32,1024]{1,0:T(8,128)(2,1)S(1)}, bf16[32,1024]{1,0:T(8,128)(2,1)S(1)}, u32[]{:S(2)}, u32[]{:S(2)}) collective-permute-start(bf16[32,1024]{1,0:T(8,128)(2,1)S(1)} %finish.1.refs_0_), channel_id=1, source_target_pairs={{0,1},{1,0},{2,3},{3,2},{4,5},{5,4},{6,7},{7,6},{8,9},{9,8},{10,11... | collective-permute-start | bytes 196616 | tf_op jit(solution)/shard_map/ppermute | solution.py:231

commit v13 on v12

--- a/solution.py
+++ b/solution.py
@@ -195,32 +195,40 @@
     return gathered[...].astype(BF16)
 
 
-def project_out(size, mask, w, x, *refs):
+def place(chunk, given):
+    return 2 * chunk + ((lax.axis_index("gy") ^ given) & 1)
+
+
+def project_out(size, chunk, given, w, *refs):
     blocks, out, gathered = refs[:size], refs[-2], refs[-1]
-    part = columns(lax.axis_index("gy") ^ mask, out.shape[1])
     heads = gather_rows(blocks, gathered)
-    total = jnp.dot(heads, w[:, part], preferred_element_type=F32)
-    if not mask:
-        total = total + x[:, part].astype(F32)
-    out[...] = total.astype(out.dtype)
-
-
-def finish(own, *refs):
-    *arrived, out = refs
-    total = own[...]
-    for item in arrived:
-        total = total + item[...].astype(F32)
-    out[...] = total.astype(BF16)
-
-
-def assemble(size, *refs):
-    blocks, out, sems = refs[:size], refs[size], refs[size + 1]
-    me = lax.axis_index("gy")
+    part = columns(place(chunk, given), out.shape[1])
+    out[...] = jnp.dot(heads, w[:, part], preferred_element_type=F32).astype(out.dtype)
+
+
+def add_near(own, arrived, out):
+    out[...] = (own[...] + arrived[...].astype(F32)).astype(BF16)
+
+
+def finish(size, chunk, x, *refs):
+    terms, out, ranked = refs[:size], refs[-2], refs[-1]
+    rank = lax.axis_index("gy") // 2
+    for mask, term in enumerate(terms):
+        ranked[rank ^ mask] = term[...].astype(F32)
+    total = ranked[0]
+    for index in range(1, size):
+        total = total + ranked[index]
+    part = columns(place(chunk, 0), out.shape[1])
+    out[...] = (x[:, part].astype(F32) + total).astype(BF16)
+
+
+def assemble(*refs):
+    *blocks, out, sems = refs
     width = blocks[0].shape[1]
     copies = []
-    for mask in range(size):
-        target = out.at[:, columns(me ^ mask, width)]
-        copies.append(pltpu.make_async_copy(blocks[mask], target, sems.at[mask]))
+    for index, block in enumerate(blocks):
+        target = out.at[:, columns(place(index // 2, index % 2), width)]
+        copies.append(pltpu.make_async_copy(block, target, sems.at[index]))
     for copy in copies:
         copy.start()
     for copy in copies:
@@ -234,16 +242,14 @@
 def solution(mesh):
     size_x = mesh.shape["gx"]
     size_y = mesh.shape["gy"]
-    struct = jax.ShapeDtypeStruct
     sems = lambda n: pltpu.SemaphoreType.DMA((n,))
-    order = [0, *range(size_y // 2, size_y), *range(1, size_y // 2)]
 
     def shards(inputs, gain, w_query, w_key, w_value, w_output, key_cache, value_cache, lengths):
         batch, depth = inputs.shape
         width = w_query.shape[1]
         rows = key_cache.shape[0]
         packed = width + 3 * HD
-        block = w_output.shape[1] // size_y
+        block = w_output.shape[1] // 4
 
         total = pl.pallas_call(
             project,
@@ -315,34 +321,49 @@
         )
         gathered = [heads] + [swap(heads, "gx", size_x, m) for m in range(1, size_x)]
 
-        terms = {}
-        for mask in order:
-            term = pl.pallas_call(
-                functools.partial(project_out, size_x, mask),
-                out_shape=pltpu.VMEM((batch, block), BF16 if mask else F32),
-                in_specs=[VMEM] * (2 + size_x),
+        gathered = [in_vmem(a) for a in gathered]
+        half = size_y // 2
+
+        def product(chunk, given):
+            return pl.pallas_call(
+                functools.partial(project_out, size_x, chunk, given),
+                out_shape=pltpu.VMEM((batch, block), BF16 if given else F32),
+                in_specs=[VMEM] * (1 + size_x),
                 out_specs=VMEM,
                 scratch_shapes=[pltpu.VMEM((batch, width), F32)],
                 compiler_params=params(8),
                 cost_estimate=cost(2 * batch * width * block, 2 * width * block),
                 name="project_out",
-            )(in_vmem(w_output), in_vmem(inputs), *[in_vmem(a) for a in gathered])
-            terms[mask] = swap(term, "gy", size_y, mask) if mask else term
-        done = pl.pallas_call(
-            finish,
-            out_shape=pltpu.VMEM((batch, block), BF16),
-            in_specs=[VMEM] * size_y,
-            out_specs=VMEM,
-            compiler_params=params(4),
-            name="finish",
-        )(*[in_vmem(terms[m]) for m in order])
-        blocks = [done] + [swap(done, "gy", size_y, m) for m in range(1, size_y)]
+            )(in_vmem(w_output), *gathered)
+
+        near = [swap(product(chunk, 1), "gy", size_y, 1) for chunk in range(2)]
+        blocks = []
+        for chunk in range(2):
+            pair = pl.pallas_call(
+                add_near,
+                out_shape=pltpu.VMEM((batch, block), BF16),
+                in_specs=[VMEM] * 2,
+                out_specs=VMEM,
+                compiler_params=params(4),
+                name="add_near",
+            )(in_vmem(product(chunk, 0)), in_vmem(near[chunk]))
+            far = [pair] + [swap(pair, "gy", size_y, 2 * m) for m in range(1, half)]
+            done = pl.pallas_call(
+                functools.partial(finish, half, chunk),
+                out_shape=pltpu.VMEM((batch, block), BF16),
+                in_specs=[VMEM] * (1 + half),
+                out_specs=VMEM,
+                scratch_shapes=[pltpu.VMEM((half, batch, block), F32)],
+                compiler_params=params(8),
+                name="finish",
+            )(in_vmem(inputs), *[in_vmem(a) for a in far])
+            blocks += [done, swap(done, "gy", size_y, 1)]
         return pl.pallas_call(
-            functools.partial(assemble, size_y),
-            out_shape=struct((batch, block * size_y), BF16),
-            in_specs=[VMEM] * size_y,
+            assemble,
+            out_shape=jax.ShapeDtypeStruct((batch, block * 4), BF16),
+            in_specs=[VMEM] * 4,
             out_specs=ANY,
-            scratch_shapes=[sems(size_y)],
+            scratch_shapes=[sems(4)],
             compiler_params=params(4),
             name="assemble",
         )(*[in_vmem(b) for b in blocks])

time: 40.4 us -> 39.1 us (0.968)
  waiting for transfers between devices: 11.8 us -> 9.46 us
  starting transfers between devices: 13.9 us -> 14.9 us
    ppermute x12, waiting for transfers between devices: 11.8 us -> 9.46 us  [swap(): return lax.ppermute(value, axis, [(i, i ^ mask) for i in range(size)])]
    ppermute x12, starting transfers between devices: 13.9 us -> 14.9 us  [swap(): return lax.ppermute(value, axis, [(i, i ^ mask) for i in range(size)])]
    pallas_call x6 -> x9, Pallas kernels: 4.1 us -> 4.16 us  [the longest x4 3.3 us: product(): pl.pallas_call(functools.partial(project_out, size_x, chunk, given), out_...]
  transfers between devices with their start and end apart: 12 -> 12, of which waited for: 7 -> 7; matrix products, arithmetic and copies ran while one was open for 1% -> 1% of each run, Pallas kernels for 9% -> 10%
where the time goes in v13:
time: 39.1 us; the launch traced here: 39 us
  starting transfers between devices  14.9 us (38%)
  Pallas kernels  14.1 us (36%)
  waiting for transfers between devices  9.46 us (24%)
    ppermute x12, starting transfers between devices, swap(): return lax.ppermute(value, axis, [(i, i ^ mask) for i in range(size)])  14.9 us
    ppermute x12, waiting for transfers between devices, swap(): return lax.ppermute(value, axis, [(i, i ^ mask) for i in range(size)])  9.46 us
    pallas_call x1, Pallas kernels, shards(): pl.pallas_call(project, out_shape=pltpu.VMEM((batch, packed), F32), in_sp...  6.92 us
    pallas_call x4, Pallas kernels, product(): pl.pallas_call(functools.partial(project_out, size_x, chunk, given), out_...  3.3 us
    pallas_call x1, Pallas kernels, shards(): pl.pallas_call(functools.partial(attention, size_x, depth * size_x), out_...  1.82 us
    pallas_call x1, Pallas kernels, shards(): pl.pallas_call(turn_keys, out_shape=pltpu.VMEM((rows, HD, key_cache.shape...  1.13 us
  transfers between devices with their start and end apart: 12, of which 7 were waited for; matrix products, arithmetic and copies ran while one was open for 1% of the time, Pallas kernels for 10%

profile of v13, /device:TPU:0, one launch (start us, length us, event | category | flops | bytes accessed | tf_op | source)
XLA Modules:
  0.0 39.0 jit_solution(18172910660416331080)
XLA Ops:
  0.0 6.9 %project.1.total = f32[32,2432]{1,0:T(8,128)S(1)} custom-call(bf16[32,4096]{1,0:T(8,128)(2,1)} %x.3, f32[1,4096]{1,0:T(1,128)} %bitcast.3, bf16[4096,2048]{1,0:T(8,128)(2,1)} %weights.3, bf16[4096,128]{1,0:T(8,128)(2,1)} %wk_hbm.1, bf16[4096,128]{1,0:T(8,128)(2,1)} %wv_hbm.1), custom_call_target="tpu_custom_call" | custom-call | flops 637534208 | bytes 19922944 | tf_op jit(solution)/shard_map/project/pallas_call | solution.py:254
  6.9 0.0 copy-start.3
  6.9 0.0 copy-start
  7.0 0.0 copy-start.1
  7.0 2.4 %collective-permute-start.2 = (f16[8,2432]{1,0:T(8,128)(2,1)S(1)}, f16[8,2432]{1,0:T(8,128)(2,1)S(1)}, u32[]{:S(2)}, u32[]{:S(2)}) collective-permute-start(f16[8,2432]{1,0:T(8,128)(2,1)S(1)} %convert_element_type.26), channel_id=1, source_target_pairs={{0,12},{4,8},{8,4},{12,0},{1,13},{5,9},{9,5},{13,1},{2,14},{6,10},... | collective-permute-start | bytes 116744 | tf_op jit(solution)/shard_map/ppermute | solution.py:239
  9.5 0.6 %collective-permute-start.1 = (f16[8,2432]{1,0:T(8,128)(2,1)S(1)}, f16[8,2432]{1,0:T(8,128)(2,1)S(1)}, u32[]{:S(2)}, u32[]{:S(2)}) collective-permute-start(f16[8,2432]{1,0:T(8,128)(2,1)S(1)} %convert_element_type.24), channel_id=1, source_target_pairs={{0,8},{4,12},{8,0},{12,4},{1,9},{5,13},{9,1},{13,5},{2,10},{6,14},... | collective-permute-start | bytes 116744 | tf_op jit(solution)/shard_map/ppermute | solution.py:239
  10.1 0.2 collective-permute-start
  10.3 0.0 copy-done.3
  10.3 0.1 fusion
  10.4 0.1 pad_maximum_fusion
  10.5 0.0 copy-done
  10.5 0.0 copy-done.1
  10.5 0.0 slice-start
  10.5 0.0 slice-start.1
  10.5 1.1 %turn_keys.1.k = bf16[8,128,2048]{2,1,0:T(8,128)(2,1)S(1)} custom-call(f32[8,2432]{1,0:T(8,128)S(1)} %get-tuple-element.9.after.refs_0_, bf16[8,2048,128]{2,1,0:T(8,128)(2,1)S(1)} %copy-done.1, bf16[8,2048,128]{2,1,0:T(8,128)(2,1)S(1)} %copy-done), custom_call_target="tpu_custom_call" | custom-call | bytes 4194304 | tf_op jit(solution)/shard_map/turn_keys/pallas_call | solution.py:285
  11.7 0.0 collective-permute-done.2
  11.7 1.9 %collective-permute-done.1 = f16[8,2432]{1,0:T(8,128)(2,1)S(1)} collective-permute-done((f16[8,2432]{1,0:T(8,128)(2,1)S(1)}, f16[8,2432]{1,0:T(8,128)(2,1)S(1)}, u32[]{:S(2)}, u32[]{:S(2)}) %collective-permute-start.1) | collective-permute-done | bytes 38944 | tf_op jit(solution)/shard_map/ppermute | solution.py:239
  13.7 0.0 collective-permute-done
  13.7 0.1 broadcast_in_dim.2.lengths
  13.8 1.8 %attention.1.refs_0_ = bf16[8,2048]{1,0:T(8,128)(2,1)S(1)} custom-call(bf16[4096,2048]{1,0:T(8,128)(2,1)} %weights.3, s32[8,128]{1,0:T(8,128)S(1)} %broadcast_in_dim.2.lengths, f32[8,128]{1,0:T(8,128)S(1)} %get-tuple-element.16.cosine, f32[8,128]{1,0:T(8,128)S(1)} %get-tuple-element.17.sine, bf16[8,128,2048]{2,1,0:T(8,128)(2,1)S(1)} %turn_keys.1.k, ...), custom_call_target="tpu_custom_call" | custom-call | flops 134217728 | bytes 8388608 | tf_op jit(solution)/shard_map/attention/pallas_call | solution.py:300
  15.6 0.8 %collective-permute-start.5 = (bf16[8,2048]{1,0:T(8,128)(2,1)S(1)}, bf16[8,2048]{1,0:T(8,128)(2,1)S(1)}, u32[]{:S(2)}, u32[]{:S(2)}) collective-permute-start(bf16[8,2048]{1,0:T(8,128)(2,1)S(1)} %attention.1.refs_0_), channel_id=1, source_target_pairs={{0,12},{4,8},{8,4},{12,0},{1,13},{5,9},{9,5},{13,1},{2,14},{6,10},... | collective-permute-start | bytes 98312 | tf_op jit(solution)/shard_map/ppermute | solution.py:239
  16.4 0.7 %collective-permute-start.4 = (bf16[8,2048]{1,0:T(8,128)(2,1)S(1)}, bf16[8,2048]{1,0:T(8,128)(2,1)S(1)}, u32[]{:S(2)}, u32[]{:S(2)}) collective-permute-start(bf16[8,2048]{1,0:T(8,128)(2,1)S(1)} %attention.1.refs_0_), channel_id=1, source_target_pairs={{0,8},{4,12},{8,0},{12,4},{1,9},{5,13},{9,1},{13,5},{2,10},{6,14},... | collective-permute-start | bytes 98312 | tf_op jit(solution)/shard_map/ppermute | solution.py:239
  17.1 0.4 %collective-permute-start.3 = (bf16[8,2048]{1,0:T(8,128)(2,1)S(1)}, bf16[8,2048]{1,0:T(8,128)(2,1)S(1)}, u32[]{:S(2)}, u32[]{:S(2)}) collective-permute-start(bf16[8,2048]{1,0:T(8,128)(2,1)S(1)} %attention.1.refs_0_), channel_id=1, source_target_pairs={{0,4},{4,0},{8,12},{12,8},{1,5},{5,1},{9,13},{13,9},{2,6},{6,2},{1... | collective-permute-start | bytes 98312 | tf_op jit(solution)/shard_map/ppermute | solution.py:239
  17.5 1.8 %collective-permute-done.5.refs_3_ = bf16[8,2048]{1,0:T(8,128)(2,1)S(1)} collective-permute-done((bf16[8,2048]{1,0:T(8,128)(2,1)S(1)}, bf16[8,2048]{1,0:T(8,128)(2,1)S(1)}, u32[]{:S(2)}, u32[]{:S(2)}) %collective-permute-start.5) | collective-permute-done | bytes 32800 | tf_op jit(solution)/shard_map/ppermute | solution.py:239
  19.3 1.0 %collective-permute-done.4.refs_2_ = bf16[8,2048]{1,0:T(8,128)(2,1)S(1)} collective-permute-done((bf16[8,2048]{1,0:T(8,128)(2,1)S(1)}, bf16[8,2048]{1,0:T(8,128)(2,1)S(1)}, u32[]{:S(2)}, u32[]{:S(2)}) %collective-permute-start.4) | collective-permute-done | bytes 32800 | tf_op jit(solution)/shard_map/ppermute | solution.py:239
  20.3 0.0 collective-permute-done.3.refs_1_
  20.3 0.0 slice-done
  20.3 0.0 slice-done.1
  20.4 0.8 %project_out.5 = bf16[32,1024]{1,0:T(8,128)(2,1)S(1)} custom-call(bf16[2048,4096]{1,0:T(8,128)(2,1)S(1)} %bitcast.2, bf16[8,2048]{1,0:T(8,128)(2,1)S(1)} %attention.1.refs_0_, bf16[8,2048]{1,0:T(8,128)(2,1)S(1)} %collective-permute-done.3.refs_1_, bf16[8,2048]{1,0:T(8,128)(2,1)S(1)} %collective-permute-done.4.refs_2_, ...), custom_call_target="tpu_custom_call" | custom-call | flops 134217728 | bytes 4194304 | tf_op jit(solution)/shard_map/project_out/pallas_call | solution.py:328
  21.2 1.6 %collective-permute-start.6 = (bf16[32,1024]{1,0:T(8,128)(2,1)S(1)}, bf16[32,1024]{1,0:T(8,128)(2,1)S(1)}, u32[]{:S(2)}, u32[]{:S(2)}) collective-permute-start(bf16[32,1024]{1,0:T(8,128)(2,1)S(1)} %project_out.5), channel_id=1, source_target_pairs={{0,1},{1,0},{2,3},{3,2},{4,5},{5,4},{6,7},{7,6},{8,9},{9,8},{10,11... | collective-permute-start | bytes 196616 | tf_op jit(solution)/shard_map/ppermute | solution.py:239
  22.8 0.8 %project_out.7 = bf16[32,1024]{1,0:T(8,128)(2,1)S(1)} custom-call(bf16[2048,4096]{1,0:T(8,128)(2,1)S(1)} %bitcast.2, bf16[8,2048]{1,0:T(8,128)(2,1)S(1)} %attention.1.refs_0_, bf16[8,2048]{1,0:T(8,128)(2,1)S(1)} %collective-permute-done.3.refs_1_, bf16[8,2048]{1,0:T(8,128)(2,1)S(1)} %collective-permute-done.4.refs_2_, ...), custom_call_target="tpu_custom_call" | custom-call | flops 134217728 | bytes 4194304 | tf_op jit(solution)/shard_map/project_out/pallas_call | solution.py:328
  23.6 0.5 %collective-permute-start.9 = (bf16[32,1024]{1,0:T(8,128)(2,1)S(1)}, bf16[32,1024]{1,0:T(8,128)(2,1)S(1)}, u32[]{:S(2)}, u32[]{:S(2)}) collective-permute-start(bf16[32,1024]{1,0:T(8,128)(2,1)S(1)} %project_out.7), channel_id=1, source_target_pairs={{0,1},{1,0},{2,3},{3,2},{4,5},{5,4},{6,7},{7,6},{8,9},{9,8},{10,11... | collective-permute-start | bytes 196616 | tf_op jit(solution)/shard_map/ppermute | solution.py:239
  24.1 0.8 %project_out.6.own = f32[32,1024]{1,0:T(8,128)S(1)} custom-call(bf16[2048,4096]{1,0:T(8,128)(2,1)S(1)} %bitcast.2, bf16[8,2048]{1,0:T(8,128)(2,1)S(1)} %attention.1.refs_0_, bf16[8,2048]{1,0:T(8,128)(2,1)S(1)} %collective-permute-done.3.refs_1_, bf16[8,2048]{1,0:T(8,128)(2,1)S(1)} %collective-permute-done.4.refs_2_, ...), custom_call_target="tpu_custom_call" | custom-call | flops 134217728 | bytes 4194304 | tf_op jit(solution)/shard_map/project_out/pallas_call | solution.py:328
  24.9 0.0 copy-start.2
  24.9 0.8 %project_out.4.own = f32[32,1024]{1,0:T(8,128)S(1)} custom-call(bf16[2048,4096]{1,0:T(8,128)(2,1)S(1)} %bitcast.2, bf16[8,2048]{1,0:T(8,128)(2,1)S(1)} %attention.1.refs_0_, bf16[8,2048]{1,0:T(8,128)(2,1)S(1)} %collective-permute-done.3.refs_1_, bf16[8,2048]{1,0:T(8,128)(2,1)S(1)} %collective-permute-done.4.refs_2_, ...), custom_call_target="tpu_custom_call" | custom-call | flops 134217728 | bytes 4194304 | tf_op jit(solution)/shard_map/project_out/pallas_call | solution.py:328
  25.8 0.0 collective-permute-done.6.arrived
  25.8 2.7 %collective-permute-start.7 = (bf16[32,1024]{1,0:T(8,128)(2,1)S(1)}, bf16[32,1024]{1,0:T(8,128)(2,1)S(1)}, u32[]{:S(2)}, u32[]{:S(2)}) collective-permute-start(bf16[32,1024]{1,0:T(8,128)(2,1)S(1)} %add_near.2.refs_0_), channel_id=1, source_target_pairs={{0,2},{1,3},{2,0},{3,1},{4,6},{5,7},{6,4},{7,5},{8,10},{9,11},{10,... | collective-permute-start | bytes 196616 | tf_op jit(solution)/shard_map/ppermute | solution.py:239
  28.5 0.0 collective-permute-done.9.arrived
  28.5 2.7 %collective-permute-start.10 = (bf16[32,1024]{1,0:T(8,128)(2,1)S(1)}, bf16[32,1024]{1,0:T(8,128)(2,1)S(1)}, u32[]{:S(2)}, u32[]{:S(2)}) collective-permute-start(bf16[32,1024]{1,0:T(8,128)(2,1)S(1)} %add_near.3.refs_0_), channel_id=1, source_target_pairs={{0,2},{1,3},{2,0},{3,1},{4,6},{5,7},{6,4},{7,5},{8,10},{9,11},{10,... | collective-permute-start | bytes 196616 | tf_op jit(solution)/shard_map/ppermute | solution.py:239
  31.2 1.9 %collective-permute-done.7.refs_1_ = bf16[32,1024]{1,0:T(8,128)(2,1)S(1)} collective-permute-done((bf16[32,1024]{1,0:T(8,128)(2,1)S(1)}, bf16[32,1024]{1,0:T(8,128)(2,1)S(1)}, u32[]{:S(2)}, u32[]{:S(2)}) %collective-permute-start.7) | collective-permute-done | bytes 65568 | tf_op jit(solution)/shard_map/ppermute | solution.py:239
  33.0 0.0 copy-done.2
  33.0 0.1 finish.2.refs_0_
  33.1 0.3 collective-permute-start.8
  33.4 0.5 %collective-permute-done.10.refs_1_ = bf16[32,1024]{1,0:T(8,128)(2,1)S(1)} collective-permute-done((bf16[32,1024]{1,0:T(8,128)(2,1)S(1)}, bf16[32,1024]{1,0:T(8,128)(2,1)S(1)}, u32[]{:S(2)}, u32[]{:S(2)}) %collective-permute-start.10) | collective-permute-done | bytes 65568 | tf_op jit(solution)/shard_map/ppermute | solution.py:239
  33.9 2.0 %collective-permute-start.11 = (bf16[32,1024]{1,0:T(8,128)(2,1)S(1)}, bf16[32,1024]{1,0:T(8,128)(2,1)S(1)}, u32[]{:S(2)}, u32[]{:S(2)}) collective-permute-start(bf16[32,1024]{1,0:T(8,128)(2,1)S(1)} %finish.3.refs_2_), channel_id=1, source_target_pairs={{0,1},{1,0},{2,3},{3,2},{4,5},{5,4},{6,7},{7,6},{8,9},{9,8},{10,11... | collective-permute-start | bytes 196616 | tf_op jit(solution)/shard_map/ppermute | solution.py:239
  35.9 1.7 %collective-permute-done.8.refs_1_ = bf16[32,1024]{1,0:T(8,128)(2,1)S(1)} collective-permute-done((bf16[32,1024]{1,0:T(8,128)(2,1)S(1)}, bf16[32,1024]{1,0:T(8,128)(2,1)S(1)}, u32[]{:S(2)}, u32[]{:S(2)}) %collective-permute-start.8) | collective-permute-done | bytes 65568 | tf_op jit(solution)/shard_map/ppermute | solution.py:239
  37.5 0.7 %collective-permute-done.11.refs_3_ = bf16[32,1024]{1,0:T(8,128)(2,1)S(1)} collective-permute-done((bf16[32,1024]{1,0:T(8,128)(2,1)S(1)}, bf16[32,1024]{1,0:T(8,128)(2,1)S(1)}, u32[]{:S(2)}, u32[]{:S(2)}) %collective-permute-start.11) | collective-permute-done | bytes 65568 | tf_op jit(solution)/shard_map/ppermute | solution.py:239
  38.3 0.7 %assemble.1 = bf16[32,4096]{1,0:T(8,128)(2,1)} custom-call(bf16[32,1024]{1,0:T(8,128)(2,1)S(1)} %finish.2.refs_0_, bf16[32,1024]{1,0:T(8,128)(2,1)S(1)} %collective-permute-done.8.refs_1_, bf16[32,1024]{1,0:T(8,128)(2,1)S(1)} %finish.3.refs_2_, bf16[32,1024]{1,0:T(8,128)(2,1)S(1)} %collective-permute-done.11.refs_3_), custom_call_target="tpu_custom_call" | custom-call | tf_op jit(solution)/shard_map/assemble/pallas_call | solution.py:361
  (17 shorter events, 0.2 us)
Async XLA Ops:
  6.9 3.4 %copy-start.3 = (s32[8]{0:T(128)S(1)}, s32[8]{0:T(128)}, u32[]{:S(2)}) copy-start(s32[8]{0:T(128)} %param.17) | copy-start | bytes 100
  6.9 3.6 %copy-start = (bf16[8,2048,128]{2,1,0:T(8,128)(2,1)S(1)}, bf16[8,2048,128]{2,1,0:T(8,128)(2,1)}, u32[]{:S(2)}) copy-start(bf16[8,2048,128]{2,1,0:T(8,128)(2,1)} %v.3) | copy-start | bytes 12582916
  7.0 3.6 %copy-start.1 = (bf16[8,2048,128]{2,1,0:T(8,128)(2,1)S(1)}, bf16[8,2048,128]{2,1,0:T(8,128)(2,1)}, u32[]{:S(2)}) copy-start(bf16[8,2048,128]{2,1,0:T(8,128)(2,1)} %k.1) | copy-start | bytes 12582916
  7.0 4.7 %collective-permute-start.2 = (f16[8,2432]{1,0:T(8,128)(2,1)S(1)}, f16[8,2432]{1,0:T(8,128)(2,1)S(1)}, u32[]{:S(2)}, u32[]{:S(2)}) collective-permute-start(f16[8,2432]{1,0:T(8,128)(2,1)S(1)} %convert_element_type.26), channel_id=1, source_target_pairs={{0,12},{4,8},{8,4},{12,0},{1,13},{5,9},{9,5},{13,1},{2,14},{6,10},... | collective-permute-start | bytes 116744 | tf_op jit(solution)/shard_map/ppermute | solution.py:239
  9.5 4.2 %collective-permute-start.1 = (f16[8,2432]{1,0:T(8,128)(2,1)S(1)}, f16[8,2432]{1,0:T(8,128)(2,1)S(1)}, u32[]{:S(2)}, u32[]{:S(2)}) collective-permute-start(f16[8,2432]{1,0:T(8,128)(2,1)S(1)} %convert_element_type.24), channel_id=1, source_target_pairs={{0,8},{4,12},{8,0},{12,4},{1,9},{5,13},{9,1},{13,5},{2,10},{6,14},... | collective-permute-start | bytes 116744 | tf_op jit(solution)/shard_map/ppermute | solution.py:239
  10.1 3.5 %collective-permute-start = (f16[8,2432]{1,0:T(8,128)(2,1)S(1)}, f16[8,2432]{1,0:T(8,128)(2,1)S(1)}, u32[]{:S(2)}, u32[]{:S(2)}) collective-permute-start(f16[8,2432]{1,0:T(8,128)(2,1)S(1)} %convert_element_type.22), channel_id=1, source_target_pairs={{0,4},{4,0},{8,12},{12,8},{1,5},{5,1},{9,13},{13,9},{2,6},{6,2},{1... | collective-permute-start | bytes 116744 | tf_op jit(solution)/shard_map/ppermute | solution.py:239
  10.5 9.8 %slice-start = ((s8[16777216]{0:T(1024)(128)(4,1)}), s8[4194304]{0:T(1024)(128)(4,1)S(1)}, s32[]{:S(2)}) async-start(s8[16777216]{0:T(1024)(128)(4,1)} %bitcast.1), calls=%async_computation | async-start | bytes 8388608
  10.5 9.8 %slice-start.1 = ((s8[16777216]{0:T(1024)(128)(4,1)}), s8[4194304]{0:T(1024)(128)(4,1)S(1)}, s32[]{:S(2)}) async-start(s8[16777216]{0:T(1024)(128)(4,1)} %bitcast.1), calls=%async_computation.1 | async-start | bytes 8388608
  13.7 6.6 %slice-start.2 = ((s8[16777216]{0:T(1024)(128)(4,1)}), s8[4194304]{0:T(1024)(128)(4,1)S(1)}, s32[]{:S(2)}) async-start(s8[16777216]{0:T(1024)(128)(4,1)} %bitcast.1), calls=%async_computation.2 | async-start | bytes 8388608
  13.8 6.6 %slice-start.3 = ((s8[16777216]{0:T(1024)(128)(4,1)}), s8[4194304]{0:T(1024)(128)(4,1)S(1)}, s32[]{:S(2)}) async-start(s8[16777216]{0:T(1024)(128)(4,1)} %bitcast.1), calls=%async_computation.3 | async-start | bytes 8388608
  15.6 3.8 %collective-permute-start.5 = (bf16[8,2048]{1,0:T(8,128)(2,1)S(1)}, bf16[8,2048]{1,0:T(8,128)(2,1)S(1)}, u32[]{:S(2)}, u32[]{:S(2)}) collective-permute-start(bf16[8,2048]{1,0:T(8,128)(2,1)S(1)} %attention.1.refs_0_), channel_id=1, source_target_pairs={{0,12},{4,8},{8,4},{12,0},{1,13},{5,9},{9,5},{13,1},{2,14},{6,10},... | collective-permute-start | bytes 98312 | tf_op jit(solution)/shard_map/ppermute | solution.py:239
  16.4 3.9 %collective-permute-start.4 = (bf16[8,2048]{1,0:T(8,128)(2,1)S(1)}, bf16[8,2048]{1,0:T(8,128)(2,1)S(1)}, u32[]{:S(2)}, u32[]{:S(2)}) collective-permute-start(bf16[8,2048]{1,0:T(8,128)(2,1)S(1)} %attention.1.refs_0_), channel_id=1, source_target_pairs={{0,8},{4,12},{8,0},{12,4},{1,9},{5,13},{9,1},{13,5},{2,10},{6,14},... | collective-permute-start | bytes 98312 | tf_op jit(solution)/shard_map/ppermute | solution.py:239
  17.1 3.2 %collective-permute-start.3 = (bf16[8,2048]{1,0:T(8,128)(2,1)S(1)}, bf16[8,2048]{1,0:T(8,128)(2,1)S(1)}, u32[]{:S(2)}, u32[]{:S(2)}) collective-permute-start(bf16[8,2048]{1,0:T(8,128)(2,1)S(1)} %attention.1.refs_0_), channel_id=1, source_target_pairs={{0,4},{4,0},{8,12},{12,8},{1,5},{5,1},{9,13},{13,9},{2,6},{6,2},{1... | collective-permute-start | bytes 98312 | tf_op jit(solution)/shard_map/ppermute | solution.py:239
  21.2 4.6 %collective-permute-start.6 = (bf16[32,1024]{1,0:T(8,128)(2,1)S(1)}, bf16[32,1024]{1,0:T(8,128)(2,1)S(1)}, u32[]{:S(2)}, u32[]{:S(2)}) collective-permute-start(bf16[32,1024]{1,0:T(8,128)(2,1)S(1)} %project_out.5), channel_id=1, source_target_pairs={{0,1},{1,0},{2,3},{3,2},{4,5},{5,4},{6,7},{7,6},{8,9},{9,8},{10,11... | collective-permute-start | bytes 196616 | tf_op jit(solution)/shard_map/ppermute | solution.py:239
  23.6 4.9 %collective-permute-start.9 = (bf16[32,1024]{1,0:T(8,128)(2,1)S(1)}, bf16[32,1024]{1,0:T(8,128)(2,1)S(1)}, u32[]{:S(2)}, u32[]{:S(2)}) collective-permute-start(bf16[32,1024]{1,0:T(8,128)(2,1)S(1)} %project_out.7), channel_id=1, source_target_pairs={{0,1},{1,0},{2,3},{3,2},{4,5},{5,4},{6,7},{7,6},{8,9},{9,8},{10,11... | collective-permute-start | bytes 196616 | tf_op jit(solution)/shard_map/ppermute | solution.py:239
  24.9 8.1 %copy-start.2 = (bf16[32,4096]{1,0:T(8,128)(2,1)S(1)}, bf16[32,4096]{1,0:T(8,128)(2,1)}, u32[]{:S(2)}) copy-start(bf16[32,4096]{1,0:T(8,128)(2,1)} %x.3) | copy-start | bytes 786436
  25.8 7.2 %collective-permute-start.7 = (bf16[32,1024]{1,0:T(8,128)(2,1)S(1)}, bf16[32,1024]{1,0:T(8,128)(2,1)S(1)}, u32[]{:S(2)}, u32[]{:S(2)}) collective-permute-start(bf16[32,1024]{1,0:T(8,128)(2,1)S(1)} %add_near.2.refs_0_), channel_id=1, source_target_pairs={{0,2},{1,3},{2,0},{3,1},{4,6},{5,7},{6,4},{7,5},{8,10},{9,11},{10,... | collective-permute-start | bytes 196616 | tf_op jit(solution)/shard_map/ppermute | solution.py:239
  28.5 5.4 %collective-permute-start.10 = (bf16[32,1024]{1,0:T(8,128)(2,1)S(1)}, bf16[32,1024]{1,0:T(8,128)(2,1)S(1)}, u32[]{:S(2)}, u32[]{:S(2)}) collective-permute-start(bf16[32,1024]{1,0:T(8,128)(2,1)S(1)} %add_near.3.refs_0_), channel_id=1, source_target_pairs={{0,2},{1,3},{2,0},{3,1},{4,6},{5,7},{6,4},{7,5},{8,10},{9,11},{10,... | collective-permute-start | bytes 196616 | tf_op jit(solution)/shard_map/ppermute | solution.py:239
  33.1 4.4 %collective-permute-start.8 = (bf16[32,1024]{1,0:T(8,128)(2,1)S(1)}, bf16[32,1024]{1,0:T(8,128)(2,1)S(1)}, u32[]{:S(2)}, u32[]{:S(2)}) collective-permute-start(bf16[32,1024]{1,0:T(8,128)(2,1)S(1)} %finish.2.refs_0_), channel_id=1, source_target_pairs={{0,1},{1,0},{2,3},{3,2},{4,5},{5,4},{6,7},{7,6},{8,9},{9,8},{10,11... | collective-permute-start | bytes 196616 | tf_op jit(solution)/shard_map/ppermute | solution.py:239
  33.9 4.3 %collective-permute-start.11 = (bf16[32,1024]{1,0:T(8,128)(2,1)S(1)}, bf16[32,1024]{1,0:T(8,128)(2,1)S(1)}, u32[]{:S(2)}, u32[]{:S(2)}) collective-permute-start(bf16[32,1024]{1,0:T(8,128)(2,1)S(1)} %finish.3.refs_2_), channel_id=1, source_target_pairs={{0,1},{1,0},{2,3},{3,2},{4,5},{5,4},{6,7},{7,6},{8,9},{9,8},{10,11... | collective-permute-start | bytes 196616 | tf_op jit(solution)/shard_map/ppermute | solution.py:239

commit v14 on v13

--- a/solution.py
+++ b/solution.py
@@ -199,15 +199,19 @@
     return 2 * chunk + ((lax.axis_index("gy") ^ given) & 1)
 
 
-def project_out(size, chunk, given, w, *refs):
+def project_out(size, chunk, w, *refs):
     blocks, out, gathered = refs[:size], refs[-2], refs[-1]
     heads = gather_rows(blocks, gathered)
-    part = columns(place(chunk, given), out.shape[1])
+    part = columns(place(chunk, 1), out.shape[1])
     out[...] = jnp.dot(heads, w[:, part], preferred_element_type=F32).astype(out.dtype)
 
 
-def add_near(own, arrived, out):
-    out[...] = (own[...] + arrived[...].astype(F32)).astype(BF16)
+def add_near(size, chunk, w, arrived, *refs):
+    blocks, out, gathered = refs[:size], refs[-2], refs[-1]
+    heads = gather_rows(blocks, gathered)
+    part = columns(place(chunk, 0), out.shape[1])
+    total = jnp.dot(heads, w[:, part], preferred_element_type=F32)
+    out[...] = (total + arrived[...].astype(F32)).astype(BF16)
 
 
 def finish(size, chunk, x, *refs):
@@ -324,29 +328,22 @@
         gathered = [in_vmem(a) for a in gathered]
         half = size_y // 2
 
-        def product(chunk, given):
+        def product(kernel, chunk, *operands):
             return pl.pallas_call(
-                functools.partial(project_out, size_x, chunk, given),
-                out_shape=pltpu.VMEM((batch, block), BF16 if given else F32),
-                in_specs=[VMEM] * (1 + size_x),
+                functools.partial(kernel, size_x, chunk),
+                out_shape=pltpu.VMEM((batch, block), BF16),
+                in_specs=[VMEM] * (1 + len(operands) + size_x),
                 out_specs=VMEM,
                 scratch_shapes=[pltpu.VMEM((batch, width), F32)],
                 compiler_params=params(8),
                 cost_estimate=cost(2 * batch * width * block, 2 * width * block),
-                name="project_out",
-            )(in_vmem(w_output), *gathered)
-
-        near = [swap(product(chunk, 1), "gy", size_y, 1) for chunk in range(2)]
+                name=kernel.__name__,
+            )(in_vmem(w_output), *[in_vmem(a) for a in operands], *gathered)
+
+        near = [swap(product(project_out, chunk), "gy", size_y, 1) for chunk in range(2)]
         blocks = []
         for chunk in range(2):
-            pair = pl.pallas_call(
-                add_near,
-                out_shape=pltpu.VMEM((batch, block), BF16),
-                in_specs=[VMEM] * 2,
-                out_specs=VMEM,
-                compiler_params=params(4),
-                name="add_near",
-            )(in_vmem(product(chunk, 0)), in_vmem(near[chunk]))
+            pair = product(add_near, chunk, near[chunk])
             far = [pair] + [swap(pair, "gy", size_y, 2 * m) for m in range(1, half)]
             done = pl.pallas_call(
                 functools.partial(finish, half, chunk),

time: 39.1 us -> 40.6 us (1.038)
  waiting for transfers between devices: 9.46 us -> 12.3 us
  starting transfers between devices: 14.9 us -> 13.6 us
    ppermute x12, waiting for transfers between devices: 9.46 us -> 12.3 us  [swap(): return lax.ppermute(value, axis, [(i, i ^ mask) for i in range(size)])]
    ppermute x12, starting transfers between devices: 14.9 us -> 13.6 us  [swap(): return lax.ppermute(value, axis, [(i, i ^ mask) for i in range(size)])]
    pallas_call x6 -> x4, Pallas kernels: 3.33 us -> 3.3 us  [product(): pl.pallas_call(functools.partial(kernel, size_x, chunk), out_shape=pltpu....]
  transfers between devices with their start and end apart: 12 -> 12, of which waited for: 7 -> 8; matrix products, arithmetic and copies ran while one was open for 1% -> 1% of each run, Pallas kernels for 10% -> 9%
where the time goes in v14:
time: 40.6 us; the launch traced here: 40.5 us
  Pallas kernels  14 us (34%)
  starting transfers between devices  13.6 us (33%)
  waiting for transfers between devices  12.3 us (30%)
    ppermute x12, starting transfers between devices, swap(): return lax.ppermute(value, axis, [(i, i ^ mask) for i in range(size)])  13.6 us
    ppermute x12, waiting for transfers between devices, swap(): return lax.ppermute(value, axis, [(i, i ^ mask) for i in range(size)])  12.3 us
    pallas_call x1, Pallas kernels, shards(): pl.pallas_call(project, out_shape=pltpu.VMEM((batch, packed), F32), in_sp...  6.92 us
    pallas_call x4, Pallas kernels, product(): pl.pallas_call(functools.partial(kernel, size_x, chunk), out_shape=pltpu....  3.3 us
    pallas_call x1, Pallas kernels, shards(): pl.pallas_call(functools.partial(attention, size_x, depth * size_x), out_...  1.82 us
    pallas_call x1, Pallas kernels, shards(): pl.pallas_call(turn_keys, out_shape=pltpu.VMEM((rows, HD, key_cache.shape...  1.13 us
  transfers between devices with their start and end apart: 12, of which 8 were waited for; matrix products, arithmetic and copies ran while one was open for 1% of the time, Pallas kernels for 9%

profile of v14, /device:TPU:0, one launch (start us, length us, event | category | flops | bytes accessed | tf_op | source)
XLA Modules:
  0.0 40.5 jit_solution(971685384673208840)
XLA Ops:
  0.0 6.9 %project.1.total = f32[32,2432]{1,0:T(8,128)S(1)} custom-call(bf16[32,4096]{1,0:T(8,128)(2,1)} %x.3, f32[1,4096]{1,0:T(1,128)} %bitcast.3, bf16[4096,2048]{1,0:T(8,128)(2,1)} %weights.3, bf16[4096,128]{1,0:T(8,128)(2,1)} %wk_hbm.1, bf16[4096,128]{1,0:T(8,128)(2,1)} %wv_hbm.1), custom_call_target="tpu_custom_call" | custom-call | flops 637534208 | bytes 19922944 | tf_op jit(solution)/shard_map/project/pallas_call | solution.py:258
  6.9 0.0 copy-start.3
  6.9 0.0 copy-start
  7.0 0.0 copy-start.1
  7.0 2.4 %collective-permute-start.2 = (f16[8,2432]{1,0:T(8,128)(2,1)S(1)}, f16[8,2432]{1,0:T(8,128)(2,1)S(1)}, u32[]{:S(2)}, u32[]{:S(2)}) collective-permute-start(f16[8,2432]{1,0:T(8,128)(2,1)S(1)} %convert_element_type.26), channel_id=1, source_target_pairs={{0,12},{4,8},{8,4},{12,0},{1,13},{5,9},{9,5},{13,1},{2,14},{6,10},... | collective-permute-start | bytes 116744 | tf_op jit(solution)/shard_map/ppermute | solution.py:243
  9.5 0.6 %collective-permute-start.1 = (f16[8,2432]{1,0:T(8,128)(2,1)S(1)}, f16[8,2432]{1,0:T(8,128)(2,1)S(1)}, u32[]{:S(2)}, u32[]{:S(2)}) collective-permute-start(f16[8,2432]{1,0:T(8,128)(2,1)S(1)} %convert_element_type.24), channel_id=1, source_target_pairs={{0,8},{4,12},{8,0},{12,4},{1,9},{5,13},{9,1},{13,5},{2,10},{6,14},... | collective-permute-start | bytes 116744 | tf_op jit(solution)/shard_map/ppermute | solution.py:243
  10.1 0.2 collective-permute-start
  10.3 0.0 copy-done.3
  10.3 0.1 fusion
  10.4 0.1 pad_maximum_fusion
  10.5 0.0 copy-done
  10.5 0.0 copy-done.1
  10.5 0.0 slice-start
  10.5 0.0 slice-start.1
  10.5 1.1 %turn_keys.1.k = bf16[8,128,2048]{2,1,0:T(8,128)(2,1)S(1)} custom-call(f32[8,2432]{1,0:T(8,128)S(1)} %get-tuple-element.9.after.refs_0_, bf16[8,2048,128]{2,1,0:T(8,128)(2,1)S(1)} %copy-done.1, bf16[8,2048,128]{2,1,0:T(8,128)(2,1)S(1)} %copy-done), custom_call_target="tpu_custom_call" | custom-call | bytes 4194304 | tf_op jit(solution)/shard_map/turn_keys/pallas_call | solution.py:289
  11.7 0.0 collective-permute-done.2
  11.7 1.9 %collective-permute-done.1 = f16[8,2432]{1,0:T(8,128)(2,1)S(1)} collective-permute-done((f16[8,2432]{1,0:T(8,128)(2,1)S(1)}, f16[8,2432]{1,0:T(8,128)(2,1)S(1)}, u32[]{:S(2)}, u32[]{:S(2)}) %collective-permute-start.1) | collective-permute-done | bytes 38944 | tf_op jit(solution)/shard_map/ppermute | solution.py:243
  13.7 0.0 collective-permute-done
  13.7 0.1 broadcast_in_dim.2.lengths
  13.8 1.8 %attention.1.refs_0_ = bf16[8,2048]{1,0:T(8,128)(2,1)S(1)} custom-call(bf16[4096,2048]{1,0:T(8,128)(2,1)} %weights.3, s32[8,128]{1,0:T(8,128)S(1)} %broadcast_in_dim.2.lengths, f32[8,128]{1,0:T(8,128)S(1)} %get-tuple-element.16.cosine, f32[8,128]{1,0:T(8,128)S(1)} %get-tuple-element.17.sine, bf16[8,128,2048]{2,1,0:T(8,128)(2,1)S(1)} %turn_keys.1.k, ...), custom_call_target="tpu_custom_call" | custom-call | flops 134217728 | bytes 8388608 | tf_op jit(solution)/shard_map/attention/pallas_call | solution.py:304
  15.6 0.8 %collective-permute-start.5 = (bf16[8,2048]{1,0:T(8,128)(2,1)S(1)}, bf16[8,2048]{1,0:T(8,128)(2,1)S(1)}, u32[]{:S(2)}, u32[]{:S(2)}) collective-permute-start(bf16[8,2048]{1,0:T(8,128)(2,1)S(1)} %attention.1.refs_0_), channel_id=1, source_target_pairs={{0,12},{4,8},{8,4},{12,0},{1,13},{5,9},{9,5},{13,1},{2,14},{6,10},... | collective-permute-start | bytes 98312 | tf_op jit(solution)/shard_map/ppermute | solution.py:243
  16.4 0.7 %collective-permute-start.4 = (bf16[8,2048]{1,0:T(8,128)(2,1)S(1)}, bf16[8,2048]{1,0:T(8,128)(2,1)S(1)}, u32[]{:S(2)}, u32[]{:S(2)}) collective-permute-start(bf16[8,2048]{1,0:T(8,128)(2,1)S(1)} %attention.1.refs_0_), channel_id=1, source_target_pairs={{0,8},{4,12},{8,0},{12,4},{1,9},{5,13},{9,1},{13,5},{2,10},{6,14},... | collective-permute-start | bytes 98312 | tf_op jit(solution)/shard_map/ppermute | solution.py:243
  17.1 0.4 %collective-permute-start.3 = (bf16[8,2048]{1,0:T(8,128)(2,1)S(1)}, bf16[8,2048]{1,0:T(8,128)(2,1)S(1)}, u32[]{:S(2)}, u32[]{:S(2)}) collective-permute-start(bf16[8,2048]{1,0:T(8,128)(2,1)S(1)} %attention.1.refs_0_), channel_id=1, source_target_pairs={{0,4},{4,0},{8,12},{12,8},{1,5},{5,1},{9,13},{13,9},{2,6},{6,2},{1... | collective-permute-start | bytes 98312 | tf_op jit(solution)/shard_map/ppermute | solution.py:243
  17.5 1.8 %collective-permute-done.5.refs_3_ = bf16[8,2048]{1,0:T(8,128)(2,1)S(1)} collective-permute-done((bf16[8,2048]{1,0:T(8,128)(2,1)S(1)}, bf16[8,2048]{1,0:T(8,128)(2,1)S(1)}, u32[]{:S(2)}, u32[]{:S(2)}) %collective-permute-start.5) | collective-permute-done | bytes 32800 | tf_op jit(solution)/shard_map/ppermute | solution.py:243
  19.3 1.0 %collective-permute-done.4.refs_2_ = bf16[8,2048]{1,0:T(8,128)(2,1)S(1)} collective-permute-done((bf16[8,2048]{1,0:T(8,128)(2,1)S(1)}, bf16[8,2048]{1,0:T(8,128)(2,1)S(1)}, u32[]{:S(2)}, u32[]{:S(2)}) %collective-permute-start.4) | collective-permute-done | bytes 32800 | tf_op jit(solution)/shard_map/ppermute | solution.py:243
  20.3 0.0 collective-permute-done.3.refs_1_
  20.3 0.0 slice-done
  20.3 0.0 slice-done.1
  20.3 0.0 slice-done.2
  20.4 0.8 %project_out.2 = bf16[32,1024]{1,0:T(8,128)(2,1)S(1)} custom-call(bf16[2048,4096]{1,0:T(8,128)(2,1)S(1)} %bitcast.2, bf16[8,2048]{1,0:T(8,128)(2,1)S(1)} %attention.1.refs_0_, bf16[8,2048]{1,0:T(8,128)(2,1)S(1)} %collective-permute-done.3.refs_1_, bf16[8,2048]{1,0:T(8,128)(2,1)S(1)} %collective-permute-done.4.refs_2_, ...), custom_call_target="tpu_custom_call" | custom-call | flops 134217728 | bytes 4194304 | tf_op jit(solution)/shard_map/project_out/pallas_call | solution.py:332
  21.2 1.6 %collective-permute-start.6 = (bf16[32,1024]{1,0:T(8,128)(2,1)S(1)}, bf16[32,1024]{1,0:T(8,128)(2,1)S(1)}, u32[]{:S(2)}, u32[]{:S(2)}) collective-permute-start(bf16[32,1024]{1,0:T(8,128)(2,1)S(1)} %project_out.2), channel_id=1, source_target_pairs={{0,1},{1,0},{2,3},{3,2},{4,5},{5,4},{6,7},{7,6},{8,9},{9,8},{10,11... | collective-permute-start | bytes 196616 | tf_op jit(solution)/shard_map/ppermute | solution.py:243
  22.8 0.8 %project_out.3 = bf16[32,1024]{1,0:T(8,128)(2,1)S(1)} custom-call(bf16[2048,4096]{1,0:T(8,128)(2,1)S(1)} %bitcast.2, bf16[8,2048]{1,0:T(8,128)(2,1)S(1)} %attention.1.refs_0_, bf16[8,2048]{1,0:T(8,128)(2,1)S(1)} %collective-permute-done.3.refs_1_, bf16[8,2048]{1,0:T(8,128)(2,1)S(1)} %collective-permute-done.4.refs_2_, ...), custom_call_target="tpu_custom_call" | custom-call | flops 134217728 | bytes 4194304 | tf_op jit(solution)/shard_map/project_out/pallas_call | solution.py:332
  23.6 0.5 %collective-permute-start.9 = (bf16[32,1024]{1,0:T(8,128)(2,1)S(1)}, bf16[32,1024]{1,0:T(8,128)(2,1)S(1)}, u32[]{:S(2)}, u32[]{:S(2)}) collective-permute-start(bf16[32,1024]{1,0:T(8,128)(2,1)S(1)} %project_out.3), channel_id=1, source_target_pairs={{0,1},{1,0},{2,3},{3,2},{4,5},{5,4},{6,7},{7,6},{8,9},{9,8},{10,11... | collective-permute-start | bytes 196616 | tf_op jit(solution)/shard_map/ppermute | solution.py:243
  24.1 1.7 %collective-permute-done.6.arrived = bf16[32,1024]{1,0:T(8,128)(2,1)S(1)} collective-permute-done((bf16[32,1024]{1,0:T(8,128)(2,1)S(1)}, bf16[32,1024]{1,0:T(8,128)(2,1)S(1)}, u32[]{:S(2)}, u32[]{:S(2)}) %collective-permute-start.6) | collective-permute-done | bytes 65568 | tf_op jit(solution)/shard_map/ppermute | solution.py:243
  25.8 0.8 %add_near.2.refs_0_ = bf16[32,1024]{1,0:T(8,128)(2,1)S(1)} custom-call(bf16[2048,4096]{1,0:T(8,128)(2,1)S(1)} %bitcast.2, bf16[32,1024]{1,0:T(8,128)(2,1)S(1)} %collective-permute-done.6.arrived, bf16[8,2048]{1,0:T(8,128)(2,1)S(1)} %attention.1.refs_0_, bf16[8,2048]{1,0:T(8,128)(2,1)S(1)} %collective-permute-done.3.refs_1_, ...), custom_call_target="tpu_custom_call" | custom-call | flops 134217728 | bytes 4194304 | tf_op jit(solution)/shard_map/add_near/pallas_call | solution.py:332
  26.6 0.0 copy-start.2
  26.6 2.7 %collective-permute-start.7 = (bf16[32,1024]{1,0:T(8,128)(2,1)S(1)}, bf16[32,1024]{1,0:T(8,128)(2,1)S(1)}, u32[]{:S(2)}, u32[]{:S(2)}) collective-permute-start(bf16[32,1024]{1,0:T(8,128)(2,1)S(1)} %add_near.2.refs_0_), channel_id=1, source_target_pairs={{0,2},{1,3},{2,0},{3,1},{4,6},{5,7},{6,4},{7,5},{8,10},{9,11},{10,... | collective-permute-start | bytes 196616 | tf_op jit(solution)/shard_map/ppermute | solution.py:243
  29.3 0.0 collective-permute-done.9.arrived
  29.3 0.8 %add_near.3.refs_0_ = bf16[32,1024]{1,0:T(8,128)(2,1)S(1)} custom-call(bf16[2048,4096]{1,0:T(8,128)(2,1)S(1)} %bitcast.2, bf16[32,1024]{1,0:T(8,128)(2,1)S(1)} %collective-permute-done.9.arrived, bf16[8,2048]{1,0:T(8,128)(2,1)S(1)} %attention.1.refs_0_, bf16[8,2048]{1,0:T(8,128)(2,1)S(1)} %collective-permute-done.3.refs_1_, ...), custom_call_target="tpu_custom_call" | custom-call | flops 134217728 | bytes 4194304 | tf_op jit(solution)/shard_map/add_near/pallas_call | solution.py:332
  30.1 1.8 %collective-permute-start.10 = (bf16[32,1024]{1,0:T(8,128)(2,1)S(1)}, bf16[32,1024]{1,0:T(8,128)(2,1)S(1)}, u32[]{:S(2)}, u32[]{:S(2)}) collective-permute-start(bf16[32,1024]{1,0:T(8,128)(2,1)S(1)} %add_near.3.refs_0_), channel_id=1, source_target_pairs={{0,2},{1,3},{2,0},{3,1},{4,6},{5,7},{6,4},{7,5},{8,10},{9,11},{10,... | collective-permute-start | bytes 196616 | tf_op jit(solution)/shard_map/ppermute | solution.py:243
  31.9 2.0 %collective-permute-done.7.refs_1_ = bf16[32,1024]{1,0:T(8,128)(2,1)S(1)} collective-permute-done((bf16[32,1024]{1,0:T(8,128)(2,1)S(1)}, bf16[32,1024]{1,0:T(8,128)(2,1)S(1)}, u32[]{:S(2)}, u32[]{:S(2)}) %collective-permute-start.7) | collective-permute-done | bytes 65568 | tf_op jit(solution)/shard_map/ppermute | solution.py:243
  33.9 0.1 finish.2.refs_0_
  34.0 0.1 collective-permute-start.8
  34.0 1.3 %collective-permute-done.10.refs_1_ = bf16[32,1024]{1,0:T(8,128)(2,1)S(1)} collective-permute-done((bf16[32,1024]{1,0:T(8,128)(2,1)S(1)}, bf16[32,1024]{1,0:T(8,128)(2,1)S(1)}, u32[]{:S(2)}, u32[]{:S(2)}) %collective-permute-start.10) | collective-permute-done | bytes 65568 | tf_op jit(solution)/shard_map/ppermute | solution.py:243
  35.4 1.8 %collective-permute-start.11 = (bf16[32,1024]{1,0:T(8,128)(2,1)S(1)}, bf16[32,1024]{1,0:T(8,128)(2,1)S(1)}, u32[]{:S(2)}, u32[]{:S(2)}) collective-permute-start(bf16[32,1024]{1,0:T(8,128)(2,1)S(1)} %finish.3.refs_2_), channel_id=1, source_target_pairs={{0,1},{1,0},{2,3},{3,2},{4,5},{5,4},{6,7},{7,6},{8,9},{9,8},{10,11... | collective-permute-start | bytes 196616 | tf_op jit(solution)/shard_map/ppermute | solution.py:243
  37.2 1.1 %collective-permute-done.8.refs_1_ = bf16[32,1024]{1,0:T(8,128)(2,1)S(1)} collective-permute-done((bf16[32,1024]{1,0:T(8,128)(2,1)S(1)}, bf16[32,1024]{1,0:T(8,128)(2,1)S(1)}, u32[]{:S(2)}, u32[]{:S(2)}) %collective-permute-start.8) | collective-permute-done | bytes 65568 | tf_op jit(solution)/shard_map/ppermute | solution.py:243
  38.3 1.5 %collective-permute-done.11.refs_3_ = bf16[32,1024]{1,0:T(8,128)(2,1)S(1)} collective-permute-done((bf16[32,1024]{1,0:T(8,128)(2,1)S(1)}, bf16[32,1024]{1,0:T(8,128)(2,1)S(1)}, u32[]{:S(2)}, u32[]{:S(2)}) %collective-permute-start.11) | collective-permute-done | bytes 65568 | tf_op jit(solution)/shard_map/ppermute | solution.py:243
  39.8 0.7 %assemble.1 = bf16[32,4096]{1,0:T(8,128)(2,1)} custom-call(bf16[32,1024]{1,0:T(8,128)(2,1)S(1)} %finish.2.refs_0_, bf16[32,1024]{1,0:T(8,128)(2,1)S(1)} %collective-permute-done.8.refs_1_, bf16[32,1024]{1,0:T(8,128)(2,1)S(1)} %finish.3.refs_2_, bf16[32,1024]{1,0:T(8,128)(2,1)S(1)} %collective-permute-done.11.refs_3_), custom_call_target="tpu_custom_call" | custom-call | tf_op jit(solution)/shard_map/assemble/pallas_call | solution.py:358
  (15 shorter events, 0.2 us)
Async XLA Ops:
  6.9 3.4 %copy-start.3 = (s32[8]{0:T(128)S(1)}, s32[8]{0:T(128)}, u32[]{:S(2)}) copy-start(s32[8]{0:T(128)} %param.17) | copy-start | bytes 100
  6.9 3.6 %copy-start = (bf16[8,2048,128]{2,1,0:T(8,128)(2,1)S(1)}, bf16[8,2048,128]{2,1,0:T(8,128)(2,1)}, u32[]{:S(2)}) copy-start(bf16[8,2048,128]{2,1,0:T(8,128)(2,1)} %v.3) | copy-start | bytes 12582916
  7.0 3.6 %copy-start.1 = (bf16[8,2048,128]{2,1,0:T(8,128)(2,1)S(1)}, bf16[8,2048,128]{2,1,0:T(8,128)(2,1)}, u32[]{:S(2)}) copy-start(bf16[8,2048,128]{2,1,0:T(8,128)(2,1)} %k.1) | copy-start | bytes 12582916
  7.0 4.7 %collective-permute-start.2 = (f16[8,2432]{1,0:T(8,128)(2,1)S(1)}, f16[8,2432]{1,0:T(8,128)(2,1)S(1)}, u32[]{:S(2)}, u32[]{:S(2)}) collective-permute-start(f16[8,2432]{1,0:T(8,128)(2,1)S(1)} %convert_element_type.26), channel_id=1, source_target_pairs={{0,12},{4,8},{8,4},{12,0},{1,13},{5,9},{9,5},{13,1},{2,14},{6,10},... | collective-permute-start | bytes 116744 | tf_op jit(solution)/shard_map/ppermute | solution.py:243
  9.5 4.2 %collective-permute-start.1 = (f16[8,2432]{1,0:T(8,128)(2,1)S(1)}, f16[8,2432]{1,0:T(8,128)(2,1)S(1)}, u32[]{:S(2)}, u32[]{:S(2)}) collective-permute-start(f16[8,2432]{1,0:T(8,128)(2,1)S(1)} %convert_element_type.24), channel_id=1, source_target_pairs={{0,8},{4,12},{8,0},{12,4},{1,9},{5,13},{9,1},{13,5},{2,10},{6,14},... | collective-permute-start | bytes 116744 | tf_op jit(solution)/shard_map/ppermute | solution.py:243
  10.1 3.5 %collective-permute-start = (f16[8,2432]{1,0:T(8,128)(2,1)S(1)}, f16[8,2432]{1,0:T(8,128)(2,1)S(1)}, u32[]{:S(2)}, u32[]{:S(2)}) collective-permute-start(f16[8,2432]{1,0:T(8,128)(2,1)S(1)} %convert_element_type.22), channel_id=1, source_target_pairs={{0,4},{4,0},{8,12},{12,8},{1,5},{5,1},{9,13},{13,9},{2,6},{6,2},{1... | collective-permute-start | bytes 116744 | tf_op jit(solution)/shard_map/ppermute | solution.py:243
  10.5 9.8 %slice-start = ((s8[16777216]{0:T(1024)(128)(4,1)}), s8[4194304]{0:T(1024)(128)(4,1)S(1)}, s32[]{:S(2)}) async-start(s8[16777216]{0:T(1024)(128)(4,1)} %bitcast.1), calls=%async_computation | async-start | bytes 8388608
  10.5 9.8 %slice-start.1 = ((s8[16777216]{0:T(1024)(128)(4,1)}), s8[4194304]{0:T(1024)(128)(4,1)S(1)}, s32[]{:S(2)}) async-start(s8[16777216]{0:T(1024)(128)(4,1)} %bitcast.1), calls=%async_computation.1 | async-start | bytes 8388608
  13.7 6.6 %slice-start.2 = ((s8[16777216]{0:T(1024)(128)(4,1)}), s8[4194304]{0:T(1024)(128)(4,1)S(1)}, s32[]{:S(2)}) async-start(s8[16777216]{0:T(1024)(128)(4,1)} %bitcast.1), calls=%async_computation.2 | async-start | bytes 8388608
  13.8 6.6 %slice-start.3 = ((s8[16777216]{0:T(1024)(128)(4,1)}), s8[4194304]{0:T(1024)(128)(4,1)S(1)}, s32[]{:S(2)}) async-start(s8[16777216]{0:T(1024)(128)(4,1)} %bitcast.1), calls=%async_computation.3 | async-start | bytes 8388608
  15.6 3.8 %collective-permute-start.5 = (bf16[8,2048]{1,0:T(8,128)(2,1)S(1)}, bf16[8,2048]{1,0:T(8,128)(2,1)S(1)}, u32[]{:S(2)}, u32[]{:S(2)}) collective-permute-start(bf16[8,2048]{1,0:T(8,128)(2,1)S(1)} %attention.1.refs_0_), channel_id=1, source_target_pairs={{0,12},{4,8},{8,4},{12,0},{1,13},{5,9},{9,5},{13,1},{2,14},{6,10},... | collective-permute-start | bytes 98312 | tf_op jit(solution)/shard_map/ppermute | solution.py:243
  16.4 3.9 %collective-permute-start.4 = (bf16[8,2048]{1,0:T(8,128)(2,1)S(1)}, bf16[8,2048]{1,0:T(8,128)(2,1)S(1)}, u32[]{:S(2)}, u32[]{:S(2)}) collective-permute-start(bf16[8,2048]{1,0:T(8,128)(2,1)S(1)} %attention.1.refs_0_), channel_id=1, source_target_pairs={{0,8},{4,12},{8,0},{12,4},{1,9},{5,13},{9,1},{13,5},{2,10},{6,14},... | collective-permute-start | bytes 98312 | tf_op jit(solution)/shard_map/ppermute | solution.py:243
  17.1 3.2 %collective-permute-start.3 = (bf16[8,2048]{1,0:T(8,128)(2,1)S(1)}, bf16[8,2048]{1,0:T(8,128)(2,1)S(1)}, u32[]{:S(2)}, u32[]{:S(2)}) collective-permute-start(bf16[8,2048]{1,0:T(8,128)(2,1)S(1)} %attention.1.refs_0_), channel_id=1, source_target_pairs={{0,4},{4,0},{8,12},{12,8},{1,5},{5,1},{9,13},{13,9},{2,6},{6,2},{1... | collective-permute-start | bytes 98312 | tf_op jit(solution)/shard_map/ppermute | solution.py:243
  21.2 4.6 %collective-permute-start.6 = (bf16[32,1024]{1,0:T(8,128)(2,1)S(1)}, bf16[32,1024]{1,0:T(8,128)(2,1)S(1)}, u32[]{:S(2)}, u32[]{:S(2)}) collective-permute-start(bf16[32,1024]{1,0:T(8,128)(2,1)S(1)} %project_out.2), channel_id=1, source_target_pairs={{0,1},{1,0},{2,3},{3,2},{4,5},{5,4},{6,7},{7,6},{8,9},{9,8},{10,11... | collective-permute-start | bytes 196616 | tf_op jit(solution)/shard_map/ppermute | solution.py:243
  23.6 5.7 %collective-permute-start.9 = (bf16[32,1024]{1,0:T(8,128)(2,1)S(1)}, bf16[32,1024]{1,0:T(8,128)(2,1)S(1)}, u32[]{:S(2)}, u32[]{:S(2)}) collective-permute-start(bf16[32,1024]{1,0:T(8,128)(2,1)S(1)} %project_out.3), channel_id=1, source_target_pairs={{0,1},{1,0},{2,3},{3,2},{4,5},{5,4},{6,7},{7,6},{8,9},{9,8},{10,11... | collective-permute-start | bytes 196616 | tf_op jit(solution)/shard_map/ppermute | solution.py:243
  26.6 7.3 %copy-start.2 = (bf16[32,4096]{1,0:T(8,128)(2,1)S(1)}, bf16[32,4096]{1,0:T(8,128)(2,1)}, u32[]{:S(2)}) copy-start(bf16[32,4096]{1,0:T(8,128)(2,1)} %x.3) | copy-start | bytes 786436
  26.6 7.3 %collective-permute-start.7 = (bf16[32,1024]{1,0:T(8,128)(2,1)S(1)}, bf16[32,1024]{1,0:T(8,128)(2,1)S(1)}, u32[]{:S(2)}, u32[]{:S(2)}) collective-permute-start(bf16[32,1024]{1,0:T(8,128)(2,1)S(1)} %add_near.2.refs_0_), channel_id=1, source_target_pairs={{0,2},{1,3},{2,0},{3,1},{4,6},{5,7},{6,4},{7,5},{8,10},{9,11},{10,... | collective-permute-start | bytes 196616 | tf_op jit(solution)/shard_map/ppermute | solution.py:243
  30.1 5.2 %collective-permute-start.10 = (bf16[32,1024]{1,0:T(8,128)(2,1)S(1)}, bf16[32,1024]{1,0:T(8,128)(2,1)S(1)}, u32[]{:S(2)}, u32[]{:S(2)}) collective-permute-start(bf16[32,1024]{1,0:T(8,128)(2,1)S(1)} %add_near.3.refs_0_), channel_id=1, source_target_pairs={{0,2},{1,3},{2,0},{3,1},{4,6},{5,7},{6,4},{7,5},{8,10},{9,11},{10,... | collective-permute-start | bytes 196616 | tf_op jit(solution)/shard_map/ppermute | solution.py:243
  34.0 4.3 %collective-permute-start.8 = (bf16[32,1024]{1,0:T(8,128)(2,1)S(1)}, bf16[32,1024]{1,0:T(8,128)(2,1)S(1)}, u32[]{:S(2)}, u32[]{:S(2)}) collective-permute-start(bf16[32,1024]{1,0:T(8,128)(2,1)S(1)} %finish.2.refs_0_), channel_id=1, source_target_pairs={{0,1},{1,0},{2,3},{3,2},{4,5},{5,4},{6,7},{7,6},{8,9},{9,8},{10,11... | collective-permute-start | bytes 196616 | tf_op jit(solution)/shard_map/ppermute | solution.py:243
  35.4 4.3 %collective-permute-start.11 = (bf16[32,1024]{1,0:T(8,128)(2,1)S(1)}, bf16[32,1024]{1,0:T(8,128)(2,1)S(1)}, u32[]{:S(2)}, u32[]{:S(2)}) collective-permute-start(bf16[32,1024]{1,0:T(8,128)(2,1)S(1)} %finish.3.refs_2_), channel_id=1, source_target_pairs={{0,1},{1,0},{2,3},{3,2},{4,5},{5,4},{6,7},{7,6},{8,9},{9,8},{10,11... | collective-permute-start | bytes 196616 | tf_op jit(solution)/shard_map/ppermute | solution.py:243

commit v15 on v13

--- a/solution.py
+++ b/solution.py
@@ -186,49 +186,47 @@
         heads[:, head * HD : (head + 1) * HD] = o_rows[head * rows : (head + 1) * rows].astype(BF16)
 
 
-def gather_rows(blocks, gathered):
+def gather_rows(masks, blocks, gathered):
     me = lax.axis_index("gx")
     rows = blocks[0].shape[0]
-    for mask, block in enumerate(blocks):
+    for mask, block in zip(masks, blocks):
         start = pl.multiple_of((me ^ mask) * rows, 8)
         gathered[pl.ds(start, rows), :] = block[...].astype(F32)
     return gathered[...].astype(BF16)
 
 
-def place(chunk, given):
-    return 2 * chunk + ((lax.axis_index("gy") ^ given) & 1)
-
-
-def project_out(size, chunk, given, w, *refs):
-    blocks, out, gathered = refs[:size], refs[-2], refs[-1]
-    heads = gather_rows(blocks, gathered)
-    part = columns(place(chunk, given), out.shape[1])
-    out[...] = jnp.dot(heads, w[:, part], preferred_element_type=F32).astype(out.dtype)
+def half_of(given, width):
+    return columns((lax.axis_index("gy") ^ given) & 1, width)
+
+
+def project_out(masks, pick, w, *refs):
+    *blocks, out, gathered = refs
+    heads = gather_rows(masks, blocks, gathered)
+    total = jnp.dot(heads, w[:, pick(out.shape[1])], preferred_element_type=F32)
+    out[...] = total.astype(out.dtype)
 
 
 def add_near(own, arrived, out):
-    out[...] = (own[...] + arrived[...].astype(F32)).astype(BF16)
-
-
-def finish(size, chunk, x, *refs):
-    terms, out, ranked = refs[:size], refs[-2], refs[-1]
+    out[...] = (own[...].astype(F32) + arrived[...].astype(F32)).astype(BF16)
+
+
+def finish(size, pick, x, *refs):
+    *terms, out, ranked = refs
     rank = lax.axis_index("gy") // 2
     for mask, term in enumerate(terms):
         ranked[rank ^ mask] = term[...].astype(F32)
     total = ranked[0]
     for index in range(1, size):
         total = total + ranked[index]
-    part = columns(place(chunk, 0), out.shape[1])
-    out[...] = (x[:, part].astype(F32) + total).astype(BF16)
-
-
-def assemble(*refs):
-    *blocks, out, sems = refs
-    width = blocks[0].shape[1]
+    out[...] = (x[:, pick(out.shape[1])].astype(F32) + total).astype(BF16)
+
+
+def assemble(kept, swapped, rest, out, sems):
+    near, far = kept.shape[1], rest.shape[1]
+    targets = [half_of(0, near), half_of(1, near), pl.ds(2 * near, far)]
     copies = []
-    for index, block in enumerate(blocks):
-        target = out.at[:, columns(place(index // 2, index % 2), width)]
-        copies.append(pltpu.make_async_copy(block, target, sems.at[index]))
+    for index, (block, target) in enumerate(zip((kept, swapped, rest), targets)):
+        copies.append(pltpu.make_async_copy(block, out.at[:, target], sems.at[index]))
     for copy in copies:
         copy.start()
     for copy in copies:
@@ -242,6 +240,7 @@
 def solution(mesh):
     size_x = mesh.shape["gx"]
     size_y = mesh.shape["gy"]
+    order = [0, *range(1, size_x, 2), *range(2, size_x, 2)]
     sems = lambda n: pltpu.SemaphoreType.DMA((n,))
 
     def shards(inputs, gain, w_query, w_key, w_value, w_output, key_cache, value_cache, lengths):
@@ -249,7 +248,6 @@
         width = w_query.shape[1]
         rows = key_cache.shape[0]
         packed = width + 3 * HD
-        block = w_output.shape[1] // 4
 
         total = pl.pallas_call(
             project,
@@ -278,7 +276,7 @@
             name="split",
         )(in_vmem(total), in_hbm(w_query))
         arrived = [sums[0]]
-        for mask in range(1, size_x):
+        for mask in order[1:]:
             arrived.append(swap(sums[mask].astype(F16), "gx", size_x, mask).astype(F32))
 
         values = in_vmem(value_cache)
@@ -319,15 +317,22 @@
             values,
             *[in_vmem(a) for a in arrived],
         )
-        gathered = [heads] + [swap(heads, "gx", size_x, m) for m in range(1, size_x)]
+        gathered = [heads] + [swap(heads, "gx", size_x, m) for m in order[1:]]
 
         gathered = [in_vmem(a) for a in gathered]
-        half = size_y // 2
-
-        def product(chunk, given):
+        model_cut = w_output.shape[1]
+        near = -(-5 * model_cut // (16 * HD)) * HD
+        rest = model_cut - 2 * near
+        picks = {
+            "kept": functools.partial(half_of, 0),
+            "given": functools.partial(half_of, 1),
+            "rest": lambda far: pl.ds(2 * near, far),
+        }
+
+        def product(pick, block, kind):
             return pl.pallas_call(
-                functools.partial(project_out, size_x, chunk, given),
-                out_shape=pltpu.VMEM((batch, block), BF16 if given else F32),
+                functools.partial(project_out, order, picks[pick]),
+                out_shape=pltpu.VMEM((batch, block), kind),
                 in_specs=[VMEM] * (1 + size_x),
                 out_specs=VMEM,
                 scratch_shapes=[pltpu.VMEM((batch, width), F32)],
@@ -336,37 +341,44 @@
                 name="project_out",
             )(in_vmem(w_output), *gathered)
 
-        near = [swap(product(chunk, 1), "gy", size_y, 1) for chunk in range(2)]
-        blocks = []
-        for chunk in range(2):
-            pair = pl.pallas_call(
+        def near_sum(own, arrived):
+            return pl.pallas_call(
                 add_near,
-                out_shape=pltpu.VMEM((batch, block), BF16),
+                out_shape=pltpu.VMEM(own.shape, BF16),
                 in_specs=[VMEM] * 2,
                 out_specs=VMEM,
                 compiler_params=params(4),
                 name="add_near",
-            )(in_vmem(product(chunk, 0)), in_vmem(near[chunk]))
-            far = [pair] + [swap(pair, "gy", size_y, 2 * m) for m in range(1, half)]
-            done = pl.pallas_call(
-                functools.partial(finish, half, chunk),
-                out_shape=pltpu.VMEM((batch, block), BF16),
+            )(in_vmem(own), in_vmem(arrived))
+
+        def far_sum(pick, pair):
+            half = size_y // 2
+            terms = [pair] + [swap(pair, "gy", size_y, 2 * m) for m in range(1, half)]
+            return pl.pallas_call(
+                functools.partial(finish, half, picks[pick]),
+                out_shape=pltpu.VMEM(pair.shape, BF16),
                 in_specs=[VMEM] * (1 + half),
                 out_specs=VMEM,
-                scratch_shapes=[pltpu.VMEM((half, batch, block), F32)],
+                scratch_shapes=[pltpu.VMEM((half, *pair.shape), F32)],
                 compiler_params=params(8),
                 name="finish",
-            )(in_vmem(inputs), *[in_vmem(a) for a in far])
-            blocks += [done, swap(done, "gy", size_y, 1)]
+            )(in_vmem(inputs), *[in_vmem(a) for a in terms])
+
+        near_a = swap(product("given", near, BF16), "gy", size_y, 1)
+        own_b = product("rest", rest, BF16)
+        near_b = swap(own_b, "gy", size_y, 1)
+        kept = far_sum("kept", near_sum(product("kept", near, F32), near_a))
+        swapped = swap(kept, "gy", size_y, 1)
+        last = far_sum("rest", near_sum(own_b, near_b))
         return pl.pallas_call(
             assemble,
-            out_shape=jax.ShapeDtypeStruct((batch, block * 4), BF16),
-            in_specs=[VMEM] * 4,
+            out_shape=jax.ShapeDtypeStruct((batch, model_cut), BF16),
+            in_specs=[VMEM] * 3,
             out_specs=ANY,
-            scratch_shapes=[sems(4)],
+            scratch_shapes=[sems(3)],
             compiler_params=params(4),
             name="assemble",
-        )(*[in_vmem(b) for b in blocks])
+        )(*[in_vmem(b) for b in (kept, swapped, last)])
 
     placed = (
         P("groups", "gx"),

time: 39.1 us -> 39.7 us (1.015)
  waiting for transfers between devices: 9.46 us -> 10.6 us
  starting transfers between devices: 14.9 us -> 14.4 us
    ppermute x12 -> x11, waiting for transfers between devices: 9.46 us -> 10.6 us  [swap(): return lax.ppermute(value, axis, [(i, i ^ mask) for i in range(size)])]
    ppermute x12 -> x11, starting transfers between devices: 14.9 us -> 14.4 us  [swap(): return lax.ppermute(value, axis, [(i, i ^ mask) for i in range(size)])]
    pallas_call x9 -> x8, Pallas kernels: 4.16 us -> 4.11 us  [the longest x3 3.21 us: product(): pl.pallas_call(functools.partial(project_out, order, picks[pick]), out_sh...]
  transfers between devices with their start and end apart: 12 -> 11, of which waited for: 7 -> 9; matrix products, arithmetic and copies ran while one was open for 1% -> 1% of each run, Pallas kernels for 10% -> 9%
where the time goes in v15:
time: 39.7 us; the launch traced here: 39.5 us
  starting transfers between devices  14.4 us (36%)
  Pallas kernels  14 us (35%)
  waiting for transfers between devices  10.6 us (27%)
    ppermute x11, starting transfers between devices, swap(): return lax.ppermute(value, axis, [(i, i ^ mask) for i in range(size)])  14.4 us
    ppermute x11, waiting for transfers between devices, swap(): return lax.ppermute(value, axis, [(i, i ^ mask) for i in range(size)])  10.6 us
    pallas_call x1, Pallas kernels, shards(): pl.pallas_call(project, out_shape=pltpu.VMEM((batch, packed), F32), in_sp...  6.92 us
    pallas_call x3, Pallas kernels, product(): pl.pallas_call(functools.partial(project_out, order, picks[pick]), out_sh...  3.21 us
    pallas_call x1, Pallas kernels, shards(): pl.pallas_call(functools.partial(attention, size_x, depth * size_x), out_...  1.82 us
    pallas_call x1, Pallas kernels, shards(): pl.pallas_call(turn_keys, out_shape=pltpu.VMEM((rows, HD, key_cache.shape...  1.13 us
  transfers between devices with their start and end apart: 11, of which 9 were waited for; matrix products, arithmetic and copies ran while one was open for 1% of the time, Pallas kernels for 9%

profile of v15, /device:TPU:0, one launch (start us, length us, event | category | flops | bytes accessed | tf_op | source)
XLA Modules:
  0.0 39.5 jit_solution(843267214312979540)
XLA Ops:
  0.0 6.9 %project.1.total = f32[32,2432]{1,0:T(8,128)S(1)} custom-call(bf16[32,4096]{1,0:T(8,128)(2,1)} %x.3, f32[1,4096]{1,0:T(1,128)} %bitcast.3, bf16[4096,2048]{1,0:T(8,128)(2,1)} %weights.3, bf16[4096,128]{1,0:T(8,128)(2,1)} %wk_hbm.1, bf16[4096,128]{1,0:T(8,128)(2,1)} %wv_hbm.1), custom_call_target="tpu_custom_call" | custom-call | flops 637534208 | bytes 19922944 | tf_op jit(solution)/shard_map/project/pallas_call | solution.py:252
  6.9 0.0 copy-start.3
  6.9 0.0 copy-start
  7.0 0.0 copy-start.1
  7.0 3.0 %collective-permute-start.2 = (f16[8,2432]{1,0:T(8,128)(2,1)S(1)}, f16[8,2432]{1,0:T(8,128)(2,1)S(1)}, u32[]{:S(2)}, u32[]{:S(2)}) collective-permute-start(f16[8,2432]{1,0:T(8,128)(2,1)S(1)} %convert_element_type.26), channel_id=1, source_target_pairs={{0,8},{4,12},{8,0},{12,4},{1,9},{5,13},{9,1},{13,5},{2,10},{6,14},... | collective-permute-start | bytes 116744 | tf_op jit(solution)/shard_map/ppermute | solution.py:237
  10.0 0.1 collective-permute-start.1
  10.1 0.2 collective-permute-start
  10.3 0.0 copy-done.3
  10.3 0.1 fusion
  10.4 0.1 pad_maximum_fusion
  10.5 0.0 copy-done
  10.5 0.0 copy-done.1
  10.5 0.0 slice-start
  10.5 0.0 slice-start.1
  10.5 1.1 %turn_keys.1.k = bf16[8,128,2048]{2,1,0:T(8,128)(2,1)S(1)} custom-call(f32[8,2432]{1,0:T(8,128)S(1)} %get-tuple-element.9.after.refs_0_, bf16[8,2048,128]{2,1,0:T(8,128)(2,1)S(1)} %copy-done.1, bf16[8,2048,128]{2,1,0:T(8,128)(2,1)S(1)} %copy-done), custom_call_target="tpu_custom_call" | custom-call | bytes 4194304 | tf_op jit(solution)/shard_map/turn_keys/pallas_call | solution.py:283
  11.7 0.3 collective-permute-done.2
  12.0 1.7 %collective-permute-done.1 = f16[8,2432]{1,0:T(8,128)(2,1)S(1)} collective-permute-done((f16[8,2432]{1,0:T(8,128)(2,1)S(1)}, f16[8,2432]{1,0:T(8,128)(2,1)S(1)}, u32[]{:S(2)}, u32[]{:S(2)}) %collective-permute-start.1) | collective-permute-done | bytes 38944 | tf_op jit(solution)/shard_map/ppermute | solution.py:237
  13.7 0.0 collective-permute-done
  13.7 0.1 broadcast_in_dim.2.lengths
  13.8 0.0 slice-start.2
  13.8 1.8 %attention.1.refs_0_ = bf16[8,2048]{1,0:T(8,128)(2,1)S(1)} custom-call(bf16[4096,2048]{1,0:T(8,128)(2,1)} %weights.3, s32[8,128]{1,0:T(8,128)S(1)} %broadcast_in_dim.2.lengths, f32[8,128]{1,0:T(8,128)S(1)} %get-tuple-element.16.cosine, f32[8,128]{1,0:T(8,128)S(1)} %get-tuple-element.17.sine, bf16[8,128,2048]{2,1,0:T(8,128)(2,1)S(1)} %turn_keys.1.k, ...), custom_call_target="tpu_custom_call" | custom-call | flops 134217728 | bytes 8388608 | tf_op jit(solution)/shard_map/attention/pallas_call | solution.py:298
  15.6 0.9 %collective-permute-start.5 = (bf16[8,2048]{1,0:T(8,128)(2,1)S(1)}, bf16[8,2048]{1,0:T(8,128)(2,1)S(1)}, u32[]{:S(2)}, u32[]{:S(2)}) collective-permute-start(bf16[8,2048]{1,0:T(8,128)(2,1)S(1)} %attention.1.refs_0_), channel_id=1, source_target_pairs={{0,8},{4,12},{8,0},{12,4},{1,9},{5,13},{9,1},{13,5},{2,10},{6,14},... | collective-permute-start | bytes 98312 | tf_op jit(solution)/shard_map/ppermute | solution.py:237
  16.5 0.3 collective-permute-start.4
  16.9 0.9 %collective-permute-start.3 = (bf16[8,2048]{1,0:T(8,128)(2,1)S(1)}, bf16[8,2048]{1,0:T(8,128)(2,1)S(1)}, u32[]{:S(2)}, u32[]{:S(2)}) collective-permute-start(bf16[8,2048]{1,0:T(8,128)(2,1)S(1)} %attention.1.refs_0_), channel_id=1, source_target_pairs={{0,4},{4,0},{8,12},{12,8},{1,5},{5,1},{9,13},{13,9},{2,6},{6,2},{1... | collective-permute-start | bytes 98312 | tf_op jit(solution)/shard_map/ppermute | solution.py:237
  17.8 1.8 %collective-permute-done.5.refs_3_ = bf16[8,2048]{1,0:T(8,128)(2,1)S(1)} collective-permute-done((bf16[8,2048]{1,0:T(8,128)(2,1)S(1)}, bf16[8,2048]{1,0:T(8,128)(2,1)S(1)}, u32[]{:S(2)}, u32[]{:S(2)}) %collective-permute-start.5) | collective-permute-done | bytes 32800 | tf_op jit(solution)/shard_map/ppermute | solution.py:237
  19.6 0.6 %collective-permute-done.4.refs_2_ = bf16[8,2048]{1,0:T(8,128)(2,1)S(1)} collective-permute-done((bf16[8,2048]{1,0:T(8,128)(2,1)S(1)}, bf16[8,2048]{1,0:T(8,128)(2,1)S(1)}, u32[]{:S(2)}, u32[]{:S(2)}) %collective-permute-start.4) | collective-permute-done | bytes 32800 | tf_op jit(solution)/shard_map/ppermute | solution.py:237
  20.2 0.0 collective-permute-done.3.refs_1_
  20.2 0.0 slice-done
  20.2 0.0 slice-done.1
  20.2 0.0 slice-done.2
  20.3 0.0 slice-done.3
  20.3 1.0 %project_out.4 = bf16[32,1280]{1,0:T(8,128)(2,1)S(1)} custom-call(bf16[2048,4096]{1,0:T(8,128)(2,1)S(1)} %bitcast.2, bf16[8,2048]{1,0:T(8,128)(2,1)S(1)} %attention.1.refs_0_, bf16[8,2048]{1,0:T(8,128)(2,1)S(1)} %collective-permute-done.3.refs_1_, bf16[8,2048]{1,0:T(8,128)(2,1)S(1)} %collective-permute-done.4.refs_2_, ...), custom_call_target="tpu_custom_call" | custom-call | flops 167772160 | bytes 5242880 | tf_op jit(solution)/shard_map/project_out/pallas_call | solution.py:333
  21.3 1.6 %collective-permute-start.6 = (bf16[32,1280]{1,0:T(8,128)(2,1)S(1)}, bf16[32,1280]{1,0:T(8,128)(2,1)S(1)}, u32[]{:S(2)}, u32[]{:S(2)}) collective-permute-start(bf16[32,1280]{1,0:T(8,128)(2,1)S(1)} %project_out.4), channel_id=1, source_target_pairs={{0,1},{1,0},{2,3},{3,2},{4,5},{5,4},{6,7},{7,6},{8,9},{9,8},{10,11... | collective-permute-start | bytes 245768 | tf_op jit(solution)/shard_map/ppermute | solution.py:237
  22.9 1.2 %project_out.5.own = bf16[32,1536]{1,0:T(8,128)(2,1)S(1)} custom-call(bf16[2048,4096]{1,0:T(8,128)(2,1)S(1)} %bitcast.2, bf16[8,2048]{1,0:T(8,128)(2,1)S(1)} %attention.1.refs_0_, bf16[8,2048]{1,0:T(8,128)(2,1)S(1)} %collective-permute-done.3.refs_1_, bf16[8,2048]{1,0:T(8,128)(2,1)S(1)} %collective-permute-done.4.refs_2_, ...), custom_call_target="tpu_custom_call" | custom-call | flops 201326592 | bytes 6291456 | tf_op jit(solution)/shard_map/project_out/pallas_call | solution.py:333
  24.1 0.5 %collective-permute-start.9 = (bf16[32,1536]{1,0:T(8,128)(2,1)S(1)}, bf16[32,1536]{1,0:T(8,128)(2,1)S(1)}, u32[]{:S(2)}, u32[]{:S(2)}) collective-permute-start(bf16[32,1536]{1,0:T(8,128)(2,1)S(1)} %project_out.5.own), channel_id=1, source_target_pairs={{0,1},{1,0},{2,3},{3,2},{4,5},{5,4},{6,7},{7,6},{8,9},{9,8},{10,11... | collective-permute-start | bytes 294920 | tf_op jit(solution)/shard_map/ppermute | solution.py:237
  24.5 1.0 %project_out.3.own = f32[32,1280]{1,0:T(8,128)S(1)} custom-call(bf16[2048,4096]{1,0:T(8,128)(2,1)S(1)} %bitcast.2, bf16[8,2048]{1,0:T(8,128)(2,1)S(1)} %attention.1.refs_0_, bf16[8,2048]{1,0:T(8,128)(2,1)S(1)} %collective-permute-done.3.refs_1_, bf16[8,2048]{1,0:T(8,128)(2,1)S(1)} %collective-permute-done.4.refs_2_, ...), custom_call_target="tpu_custom_call" | custom-call | flops 167772160 | bytes 5242880 | tf_op jit(solution)/shard_map/project_out/pallas_call | solution.py:333
  25.6 0.2 collective-permute-done.6.arrived
  25.8 2.7 %collective-permute-start.7 = (bf16[32,1280]{1,0:T(8,128)(2,1)S(1)}, bf16[32,1280]{1,0:T(8,128)(2,1)S(1)}, u32[]{:S(2)}, u32[]{:S(2)}) collective-permute-start(bf16[32,1280]{1,0:T(8,128)(2,1)S(1)} %add_near.2.refs_0_), channel_id=1, source_target_pairs={{0,2},{1,3},{2,0},{3,1},{4,6},{5,7},{6,4},{7,5},{8,10},{9,11},{10,... | collective-permute-start | bytes 245768 | tf_op jit(solution)/shard_map/ppermute | solution.py:237
  28.4 0.2 collective-permute-done.9.arrived
  28.7 3.5 %collective-permute-start.10 = (bf16[32,1536]{1,0:T(8,128)(2,1)S(1)}, bf16[32,1536]{1,0:T(8,128)(2,1)S(1)}, u32[]{:S(2)}, u32[]{:S(2)}) collective-permute-start(bf16[32,1536]{1,0:T(8,128)(2,1)S(1)} %add_near.3.refs_0_), channel_id=1, source_target_pairs={{0,2},{1,3},{2,0},{3,1},{4,6},{5,7},{6,4},{7,5},{8,10},{9,11},{10,... | collective-permute-start | bytes 294920 | tf_op jit(solution)/shard_map/ppermute | solution.py:237
  32.3 2.0 %collective-permute-done.7.refs_1_ = bf16[32,1280]{1,0:T(8,128)(2,1)S(1)} collective-permute-done((bf16[32,1280]{1,0:T(8,128)(2,1)S(1)}, bf16[32,1280]{1,0:T(8,128)(2,1)S(1)}, u32[]{:S(2)}, u32[]{:S(2)}) %collective-permute-start.7) | collective-permute-done | bytes 81952 | tf_op jit(solution)/shard_map/ppermute | solution.py:237
  34.2 0.0 copy-done.2
  34.2 0.1 finish.2.kept
  34.3 0.7 %collective-permute-start.8 = (bf16[32,1280]{1,0:T(8,128)(2,1)S(1)}, bf16[32,1280]{1,0:T(8,128)(2,1)S(1)}, u32[]{:S(2)}, u32[]{:S(2)}) collective-permute-start(bf16[32,1280]{1,0:T(8,128)(2,1)S(1)} %finish.2.kept), channel_id=1, source_target_pairs={{0,1},{1,0},{2,3},{3,2},{4,5},{5,4},{6,7},{7,6},{8,9},{9,8},{10,11... | collective-permute-start | bytes 245768 | tf_op jit(solution)/shard_map/ppermute | solution.py:237
  35.0 1.9 %collective-permute-done.10.refs_1_ = bf16[32,1536]{1,0:T(8,128)(2,1)S(1)} collective-permute-done((bf16[32,1536]{1,0:T(8,128)(2,1)S(1)}, bf16[32,1536]{1,0:T(8,128)(2,1)S(1)}, u32[]{:S(2)}, u32[]{:S(2)}) %collective-permute-start.10) | collective-permute-done | bytes 98336 | tf_op jit(solution)/shard_map/ppermute | solution.py:237
  36.9 0.1 finish.3.rest
  36.9 1.8 %collective-permute-done.8.swapped = bf16[32,1280]{1,0:T(8,128)(2,1)S(1)} collective-permute-done((bf16[32,1280]{1,0:T(8,128)(2,1)S(1)}, bf16[32,1280]{1,0:T(8,128)(2,1)S(1)}, u32[]{:S(2)}, u32[]{:S(2)}) %collective-permute-start.8) | collective-permute-done | bytes 81952 | tf_op jit(solution)/shard_map/ppermute | solution.py:237
  38.8 0.7 %assemble.1 = bf16[32,4096]{1,0:T(8,128)(2,1)} custom-call(bf16[32,1280]{1,0:T(8,128)(2,1)S(1)} %finish.2.kept, bf16[32,1280]{1,0:T(8,128)(2,1)S(1)} %collective-permute-done.8.swapped, bf16[32,1536]{1,0:T(8,128)(2,1)S(1)} %finish.3.rest), custom_call_target="tpu_custom_call" | custom-call | tf_op jit(solution)/shard_map/assemble/pallas_call | solution.py:373
  (14 shorter events, 0.1 us)
Async XLA Ops:
  6.9 3.4 %copy-start.3 = (s32[8]{0:T(128)S(1)}, s32[8]{0:T(128)}, u32[]{:S(2)}) copy-start(s32[8]{0:T(128)} %param.17) | copy-start | bytes 100
  6.9 3.6 %copy-start = (bf16[8,2048,128]{2,1,0:T(8,128)(2,1)S(1)}, bf16[8,2048,128]{2,1,0:T(8,128)(2,1)}, u32[]{:S(2)}) copy-start(bf16[8,2048,128]{2,1,0:T(8,128)(2,1)} %v.3) | copy-start | bytes 12582916
  7.0 3.6 %copy-start.1 = (bf16[8,2048,128]{2,1,0:T(8,128)(2,1)S(1)}, bf16[8,2048,128]{2,1,0:T(8,128)(2,1)}, u32[]{:S(2)}) copy-start(bf16[8,2048,128]{2,1,0:T(8,128)(2,1)} %k.1) | copy-start | bytes 12582916
  7.0 5.0 %collective-permute-start.2 = (f16[8,2432]{1,0:T(8,128)(2,1)S(1)}, f16[8,2432]{1,0:T(8,128)(2,1)S(1)}, u32[]{:S(2)}, u32[]{:S(2)}) collective-permute-start(f16[8,2432]{1,0:T(8,128)(2,1)S(1)} %convert_element_type.26), channel_id=1, source_target_pairs={{0,8},{4,12},{8,0},{12,4},{1,9},{5,13},{9,1},{13,5},{2,10},{6,14},... | collective-permute-start | bytes 116744 | tf_op jit(solution)/shard_map/ppermute | solution.py:237
  10.0 3.6 %collective-permute-start.1 = (f16[8,2432]{1,0:T(8,128)(2,1)S(1)}, f16[8,2432]{1,0:T(8,128)(2,1)S(1)}, u32[]{:S(2)}, u32[]{:S(2)}) collective-permute-start(f16[8,2432]{1,0:T(8,128)(2,1)S(1)} %convert_element_type.24), channel_id=1, source_target_pairs={{0,12},{4,8},{8,4},{12,0},{1,13},{5,9},{9,5},{13,1},{2,14},{6,10},... | collective-permute-start | bytes 116744 | tf_op jit(solution)/shard_map/ppermute | solution.py:237
  10.1 3.5 %collective-permute-start = (f16[8,2432]{1,0:T(8,128)(2,1)S(1)}, f16[8,2432]{1,0:T(8,128)(2,1)S(1)}, u32[]{:S(2)}, u32[]{:S(2)}) collective-permute-start(f16[8,2432]{1,0:T(8,128)(2,1)S(1)} %convert_element_type.22), channel_id=1, source_target_pairs={{0,4},{4,0},{8,12},{12,8},{1,5},{5,1},{9,13},{13,9},{2,6},{6,2},{1... | collective-permute-start | bytes 116744 | tf_op jit(solution)/shard_map/ppermute | solution.py:237
  10.5 9.7 %slice-start = ((s8[16777216]{0:T(1024)(128)(4,1)}), s8[4194304]{0:T(1024)(128)(4,1)S(1)}, s32[]{:S(2)}) async-start(s8[16777216]{0:T(1024)(128)(4,1)} %bitcast.1), calls=%async_computation | async-start | bytes 8388608
  10.5 9.7 %slice-start.1 = ((s8[16777216]{0:T(1024)(128)(4,1)}), s8[4194304]{0:T(1024)(128)(4,1)S(1)}, s32[]{:S(2)}) async-start(s8[16777216]{0:T(1024)(128)(4,1)} %bitcast.1), calls=%async_computation.1 | async-start | bytes 8388608
  13.8 6.5 %slice-start.2 = ((s8[16777216]{0:T(1024)(128)(4,1)}), s8[4194304]{0:T(1024)(128)(4,1)S(1)}, s32[]{:S(2)}) async-start(s8[16777216]{0:T(1024)(128)(4,1)} %bitcast.1), calls=%async_computation.2 | async-start | bytes 8388608
  13.8 6.5 %slice-start.3 = ((s8[16777216]{0:T(1024)(128)(4,1)}), s8[4194304]{0:T(1024)(128)(4,1)S(1)}, s32[]{:S(2)}) async-start(s8[16777216]{0:T(1024)(128)(4,1)} %bitcast.1), calls=%async_computation.3 | async-start | bytes 8388608
  15.6 4.0 %collective-permute-start.5 = (bf16[8,2048]{1,0:T(8,128)(2,1)S(1)}, bf16[8,2048]{1,0:T(8,128)(2,1)S(1)}, u32[]{:S(2)}, u32[]{:S(2)}) collective-permute-start(bf16[8,2048]{1,0:T(8,128)(2,1)S(1)} %attention.1.refs_0_), channel_id=1, source_target_pairs={{0,8},{4,12},{8,0},{12,4},{1,9},{5,13},{9,1},{13,5},{2,10},{6,14},... | collective-permute-start | bytes 98312 | tf_op jit(solution)/shard_map/ppermute | solution.py:237
  16.5 3.7 %collective-permute-start.4 = (bf16[8,2048]{1,0:T(8,128)(2,1)S(1)}, bf16[8,2048]{1,0:T(8,128)(2,1)S(1)}, u32[]{:S(2)}, u32[]{:S(2)}) collective-permute-start(bf16[8,2048]{1,0:T(8,128)(2,1)S(1)} %attention.1.refs_0_), channel_id=1, source_target_pairs={{0,12},{4,8},{8,4},{12,0},{1,13},{5,9},{9,5},{13,1},{2,14},{6,10},... | collective-permute-start | bytes 98312 | tf_op jit(solution)/shard_map/ppermute | solution.py:237
  16.9 3.4 %collective-permute-start.3 = (bf16[8,2048]{1,0:T(8,128)(2,1)S(1)}, bf16[8,2048]{1,0:T(8,128)(2,1)S(1)}, u32[]{:S(2)}, u32[]{:S(2)}) collective-permute-start(bf16[8,2048]{1,0:T(8,128)(2,1)S(1)} %attention.1.refs_0_), channel_id=1, source_target_pairs={{0,4},{4,0},{8,12},{12,8},{1,5},{5,1},{9,13},{13,9},{2,6},{6,2},{1... | collective-permute-start | bytes 98312 | tf_op jit(solution)/shard_map/ppermute | solution.py:237
  21.3 4.5 %collective-permute-start.6 = (bf16[32,1280]{1,0:T(8,128)(2,1)S(1)}, bf16[32,1280]{1,0:T(8,128)(2,1)S(1)}, u32[]{:S(2)}, u32[]{:S(2)}) collective-permute-start(bf16[32,1280]{1,0:T(8,128)(2,1)S(1)} %project_out.4), channel_id=1, source_target_pairs={{0,1},{1,0},{2,3},{3,2},{4,5},{5,4},{6,7},{7,6},{8,9},{9,8},{10,11... | collective-permute-start | bytes 245768 | tf_op jit(solution)/shard_map/ppermute | solution.py:237
  24.1 10.2 %copy-start.2 = (bf16[32,4096]{1,0:T(8,128)(2,1)S(1)}, bf16[32,4096]{1,0:T(8,128)(2,1)}, u32[]{:S(2)}) copy-start(bf16[32,4096]{1,0:T(8,128)(2,1)} %x.3) | copy-start | bytes 786436
  24.1 4.6 %collective-permute-start.9 = (bf16[32,1536]{1,0:T(8,128)(2,1)S(1)}, bf16[32,1536]{1,0:T(8,128)(2,1)S(1)}, u32[]{:S(2)}, u32[]{:S(2)}) collective-permute-start(bf16[32,1536]{1,0:T(8,128)(2,1)S(1)} %project_out.5.own), channel_id=1, source_target_pairs={{0,1},{1,0},{2,3},{3,2},{4,5},{5,4},{6,7},{7,6},{8,9},{9,8},{10,11... | collective-permute-start | bytes 294920 | tf_op jit(solution)/shard_map/ppermute | solution.py:237
  25.8 8.4 %collective-permute-start.7 = (bf16[32,1280]{1,0:T(8,128)(2,1)S(1)}, bf16[32,1280]{1,0:T(8,128)(2,1)S(1)}, u32[]{:S(2)}, u32[]{:S(2)}) collective-permute-start(bf16[32,1280]{1,0:T(8,128)(2,1)S(1)} %add_near.2.refs_0_), channel_id=1, source_target_pairs={{0,2},{1,3},{2,0},{3,1},{4,6},{5,7},{6,4},{7,5},{8,10},{9,11},{10,... | collective-permute-start | bytes 245768 | tf_op jit(solution)/shard_map/ppermute | solution.py:237
  28.7 8.1 %collective-permute-start.10 = (bf16[32,1536]{1,0:T(8,128)(2,1)S(1)}, bf16[32,1536]{1,0:T(8,128)(2,1)S(1)}, u32[]{:S(2)}, u32[]{:S(2)}) collective-permute-start(bf16[32,1536]{1,0:T(8,128)(2,1)S(1)} %add_near.3.refs_0_), channel_id=1, source_target_pairs={{0,2},{1,3},{2,0},{3,1},{4,6},{5,7},{6,4},{7,5},{8,10},{9,11},{10,... | collective-permute-start | bytes 294920 | tf_op jit(solution)/shard_map/ppermute | solution.py:237
  34.3 4.5 %collective-permute-start.8 = (bf16[32,1280]{1,0:T(8,128)(2,1)S(1)}, bf16[32,1280]{1,0:T(8,128)(2,1)S(1)}, u32[]{:S(2)}, u32[]{:S(2)}) collective-permute-start(bf16[32,1280]{1,0:T(8,128)(2,1)S(1)} %finish.2.kept), channel_id=1, source_target_pairs={{0,1},{1,0},{2,3},{3,2},{4,5},{5,4},{6,7},{7,6},{8,9},{9,8},{10,11... | collective-permute-start | bytes 245768 | tf_op jit(solution)/shard_map/ppermute | solution.py:237

commit v16 on v13

--- a/solution.py
+++ b/solution.py
@@ -186,49 +186,58 @@
         heads[:, head * HD : (head + 1) * HD] = o_rows[head * rows : (head + 1) * rows].astype(BF16)
 
 
-def gather_rows(blocks, gathered):
-    me = lax.axis_index("gx")
+def chip_rows(distance, rows):
+    chip = (lax.axis_index("gx") // 2) ^ distance
+    return pl.ds(pl.multiple_of(chip * 2 * rows, 16), 2 * rows)
+
+
+def half_of(given, width):
+    return columns((lax.axis_index("gy") ^ given) & 1, width)
+
+
+def project_out(given, arrivals, w, *refs):
+    arrived, blocks = refs[:arrivals], refs[arrivals:-2]
+    out, gathered = refs[-2:]
     rows = blocks[0].shape[0]
-    for mask, block in enumerate(blocks):
-        start = pl.multiple_of((me ^ mask) * rows, 8)
-        gathered[pl.ds(start, rows), :] = block[...].astype(F32)
-    return gathered[...].astype(BF16)
-
-
-def place(chunk, given):
-    return 2 * chunk + ((lax.axis_index("gy") ^ given) & 1)
-
-
-def project_out(size, chunk, given, w, *refs):
-    blocks, out, gathered = refs[:size], refs[-2], refs[-1]
-    heads = gather_rows(blocks, gathered)
-    part = columns(place(chunk, given), out.shape[1])
-    out[...] = jnp.dot(heads, w[:, part], preferred_element_type=F32).astype(out.dtype)
+    core = lax.axis_index("gx") & 1
+    for index, block in enumerate(blocks):
+        start = (index // 2) * 2 * rows + ((core ^ index) & 1) * rows
+        gathered[pl.ds(pl.multiple_of(start, 8), rows), :] = block[...].astype(F32)
+    heads = gathered[...].astype(BF16)
+    width = out.shape[1]
+    total = jnp.dot(heads, w[:, half_of(given, width)], preferred_element_type=F32)
+    for item in arrived:
+        total = total + item[...].astype(F32)
+    out[...] = total.astype(out.dtype)
 
 
 def add_near(own, arrived, out):
     out[...] = (own[...] + arrived[...].astype(F32)).astype(BF16)
 
 
-def finish(size, chunk, x, *refs):
-    terms, out, ranked = refs[:size], refs[-2], refs[-1]
+def finish(distances, rows, x, *refs):
+    *terms, out, ranked = refs
     rank = lax.axis_index("gy") // 2
     for mask, term in enumerate(terms):
         ranked[rank ^ mask] = term[...].astype(F32)
-    total = ranked[0]
-    for index in range(1, size):
-        total = total + ranked[index]
-    part = columns(place(chunk, 0), out.shape[1])
-    out[...] = (x[:, part].astype(F32) + total).astype(BF16)
-
-
-def assemble(*refs):
+    part = half_of(0, out.shape[1])
+    for index, distance in enumerate(distances):
+        mine = slice(index * 2 * rows, (index + 1) * 2 * rows)
+        total = ranked[0, mine]
+        for other in range(1, len(terms)):
+            total = total + ranked[other, mine]
+        out[mine] = (x[chip_rows(distance, rows), part].astype(F32) + total).astype(BF16)
+
+
+def assemble(chunks, rows, *refs):
     *blocks, out, sems = refs
-    width = blocks[0].shape[1]
     copies = []
     for index, block in enumerate(blocks):
-        target = out.at[:, columns(place(index // 2, index % 2), width)]
-        copies.append(pltpu.make_async_copy(block, target, sems.at[index]))
+        part = half_of(index % 2, block.shape[1])
+        for place, distance in enumerate(chunks[index // 2]):
+            source = block.at[pl.ds(place * 2 * rows, 2 * rows)]
+            target = out.at[chip_rows(distance, rows), part]
+            copies.append(pltpu.make_async_copy(source, target, sems.at[len(copies)]))
     for copy in copies:
         copy.start()
     for copy in copies:
@@ -249,7 +258,6 @@
         width = w_query.shape[1]
         rows = key_cache.shape[0]
         packed = width + 3 * HD
-        block = w_output.shape[1] // 4
 
         total = pl.pallas_call(
             project,
@@ -323,47 +331,55 @@
 
         gathered = [in_vmem(a) for a in gathered]
         half = size_y // 2
-
-        def product(chunk, given):
+        block = w_output.shape[1] // 2
+        chunks = [list(range(1, size_x // 2)), [0]]
+
+        def product(chunk, given, kind, *arrived):
+            pieces = gathered[2:] if chunk == 0 else gathered[:2]
+            tall = rows * len(pieces)
             return pl.pallas_call(
-                functools.partial(project_out, size_x, chunk, given),
-                out_shape=pltpu.VMEM((batch, block), BF16 if given else F32),
-                in_specs=[VMEM] * (1 + size_x),
+                functools.partial(project_out, given, len(arrived)),
+                out_shape=pltpu.VMEM((tall, block), kind),
+                in_specs=[VMEM] * (1 + len(arrived) + len(pieces)),
                 out_specs=VMEM,
-                scratch_shapes=[pltpu.VMEM((batch, width), F32)],
+                scratch_shapes=[pltpu.VMEM((tall, width), F32)],
                 compiler_params=params(8),
-                cost_estimate=cost(2 * batch * width * block, 2 * width * block),
+                cost_estimate=cost(2 * tall * width * block, 2 * width * block),
                 name="project_out",
-            )(in_vmem(w_output), *gathered)
-
-        near = [swap(product(chunk, 1), "gy", size_y, 1) for chunk in range(2)]
+            )(in_vmem(w_output), *[in_vmem(a) for a in arrived], *pieces)
+
+        near = [swap(product(chunk, 1, BF16), "gy", size_y, 1) for chunk in range(2)]
         blocks = []
-        for chunk in range(2):
-            pair = pl.pallas_call(
-                add_near,
-                out_shape=pltpu.VMEM((batch, block), BF16),
-                in_specs=[VMEM] * 2,
-                out_specs=VMEM,
-                compiler_params=params(4),
-                name="add_near",
-            )(in_vmem(product(chunk, 0)), in_vmem(near[chunk]))
+        for chunk, distances in enumerate(chunks):
+            tall = 2 * rows * len(distances)
+            if chunk == 0:
+                pair = product(chunk, 0, BF16, near[chunk])
+            else:
+                pair = pl.pallas_call(
+                    add_near,
+                    out_shape=pltpu.VMEM((tall, block), BF16),
+                    in_specs=[VMEM] * 2,
+                    out_specs=VMEM,
+                    compiler_params=params(4),
+                    name="add_near",
+                )(in_vmem(product(chunk, 0, F32)), in_vmem(near[chunk]))
             far = [pair] + [swap(pair, "gy", size_y, 2 * m) for m in range(1, half)]
             done = pl.pallas_call(
-                functools.partial(finish, half, chunk),
-                out_shape=pltpu.VMEM((batch, block), BF16),
+                functools.partial(finish, distances, rows),
+                out_shape=pltpu.VMEM((tall, block), BF16),
                 in_specs=[VMEM] * (1 + half),
                 out_specs=VMEM,
-                scratch_shapes=[pltpu.VMEM((half, batch, block), F32)],
+                scratch_shapes=[pltpu.VMEM((half, tall, block), F32)],
                 compiler_params=params(8),
                 name="finish",
             )(in_vmem(inputs), *[in_vmem(a) for a in far])
             blocks += [done, swap(done, "gy", size_y, 1)]
         return pl.pallas_call(
-            assemble,
-            out_shape=jax.ShapeDtypeStruct((batch, block * 4), BF16),
+            functools.partial(assemble, chunks, rows),
+            out_shape=jax.ShapeDtypeStruct((batch, 2 * block), BF16),
             in_specs=[VMEM] * 4,
             out_specs=ANY,
-            scratch_shapes=[sems(4)],
+            scratch_shapes=[sems(size_x)],
             compiler_params=params(4),
             name="assemble",
         )(*[in_vmem(b) for b in blocks])

time: 39.1 us -> 39.7 us (1.015)
  Pallas kernels: 14.1 us -> 15.5 us
  waiting for transfers between devices: 9.46 us -> 8.73 us
    pallas_call x9 -> x8, Pallas kernels: 4.16 us -> 5.63 us  [the longest x4 4.77 us: product(): pl.pallas_call(functools.partial(project_out, given, len(arrived)), out_s...]
    ppermute x12, waiting for transfers between devices: 9.46 us -> 8.73 us  [swap(): return lax.ppermute(value, axis, [(i, i ^ mask) for i in range(size)])]
  transfers between devices with their start and end apart: 12 -> 12, of which waited for: 7 -> 4; matrix products, arithmetic and copies ran while one was open for 1% -> 1% of each run, Pallas kernels for 10% -> 15%
where the time goes in v16:
time: 39.7 us; the launch traced here: 39.5 us
  Pallas kernels  15.5 us (39%)
  starting transfers between devices  14.7 us (37%)
  waiting for transfers between devices  8.73 us (22%)
    ppermute x12, starting transfers between devices, swap(): return lax.ppermute(value, axis, [(i, i ^ mask) for i in range(size)])  14.7 us
    ppermute x12, waiting for transfers between devices, swap(): return lax.ppermute(value, axis, [(i, i ^ mask) for i in range(size)])  8.73 us
    pallas_call x1, Pallas kernels, shards(): pl.pallas_call(project, out_shape=pltpu.VMEM((batch, packed), F32), in_sp...  6.92 us
    pallas_call x4, Pallas kernels, product(): pl.pallas_call(functools.partial(project_out, given, len(arrived)), out_s...  4.77 us
    pallas_call x1, Pallas kernels, shards(): pl.pallas_call(functools.partial(attention, size_x, depth * size_x), out_...  1.82 us
    pallas_call x1, Pallas kernels, shards(): pl.pallas_call(turn_keys, out_shape=pltpu.VMEM((rows, HD, key_cache.shape...  1.13 us
  transfers between devices with their start and end apart: 12, of which 4 were waited for; matrix products, arithmetic and copies ran while one was open for 1% of the time, Pallas kernels for 15%

profile of v16, /device:TPU:0, one launch (start us, length us, event | category | flops | bytes accessed | tf_op | source)
XLA Modules:
  0.0 39.5 jit_solution(9107508084458059659)
XLA Ops:
  0.0 6.9 %project.1.total = f32[32,2432]{1,0:T(8,128)S(1)} custom-call(bf16[32,4096]{1,0:T(8,128)(2,1)} %x.3, f32[1,4096]{1,0:T(1,128)} %bitcast.3, bf16[4096,2048]{1,0:T(8,128)(2,1)} %weights.3, bf16[4096,128]{1,0:T(8,128)(2,1)} %wk_hbm.1, bf16[4096,128]{1,0:T(8,128)(2,1)} %wv_hbm.1), custom_call_target="tpu_custom_call" | custom-call | flops 637534208 | bytes 19922944 | tf_op jit(solution)/shard_map/project/pallas_call | solution.py:262
  6.9 0.0 copy-start.3
  6.9 0.0 copy-start
  7.0 0.0 copy-start.1
  7.0 2.4 %collective-permute-start.2 = (f16[8,2432]{1,0:T(8,128)(2,1)S(1)}, f16[8,2432]{1,0:T(8,128)(2,1)S(1)}, u32[]{:S(2)}, u32[]{:S(2)}) collective-permute-start(f16[8,2432]{1,0:T(8,128)(2,1)S(1)} %convert_element_type.26), channel_id=1, source_target_pairs={{0,12},{4,8},{8,4},{12,0},{1,13},{5,9},{9,5},{13,1},{2,14},{6,10},... | collective-permute-start | bytes 116744 | tf_op jit(solution)/shard_map/ppermute | solution.py:248
  9.5 0.6 %collective-permute-start.1 = (f16[8,2432]{1,0:T(8,128)(2,1)S(1)}, f16[8,2432]{1,0:T(8,128)(2,1)S(1)}, u32[]{:S(2)}, u32[]{:S(2)}) collective-permute-start(f16[8,2432]{1,0:T(8,128)(2,1)S(1)} %convert_element_type.24), channel_id=1, source_target_pairs={{0,8},{4,12},{8,0},{12,4},{1,9},{5,13},{9,1},{13,5},{2,10},{6,14},... | collective-permute-start | bytes 116744 | tf_op jit(solution)/shard_map/ppermute | solution.py:248
  10.1 0.2 collective-permute-start
  10.3 0.0 copy-done.3
  10.3 0.1 fusion
  10.4 0.1 pad_maximum_fusion
  10.5 0.0 copy-done
  10.5 0.0 copy-done.1
  10.5 0.0 slice-start
  10.5 0.0 slice-start.1
  10.5 1.1 %turn_keys.1.k = bf16[8,128,2048]{2,1,0:T(8,128)(2,1)S(1)} custom-call(f32[8,2432]{1,0:T(8,128)S(1)} %get-tuple-element.9.after.refs_0_, bf16[8,2048,128]{2,1,0:T(8,128)(2,1)S(1)} %copy-done.1, bf16[8,2048,128]{2,1,0:T(8,128)(2,1)S(1)} %copy-done), custom_call_target="tpu_custom_call" | custom-call | bytes 4194304 | tf_op jit(solution)/shard_map/turn_keys/pallas_call | solution.py:293
  11.7 0.0 collective-permute-done.2
  11.7 1.9 %collective-permute-done.1 = f16[8,2432]{1,0:T(8,128)(2,1)S(1)} collective-permute-done((f16[8,2432]{1,0:T(8,128)(2,1)S(1)}, f16[8,2432]{1,0:T(8,128)(2,1)S(1)}, u32[]{:S(2)}, u32[]{:S(2)}) %collective-permute-start.1) | collective-permute-done | bytes 38944 | tf_op jit(solution)/shard_map/ppermute | solution.py:248
  13.7 0.0 collective-permute-done
  13.7 0.1 broadcast_in_dim.2.lengths
  13.8 1.8 %attention.1.refs_0_ = bf16[8,2048]{1,0:T(8,128)(2,1)S(1)} custom-call(bf16[4096,2048]{1,0:T(8,128)(2,1)} %weights.3, s32[8,128]{1,0:T(8,128)S(1)} %broadcast_in_dim.2.lengths, f32[8,128]{1,0:T(8,128)S(1)} %get-tuple-element.16.cosine, f32[8,128]{1,0:T(8,128)S(1)} %get-tuple-element.17.sine, bf16[8,128,2048]{2,1,0:T(8,128)(2,1)S(1)} %turn_keys.1.k, ...), custom_call_target="tpu_custom_call" | custom-call | flops 134217728 | bytes 8388608 | tf_op jit(solution)/shard_map/attention/pallas_call | solution.py:308
  15.6 0.1 collective-permute-start.8
  15.7 1.2 %collective-permute-start.4 = (bf16[8,2048]{1,0:T(8,128)(2,1)S(1)}, bf16[8,2048]{1,0:T(8,128)(2,1)S(1)}, u32[]{:S(2)}, u32[]{:S(2)}) collective-permute-start(bf16[8,2048]{1,0:T(8,128)(2,1)S(1)} %attention.1.refs_0_), channel_id=1, source_target_pairs={{0,12},{4,8},{8,4},{12,0},{1,13},{5,9},{9,5},{13,1},{2,14},{6,10},... | collective-permute-start | bytes 98312 | tf_op jit(solution)/shard_map/ppermute | solution.py:248
  16.8 1.0 %collective-permute-start.3 = (bf16[8,2048]{1,0:T(8,128)(2,1)S(1)}, bf16[8,2048]{1,0:T(8,128)(2,1)S(1)}, u32[]{:S(2)}, u32[]{:S(2)}) collective-permute-start(bf16[8,2048]{1,0:T(8,128)(2,1)S(1)} %attention.1.refs_0_), channel_id=1, source_target_pairs={{0,8},{4,12},{8,0},{12,4},{1,9},{5,13},{9,1},{13,5},{2,10},{6,14},... | collective-permute-start | bytes 98312 | tf_op jit(solution)/shard_map/ppermute | solution.py:248
  17.8 0.0 collective-permute-done.8.refs_1_
  17.8 0.0 slice-done
  17.8 0.0 slice-done.1
  17.8 1.2 %project_out.7 = bf16[16,2048]{1,0:T(8,128)(2,1)S(1)} custom-call(bf16[2048,4096]{1,0:T(8,128)(2,1)S(1)} %bitcast.2, bf16[8,2048]{1,0:T(8,128)(2,1)S(1)} %attention.1.refs_0_, bf16[8,2048]{1,0:T(8,128)(2,1)S(1)} %collective-permute-done.8.refs_1_), custom_call_target="tpu_custom_call" | custom-call | flops 134217728 | bytes 8388608 | tf_op jit(solution)/shard_map/project_out/pallas_call | solution.py:340
  19.0 1.7 %collective-permute-start.9 = (bf16[16,2048]{1,0:T(8,128)(2,1)S(1)}, bf16[16,2048]{1,0:T(8,128)(2,1)S(1)}, u32[]{:S(2)}, u32[]{:S(2)}) collective-permute-start(bf16[16,2048]{1,0:T(8,128)(2,1)S(1)} %project_out.7), channel_id=1, source_target_pairs={{0,1},{1,0},{2,3},{3,2},{4,5},{5,4},{6,7},{7,6},{8,9},{9,8},{10,11... | collective-permute-start | bytes 196616 | tf_op jit(solution)/shard_map/ppermute | solution.py:248
  20.7 0.0 collective-permute-done.4.refs_1_.refs_2_
  20.7 0.0 collective-permute-done.3.refs_0_.refs_1_
  20.7 1.2 %project_out.4 = bf16[16,2048]{1,0:T(8,128)(2,1)S(1)} custom-call(bf16[2048,4096]{1,0:T(8,128)(2,1)S(1)} %bitcast.2, bf16[8,2048]{1,0:T(8,128)(2,1)S(1)} %collective-permute-done.3.refs_0_.refs_1_, bf16[8,2048]{1,0:T(8,128)(2,1)S(1)} %collective-permute-done.4.refs_1_.refs_2_), custom_call_target="tpu_custom_call" | custom-call | flops 134217728 | bytes 8388608 | tf_op jit(solution)/shard_map/project_out/pallas_call | solution.py:340
  21.9 1.6 %collective-permute-start.5 = (bf16[16,2048]{1,0:T(8,128)(2,1)S(1)}, bf16[16,2048]{1,0:T(8,128)(2,1)S(1)}, u32[]{:S(2)}, u32[]{:S(2)}) collective-permute-start(bf16[16,2048]{1,0:T(8,128)(2,1)S(1)} %project_out.4), channel_id=1, source_target_pairs={{0,1},{1,0},{2,3},{3,2},{4,5},{5,4},{6,7},{7,6},{8,9},{9,8},{10,11... | collective-permute-start | bytes 196616 | tf_op jit(solution)/shard_map/ppermute | solution.py:248
  23.5 1.2 %project_out.6.own = f32[16,2048]{1,0:T(8,128)S(1)} custom-call(bf16[2048,4096]{1,0:T(8,128)(2,1)S(1)} %bitcast.2, bf16[8,2048]{1,0:T(8,128)(2,1)S(1)} %attention.1.refs_0_, bf16[8,2048]{1,0:T(8,128)(2,1)S(1)} %collective-permute-done.8.refs_1_), custom_call_target="tpu_custom_call" | custom-call | flops 134217728 | bytes 8388608 | tf_op jit(solution)/shard_map/project_out/pallas_call | solution.py:340
  24.7 0.0 collective-permute-done.9.arrived
  24.8 0.0 copy-start.2
  24.8 2.7 %collective-permute-start.10 = (bf16[16,2048]{1,0:T(8,128)(2,1)S(1)}, bf16[16,2048]{1,0:T(8,128)(2,1)S(1)}, u32[]{:S(2)}, u32[]{:S(2)}) collective-permute-start(bf16[16,2048]{1,0:T(8,128)(2,1)S(1)} %add_near.1.refs_0_), channel_id=1, source_target_pairs={{0,2},{1,3},{2,0},{3,1},{4,6},{5,7},{6,4},{7,5},{8,10},{9,11},{10,... | collective-permute-start | bytes 196616 | tf_op jit(solution)/shard_map/ppermute | solution.py:248
  27.4 0.0 collective-permute-done.5.refs_0_
  27.4 1.2 %project_out.5.refs_0_ = bf16[16,2048]{1,0:T(8,128)(2,1)S(1)} custom-call(bf16[2048,4096]{1,0:T(8,128)(2,1)S(1)} %bitcast.2, bf16[16,2048]{1,0:T(8,128)(2,1)S(1)} %collective-permute-done.5.refs_0_, bf16[8,2048]{1,0:T(8,128)(2,1)S(1)} %collective-permute-done.3.refs_0_.refs_1_, bf16[8,2048]{1,0:T(8,128)(2,1)S(1)} %collective-permute-done.4.refs_1_.refs_2_), custom_call_target="tpu_custom_call" | custom-call | flops 134217728 | bytes 8388608 | tf_op jit(solution)/shard_map/project_out/pallas_call | solution.py:340
  28.6 2.0 %collective-permute-start.6 = (bf16[16,2048]{1,0:T(8,128)(2,1)S(1)}, bf16[16,2048]{1,0:T(8,128)(2,1)S(1)}, u32[]{:S(2)}, u32[]{:S(2)}) collective-permute-start(bf16[16,2048]{1,0:T(8,128)(2,1)S(1)} %project_out.5.refs_0_), channel_id=1, source_target_pairs={{0,2},{1,3},{2,0},{3,1},{4,6},{5,7},{6,4},{7,5},{8,10},{9,11},{10,... | collective-permute-start | bytes 196616 | tf_op jit(solution)/shard_map/ppermute | solution.py:248
  30.6 0.0 collective-permute-done.10.refs_1_
  30.6 0.1 finish.3.refs_2_
  30.7 1.0 %collective-permute-start.11 = (bf16[16,2048]{1,0:T(8,128)(2,1)S(1)}, bf16[16,2048]{1,0:T(8,128)(2,1)S(1)}, u32[]{:S(2)}, u32[]{:S(2)}) collective-permute-start(bf16[16,2048]{1,0:T(8,128)(2,1)S(1)} %finish.3.refs_2_), channel_id=1, source_target_pairs={{0,1},{1,0},{2,3},{3,2},{4,5},{5,4},{6,7},{7,6},{8,9},{9,8},{10,11... | collective-permute-start | bytes 196616 | tf_op jit(solution)/shard_map/ppermute | solution.py:248
  31.7 2.7 %collective-permute-done.6.refs_1_ = bf16[16,2048]{1,0:T(8,128)(2,1)S(1)} collective-permute-done((bf16[16,2048]{1,0:T(8,128)(2,1)S(1)}, bf16[16,2048]{1,0:T(8,128)(2,1)S(1)}, u32[]{:S(2)}, u32[]{:S(2)}) %collective-permute-start.6) | collective-permute-done | bytes 65568 | tf_op jit(solution)/shard_map/ppermute | solution.py:248
  34.4 0.1 finish.2.refs_0_
  34.5 0.3 collective-permute-start.7
  34.7 0.9 %collective-permute-done.11.refs_3_ = bf16[16,2048]{1,0:T(8,128)(2,1)S(1)} collective-permute-done((bf16[16,2048]{1,0:T(8,128)(2,1)S(1)}, bf16[16,2048]{1,0:T(8,128)(2,1)S(1)}, u32[]{:S(2)}, u32[]{:S(2)}) %collective-permute-start.11) | collective-permute-done | bytes 65568 | tf_op jit(solution)/shard_map/ppermute | solution.py:248
  35.6 3.2 %collective-permute-done.7.refs_1_ = bf16[16,2048]{1,0:T(8,128)(2,1)S(1)} collective-permute-done((bf16[16,2048]{1,0:T(8,128)(2,1)S(1)}, bf16[16,2048]{1,0:T(8,128)(2,1)S(1)}, u32[]{:S(2)}, u32[]{:S(2)}) %collective-permute-start.7) | collective-permute-done | bytes 65568 | tf_op jit(solution)/shard_map/ppermute | solution.py:248
  38.8 0.7 %assemble.1 = bf16[32,4096]{1,0:T(8,128)(2,1)} custom-call(bf16[16,2048]{1,0:T(8,128)(2,1)S(1)} %finish.2.refs_0_, bf16[16,2048]{1,0:T(8,128)(2,1)S(1)} %collective-permute-done.7.refs_1_, bf16[16,2048]{1,0:T(8,128)(2,1)S(1)} %finish.3.refs_2_, bf16[16,2048]{1,0:T(8,128)(2,1)S(1)} %collective-permute-done.11.refs_3_), custom_call_target="tpu_custom_call" | custom-call | tf_op jit(solution)/shard_map/assemble/pallas_call | solution.py:377
  (16 shorter events, 0.1 us)
Async XLA Ops:
  6.9 3.4 %copy-start.3 = (s32[8]{0:T(128)S(1)}, s32[8]{0:T(128)}, u32[]{:S(2)}) copy-start(s32[8]{0:T(128)} %param.17) | copy-start | bytes 100
  6.9 3.6 %copy-start = (bf16[8,2048,128]{2,1,0:T(8,128)(2,1)S(1)}, bf16[8,2048,128]{2,1,0:T(8,128)(2,1)}, u32[]{:S(2)}) copy-start(bf16[8,2048,128]{2,1,0:T(8,128)(2,1)} %v.3) | copy-start | bytes 12582916
  7.0 3.6 %copy-start.1 = (bf16[8,2048,128]{2,1,0:T(8,128)(2,1)S(1)}, bf16[8,2048,128]{2,1,0:T(8,128)(2,1)}, u32[]{:S(2)}) copy-start(bf16[8,2048,128]{2,1,0:T(8,128)(2,1)} %k.1) | copy-start | bytes 12582916
  7.0 4.7 %collective-permute-start.2 = (f16[8,2432]{1,0:T(8,128)(2,1)S(1)}, f16[8,2432]{1,0:T(8,128)(2,1)S(1)}, u32[]{:S(2)}, u32[]{:S(2)}) collective-permute-start(f16[8,2432]{1,0:T(8,128)(2,1)S(1)} %convert_element_type.26), channel_id=1, source_target_pairs={{0,12},{4,8},{8,4},{12,0},{1,13},{5,9},{9,5},{13,1},{2,14},{6,10},... | collective-permute-start | bytes 116744 | tf_op jit(solution)/shard_map/ppermute | solution.py:248
  9.5 4.2 %collective-permute-start.1 = (f16[8,2432]{1,0:T(8,128)(2,1)S(1)}, f16[8,2432]{1,0:T(8,128)(2,1)S(1)}, u32[]{:S(2)}, u32[]{:S(2)}) collective-permute-start(f16[8,2432]{1,0:T(8,128)(2,1)S(1)} %convert_element_type.24), channel_id=1, source_target_pairs={{0,8},{4,12},{8,0},{12,4},{1,9},{5,13},{9,1},{13,5},{2,10},{6,14},... | collective-permute-start | bytes 116744 | tf_op jit(solution)/shard_map/ppermute | solution.py:248
  10.1 3.5 %collective-permute-start = (f16[8,2432]{1,0:T(8,128)(2,1)S(1)}, f16[8,2432]{1,0:T(8,128)(2,1)S(1)}, u32[]{:S(2)}, u32[]{:S(2)}) collective-permute-start(f16[8,2432]{1,0:T(8,128)(2,1)S(1)} %convert_element_type.22), channel_id=1, source_target_pairs={{0,4},{4,0},{8,12},{12,8},{1,5},{5,1},{9,13},{13,9},{2,6},{6,2},{1... | collective-permute-start | bytes 116744 | tf_op jit(solution)/shard_map/ppermute | solution.py:248
  10.5 7.3 %slice-start = ((s8[16777216]{0:T(1024)(128)(4,1)}), s8[4194304]{0:T(1024)(128)(4,1)S(1)}, s32[]{:S(2)}) async-start(s8[16777216]{0:T(1024)(128)(4,1)} %bitcast.1), calls=%async_computation | async-start | bytes 8388608
  10.5 7.3 %slice-start.1 = ((s8[16777216]{0:T(1024)(128)(4,1)}), s8[4194304]{0:T(1024)(128)(4,1)S(1)}, s32[]{:S(2)}) async-start(s8[16777216]{0:T(1024)(128)(4,1)} %bitcast.1), calls=%async_computation.1 | async-start | bytes 8388608
  13.7 4.1 %slice-start.2 = ((s8[16777216]{0:T(1024)(128)(4,1)}), s8[4194304]{0:T(1024)(128)(4,1)S(1)}, s32[]{:S(2)}) async-start(s8[16777216]{0:T(1024)(128)(4,1)} %bitcast.1), calls=%async_computation.2 | async-start | bytes 8388608
  13.8 4.1 %slice-start.3 = ((s8[16777216]{0:T(1024)(128)(4,1)}), s8[4194304]{0:T(1024)(128)(4,1)S(1)}, s32[]{:S(2)}) async-start(s8[16777216]{0:T(1024)(128)(4,1)} %bitcast.1), calls=%async_computation.3 | async-start | bytes 8388608
  15.6 2.2 %collective-permute-start.8 = (bf16[8,2048]{1,0:T(8,128)(2,1)S(1)}, bf16[8,2048]{1,0:T(8,128)(2,1)S(1)}, u32[]{:S(2)}, u32[]{:S(2)}) collective-permute-start(bf16[8,2048]{1,0:T(8,128)(2,1)S(1)} %attention.1.refs_0_), channel_id=1, source_target_pairs={{0,4},{4,0},{8,12},{12,8},{1,5},{5,1},{9,13},{13,9},{2,6},{6,2},{1... | collective-permute-start | bytes 98312 | tf_op jit(solution)/shard_map/ppermute | solution.py:248
  15.7 5.0 %collective-permute-start.4 = (bf16[8,2048]{1,0:T(8,128)(2,1)S(1)}, bf16[8,2048]{1,0:T(8,128)(2,1)S(1)}, u32[]{:S(2)}, u32[]{:S(2)}) collective-permute-start(bf16[8,2048]{1,0:T(8,128)(2,1)S(1)} %attention.1.refs_0_), channel_id=1, source_target_pairs={{0,12},{4,8},{8,4},{12,0},{1,13},{5,9},{9,5},{13,1},{2,14},{6,10},... | collective-permute-start | bytes 98312 | tf_op jit(solution)/shard_map/ppermute | solution.py:248
  16.8 3.9 %collective-permute-start.3 = (bf16[8,2048]{1,0:T(8,128)(2,1)S(1)}, bf16[8,2048]{1,0:T(8,128)(2,1)S(1)}, u32[]{:S(2)}, u32[]{:S(2)}) collective-permute-start(bf16[8,2048]{1,0:T(8,128)(2,1)S(1)} %attention.1.refs_0_), channel_id=1, source_target_pairs={{0,8},{4,12},{8,0},{12,4},{1,9},{5,13},{9,1},{13,5},{2,10},{6,14},... | collective-permute-start | bytes 98312 | tf_op jit(solution)/shard_map/ppermute | solution.py:248
  19.0 5.7 %collective-permute-start.9 = (bf16[16,2048]{1,0:T(8,128)(2,1)S(1)}, bf16[16,2048]{1,0:T(8,128)(2,1)S(1)}, u32[]{:S(2)}, u32[]{:S(2)}) collective-permute-start(bf16[16,2048]{1,0:T(8,128)(2,1)S(1)} %project_out.7), channel_id=1, source_target_pairs={{0,1},{1,0},{2,3},{3,2},{4,5},{5,4},{6,7},{7,6},{8,9},{9,8},{10,11... | collective-permute-start | bytes 196616 | tf_op jit(solution)/shard_map/ppermute | solution.py:248
  21.9 5.5 %collective-permute-start.5 = (bf16[16,2048]{1,0:T(8,128)(2,1)S(1)}, bf16[16,2048]{1,0:T(8,128)(2,1)S(1)}, u32[]{:S(2)}, u32[]{:S(2)}) collective-permute-start(bf16[16,2048]{1,0:T(8,128)(2,1)S(1)} %project_out.4), channel_id=1, source_target_pairs={{0,1},{1,0},{2,3},{3,2},{4,5},{5,4},{6,7},{7,6},{8,9},{9,8},{10,11... | collective-permute-start | bytes 196616 | tf_op jit(solution)/shard_map/ppermute | solution.py:248
  24.8 5.9 %copy-start.2 = (bf16[32,4096]{1,0:T(8,128)(2,1)S(1)}, bf16[32,4096]{1,0:T(8,128)(2,1)}, u32[]{:S(2)}) copy-start(bf16[32,4096]{1,0:T(8,128)(2,1)} %x.3) | copy-start | bytes 786436
  24.8 5.9 %collective-permute-start.10 = (bf16[16,2048]{1,0:T(8,128)(2,1)S(1)}, bf16[16,2048]{1,0:T(8,128)(2,1)S(1)}, u32[]{:S(2)}, u32[]{:S(2)}) collective-permute-start(bf16[16,2048]{1,0:T(8,128)(2,1)S(1)} %add_near.1.refs_0_), channel_id=1, source_target_pairs={{0,2},{1,3},{2,0},{3,1},{4,6},{5,7},{6,4},{7,5},{8,10},{9,11},{10,... | collective-permute-start | bytes 196616 | tf_op jit(solution)/shard_map/ppermute | solution.py:248
  28.6 5.8 %collective-permute-start.6 = (bf16[16,2048]{1,0:T(8,128)(2,1)S(1)}, bf16[16,2048]{1,0:T(8,128)(2,1)S(1)}, u32[]{:S(2)}, u32[]{:S(2)}) collective-permute-start(bf16[16,2048]{1,0:T(8,128)(2,1)S(1)} %project_out.5.refs_0_), channel_id=1, source_target_pairs={{0,2},{1,3},{2,0},{3,1},{4,6},{5,7},{6,4},{7,5},{8,10},{9,11},{10,... | collective-permute-start | bytes 196616 | tf_op jit(solution)/shard_map/ppermute | solution.py:248
  30.7 4.9 %collective-permute-start.11 = (bf16[16,2048]{1,0:T(8,128)(2,1)S(1)}, bf16[16,2048]{1,0:T(8,128)(2,1)S(1)}, u32[]{:S(2)}, u32[]{:S(2)}) collective-permute-start(bf16[16,2048]{1,0:T(8,128)(2,1)S(1)} %finish.3.refs_2_), channel_id=1, source_target_pairs={{0,1},{1,0},{2,3},{3,2},{4,5},{5,4},{6,7},{7,6},{8,9},{9,8},{10,11... | collective-permute-start | bytes 196616 | tf_op jit(solution)/shard_map/ppermute | solution.py:248
  34.5 4.3 %collective-permute-start.7 = (bf16[16,2048]{1,0:T(8,128)(2,1)S(1)}, bf16[16,2048]{1,0:T(8,128)(2,1)S(1)}, u32[]{:S(2)}, u32[]{:S(2)}) collective-permute-start(bf16[16,2048]{1,0:T(8,128)(2,1)S(1)} %finish.2.refs_0_), channel_id=1, source_target_pairs={{0,1},{1,0},{2,3},{3,2},{4,5},{5,4},{6,7},{7,6},{8,9},{9,8},{10,11... | collective-permute-start | bytes 196616 | tf_op jit(solution)/shard_map/ppermute | solution.py:248

commit v17 on v16

--- a/solution.py
+++ b/solution.py
@@ -195,8 +195,8 @@
     return columns((lax.axis_index("gy") ^ given) & 1, width)
 
 
-def project_out(given, arrivals, w, *refs):
-    arrived, blocks = refs[:arrivals], refs[arrivals:-2]
+def project_out(given, w, *refs):
+    blocks = refs[:-2]
     out, gathered = refs[-2:]
     rows = blocks[0].shape[0]
     core = lax.axis_index("gx") & 1
@@ -206,8 +206,6 @@
     heads = gathered[...].astype(BF16)
     width = out.shape[1]
     total = jnp.dot(heads, w[:, half_of(given, width)], preferred_element_type=F32)
-    for item in arrived:
-        total = total + item[...].astype(F32)
     out[...] = total.astype(out.dtype)
 
 
@@ -334,35 +332,33 @@
         block = w_output.shape[1] // 2
         chunks = [list(range(1, size_x // 2)), [0]]
 
-        def product(chunk, given, kind, *arrived):
+        def product(chunk, given, kind):
             pieces = gathered[2:] if chunk == 0 else gathered[:2]
             tall = rows * len(pieces)
             return pl.pallas_call(
-                functools.partial(project_out, given, len(arrived)),
+                functools.partial(project_out, given),
                 out_shape=pltpu.VMEM((tall, block), kind),
-                in_specs=[VMEM] * (1 + len(arrived) + len(pieces)),
+                in_specs=[VMEM] * (1 + len(pieces)),
                 out_specs=VMEM,
                 scratch_shapes=[pltpu.VMEM((tall, width), F32)],
                 compiler_params=params(8),
                 cost_estimate=cost(2 * tall * width * block, 2 * width * block),
                 name="project_out",
-            )(in_vmem(w_output), *[in_vmem(a) for a in arrived], *pieces)
+            )(in_vmem(w_output), *pieces)
 
         near = [swap(product(chunk, 1, BF16), "gy", size_y, 1) for chunk in range(2)]
         blocks = []
         for chunk, distances in enumerate(chunks):
             tall = 2 * rows * len(distances)
-            if chunk == 0:
-                pair = product(chunk, 0, BF16, near[chunk])
-            else:
-                pair = pl.pallas_call(
-                    add_near,
-                    out_shape=pltpu.VMEM((tall, block), BF16),
-                    in_specs=[VMEM] * 2,
-                    out_specs=VMEM,
-                    compiler_params=params(4),
-                    name="add_near",
-                )(in_vmem(product(chunk, 0, F32)), in_vmem(near[chunk]))
+            own = product(chunk, 0, F32)
+            pair = pl.pallas_call(
+                add_near,
+                out_shape=pltpu.VMEM((tall, block), BF16),
+                in_specs=[VMEM] * 2,
+                out_specs=VMEM,
+                compiler_params=params(4),
+                name="add_near",
+            )(in_vmem(own), in_vmem(near[chunk]))
             far = [pair] + [swap(pair, "gy", size_y, 2 * m) for m in range(1, half)]
             done = pl.pallas_call(
                 functools.partial(finish, distances, rows),

time: 39.7 us -> 39.8 us (level)
  waiting for transfers between devices: 8.73 us -> 10.2 us
  starting transfers between devices: 14.7 us -> 13.4 us
    ppermute x12, waiting for transfers between devices: 8.73 us -> 10.2 us  [swap(): return lax.ppermute(value, axis, [(i, i ^ mask) for i in range(size)])]
    ppermute x12, starting transfers between devices: 14.7 us -> 13.4 us  [swap(): return lax.ppermute(value, axis, [(i, i ^ mask) for i in range(size)])]
  transfers between devices with their start and end apart: 12 -> 12, of which waited for: 4 -> 5; matrix products, arithmetic and copies ran while one was open for 1% -> 1% of each run, Pallas kernels for 15% -> 15%
where the time goes in v17:
time: 39.8 us; the launch traced here: 39.7 us
  Pallas kernels  15.6 us (39%)
  starting transfers between devices  13.4 us (34%)
  waiting for transfers between devices  10.2 us (26%)
    ppermute x12, starting transfers between devices, swap(): return lax.ppermute(value, axis, [(i, i ^ mask) for i in range(size)])  13.4 us
    ppermute x12, waiting for transfers between devices, swap(): return lax.ppermute(value, axis, [(i, i ^ mask) for i in range(size)])  10.2 us
    pallas_call x1, Pallas kernels, shards(): pl.pallas_call(project, out_shape=pltpu.VMEM((batch, packed), F32), in_sp...  6.92 us
    pallas_call x4, Pallas kernels, product(): pl.pallas_call(functools.partial(project_out, given), out_shape=pltpu.VME...  4.78 us
    pallas_call x1, Pallas kernels, shards(): pl.pallas_call(functools.partial(attention, size_x, depth * size_x), out_...  1.82 us
    pallas_call x1, Pallas kernels, shards(): pl.pallas_call(turn_keys, out_shape=pltpu.VMEM((rows, HD, key_cache.shape...  1.13 us
  transfers between devices with their start and end apart: 12, of which 5 were waited for; matrix products, arithmetic and copies ran while one was open for 1% of the time, Pallas kernels for 15%

profile of v17, /device:TPU:0, one launch (start us, length us, event | category | flops | bytes accessed | tf_op | source)
XLA Modules:
  0.0 39.7 jit_solution(12655344853775983408)
XLA Ops:
  0.0 6.9 %project.1.total = f32[32,2432]{1,0:T(8,128)S(1)} custom-call(bf16[32,4096]{1,0:T(8,128)(2,1)} %x.3, f32[1,4096]{1,0:T(1,128)} %bitcast.3, bf16[4096,2048]{1,0:T(8,128)(2,1)} %weights.3, bf16[4096,128]{1,0:T(8,128)(2,1)} %wk_hbm.1, bf16[4096,128]{1,0:T(8,128)(2,1)} %wv_hbm.1), custom_call_target="tpu_custom_call" | custom-call | flops 637534208 | bytes 19922944 | tf_op jit(solution)/shard_map/project/pallas_call | solution.py:260
  6.9 0.0 copy-start.3
  6.9 0.0 copy-start
  7.0 0.0 copy-start.1
  7.0 2.4 %collective-permute-start.2 = (f16[8,2432]{1,0:T(8,128)(2,1)S(1)}, f16[8,2432]{1,0:T(8,128)(2,1)S(1)}, u32[]{:S(2)}, u32[]{:S(2)}) collective-permute-start(f16[8,2432]{1,0:T(8,128)(2,1)S(1)} %convert_element_type.26), channel_id=1, source_target_pairs={{0,12},{4,8},{8,4},{12,0},{1,13},{5,9},{9,5},{13,1},{2,14},{6,10},... | collective-permute-start | bytes 116744 | tf_op jit(solution)/shard_map/ppermute | solution.py:246
  9.5 0.6 %collective-permute-start.1 = (f16[8,2432]{1,0:T(8,128)(2,1)S(1)}, f16[8,2432]{1,0:T(8,128)(2,1)S(1)}, u32[]{:S(2)}, u32[]{:S(2)}) collective-permute-start(f16[8,2432]{1,0:T(8,128)(2,1)S(1)} %convert_element_type.24), channel_id=1, source_target_pairs={{0,8},{4,12},{8,0},{12,4},{1,9},{5,13},{9,1},{13,5},{2,10},{6,14},... | collective-permute-start | bytes 116744 | tf_op jit(solution)/shard_map/ppermute | solution.py:246
  10.1 0.2 collective-permute-start
  10.3 0.0 copy-done.3
  10.3 0.1 fusion
  10.4 0.1 pad_maximum_fusion
  10.5 0.0 copy-done
  10.5 0.0 copy-done.1
  10.5 0.0 slice-start
  10.5 0.0 slice-start.1
  10.5 1.1 %turn_keys.1.k = bf16[8,128,2048]{2,1,0:T(8,128)(2,1)S(1)} custom-call(f32[8,2432]{1,0:T(8,128)S(1)} %get-tuple-element.9.after.refs_0_, bf16[8,2048,128]{2,1,0:T(8,128)(2,1)S(1)} %copy-done.1, bf16[8,2048,128]{2,1,0:T(8,128)(2,1)S(1)} %copy-done), custom_call_target="tpu_custom_call" | custom-call | bytes 4194304 | tf_op jit(solution)/shard_map/turn_keys/pallas_call | solution.py:291
  11.7 0.0 collective-permute-done.2
  11.7 1.9 %collective-permute-done.1 = f16[8,2432]{1,0:T(8,128)(2,1)S(1)} collective-permute-done((f16[8,2432]{1,0:T(8,128)(2,1)S(1)}, f16[8,2432]{1,0:T(8,128)(2,1)S(1)}, u32[]{:S(2)}, u32[]{:S(2)}) %collective-permute-start.1) | collective-permute-done | bytes 38944 | tf_op jit(solution)/shard_map/ppermute | solution.py:246
  13.7 0.0 collective-permute-done
  13.7 0.1 broadcast_in_dim.2.lengths
  13.8 1.8 %attention.1.refs_0_ = bf16[8,2048]{1,0:T(8,128)(2,1)S(1)} custom-call(bf16[4096,2048]{1,0:T(8,128)(2,1)} %weights.3, s32[8,128]{1,0:T(8,128)S(1)} %broadcast_in_dim.2.lengths, f32[8,128]{1,0:T(8,128)S(1)} %get-tuple-element.16.cosine, f32[8,128]{1,0:T(8,128)S(1)} %get-tuple-element.17.sine, bf16[8,128,2048]{2,1,0:T(8,128)(2,1)S(1)} %turn_keys.1.k, ...), custom_call_target="tpu_custom_call" | custom-call | flops 134217728 | bytes 8388608 | tf_op jit(solution)/shard_map/attention/pallas_call | solution.py:306
  15.6 0.1 collective-permute-start.8
  15.7 1.2 %collective-permute-start.4 = (bf16[8,2048]{1,0:T(8,128)(2,1)S(1)}, bf16[8,2048]{1,0:T(8,128)(2,1)S(1)}, u32[]{:S(2)}, u32[]{:S(2)}) collective-permute-start(bf16[8,2048]{1,0:T(8,128)(2,1)S(1)} %attention.1.refs_0_), channel_id=1, source_target_pairs={{0,12},{4,8},{8,4},{12,0},{1,13},{5,9},{9,5},{13,1},{2,14},{6,10},... | collective-permute-start | bytes 98312 | tf_op jit(solution)/shard_map/ppermute | solution.py:246
  16.8 1.0 %collective-permute-start.3 = (bf16[8,2048]{1,0:T(8,128)(2,1)S(1)}, bf16[8,2048]{1,0:T(8,128)(2,1)S(1)}, u32[]{:S(2)}, u32[]{:S(2)}) collective-permute-start(bf16[8,2048]{1,0:T(8,128)(2,1)S(1)} %attention.1.refs_0_), channel_id=1, source_target_pairs={{0,8},{4,12},{8,0},{12,4},{1,9},{5,13},{9,1},{13,5},{2,10},{6,14},... | collective-permute-start | bytes 98312 | tf_op jit(solution)/shard_map/ppermute | solution.py:246
  17.8 0.0 collective-permute-done.8.refs_1_
  17.8 0.0 slice-done
  17.8 0.0 slice-done.2
  17.8 0.0 slice-done.3
  17.8 1.2 %project_out.7 = bf16[16,2048]{1,0:T(8,128)(2,1)S(1)} custom-call(bf16[2048,4096]{1,0:T(8,128)(2,1)S(1)} %bitcast.2, bf16[8,2048]{1,0:T(8,128)(2,1)S(1)} %attention.1.refs_0_, bf16[8,2048]{1,0:T(8,128)(2,1)S(1)} %collective-permute-done.8.refs_1_), custom_call_target="tpu_custom_call" | custom-call | flops 134217728 | bytes 8388608 | tf_op jit(solution)/shard_map/project_out/pallas_call | solution.py:338
  19.0 1.7 %collective-permute-start.9 = (bf16[16,2048]{1,0:T(8,128)(2,1)S(1)}, bf16[16,2048]{1,0:T(8,128)(2,1)S(1)}, u32[]{:S(2)}, u32[]{:S(2)}) collective-permute-start(bf16[16,2048]{1,0:T(8,128)(2,1)S(1)} %project_out.7), channel_id=1, source_target_pairs={{0,1},{1,0},{2,3},{3,2},{4,5},{5,4},{6,7},{7,6},{8,9},{9,8},{10,11... | collective-permute-start | bytes 196616 | tf_op jit(solution)/shard_map/ppermute | solution.py:246
  20.7 0.0 collective-permute-done.4.refs_1_
  20.7 0.0 collective-permute-done.3.refs_0_
  20.7 1.2 %project_out.5 = bf16[16,2048]{1,0:T(8,128)(2,1)S(1)} custom-call(bf16[2048,4096]{1,0:T(8,128)(2,1)S(1)} %bitcast.2, bf16[8,2048]{1,0:T(8,128)(2,1)S(1)} %collective-permute-done.3.refs_0_, bf16[8,2048]{1,0:T(8,128)(2,1)S(1)} %collective-permute-done.4.refs_1_), custom_call_target="tpu_custom_call" | custom-call | flops 134217728 | bytes 8388608 | tf_op jit(solution)/shard_map/project_out/pallas_call | solution.py:338
  21.9 1.6 %collective-permute-start.5 = (bf16[16,2048]{1,0:T(8,128)(2,1)S(1)}, bf16[16,2048]{1,0:T(8,128)(2,1)S(1)}, u32[]{:S(2)}, u32[]{:S(2)}) collective-permute-start(bf16[16,2048]{1,0:T(8,128)(2,1)S(1)} %project_out.5), channel_id=1, source_target_pairs={{0,1},{1,0},{2,3},{3,2},{4,5},{5,4},{6,7},{7,6},{8,9},{9,8},{10,11... | collective-permute-start | bytes 196616 | tf_op jit(solution)/shard_map/ppermute | solution.py:246
  23.5 1.2 %project_out.4.own = f32[16,2048]{1,0:T(8,128)S(1)} custom-call(bf16[2048,4096]{1,0:T(8,128)(2,1)S(1)} %bitcast.2, bf16[8,2048]{1,0:T(8,128)(2,1)S(1)} %collective-permute-done.3.refs_0_, bf16[8,2048]{1,0:T(8,128)(2,1)S(1)} %collective-permute-done.4.refs_1_), custom_call_target="tpu_custom_call" | custom-call | flops 134217728 | bytes 8388608 | tf_op jit(solution)/shard_map/project_out/pallas_call | solution.py:338
  24.7 1.2 %project_out.6.own = f32[16,2048]{1,0:T(8,128)S(1)} custom-call(bf16[2048,4096]{1,0:T(8,128)(2,1)S(1)} %bitcast.2, bf16[8,2048]{1,0:T(8,128)(2,1)S(1)} %attention.1.refs_0_, bf16[8,2048]{1,0:T(8,128)(2,1)S(1)} %collective-permute-done.8.refs_1_), custom_call_target="tpu_custom_call" | custom-call | flops 134217728 | bytes 8388608 | tf_op jit(solution)/shard_map/project_out/pallas_call | solution.py:338
  25.9 0.0 collective-permute-done.9.arrived
  26.0 2.7 %collective-permute-start.10 = (bf16[16,2048]{1,0:T(8,128)(2,1)S(1)}, bf16[16,2048]{1,0:T(8,128)(2,1)S(1)}, u32[]{:S(2)}, u32[]{:S(2)}) collective-permute-start(bf16[16,2048]{1,0:T(8,128)(2,1)S(1)} %add_near.3.refs_0_), channel_id=1, source_target_pairs={{0,2},{1,3},{2,0},{3,1},{4,6},{5,7},{6,4},{7,5},{8,10},{9,11},{10,... | collective-permute-start | bytes 196616 | tf_op jit(solution)/shard_map/ppermute | solution.py:246
  28.6 0.0 collective-permute-done.5.arrived
  28.6 0.4 %collective-permute-start.6 = (bf16[16,2048]{1,0:T(8,128)(2,1)S(1)}, bf16[16,2048]{1,0:T(8,128)(2,1)S(1)}, u32[]{:S(2)}, u32[]{:S(2)}) collective-permute-start(bf16[16,2048]{1,0:T(8,128)(2,1)S(1)} %add_near.2.refs_0_), channel_id=1, source_target_pairs={{0,2},{1,3},{2,0},{3,1},{4,6},{5,7},{6,4},{7,5},{8,10},{9,11},{10,... | collective-permute-start | bytes 196616 | tf_op jit(solution)/shard_map/ppermute | solution.py:246
  29.0 4.8 %collective-permute-done.10.refs_1_ = bf16[16,2048]{1,0:T(8,128)(2,1)S(1)} collective-permute-done((bf16[16,2048]{1,0:T(8,128)(2,1)S(1)}, bf16[16,2048]{1,0:T(8,128)(2,1)S(1)}, u32[]{:S(2)}, u32[]{:S(2)}) %collective-permute-start.10) | collective-permute-done | bytes 65568 | tf_op jit(solution)/shard_map/ppermute | solution.py:246
  33.9 0.1 finish.3.refs_2_
  33.9 0.1 collective-permute-start.11
  34.0 0.6 %collective-permute-done.6.refs_1_ = bf16[16,2048]{1,0:T(8,128)(2,1)S(1)} collective-permute-done((bf16[16,2048]{1,0:T(8,128)(2,1)S(1)}, bf16[16,2048]{1,0:T(8,128)(2,1)S(1)}, u32[]{:S(2)}, u32[]{:S(2)}) %collective-permute-start.6) | collective-permute-done | bytes 65568 | tf_op jit(solution)/shard_map/ppermute | solution.py:246
  34.6 0.1 finish.2.refs_0_
  34.6 1.5 %collective-permute-start.7 = (bf16[16,2048]{1,0:T(8,128)(2,1)S(1)}, bf16[16,2048]{1,0:T(8,128)(2,1)S(1)}, u32[]{:S(2)}, u32[]{:S(2)}) collective-permute-start(bf16[16,2048]{1,0:T(8,128)(2,1)S(1)} %finish.2.refs_0_), channel_id=1, source_target_pairs={{0,1},{1,0},{2,3},{3,2},{4,5},{5,4},{6,7},{7,6},{8,9},{9,8},{10,11... | collective-permute-start | bytes 196616 | tf_op jit(solution)/shard_map/ppermute | solution.py:246
  36.1 2.1 %collective-permute-done.11.refs_3_ = bf16[16,2048]{1,0:T(8,128)(2,1)S(1)} collective-permute-done((bf16[16,2048]{1,0:T(8,128)(2,1)S(1)}, bf16[16,2048]{1,0:T(8,128)(2,1)S(1)}, u32[]{:S(2)}, u32[]{:S(2)}) %collective-permute-start.11) | collective-permute-done | bytes 65568 | tf_op jit(solution)/shard_map/ppermute | solution.py:246
  38.3 0.7 %collective-permute-done.7.refs_1_ = bf16[16,2048]{1,0:T(8,128)(2,1)S(1)} collective-permute-done((bf16[16,2048]{1,0:T(8,128)(2,1)S(1)}, bf16[16,2048]{1,0:T(8,128)(2,1)S(1)}, u32[]{:S(2)}, u32[]{:S(2)}) %collective-permute-start.7) | collective-permute-done | bytes 65568 | tf_op jit(solution)/shard_map/ppermute | solution.py:246
  39.0 0.7 %assemble.1 = bf16[32,4096]{1,0:T(8,128)(2,1)} custom-call(bf16[16,2048]{1,0:T(8,128)(2,1)S(1)} %finish.2.refs_0_, bf16[16,2048]{1,0:T(8,128)(2,1)S(1)} %collective-permute-done.7.refs_1_, bf16[16,2048]{1,0:T(8,128)(2,1)S(1)} %finish.3.refs_2_, bf16[16,2048]{1,0:T(8,128)(2,1)S(1)} %collective-permute-done.11.refs_3_), custom_call_target="tpu_custom_call" | custom-call | tf_op jit(solution)/shard_map/assemble/pallas_call | solution.py:373
  (17 shorter events, 0.1 us)
Async XLA Ops:
  6.9 3.4 %copy-start.3 = (s32[8]{0:T(128)S(1)}, s32[8]{0:T(128)}, u32[]{:S(2)}) copy-start(s32[8]{0:T(128)} %param.17) | copy-start | bytes 100
  6.9 3.6 %copy-start = (bf16[8,2048,128]{2,1,0:T(8,128)(2,1)S(1)}, bf16[8,2048,128]{2,1,0:T(8,128)(2,1)}, u32[]{:S(2)}) copy-start(bf16[8,2048,128]{2,1,0:T(8,128)(2,1)} %v.3) | copy-start | bytes 12582916
  7.0 3.6 %copy-start.1 = (bf16[8,2048,128]{2,1,0:T(8,128)(2,1)S(1)}, bf16[8,2048,128]{2,1,0:T(8,128)(2,1)}, u32[]{:S(2)}) copy-start(bf16[8,2048,128]{2,1,0:T(8,128)(2,1)} %k.1) | copy-start | bytes 12582916
  7.0 4.7 %collective-permute-start.2 = (f16[8,2432]{1,0:T(8,128)(2,1)S(1)}, f16[8,2432]{1,0:T(8,128)(2,1)S(1)}, u32[]{:S(2)}, u32[]{:S(2)}) collective-permute-start(f16[8,2432]{1,0:T(8,128)(2,1)S(1)} %convert_element_type.26), channel_id=1, source_target_pairs={{0,12},{4,8},{8,4},{12,0},{1,13},{5,9},{9,5},{13,1},{2,14},{6,10},... | collective-permute-start | bytes 116744 | tf_op jit(solution)/shard_map/ppermute | solution.py:246
  9.5 4.2 %collective-permute-start.1 = (f16[8,2432]{1,0:T(8,128)(2,1)S(1)}, f16[8,2432]{1,0:T(8,128)(2,1)S(1)}, u32[]{:S(2)}, u32[]{:S(2)}) collective-permute-start(f16[8,2432]{1,0:T(8,128)(2,1)S(1)} %convert_element_type.24), channel_id=1, source_target_pairs={{0,8},{4,12},{8,0},{12,4},{1,9},{5,13},{9,1},{13,5},{2,10},{6,14},... | collective-permute-start | bytes 116744 | tf_op jit(solution)/shard_map/ppermute | solution.py:246
  10.1 3.5 %collective-permute-start = (f16[8,2432]{1,0:T(8,128)(2,1)S(1)}, f16[8,2432]{1,0:T(8,128)(2,1)S(1)}, u32[]{:S(2)}, u32[]{:S(2)}) collective-permute-start(f16[8,2432]{1,0:T(8,128)(2,1)S(1)} %convert_element_type.22), channel_id=1, source_target_pairs={{0,4},{4,0},{8,12},{12,8},{1,5},{5,1},{9,13},{13,9},{2,6},{6,2},{1... | collective-permute-start | bytes 116744 | tf_op jit(solution)/shard_map/ppermute | solution.py:246
  10.5 7.3 %slice-start = ((s8[16777216]{0:T(1024)(128)(4,1)}), s8[4194304]{0:T(1024)(128)(4,1)S(1)}, s32[]{:S(2)}) async-start(s8[16777216]{0:T(1024)(128)(4,1)} %bitcast.1), calls=%async_computation | async-start | bytes 8388608
  10.5 7.3 %slice-start.1 = ((s8[16777216]{0:T(1024)(128)(4,1)}), s8[4194304]{0:T(1024)(128)(4,1)S(1)}, s32[]{:S(2)}) async-start(s8[16777216]{0:T(1024)(128)(4,1)} %bitcast.1), calls=%async_computation.1 | async-start | bytes 8388608
  13.7 4.1 %slice-start.2 = ((s8[16777216]{0:T(1024)(128)(4,1)}), s8[4194304]{0:T(1024)(128)(4,1)S(1)}, s32[]{:S(2)}) async-start(s8[16777216]{0:T(1024)(128)(4,1)} %bitcast.1), calls=%async_computation.2 | async-start | bytes 8388608
  13.8 4.1 %slice-start.3 = ((s8[16777216]{0:T(1024)(128)(4,1)}), s8[4194304]{0:T(1024)(128)(4,1)S(1)}, s32[]{:S(2)}) async-start(s8[16777216]{0:T(1024)(128)(4,1)} %bitcast.1), calls=%async_computation.3 | async-start | bytes 8388608
  15.6 2.2 %collective-permute-start.8 = (bf16[8,2048]{1,0:T(8,128)(2,1)S(1)}, bf16[8,2048]{1,0:T(8,128)(2,1)S(1)}, u32[]{:S(2)}, u32[]{:S(2)}) collective-permute-start(bf16[8,2048]{1,0:T(8,128)(2,1)S(1)} %attention.1.refs_0_), channel_id=1, source_target_pairs={{0,4},{4,0},{8,12},{12,8},{1,5},{5,1},{9,13},{13,9},{2,6},{6,2},{1... | collective-permute-start | bytes 98312 | tf_op jit(solution)/shard_map/ppermute | solution.py:246
  15.7 5.0 %collective-permute-start.4 = (bf16[8,2048]{1,0:T(8,128)(2,1)S(1)}, bf16[8,2048]{1,0:T(8,128)(2,1)S(1)}, u32[]{:S(2)}, u32[]{:S(2)}) collective-permute-start(bf16[8,2048]{1,0:T(8,128)(2,1)S(1)} %attention.1.refs_0_), channel_id=1, source_target_pairs={{0,12},{4,8},{8,4},{12,0},{1,13},{5,9},{9,5},{13,1},{2,14},{6,10},... | collective-permute-start | bytes 98312 | tf_op jit(solution)/shard_map/ppermute | solution.py:246
  16.8 3.9 %collective-permute-start.3 = (bf16[8,2048]{1,0:T(8,128)(2,1)S(1)}, bf16[8,2048]{1,0:T(8,128)(2,1)S(1)}, u32[]{:S(2)}, u32[]{:S(2)}) collective-permute-start(bf16[8,2048]{1,0:T(8,128)(2,1)S(1)} %attention.1.refs_0_), channel_id=1, source_target_pairs={{0,8},{4,12},{8,0},{12,4},{1,9},{5,13},{9,1},{13,5},{2,10},{6,14},... | collective-permute-start | bytes 98312 | tf_op jit(solution)/shard_map/ppermute | solution.py:246
  19.0 6.9 %collective-permute-start.9 = (bf16[16,2048]{1,0:T(8,128)(2,1)S(1)}, bf16[16,2048]{1,0:T(8,128)(2,1)S(1)}, u32[]{:S(2)}, u32[]{:S(2)}) collective-permute-start(bf16[16,2048]{1,0:T(8,128)(2,1)S(1)} %project_out.7), channel_id=1, source_target_pairs={{0,1},{1,0},{2,3},{3,2},{4,5},{5,4},{6,7},{7,6},{8,9},{9,8},{10,11... | collective-permute-start | bytes 196616 | tf_op jit(solution)/shard_map/ppermute | solution.py:246
  21.9 6.7 %collective-permute-start.5 = (bf16[16,2048]{1,0:T(8,128)(2,1)S(1)}, bf16[16,2048]{1,0:T(8,128)(2,1)S(1)}, u32[]{:S(2)}, u32[]{:S(2)}) collective-permute-start(bf16[16,2048]{1,0:T(8,128)(2,1)S(1)} %project_out.5), channel_id=1, source_target_pairs={{0,1},{1,0},{2,3},{3,2},{4,5},{5,4},{6,7},{7,6},{8,9},{9,8},{10,11... | collective-permute-start | bytes 196616 | tf_op jit(solution)/shard_map/ppermute | solution.py:246
  24.7 9.1 %copy-start.2 = (bf16[32,4096]{1,0:T(8,128)(2,1)S(1)}, bf16[32,4096]{1,0:T(8,128)(2,1)}, u32[]{:S(2)}) copy-start(bf16[32,4096]{1,0:T(8,128)(2,1)} %x.3) | copy-start | bytes 786436
  26.0 7.9 %collective-permute-start.10 = (bf16[16,2048]{1,0:T(8,128)(2,1)S(1)}, bf16[16,2048]{1,0:T(8,128)(2,1)S(1)}, u32[]{:S(2)}, u32[]{:S(2)}) collective-permute-start(bf16[16,2048]{1,0:T(8,128)(2,1)S(1)} %add_near.3.refs_0_), channel_id=1, source_target_pairs={{0,2},{1,3},{2,0},{3,1},{4,6},{5,7},{6,4},{7,5},{8,10},{9,11},{10,... | collective-permute-start | bytes 196616 | tf_op jit(solution)/shard_map/ppermute | solution.py:246
  28.6 5.9 %collective-permute-start.6 = (bf16[16,2048]{1,0:T(8,128)(2,1)S(1)}, bf16[16,2048]{1,0:T(8,128)(2,1)S(1)}, u32[]{:S(2)}, u32[]{:S(2)}) collective-permute-start(bf16[16,2048]{1,0:T(8,128)(2,1)S(1)} %add_near.2.refs_0_), channel_id=1, source_target_pairs={{0,2},{1,3},{2,0},{3,1},{4,6},{5,7},{6,4},{7,5},{8,10},{9,11},{10,... | collective-permute-start | bytes 196616 | tf_op jit(solution)/shard_map/ppermute | solution.py:246
  33.9 4.3 %collective-permute-start.11 = (bf16[16,2048]{1,0:T(8,128)(2,1)S(1)}, bf16[16,2048]{1,0:T(8,128)(2,1)S(1)}, u32[]{:S(2)}, u32[]{:S(2)}) collective-permute-start(bf16[16,2048]{1,0:T(8,128)(2,1)S(1)} %finish.3.refs_2_), channel_id=1, source_target_pairs={{0,1},{1,0},{2,3},{3,2},{4,5},{5,4},{6,7},{7,6},{8,9},{9,8},{10,11... | collective-permute-start | bytes 196616 | tf_op jit(solution)/shard_map/ppermute | solution.py:246
  34.6 4.3 %collective-permute-start.7 = (bf16[16,2048]{1,0:T(8,128)(2,1)S(1)}, bf16[16,2048]{1,0:T(8,128)(2,1)S(1)}, u32[]{:S(2)}, u32[]{:S(2)}) collective-permute-start(bf16[16,2048]{1,0:T(8,128)(2,1)S(1)} %finish.2.refs_0_), channel_id=1, source_target_pairs={{0,1},{1,0},{2,3},{3,2},{4,5},{5,4},{6,7},{7,6},{8,9},{9,8},{10,11... | collective-permute-start | bytes 196616 | tf_op jit(solution)/shard_map/ppermute | solution.py:246

commit v18 on v13

--- a/solution.py
+++ b/solution.py
@@ -199,11 +199,16 @@
     return 2 * chunk + ((lax.axis_index("gy") ^ given) & 1)
 
 
-def project_out(size, chunk, given, w, *refs):
-    blocks, out, gathered = refs[:size], refs[-2], refs[-1]
-    heads = gather_rows(blocks, gathered)
+def project_first(w, *refs):
+    *blocks, out, heads, gathered = refs
+    heads[...] = gather_rows(blocks, gathered)
+    part = columns(place(0, 1), out.shape[1])
+    out[...] = jnp.dot(heads[...], w[:, part], preferred_element_type=F32).astype(out.dtype)
+
+
+def project_out(chunk, given, w, heads, out):
     part = columns(place(chunk, given), out.shape[1])
-    out[...] = jnp.dot(heads, w[:, part], preferred_element_type=F32).astype(out.dtype)
+    out[...] = jnp.dot(heads[...], w[:, part], preferred_element_type=F32).astype(out.dtype)
 
 
 def add_near(own, arrived, out):
@@ -222,12 +227,11 @@
     out[...] = (x[:, part].astype(F32) + total).astype(BF16)
 
 
-def assemble(*refs):
-    *blocks, out, sems = refs
-    width = blocks[0].shape[1]
+def write(places, *refs):
+    blocks, out, sems = refs[: len(places)], refs[-2], refs[-1]
     copies = []
-    for index, block in enumerate(blocks):
-        target = out.at[:, columns(place(index // 2, index % 2), width)]
+    for index, (block, (chunk, given)) in enumerate(zip(blocks, places)):
+        target = out.at[:, columns(place(chunk, given), block.shape[1])]
         copies.append(pltpu.make_async_copy(block, target, sems.at[index]))
     for copy in copies:
         copy.start()
@@ -324,19 +328,30 @@
         gathered = [in_vmem(a) for a in gathered]
         half = size_y // 2
 
+        work = cost(2 * batch * width * block, 2 * width * block)
+        first, everyone = pl.pallas_call(
+            project_first,
+            out_shape=[pltpu.VMEM((batch, block), BF16), pltpu.VMEM((batch, width), BF16)],
+            in_specs=[VMEM] * (1 + size_x),
+            out_specs=[VMEM] * 2,
+            scratch_shapes=[pltpu.VMEM((batch, width), F32)],
+            compiler_params=params(8),
+            cost_estimate=work,
+            name="project_first",
+        )(in_vmem(w_output), *gathered)
+
         def product(chunk, given):
             return pl.pallas_call(
-                functools.partial(project_out, size_x, chunk, given),
+                functools.partial(project_out, chunk, given),
                 out_shape=pltpu.VMEM((batch, block), BF16 if given else F32),
-                in_specs=[VMEM] * (1 + size_x),
+                in_specs=[VMEM] * 2,
                 out_specs=VMEM,
-                scratch_shapes=[pltpu.VMEM((batch, width), F32)],
                 compiler_params=params(8),
-                cost_estimate=cost(2 * batch * width * block, 2 * width * block),
+                cost_estimate=work,
                 name="project_out",
-            )(in_vmem(w_output), *gathered)
-
-        near = [swap(product(chunk, 1), "gy", size_y, 1) for chunk in range(2)]
+            )(in_vmem(w_output), in_vmem(everyone))
+
+        near = [swap(term, "gy", size_y, 1) for term in (first, product(1, 1))]
         blocks = []
         for chunk in range(2):
             pair = pl.pallas_call(
@@ -358,15 +373,26 @@
                 name="finish",
             )(in_vmem(inputs), *[in_vmem(a) for a in far])
             blocks += [done, swap(done, "gy", size_y, 1)]
+        shape = jax.ShapeDtypeStruct((batch, block * 4), BF16)
+        most = pl.pallas_call(
+            functools.partial(write, [(0, 0), (0, 1), (1, 0)]),
+            out_shape=shape,
+            in_specs=[VMEM] * 3,
+            out_specs=ANY,
+            scratch_shapes=[sems(3)],
+            compiler_params=params(4),
+            name="write_most",
+        )(*[in_vmem(b) for b in blocks[:3]])
         return pl.pallas_call(
-            assemble,
-            out_shape=jax.ShapeDtypeStruct((batch, block * 4), BF16),
-            in_specs=[VMEM] * 4,
+            functools.partial(write, [(1, 1)]),
+            out_shape=shape,
+            in_specs=[VMEM, ANY],
             out_specs=ANY,
-            scratch_shapes=[sems(4)],
+            scratch_shapes=[sems(1)],
+            input_output_aliases={1: 0},
             compiler_params=params(4),
-            name="assemble",
-        )(*[in_vmem(b) for b in blocks])
+            name="write_last",
+        )(in_vmem(blocks[3]), in_hbm(most))
 
     placed = (
         P("groups", "gx"),

time: 39.1 us -> 39.1 us (level)
  Pallas kernels: 14.1 us -> 14.7 us
  waiting for transfers between devices: 9.46 us -> 9.05 us
    pallas_call x5 -> x6, Pallas kernels: 4.02 us -> 4.63 us  [the longest x3 2.47 us: product(): pl.pallas_call(functools.partial(project_out, chunk, given), out_shape=pl...]
    ppermute x12, waiting for transfers between devices: 9.46 us -> 9.05 us  [swap(): return lax.ppermute(value, axis, [(i, i ^ mask) for i in range(size)])]
  transfers between devices with their start and end apart: 12 -> 12, of which waited for: 7 -> 8; matrix products, arithmetic and copies ran while one was open for 1% -> 1% of each run, Pallas kernels for 10% -> 11%
where the time goes in v18:
time: 39.1 us; the launch traced here: 38.9 us
  Pallas kernels  14.7 us (38%)
  starting transfers between devices  14.6 us (37%)
  waiting for transfers between devices  9.05 us (23%)
    ppermute x12, starting transfers between devices, swap(): return lax.ppermute(value, axis, [(i, i ^ mask) for i in range(size)])  14.6 us
    ppermute x12, waiting for transfers between devices, swap(): return lax.ppermute(value, axis, [(i, i ^ mask) for i in range(size)])  9.05 us
    pallas_call x1, Pallas kernels, shards(): pl.pallas_call(project, out_shape=pltpu.VMEM((batch, packed), F32), in_sp...  6.92 us
    pallas_call x3, Pallas kernels, product(): pl.pallas_call(functools.partial(project_out, chunk, given), out_shape=pl...  2.47 us
    pallas_call x1, Pallas kernels, shards(): pl.pallas_call(functools.partial(attention, size_x, depth * size_x), out_...  1.82 us
    pallas_call x1, Pallas kernels, shards(): pl.pallas_call(turn_keys, out_shape=pltpu.VMEM((rows, HD, key_cache.shape...  1.13 us
    pallas_call x1, Pallas kernels, shards(): pl.pallas_call(project_first, out_shape=[pltpu.VMEM((batch, block), BF16)...  0.83 us
  transfers between devices with their start and end apart: 12, of which 8 were waited for; matrix products, arithmetic and copies ran while one was open for 1% of the time, Pallas kernels for 11%

profile of v18, /device:TPU:0, one launch (start us, length us, event | category | flops | bytes accessed | tf_op | source)
XLA Modules:
  0.0 38.9 jit_solution(14427327079920487806)
XLA Ops:
  0.0 6.9 %project.1.total = f32[32,2432]{1,0:T(8,128)S(1)} custom-call(bf16[32,4096]{1,0:T(8,128)(2,1)} %x.3, f32[1,4096]{1,0:T(1,128)} %bitcast.3, bf16[4096,2048]{1,0:T(8,128)(2,1)} %weights.3, bf16[4096,128]{1,0:T(8,128)(2,1)} %wk_hbm.1, bf16[4096,128]{1,0:T(8,128)(2,1)} %wv_hbm.1), custom_call_target="tpu_custom_call" | custom-call | flops 637534208 | bytes 19922944 | tf_op jit(solution)/shard_map/project/pallas_call | solution.py:258
  6.9 0.0 copy-start.3
  6.9 0.0 copy-start
  7.0 0.0 copy-start.1
  7.0 2.4 %collective-permute-start.2 = (f16[8,2432]{1,0:T(8,128)(2,1)S(1)}, f16[8,2432]{1,0:T(8,128)(2,1)S(1)}, u32[]{:S(2)}, u32[]{:S(2)}) collective-permute-start(f16[8,2432]{1,0:T(8,128)(2,1)S(1)} %convert_element_type.26), channel_id=1, source_target_pairs={{0,12},{4,8},{8,4},{12,0},{1,13},{5,9},{9,5},{13,1},{2,14},{6,10},... | collective-permute-start | bytes 116744 | tf_op jit(solution)/shard_map/ppermute | solution.py:243
  9.5 0.6 %collective-permute-start.1 = (f16[8,2432]{1,0:T(8,128)(2,1)S(1)}, f16[8,2432]{1,0:T(8,128)(2,1)S(1)}, u32[]{:S(2)}, u32[]{:S(2)}) collective-permute-start(f16[8,2432]{1,0:T(8,128)(2,1)S(1)} %convert_element_type.24), channel_id=1, source_target_pairs={{0,8},{4,12},{8,0},{12,4},{1,9},{5,13},{9,1},{13,5},{2,10},{6,14},... | collective-permute-start | bytes 116744 | tf_op jit(solution)/shard_map/ppermute | solution.py:243
  10.1 0.2 collective-permute-start
  10.3 0.0 copy-done.3
  10.3 0.1 fusion
  10.4 0.1 pad_maximum_fusion
  10.5 0.0 copy-done
  10.5 0.0 copy-done.1
  10.5 0.0 slice-start
  10.5 0.0 slice-start.1
  10.5 1.1 %turn_keys.1.k = bf16[8,128,2048]{2,1,0:T(8,128)(2,1)S(1)} custom-call(f32[8,2432]{1,0:T(8,128)S(1)} %get-tuple-element.11.after.refs_0_, bf16[8,2048,128]{2,1,0:T(8,128)(2,1)S(1)} %copy-done.1, bf16[8,2048,128]{2,1,0:T(8,128)(2,1)S(1)} %copy-done), custom_call_target="tpu_custom_call" | custom-call | bytes 4194304 | tf_op jit(solution)/shard_map/turn_keys/pallas_call | solution.py:289
  11.7 0.0 collective-permute-done.2
  11.7 1.9 %collective-permute-done.1 = f16[8,2432]{1,0:T(8,128)(2,1)S(1)} collective-permute-done((f16[8,2432]{1,0:T(8,128)(2,1)S(1)}, f16[8,2432]{1,0:T(8,128)(2,1)S(1)}, u32[]{:S(2)}, u32[]{:S(2)}) %collective-permute-start.1) | collective-permute-done | bytes 38944 | tf_op jit(solution)/shard_map/ppermute | solution.py:243
  13.7 0.0 collective-permute-done
  13.7 0.1 broadcast_in_dim.2.lengths
  13.8 1.8 %attention.1.refs_0_ = bf16[8,2048]{1,0:T(8,128)(2,1)S(1)} custom-call(bf16[4096,2048]{1,0:T(8,128)(2,1)} %weights.3, s32[8,128]{1,0:T(8,128)S(1)} %broadcast_in_dim.2.lengths, f32[8,128]{1,0:T(8,128)S(1)} %get-tuple-element.20.cosine, f32[8,128]{1,0:T(8,128)S(1)} %get-tuple-element.21.sine, bf16[8,128,2048]{2,1,0:T(8,128)(2,1)S(1)} %turn_keys.1.k, ...), custom_call_target="tpu_custom_call" | custom-call | flops 134217728 | bytes 8388608 | tf_op jit(solution)/shard_map/attention/pallas_call | solution.py:304
  15.6 0.8 %collective-permute-start.5 = (bf16[8,2048]{1,0:T(8,128)(2,1)S(1)}, bf16[8,2048]{1,0:T(8,128)(2,1)S(1)}, u32[]{:S(2)}, u32[]{:S(2)}) collective-permute-start(bf16[8,2048]{1,0:T(8,128)(2,1)S(1)} %attention.1.refs_0_), channel_id=1, source_target_pairs={{0,12},{4,8},{8,4},{12,0},{1,13},{5,9},{9,5},{13,1},{2,14},{6,10},... | collective-permute-start | bytes 98312 | tf_op jit(solution)/shard_map/ppermute | solution.py:243
  16.4 0.7 %collective-permute-start.4 = (bf16[8,2048]{1,0:T(8,128)(2,1)S(1)}, bf16[8,2048]{1,0:T(8,128)(2,1)S(1)}, u32[]{:S(2)}, u32[]{:S(2)}) collective-permute-start(bf16[8,2048]{1,0:T(8,128)(2,1)S(1)} %attention.1.refs_0_), channel_id=1, source_target_pairs={{0,8},{4,12},{8,0},{12,4},{1,9},{5,13},{9,1},{13,5},{2,10},{6,14},... | collective-permute-start | bytes 98312 | tf_op jit(solution)/shard_map/ppermute | solution.py:243
  17.1 0.4 %collective-permute-start.3 = (bf16[8,2048]{1,0:T(8,128)(2,1)S(1)}, bf16[8,2048]{1,0:T(8,128)(2,1)S(1)}, u32[]{:S(2)}, u32[]{:S(2)}) collective-permute-start(bf16[8,2048]{1,0:T(8,128)(2,1)S(1)} %attention.1.refs_0_), channel_id=1, source_target_pairs={{0,4},{4,0},{8,12},{12,8},{1,5},{5,1},{9,13},{13,9},{2,6},{6,2},{1... | collective-permute-start | bytes 98312 | tf_op jit(solution)/shard_map/ppermute | solution.py:243
  17.5 1.8 %collective-permute-done.5.refs_3_ = bf16[8,2048]{1,0:T(8,128)(2,1)S(1)} collective-permute-done((bf16[8,2048]{1,0:T(8,128)(2,1)S(1)}, bf16[8,2048]{1,0:T(8,128)(2,1)S(1)}, u32[]{:S(2)}, u32[]{:S(2)}) %collective-permute-start.5) | collective-permute-done | bytes 32800 | tf_op jit(solution)/shard_map/ppermute | solution.py:243
  19.3 1.0 %collective-permute-done.4.refs_2_ = bf16[8,2048]{1,0:T(8,128)(2,1)S(1)} collective-permute-done((bf16[8,2048]{1,0:T(8,128)(2,1)S(1)}, bf16[8,2048]{1,0:T(8,128)(2,1)S(1)}, u32[]{:S(2)}, u32[]{:S(2)}) %collective-permute-start.4) | collective-permute-done | bytes 32800 | tf_op jit(solution)/shard_map/ppermute | solution.py:243
  20.3 0.0 collective-permute-done.3.refs_1_
  20.3 0.0 slice-done
  20.3 0.0 slice-done.1
  20.3 0.0 slice-done.2
  20.4 0.8 %project_first.1 = (bf16[32,1024]{1,0:T(8,128)(2,1)S(1)}, bf16[32,2048]{1,0:T(8,128)(2,1)S(1)}) custom-call(bf16[2048,4096]{1,0:T(8,128)(2,1)S(1)} %bitcast.2, bf16[8,2048]{1,0:T(8,128)(2,1)S(1)} %attention.1.refs_0_, bf16[8,2048]{1,0:T(8,128)(2,1)S(1)} %collective-permute-done.3.refs_1_, bf16[8,2048]{1,0:T(8,128)(2,1)S(1)} %collective-permute-done.4.refs_2_, ...), custom_call_target="tpu_custom_call" | custom-call | flops 134217728 | bytes 4194304 | tf_op jit(solution)/shard_map/project_first/pallas_call | solution.py:332
  21.2 1.6 %collective-permute-start.9 = (bf16[32,1024]{1,0:T(8,128)(2,1)S(1)}, bf16[32,1024]{1,0:T(8,128)(2,1)S(1)}, u32[]{:S(2)}, u32[]{:S(2)}) collective-permute-start(bf16[32,1024]{1,0:T(8,128)(2,1)S(1)} %get-tuple-element.16), channel_id=1, source_target_pairs={{0,1},{1,0},{2,3},{3,2},{4,5},{5,4},{6,7},{7,6},{8,9},{9,8},{10,11... | collective-permute-start | bytes 196616 | tf_op jit(solution)/shard_map/ppermute | solution.py:243
  22.8 0.8 %project_out.4 = bf16[32,1024]{1,0:T(8,128)(2,1)S(1)} custom-call(bf16[2048,4096]{1,0:T(8,128)(2,1)S(1)} %bitcast.2, bf16[32,2048]{1,0:T(8,128)(2,1)S(1)} %get-tuple-element.15.heads), custom_call_target="tpu_custom_call" | custom-call | flops 134217728 | bytes 4194304 | tf_op jit(solution)/shard_map/project_out/pallas_call | solution.py:344
  23.6 0.5 %collective-permute-start.6 = (bf16[32,1024]{1,0:T(8,128)(2,1)S(1)}, bf16[32,1024]{1,0:T(8,128)(2,1)S(1)}, u32[]{:S(2)}, u32[]{:S(2)}) collective-permute-start(bf16[32,1024]{1,0:T(8,128)(2,1)S(1)} %project_out.4), channel_id=1, source_target_pairs={{0,1},{1,0},{2,3},{3,2},{4,5},{5,4},{6,7},{7,6},{8,9},{9,8},{10,11... | collective-permute-start | bytes 196616 | tf_op jit(solution)/shard_map/ppermute | solution.py:243
  24.1 0.8 %project_out.5.own = f32[32,1024]{1,0:T(8,128)S(1)} custom-call(bf16[2048,4096]{1,0:T(8,128)(2,1)S(1)} %bitcast.2, bf16[32,2048]{1,0:T(8,128)(2,1)S(1)} %get-tuple-element.15.heads), custom_call_target="tpu_custom_call" | custom-call | flops 134217728 | bytes 4194304 | tf_op jit(solution)/shard_map/project_out/pallas_call | solution.py:344
  24.9 0.8 %project_out.3.own = f32[32,1024]{1,0:T(8,128)S(1)} custom-call(bf16[2048,4096]{1,0:T(8,128)(2,1)S(1)} %bitcast.2, bf16[32,2048]{1,0:T(8,128)(2,1)S(1)} %get-tuple-element.15.heads), custom_call_target="tpu_custom_call" | custom-call | flops 134217728 | bytes 4194304 | tf_op jit(solution)/shard_map/project_out/pallas_call | solution.py:344
  25.7 0.1 collective-permute-done.9.arrived
  25.8 2.7 %collective-permute-start.10 = (bf16[32,1024]{1,0:T(8,128)(2,1)S(1)}, bf16[32,1024]{1,0:T(8,128)(2,1)S(1)}, u32[]{:S(2)}, u32[]{:S(2)}) collective-permute-start(bf16[32,1024]{1,0:T(8,128)(2,1)S(1)} %add_near.3.refs_0_), channel_id=1, source_target_pairs={{0,2},{1,3},{2,0},{3,1},{4,6},{5,7},{6,4},{7,5},{8,10},{9,11},{10,... | collective-permute-start | bytes 196616 | tf_op jit(solution)/shard_map/ppermute | solution.py:243
  28.5 0.0 collective-permute-done.6.arrived
  28.5 2.6 %collective-permute-start.7 = (bf16[32,1024]{1,0:T(8,128)(2,1)S(1)}, bf16[32,1024]{1,0:T(8,128)(2,1)S(1)}, u32[]{:S(2)}, u32[]{:S(2)}) collective-permute-start(bf16[32,1024]{1,0:T(8,128)(2,1)S(1)} %add_near.2.refs_0_), channel_id=1, source_target_pairs={{0,2},{1,3},{2,0},{3,1},{4,6},{5,7},{6,4},{7,5},{8,10},{9,11},{10,... | collective-permute-start | bytes 196616 | tf_op jit(solution)/shard_map/ppermute | solution.py:243
  31.1 2.0 %collective-permute-done.10.refs_1_ = bf16[32,1024]{1,0:T(8,128)(2,1)S(1)} collective-permute-done((bf16[32,1024]{1,0:T(8,128)(2,1)S(1)}, bf16[32,1024]{1,0:T(8,128)(2,1)S(1)}, u32[]{:S(2)}, u32[]{:S(2)}) %collective-permute-start.10) | collective-permute-done | bytes 65568 | tf_op jit(solution)/shard_map/ppermute | solution.py:243
  33.1 0.1 finish.3.refs_0_
  33.2 0.2 collective-permute-start.11
  33.4 0.5 %collective-permute-done.7.refs_1_ = bf16[32,1024]{1,0:T(8,128)(2,1)S(1)} collective-permute-done((bf16[32,1024]{1,0:T(8,128)(2,1)S(1)}, bf16[32,1024]{1,0:T(8,128)(2,1)S(1)}, u32[]{:S(2)}, u32[]{:S(2)}) %collective-permute-start.7) | collective-permute-done | bytes 65568 | tf_op jit(solution)/shard_map/ppermute | solution.py:243
  33.9 1.9 %collective-permute-start.8 = (bf16[32,1024]{1,0:T(8,128)(2,1)S(1)}, bf16[32,1024]{1,0:T(8,128)(2,1)S(1)}, u32[]{:S(2)}, u32[]{:S(2)}) collective-permute-start(bf16[32,1024]{1,0:T(8,128)(2,1)S(1)} %finish.2.refs_2_), channel_id=1, source_target_pairs={{0,1},{1,0},{2,3},{3,2},{4,5},{5,4},{6,7},{7,6},{8,9},{9,8},{10,11... | collective-permute-start | bytes 196616 | tf_op jit(solution)/shard_map/ppermute | solution.py:243
  35.8 1.7 %collective-permute-done.11.refs_1_ = bf16[32,1024]{1,0:T(8,128)(2,1)S(1)} collective-permute-done((bf16[32,1024]{1,0:T(8,128)(2,1)S(1)}, bf16[32,1024]{1,0:T(8,128)(2,1)S(1)}, u32[]{:S(2)}, u32[]{:S(2)}) %collective-permute-start.11) | collective-permute-done | bytes 65568 | tf_op jit(solution)/shard_map/ppermute | solution.py:243
  37.5 0.7 %write_most.1.refs_1_ = bf16[32,4096]{1,0:T(8,128)(2,1)} custom-call(bf16[32,1024]{1,0:T(8,128)(2,1)S(1)} %finish.3.refs_0_, bf16[32,1024]{1,0:T(8,128)(2,1)S(1)} %collective-permute-done.11.refs_1_, bf16[32,1024]{1,0:T(8,128)(2,1)S(1)} %finish.2.refs_2_), custom_call_target="tpu_custom_call" | custom-call | tf_op jit(solution)/shard_map/write_most/pallas_call | solution.py:377
  38.2 0.1 collective-permute-done.8.refs_0_
  38.3 0.6 %write_last.1 = bf16[32,4096]{1,0:T(8,128)(2,1)} custom-call(bf16[32,1024]{1,0:T(8,128)(2,1)S(1)} %collective-permute-done.8.refs_0_, bf16[32,4096]{1,0:T(8,128)(2,1)} %write_most.1.refs_1_), custom_call_target="tpu_custom_call", output_to_operand_aliasing={{}: (1, {})} | custom-call | tf_op jit(solution)/shard_map/write_last/pallas_call | solution.py:386
  (18 shorter events, 0.2 us)
Async XLA Ops:
  6.9 3.4 %copy-start.3 = (s32[8]{0:T(128)S(1)}, s32[8]{0:T(128)}, u32[]{:S(2)}) copy-start(s32[8]{0:T(128)} %param.17) | copy-start | bytes 100
  6.9 3.6 %copy-start = (bf16[8,2048,128]{2,1,0:T(8,128)(2,1)S(1)}, bf16[8,2048,128]{2,1,0:T(8,128)(2,1)}, u32[]{:S(2)}) copy-start(bf16[8,2048,128]{2,1,0:T(8,128)(2,1)} %v.3) | copy-start | bytes 12582916
  7.0 3.6 %copy-start.1 = (bf16[8,2048,128]{2,1,0:T(8,128)(2,1)S(1)}, bf16[8,2048,128]{2,1,0:T(8,128)(2,1)}, u32[]{:S(2)}) copy-start(bf16[8,2048,128]{2,1,0:T(8,128)(2,1)} %k.1) | copy-start | bytes 12582916
  7.0 4.7 %collective-permute-start.2 = (f16[8,2432]{1,0:T(8,128)(2,1)S(1)}, f16[8,2432]{1,0:T(8,128)(2,1)S(1)}, u32[]{:S(2)}, u32[]{:S(2)}) collective-permute-start(f16[8,2432]{1,0:T(8,128)(2,1)S(1)} %convert_element_type.26), channel_id=1, source_target_pairs={{0,12},{4,8},{8,4},{12,0},{1,13},{5,9},{9,5},{13,1},{2,14},{6,10},... | collective-permute-start | bytes 116744 | tf_op jit(solution)/shard_map/ppermute | solution.py:243
  9.5 4.2 %collective-permute-start.1 = (f16[8,2432]{1,0:T(8,128)(2,1)S(1)}, f16[8,2432]{1,0:T(8,128)(2,1)S(1)}, u32[]{:S(2)}, u32[]{:S(2)}) collective-permute-start(f16[8,2432]{1,0:T(8,128)(2,1)S(1)} %convert_element_type.24), channel_id=1, source_target_pairs={{0,8},{4,12},{8,0},{12,4},{1,9},{5,13},{9,1},{13,5},{2,10},{6,14},... | collective-permute-start | bytes 116744 | tf_op jit(solution)/shard_map/ppermute | solution.py:243
  10.1 3.5 %collective-permute-start = (f16[8,2432]{1,0:T(8,128)(2,1)S(1)}, f16[8,2432]{1,0:T(8,128)(2,1)S(1)}, u32[]{:S(2)}, u32[]{:S(2)}) collective-permute-start(f16[8,2432]{1,0:T(8,128)(2,1)S(1)} %convert_element_type.22), channel_id=1, source_target_pairs={{0,4},{4,0},{8,12},{12,8},{1,5},{5,1},{9,13},{13,9},{2,6},{6,2},{1... | collective-permute-start | bytes 116744 | tf_op jit(solution)/shard_map/ppermute | solution.py:243
  10.5 9.8 %slice-start = ((s8[16777216]{0:T(1024)(128)(4,1)}), s8[4194304]{0:T(1024)(128)(4,1)S(1)}, s32[]{:S(2)}) async-start(s8[16777216]{0:T(1024)(128)(4,1)} %bitcast.1), calls=%async_computation | async-start | bytes 8388608
  10.5 9.8 %slice-start.1 = ((s8[16777216]{0:T(1024)(128)(4,1)}), s8[4194304]{0:T(1024)(128)(4,1)S(1)}, s32[]{:S(2)}) async-start(s8[16777216]{0:T(1024)(128)(4,1)} %bitcast.1), calls=%async_computation.1 | async-start | bytes 8388608
  13.7 6.6 %slice-start.2 = ((s8[16777216]{0:T(1024)(128)(4,1)}), s8[4194304]{0:T(1024)(128)(4,1)S(1)}, s32[]{:S(2)}) async-start(s8[16777216]{0:T(1024)(128)(4,1)} %bitcast.1), calls=%async_computation.2 | async-start | bytes 8388608
  13.8 6.6 %slice-start.3 = ((s8[16777216]{0:T(1024)(128)(4,1)}), s8[4194304]{0:T(1024)(128)(4,1)S(1)}, s32[]{:S(2)}) async-start(s8[16777216]{0:T(1024)(128)(4,1)} %bitcast.1), calls=%async_computation.3 | async-start | bytes 8388608
  15.6 3.8 %collective-permute-start.5 = (bf16[8,2048]{1,0:T(8,128)(2,1)S(1)}, bf16[8,2048]{1,0:T(8,128)(2,1)S(1)}, u32[]{:S(2)}, u32[]{:S(2)}) collective-permute-start(bf16[8,2048]{1,0:T(8,128)(2,1)S(1)} %attention.1.refs_0_), channel_id=1, source_target_pairs={{0,12},{4,8},{8,4},{12,0},{1,13},{5,9},{9,5},{13,1},{2,14},{6,10},... | collective-permute-start | bytes 98312 | tf_op jit(solution)/shard_map/ppermute | solution.py:243
  16.4 3.9 %collective-permute-start.4 = (bf16[8,2048]{1,0:T(8,128)(2,1)S(1)}, bf16[8,2048]{1,0:T(8,128)(2,1)S(1)}, u32[]{:S(2)}, u32[]{:S(2)}) collective-permute-start(bf16[8,2048]{1,0:T(8,128)(2,1)S(1)} %attention.1.refs_0_), channel_id=1, source_target_pairs={{0,8},{4,12},{8,0},{12,4},{1,9},{5,13},{9,1},{13,5},{2,10},{6,14},... | collective-permute-start | bytes 98312 | tf_op jit(solution)/shard_map/ppermute | solution.py:243
  17.1 3.2 %collective-permute-start.3 = (bf16[8,2048]{1,0:T(8,128)(2,1)S(1)}, bf16[8,2048]{1,0:T(8,128)(2,1)S(1)}, u32[]{:S(2)}, u32[]{:S(2)}) collective-permute-start(bf16[8,2048]{1,0:T(8,128)(2,1)S(1)} %attention.1.refs_0_), channel_id=1, source_target_pairs={{0,4},{4,0},{8,12},{12,8},{1,5},{5,1},{9,13},{13,9},{2,6},{6,2},{1... | collective-permute-start | bytes 98312 | tf_op jit(solution)/shard_map/ppermute | solution.py:243
  21.2 4.7 %collective-permute-start.9 = (bf16[32,1024]{1,0:T(8,128)(2,1)S(1)}, bf16[32,1024]{1,0:T(8,128)(2,1)S(1)}, u32[]{:S(2)}, u32[]{:S(2)}) collective-permute-start(bf16[32,1024]{1,0:T(8,128)(2,1)S(1)} %get-tuple-element.16), channel_id=1, source_target_pairs={{0,1},{1,0},{2,3},{3,2},{4,5},{5,4},{6,7},{7,6},{8,9},{9,8},{10,11... | collective-permute-start | bytes 196616 | tf_op jit(solution)/shard_map/ppermute | solution.py:243
  23.6 4.9 %collective-permute-start.6 = (bf16[32,1024]{1,0:T(8,128)(2,1)S(1)}, bf16[32,1024]{1,0:T(8,128)(2,1)S(1)}, u32[]{:S(2)}, u32[]{:S(2)}) collective-permute-start(bf16[32,1024]{1,0:T(8,128)(2,1)S(1)} %project_out.4), channel_id=1, source_target_pairs={{0,1},{1,0},{2,3},{3,2},{4,5},{5,4},{6,7},{7,6},{8,9},{9,8},{10,11... | collective-permute-start | bytes 196616 | tf_op jit(solution)/shard_map/ppermute | solution.py:243
  24.9 8.2 %copy-start.2 = (bf16[32,4096]{1,0:T(8,128)(2,1)S(1)}, bf16[32,4096]{1,0:T(8,128)(2,1)}, u32[]{:S(2)}) copy-start(bf16[32,4096]{1,0:T(8,128)(2,1)} %x.3) | copy-start | bytes 786436
  25.8 7.3 %collective-permute-start.10 = (bf16[32,1024]{1,0:T(8,128)(2,1)S(1)}, bf16[32,1024]{1,0:T(8,128)(2,1)S(1)}, u32[]{:S(2)}, u32[]{:S(2)}) collective-permute-start(bf16[32,1024]{1,0:T(8,128)(2,1)S(1)} %add_near.3.refs_0_), channel_id=1, source_target_pairs={{0,2},{1,3},{2,0},{3,1},{4,6},{5,7},{6,4},{7,5},{8,10},{9,11},{10,... | collective-permute-start | bytes 196616 | tf_op jit(solution)/shard_map/ppermute | solution.py:243
  28.5 5.4 %collective-permute-start.7 = (bf16[32,1024]{1,0:T(8,128)(2,1)S(1)}, bf16[32,1024]{1,0:T(8,128)(2,1)S(1)}, u32[]{:S(2)}, u32[]{:S(2)}) collective-permute-start(bf16[32,1024]{1,0:T(8,128)(2,1)S(1)} %add_near.2.refs_0_), channel_id=1, source_target_pairs={{0,2},{1,3},{2,0},{3,1},{4,6},{5,7},{6,4},{7,5},{8,10},{9,11},{10,... | collective-permute-start | bytes 196616 | tf_op jit(solution)/shard_map/ppermute | solution.py:243
  33.2 4.3 %collective-permute-start.11 = (bf16[32,1024]{1,0:T(8,128)(2,1)S(1)}, bf16[32,1024]{1,0:T(8,128)(2,1)S(1)}, u32[]{:S(2)}, u32[]{:S(2)}) collective-permute-start(bf16[32,1024]{1,0:T(8,128)(2,1)S(1)} %finish.3.refs_0_), channel_id=1, source_target_pairs={{0,1},{1,0},{2,3},{3,2},{4,5},{5,4},{6,7},{7,6},{8,9},{9,8},{10,11... | collective-permute-start | bytes 196616 | tf_op jit(solution)/shard_map/ppermute | solution.py:243
  33.9 4.3 %collective-permute-start.8 = (bf16[32,1024]{1,0:T(8,128)(2,1)S(1)}, bf16[32,1024]{1,0:T(8,128)(2,1)S(1)}, u32[]{:S(2)}, u32[]{:S(2)}) collective-permute-start(bf16[32,1024]{1,0:T(8,128)(2,1)S(1)} %finish.2.refs_2_), channel_id=1, source_target_pairs={{0,1},{1,0},{2,3},{3,2},{4,5},{5,4},{6,7},{7,6},{8,9},{9,8},{10,11... | collective-permute-start | bytes 196616 | tf_op jit(solution)/shard_map/ppermute | solution.py:243

commit v19 on v18

--- a/solution.py
+++ b/solution.py
@@ -374,25 +374,25 @@
             )(in_vmem(inputs), *[in_vmem(a) for a in far])
             blocks += [done, swap(done, "gy", size_y, 1)]
         shape = jax.ShapeDtypeStruct((batch, block * 4), BF16)
-        most = pl.pallas_call(
-            functools.partial(write, [(0, 0), (0, 1), (1, 0)]),
+        own_half = pl.pallas_call(
+            functools.partial(write, [(0, 0), (1, 0)]),
             out_shape=shape,
-            in_specs=[VMEM] * 3,
+            in_specs=[VMEM] * 2,
             out_specs=ANY,
-            scratch_shapes=[sems(3)],
+            scratch_shapes=[sems(2)],
             compiler_params=params(4),
-            name="write_most",
-        )(*[in_vmem(b) for b in blocks[:3]])
+            name="write_own",
+        )(*[in_vmem(b) for b in blocks[::2]])
         return pl.pallas_call(
-            functools.partial(write, [(1, 1)]),
+            functools.partial(write, [(0, 1), (1, 1)]),
             out_shape=shape,
-            in_specs=[VMEM, ANY],
+            in_specs=[VMEM, VMEM, ANY],
             out_specs=ANY,
-            scratch_shapes=[sems(1)],
-            input_output_aliases={1: 0},
+            scratch_shapes=[sems(2)],
+            input_output_aliases={2: 0},
             compiler_params=params(4),
             name="write_last",
-        )(in_vmem(blocks[3]), in_hbm(most))
+        )(*[in_vmem(b) for b in blocks[1::2]], in_hbm(own_half))
 
     placed = (
         P("groups", "gx"),

time: 39.1 us -> 39.1 us (level)
  no operation moved by 1% of the time
where the time goes in v19:
time: 39.1 us; the launch traced here: 38.9 us
  Pallas kernels  14.7 us (38%)
  starting transfers between devices  14.6 us (37%)
  waiting for transfers between devices  9.08 us (23%)
    ppermute x12, starting transfers between devices, swap(): return lax.ppermute(value, axis, [(i, i ^ mask) for i in range(size)])  14.6 us
    ppermute x12, waiting for transfers between devices, swap(): return lax.ppermute(value, axis, [(i, i ^ mask) for i in range(size)])  9.08 us
    pallas_call x1, Pallas kernels, shards(): pl.pallas_call(project, out_shape=pltpu.VMEM((batch, packed), F32), in_sp...  6.92 us
    pallas_call x3, Pallas kernels, product(): pl.pallas_call(functools.partial(project_out, chunk, given), out_shape=pl...  2.47 us
    pallas_call x1, Pallas kernels, shards(): pl.pallas_call(functools.partial(attention, size_x, depth * size_x), out_...  1.82 us
    pallas_call x1, Pallas kernels, shards(): pl.pallas_call(turn_keys, out_shape=pltpu.VMEM((rows, HD, key_cache.shape...  1.13 us
    pallas_call x1, Pallas kernels, shards(): pl.pallas_call(project_first, out_shape=[pltpu.VMEM((batch, block), BF16)...  0.83 us
  transfers between devices with their start and end apart: 12, of which 8 were waited for; matrix products, arithmetic and copies ran while one was open for 1% of the time, Pallas kernels for 11%

profile of v19, /device:TPU:0, one launch (start us, length us, event | category | flops | bytes accessed | tf_op | source)
XLA Modules:
  0.0 38.9 jit_solution(8044966129979117958)
XLA Ops:
  0.0 6.9 %project.1.total = f32[32,2432]{1,0:T(8,128)S(1)} custom-call(bf16[32,4096]{1,0:T(8,128)(2,1)} %x.3, f32[1,4096]{1,0:T(1,128)} %bitcast.3, bf16[4096,2048]{1,0:T(8,128)(2,1)} %weights.3, bf16[4096,128]{1,0:T(8,128)(2,1)} %wk_hbm.1, bf16[4096,128]{1,0:T(8,128)(2,1)} %wv_hbm.1), custom_call_target="tpu_custom_call" | custom-call | flops 637534208 | bytes 19922944 | tf_op jit(solution)/shard_map/project/pallas_call | solution.py:258
  6.9 0.0 copy-start.3
  6.9 0.0 copy-start
  7.0 0.0 copy-start.1
  7.0 2.4 %collective-permute-start.2 = (f16[8,2432]{1,0:T(8,128)(2,1)S(1)}, f16[8,2432]{1,0:T(8,128)(2,1)S(1)}, u32[]{:S(2)}, u32[]{:S(2)}) collective-permute-start(f16[8,2432]{1,0:T(8,128)(2,1)S(1)} %convert_element_type.26), channel_id=1, source_target_pairs={{0,12},{4,8},{8,4},{12,0},{1,13},{5,9},{9,5},{13,1},{2,14},{6,10},... | collective-permute-start | bytes 116744 | tf_op jit(solution)/shard_map/ppermute | solution.py:243
  9.5 0.6 %collective-permute-start.1 = (f16[8,2432]{1,0:T(8,128)(2,1)S(1)}, f16[8,2432]{1,0:T(8,128)(2,1)S(1)}, u32[]{:S(2)}, u32[]{:S(2)}) collective-permute-start(f16[8,2432]{1,0:T(8,128)(2,1)S(1)} %convert_element_type.24), channel_id=1, source_target_pairs={{0,8},{4,12},{8,0},{12,4},{1,9},{5,13},{9,1},{13,5},{2,10},{6,14},... | collective-permute-start | bytes 116744 | tf_op jit(solution)/shard_map/ppermute | solution.py:243
  10.1 0.2 collective-permute-start
  10.3 0.0 copy-done.3
  10.3 0.1 fusion
  10.4 0.1 pad_maximum_fusion
  10.5 0.0 copy-done
  10.5 0.0 copy-done.1
  10.5 0.0 slice-start
  10.5 0.0 slice-start.1
  10.5 1.1 %turn_keys.1.k = bf16[8,128,2048]{2,1,0:T(8,128)(2,1)S(1)} custom-call(f32[8,2432]{1,0:T(8,128)S(1)} %get-tuple-element.11.after.refs_0_, bf16[8,2048,128]{2,1,0:T(8,128)(2,1)S(1)} %copy-done.1, bf16[8,2048,128]{2,1,0:T(8,128)(2,1)S(1)} %copy-done), custom_call_target="tpu_custom_call" | custom-call | bytes 4194304 | tf_op jit(solution)/shard_map/turn_keys/pallas_call | solution.py:289
  11.7 0.0 collective-permute-done.2
  11.7 1.9 %collective-permute-done.1 = f16[8,2432]{1,0:T(8,128)(2,1)S(1)} collective-permute-done((f16[8,2432]{1,0:T(8,128)(2,1)S(1)}, f16[8,2432]{1,0:T(8,128)(2,1)S(1)}, u32[]{:S(2)}, u32[]{:S(2)}) %collective-permute-start.1) | collective-permute-done | bytes 38944 | tf_op jit(solution)/shard_map/ppermute | solution.py:243
  13.7 0.0 collective-permute-done
  13.7 0.1 broadcast_in_dim.2.lengths
  13.8 1.8 %attention.1.refs_0_ = bf16[8,2048]{1,0:T(8,128)(2,1)S(1)} custom-call(bf16[4096,2048]{1,0:T(8,128)(2,1)} %weights.3, s32[8,128]{1,0:T(8,128)S(1)} %broadcast_in_dim.2.lengths, f32[8,128]{1,0:T(8,128)S(1)} %get-tuple-element.20.cosine, f32[8,128]{1,0:T(8,128)S(1)} %get-tuple-element.21.sine, bf16[8,128,2048]{2,1,0:T(8,128)(2,1)S(1)} %turn_keys.1.k, ...), custom_call_target="tpu_custom_call" | custom-call | flops 134217728 | bytes 8388608 | tf_op jit(solution)/shard_map/attention/pallas_call | solution.py:304
  15.6 0.8 %collective-permute-start.5 = (bf16[8,2048]{1,0:T(8,128)(2,1)S(1)}, bf16[8,2048]{1,0:T(8,128)(2,1)S(1)}, u32[]{:S(2)}, u32[]{:S(2)}) collective-permute-start(bf16[8,2048]{1,0:T(8,128)(2,1)S(1)} %attention.1.refs_0_), channel_id=1, source_target_pairs={{0,12},{4,8},{8,4},{12,0},{1,13},{5,9},{9,5},{13,1},{2,14},{6,10},... | collective-permute-start | bytes 98312 | tf_op jit(solution)/shard_map/ppermute | solution.py:243
  16.4 0.7 %collective-permute-start.4 = (bf16[8,2048]{1,0:T(8,128)(2,1)S(1)}, bf16[8,2048]{1,0:T(8,128)(2,1)S(1)}, u32[]{:S(2)}, u32[]{:S(2)}) collective-permute-start(bf16[8,2048]{1,0:T(8,128)(2,1)S(1)} %attention.1.refs_0_), channel_id=1, source_target_pairs={{0,8},{4,12},{8,0},{12,4},{1,9},{5,13},{9,1},{13,5},{2,10},{6,14},... | collective-permute-start | bytes 98312 | tf_op jit(solution)/shard_map/ppermute | solution.py:243
  17.1 0.4 %collective-permute-start.3 = (bf16[8,2048]{1,0:T(8,128)(2,1)S(1)}, bf16[8,2048]{1,0:T(8,128)(2,1)S(1)}, u32[]{:S(2)}, u32[]{:S(2)}) collective-permute-start(bf16[8,2048]{1,0:T(8,128)(2,1)S(1)} %attention.1.refs_0_), channel_id=1, source_target_pairs={{0,4},{4,0},{8,12},{12,8},{1,5},{5,1},{9,13},{13,9},{2,6},{6,2},{1... | collective-permute-start | bytes 98312 | tf_op jit(solution)/shard_map/ppermute | solution.py:243
  17.5 1.8 %collective-permute-done.5.refs_3_ = bf16[8,2048]{1,0:T(8,128)(2,1)S(1)} collective-permute-done((bf16[8,2048]{1,0:T(8,128)(2,1)S(1)}, bf16[8,2048]{1,0:T(8,128)(2,1)S(1)}, u32[]{:S(2)}, u32[]{:S(2)}) %collective-permute-start.5) | collective-permute-done | bytes 32800 | tf_op jit(solution)/shard_map/ppermute | solution.py:243
  19.3 1.0 %collective-permute-done.4.refs_2_ = bf16[8,2048]{1,0:T(8,128)(2,1)S(1)} collective-permute-done((bf16[8,2048]{1,0:T(8,128)(2,1)S(1)}, bf16[8,2048]{1,0:T(8,128)(2,1)S(1)}, u32[]{:S(2)}, u32[]{:S(2)}) %collective-permute-start.4) | collective-permute-done | bytes 32800 | tf_op jit(solution)/shard_map/ppermute | solution.py:243
  20.3 0.0 collective-permute-done.3.refs_1_
  20.3 0.0 slice-done
  20.3 0.0 slice-done.1
  20.3 0.0 slice-done.2
  20.4 0.8 %project_first.1 = (bf16[32,1024]{1,0:T(8,128)(2,1)S(1)}, bf16[32,2048]{1,0:T(8,128)(2,1)S(1)}) custom-call(bf16[2048,4096]{1,0:T(8,128)(2,1)S(1)} %bitcast.2, bf16[8,2048]{1,0:T(8,128)(2,1)S(1)} %attention.1.refs_0_, bf16[8,2048]{1,0:T(8,128)(2,1)S(1)} %collective-permute-done.3.refs_1_, bf16[8,2048]{1,0:T(8,128)(2,1)S(1)} %collective-permute-done.4.refs_2_, ...), custom_call_target="tpu_custom_call" | custom-call | flops 134217728 | bytes 4194304 | tf_op jit(solution)/shard_map/project_first/pallas_call | solution.py:332
  21.2 1.6 %collective-permute-start.6 = (bf16[32,1024]{1,0:T(8,128)(2,1)S(1)}, bf16[32,1024]{1,0:T(8,128)(2,1)S(1)}, u32[]{:S(2)}, u32[]{:S(2)}) collective-permute-start(bf16[32,1024]{1,0:T(8,128)(2,1)S(1)} %get-tuple-element.16), channel_id=1, source_target_pairs={{0,1},{1,0},{2,3},{3,2},{4,5},{5,4},{6,7},{7,6},{8,9},{9,8},{10,11... | collective-permute-start | bytes 196616 | tf_op jit(solution)/shard_map/ppermute | solution.py:243
  22.8 0.8 %project_out.5 = bf16[32,1024]{1,0:T(8,128)(2,1)S(1)} custom-call(bf16[2048,4096]{1,0:T(8,128)(2,1)S(1)} %bitcast.2, bf16[32,2048]{1,0:T(8,128)(2,1)S(1)} %get-tuple-element.15.heads), custom_call_target="tpu_custom_call" | custom-call | flops 134217728 | bytes 4194304 | tf_op jit(solution)/shard_map/project_out/pallas_call | solution.py:344
  23.6 0.5 %collective-permute-start.9 = (bf16[32,1024]{1,0:T(8,128)(2,1)S(1)}, bf16[32,1024]{1,0:T(8,128)(2,1)S(1)}, u32[]{:S(2)}, u32[]{:S(2)}) collective-permute-start(bf16[32,1024]{1,0:T(8,128)(2,1)S(1)} %project_out.5), channel_id=1, source_target_pairs={{0,1},{1,0},{2,3},{3,2},{4,5},{5,4},{6,7},{7,6},{8,9},{9,8},{10,11... | collective-permute-start | bytes 196616 | tf_op jit(solution)/shard_map/ppermute | solution.py:243
  24.1 0.8 %project_out.4.own = f32[32,1024]{1,0:T(8,128)S(1)} custom-call(bf16[2048,4096]{1,0:T(8,128)(2,1)S(1)} %bitcast.2, bf16[32,2048]{1,0:T(8,128)(2,1)S(1)} %get-tuple-element.15.heads), custom_call_target="tpu_custom_call" | custom-call | flops 134217728 | bytes 4194304 | tf_op jit(solution)/shard_map/project_out/pallas_call | solution.py:344
  24.9 0.8 %project_out.3.own = f32[32,1024]{1,0:T(8,128)S(1)} custom-call(bf16[2048,4096]{1,0:T(8,128)(2,1)S(1)} %bitcast.2, bf16[32,2048]{1,0:T(8,128)(2,1)S(1)} %get-tuple-element.15.heads), custom_call_target="tpu_custom_call" | custom-call | flops 134217728 | bytes 4194304 | tf_op jit(solution)/shard_map/project_out/pallas_call | solution.py:344
  25.7 0.1 collective-permute-done.6.arrived
  25.8 2.7 %collective-permute-start.7 = (bf16[32,1024]{1,0:T(8,128)(2,1)S(1)}, bf16[32,1024]{1,0:T(8,128)(2,1)S(1)}, u32[]{:S(2)}, u32[]{:S(2)}) collective-permute-start(bf16[32,1024]{1,0:T(8,128)(2,1)S(1)} %add_near.2.refs_0_), channel_id=1, source_target_pairs={{0,2},{1,3},{2,0},{3,1},{4,6},{5,7},{6,4},{7,5},{8,10},{9,11},{10,... | collective-permute-start | bytes 196616 | tf_op jit(solution)/shard_map/ppermute | solution.py:243
  28.5 0.0 collective-permute-done.9.arrived
  28.5 2.6 %collective-permute-start.10 = (bf16[32,1024]{1,0:T(8,128)(2,1)S(1)}, bf16[32,1024]{1,0:T(8,128)(2,1)S(1)}, u32[]{:S(2)}, u32[]{:S(2)}) collective-permute-start(bf16[32,1024]{1,0:T(8,128)(2,1)S(1)} %add_near.3.refs_0_), channel_id=1, source_target_pairs={{0,2},{1,3},{2,0},{3,1},{4,6},{5,7},{6,4},{7,5},{8,10},{9,11},{10,... | collective-permute-start | bytes 196616 | tf_op jit(solution)/shard_map/ppermute | solution.py:243
  31.1 2.0 %collective-permute-done.7.refs_1_ = bf16[32,1024]{1,0:T(8,128)(2,1)S(1)} collective-permute-done((bf16[32,1024]{1,0:T(8,128)(2,1)S(1)}, bf16[32,1024]{1,0:T(8,128)(2,1)S(1)}, u32[]{:S(2)}, u32[]{:S(2)}) %collective-permute-start.7) | collective-permute-done | bytes 65568 | tf_op jit(solution)/shard_map/ppermute | solution.py:243
  33.1 0.1 finish.2.refs_0_
  33.2 0.2 collective-permute-start.8
  33.4 0.5 %collective-permute-done.10.refs_1_ = bf16[32,1024]{1,0:T(8,128)(2,1)S(1)} collective-permute-done((bf16[32,1024]{1,0:T(8,128)(2,1)S(1)}, bf16[32,1024]{1,0:T(8,128)(2,1)S(1)}, u32[]{:S(2)}, u32[]{:S(2)}) %collective-permute-start.10) | collective-permute-done | bytes 65568 | tf_op jit(solution)/shard_map/ppermute | solution.py:243
  33.9 1.9 %collective-permute-start.11 = (bf16[32,1024]{1,0:T(8,128)(2,1)S(1)}, bf16[32,1024]{1,0:T(8,128)(2,1)S(1)}, u32[]{:S(2)}, u32[]{:S(2)}) collective-permute-start(bf16[32,1024]{1,0:T(8,128)(2,1)S(1)} %finish.3.refs_1_), channel_id=1, source_target_pairs={{0,1},{1,0},{2,3},{3,2},{4,5},{5,4},{6,7},{7,6},{8,9},{9,8},{10,11... | collective-permute-start | bytes 196616 | tf_op jit(solution)/shard_map/ppermute | solution.py:243
  35.8 0.7 %write_own.1.refs_2_ = bf16[32,4096]{1,0:T(8,128)(2,1)} custom-call(bf16[32,1024]{1,0:T(8,128)(2,1)S(1)} %finish.2.refs_0_, bf16[32,1024]{1,0:T(8,128)(2,1)S(1)} %finish.3.refs_1_), custom_call_target="tpu_custom_call" | custom-call | tf_op jit(solution)/shard_map/write_own/pallas_call | solution.py:377
  36.5 1.0 %collective-permute-done.8.refs_0_ = bf16[32,1024]{1,0:T(8,128)(2,1)S(1)} collective-permute-done((bf16[32,1024]{1,0:T(8,128)(2,1)S(1)}, bf16[32,1024]{1,0:T(8,128)(2,1)S(1)}, u32[]{:S(2)}, u32[]{:S(2)}) %collective-permute-start.8) | collective-permute-done | bytes 65568 | tf_op jit(solution)/shard_map/ppermute | solution.py:243
  37.5 0.8 %collective-permute-done.11.refs_1_ = bf16[32,1024]{1,0:T(8,128)(2,1)S(1)} collective-permute-done((bf16[32,1024]{1,0:T(8,128)(2,1)S(1)}, bf16[32,1024]{1,0:T(8,128)(2,1)S(1)}, u32[]{:S(2)}, u32[]{:S(2)}) %collective-permute-start.11) | collective-permute-done | bytes 65568 | tf_op jit(solution)/shard_map/ppermute | solution.py:243
  38.3 0.7 %write_last.1 = bf16[32,4096]{1,0:T(8,128)(2,1)} custom-call(bf16[32,1024]{1,0:T(8,128)(2,1)S(1)} %collective-permute-done.8.refs_0_, bf16[32,1024]{1,0:T(8,128)(2,1)S(1)} %collective-permute-done.11.refs_1_, bf16[32,4096]{1,0:T(8,128)(2,1)} %write_own.1.refs_2_), custom_call_target="tpu_custom_call", output_to_operand_aliasing={{}: (2, {})} | custom-call | tf_op jit(solution)/shard_map/write_last/pallas_call | solution.py:386
  (18 shorter events, 0.2 us)
Async XLA Ops:
  6.9 3.4 %copy-start.3 = (s32[8]{0:T(128)S(1)}, s32[8]{0:T(128)}, u32[]{:S(2)}) copy-start(s32[8]{0:T(128)} %param.17) | copy-start | bytes 100
  6.9 3.6 %copy-start = (bf16[8,2048,128]{2,1,0:T(8,128)(2,1)S(1)}, bf16[8,2048,128]{2,1,0:T(8,128)(2,1)}, u32[]{:S(2)}) copy-start(bf16[8,2048,128]{2,1,0:T(8,128)(2,1)} %v.3) | copy-start | bytes 12582916
  7.0 3.6 %copy-start.1 = (bf16[8,2048,128]{2,1,0:T(8,128)(2,1)S(1)}, bf16[8,2048,128]{2,1,0:T(8,128)(2,1)}, u32[]{:S(2)}) copy-start(bf16[8,2048,128]{2,1,0:T(8,128)(2,1)} %k.1) | copy-start | bytes 12582916
  7.0 4.7 %collective-permute-start.2 = (f16[8,2432]{1,0:T(8,128)(2,1)S(1)}, f16[8,2432]{1,0:T(8,128)(2,1)S(1)}, u32[]{:S(2)}, u32[]{:S(2)}) collective-permute-start(f16[8,2432]{1,0:T(8,128)(2,1)S(1)} %convert_element_type.26), channel_id=1, source_target_pairs={{0,12},{4,8},{8,4},{12,0},{1,13},{5,9},{9,5},{13,1},{2,14},{6,10},... | collective-permute-start | bytes 116744 | tf_op jit(solution)/shard_map/ppermute | solution.py:243
  9.5 4.2 %collective-permute-start.1 = (f16[8,2432]{1,0:T(8,128)(2,1)S(1)}, f16[8,2432]{1,0:T(8,128)(2,1)S(1)}, u32[]{:S(2)}, u32[]{:S(2)}) collective-permute-start(f16[8,2432]{1,0:T(8,128)(2,1)S(1)} %convert_element_type.24), channel_id=1, source_target_pairs={{0,8},{4,12},{8,0},{12,4},{1,9},{5,13},{9,1},{13,5},{2,10},{6,14},... | collective-permute-start | bytes 116744 | tf_op jit(solution)/shard_map/ppermute | solution.py:243
  10.1 3.5 %collective-permute-start = (f16[8,2432]{1,0:T(8,128)(2,1)S(1)}, f16[8,2432]{1,0:T(8,128)(2,1)S(1)}, u32[]{:S(2)}, u32[]{:S(2)}) collective-permute-start(f16[8,2432]{1,0:T(8,128)(2,1)S(1)} %convert_element_type.22), channel_id=1, source_target_pairs={{0,4},{4,0},{8,12},{12,8},{1,5},{5,1},{9,13},{13,9},{2,6},{6,2},{1... | collective-permute-start | bytes 116744 | tf_op jit(solution)/shard_map/ppermute | solution.py:243
  10.5 9.8 %slice-start = ((s8[16777216]{0:T(1024)(128)(4,1)}), s8[4194304]{0:T(1024)(128)(4,1)S(1)}, s32[]{:S(2)}) async-start(s8[16777216]{0:T(1024)(128)(4,1)} %bitcast.1), calls=%async_computation | async-start | bytes 8388608
  10.5 9.8 %slice-start.1 = ((s8[16777216]{0:T(1024)(128)(4,1)}), s8[4194304]{0:T(1024)(128)(4,1)S(1)}, s32[]{:S(2)}) async-start(s8[16777216]{0:T(1024)(128)(4,1)} %bitcast.1), calls=%async_computation.1 | async-start | bytes 8388608
  13.7 6.6 %slice-start.2 = ((s8[16777216]{0:T(1024)(128)(4,1)}), s8[4194304]{0:T(1024)(128)(4,1)S(1)}, s32[]{:S(2)}) async-start(s8[16777216]{0:T(1024)(128)(4,1)} %bitcast.1), calls=%async_computation.2 | async-start | bytes 8388608
  13.8 6.6 %slice-start.3 = ((s8[16777216]{0:T(1024)(128)(4,1)}), s8[4194304]{0:T(1024)(128)(4,1)S(1)}, s32[]{:S(2)}) async-start(s8[16777216]{0:T(1024)(128)(4,1)} %bitcast.1), calls=%async_computation.3 | async-start | bytes 8388608
  15.6 3.8 %collective-permute-start.5 = (bf16[8,2048]{1,0:T(8,128)(2,1)S(1)}, bf16[8,2048]{1,0:T(8,128)(2,1)S(1)}, u32[]{:S(2)}, u32[]{:S(2)}) collective-permute-start(bf16[8,2048]{1,0:T(8,128)(2,1)S(1)} %attention.1.refs_0_), channel_id=1, source_target_pairs={{0,12},{4,8},{8,4},{12,0},{1,13},{5,9},{9,5},{13,1},{2,14},{6,10},... | collective-permute-start | bytes 98312 | tf_op jit(solution)/shard_map/ppermute | solution.py:243
  16.4 3.9 %collective-permute-start.4 = (bf16[8,2048]{1,0:T(8,128)(2,1)S(1)}, bf16[8,2048]{1,0:T(8,128)(2,1)S(1)}, u32[]{:S(2)}, u32[]{:S(2)}) collective-permute-start(bf16[8,2048]{1,0:T(8,128)(2,1)S(1)} %attention.1.refs_0_), channel_id=1, source_target_pairs={{0,8},{4,12},{8,0},{12,4},{1,9},{5,13},{9,1},{13,5},{2,10},{6,14},... | collective-permute-start | bytes 98312 | tf_op jit(solution)/shard_map/ppermute | solution.py:243
  17.1 3.2 %collective-permute-start.3 = (bf16[8,2048]{1,0:T(8,128)(2,1)S(1)}, bf16[8,2048]{1,0:T(8,128)(2,1)S(1)}, u32[]{:S(2)}, u32[]{:S(2)}) collective-permute-start(bf16[8,2048]{1,0:T(8,128)(2,1)S(1)} %attention.1.refs_0_), channel_id=1, source_target_pairs={{0,4},{4,0},{8,12},{12,8},{1,5},{5,1},{9,13},{13,9},{2,6},{6,2},{1... | collective-permute-start | bytes 98312 | tf_op jit(solution)/shard_map/ppermute | solution.py:243
  21.2 4.7 %collective-permute-start.6 = (bf16[32,1024]{1,0:T(8,128)(2,1)S(1)}, bf16[32,1024]{1,0:T(8,128)(2,1)S(1)}, u32[]{:S(2)}, u32[]{:S(2)}) collective-permute-start(bf16[32,1024]{1,0:T(8,128)(2,1)S(1)} %get-tuple-element.16), channel_id=1, source_target_pairs={{0,1},{1,0},{2,3},{3,2},{4,5},{5,4},{6,7},{7,6},{8,9},{9,8},{10,11... | collective-permute-start | bytes 196616 | tf_op jit(solution)/shard_map/ppermute | solution.py:243
  23.6 4.9 %collective-permute-start.9 = (bf16[32,1024]{1,0:T(8,128)(2,1)S(1)}, bf16[32,1024]{1,0:T(8,128)(2,1)S(1)}, u32[]{:S(2)}, u32[]{:S(2)}) collective-permute-start(bf16[32,1024]{1,0:T(8,128)(2,1)S(1)} %project_out.5), channel_id=1, source_target_pairs={{0,1},{1,0},{2,3},{3,2},{4,5},{5,4},{6,7},{7,6},{8,9},{9,8},{10,11... | collective-permute-start | bytes 196616 | tf_op jit(solution)/shard_map/ppermute | solution.py:243
  24.9 8.2 %copy-start.2 = (bf16[32,4096]{1,0:T(8,128)(2,1)S(1)}, bf16[32,4096]{1,0:T(8,128)(2,1)}, u32[]{:S(2)}) copy-start(bf16[32,4096]{1,0:T(8,128)(2,1)} %x.3) | copy-start | bytes 786436
  25.8 7.3 %collective-permute-start.7 = (bf16[32,1024]{1,0:T(8,128)(2,1)S(1)}, bf16[32,1024]{1,0:T(8,128)(2,1)S(1)}, u32[]{:S(2)}, u32[]{:S(2)}) collective-permute-start(bf16[32,1024]{1,0:T(8,128)(2,1)S(1)} %add_near.2.refs_0_), channel_id=1, source_target_pairs={{0,2},{1,3},{2,0},{3,1},{4,6},{5,7},{6,4},{7,5},{8,10},{9,11},{10,... | collective-permute-start | bytes 196616 | tf_op jit(solution)/shard_map/ppermute | solution.py:243
  28.5 5.4 %collective-permute-start.10 = (bf16[32,1024]{1,0:T(8,128)(2,1)S(1)}, bf16[32,1024]{1,0:T(8,128)(2,1)S(1)}, u32[]{:S(2)}, u32[]{:S(2)}) collective-permute-start(bf16[32,1024]{1,0:T(8,128)(2,1)S(1)} %add_near.3.refs_0_), channel_id=1, source_target_pairs={{0,2},{1,3},{2,0},{3,1},{4,6},{5,7},{6,4},{7,5},{8,10},{9,11},{10,... | collective-permute-start | bytes 196616 | tf_op jit(solution)/shard_map/ppermute | solution.py:243
  33.2 4.3 %collective-permute-start.8 = (bf16[32,1024]{1,0:T(8,128)(2,1)S(1)}, bf16[32,1024]{1,0:T(8,128)(2,1)S(1)}, u32[]{:S(2)}, u32[]{:S(2)}) collective-permute-start(bf16[32,1024]{1,0:T(8,128)(2,1)S(1)} %finish.2.refs_0_), channel_id=1, source_target_pairs={{0,1},{1,0},{2,3},{3,2},{4,5},{5,4},{6,7},{7,6},{8,9},{9,8},{10,11... | collective-permute-start | bytes 196616 | tf_op jit(solution)/shard_map/ppermute | solution.py:243
  33.9 4.3 %collective-permute-start.11 = (bf16[32,1024]{1,0:T(8,128)(2,1)S(1)}, bf16[32,1024]{1,0:T(8,128)(2,1)S(1)}, u32[]{:S(2)}, u32[]{:S(2)}) collective-permute-start(bf16[32,1024]{1,0:T(8,128)(2,1)S(1)} %finish.3.refs_1_), channel_id=1, source_target_pairs={{0,1},{1,0},{2,3},{3,2},{4,5},{5,4},{6,7},{7,6},{8,9},{9,8},{10,11... | collective-permute-start | bytes 196616 | tf_op jit(solution)/shard_map/ppermute | solution.py:243

commit v20 on v17

--- a/solution.py
+++ b/solution.py
@@ -195,8 +195,8 @@
     return columns((lax.axis_index("gy") ^ given) & 1, width)
 
 
-def project_out(given, w, *refs):
-    blocks = refs[:-2]
+def project_out(given, afters, w, *refs):
+    blocks = refs[afters:-2]
     out, gathered = refs[-2:]
     rows = blocks[0].shape[0]
     core = lax.axis_index("gx") & 1
@@ -332,25 +332,30 @@
         block = w_output.shape[1] // 2
         chunks = [list(range(1, size_x // 2)), [0]]
 
-        def product(chunk, given, kind):
+        def product(chunk, given, kind, *after):
             pieces = gathered[2:] if chunk == 0 else gathered[:2]
             tall = rows * len(pieces)
             return pl.pallas_call(
-                functools.partial(project_out, given),
+                functools.partial(project_out, given, len(after)),
                 out_shape=pltpu.VMEM((tall, block), kind),
-                in_specs=[VMEM] * (1 + len(pieces)),
+                in_specs=[VMEM] + [ANY] * len(after) + [VMEM] * len(pieces),
                 out_specs=VMEM,
                 scratch_shapes=[pltpu.VMEM((tall, width), F32)],
                 compiler_params=params(8),
                 cost_estimate=cost(2 * tall * width * block, 2 * width * block),
                 name="project_out",
-            )(in_vmem(w_output), *pieces)
-
-        near = [swap(product(chunk, 1, BF16), "gy", size_y, 1) for chunk in range(2)]
+            )(in_vmem(w_output), *after, *pieces)
+
+        given_near = product(1, 1, BF16)
+        near_near = swap(given_near, "gy", size_y, 1)
+        own_near = product(1, 0, F32, gathered[2])
+        given_far = product(0, 1, BF16)
+        near_far = swap(given_far, "gy", size_y, 1)
+        owns = [product(0, 0, F32, near_near), own_near]
+        near = [near_far, near_near]
         blocks = []
         for chunk, distances in enumerate(chunks):
             tall = 2 * rows * len(distances)
-            own = product(chunk, 0, F32)
             pair = pl.pallas_call(
                 add_near,
                 out_shape=pltpu.VMEM((tall, block), BF16),
@@ -358,7 +363,7 @@
                 out_specs=VMEM,
                 compiler_params=params(4),
                 name="add_near",
-            )(in_vmem(own), in_vmem(near[chunk]))
+            )(in_vmem(owns[chunk]), in_vmem(near[chunk]))
             far = [pair] + [swap(pair, "gy", size_y, 2 * m) for m in range(1, half)]
             done = pl.pallas_call(
                 functools.partial(finish, distances, rows),
@@ -371,14 +376,14 @@
             )(in_vmem(inputs), *[in_vmem(a) for a in far])
             blocks += [done, swap(done, "gy", size_y, 1)]
         return pl.pallas_call(
-            functools.partial(assemble, chunks, rows),
+            functools.partial(assemble, chunks[::-1], rows),
             out_shape=jax.ShapeDtypeStruct((batch, 2 * block), BF16),
             in_specs=[VMEM] * 4,
             out_specs=ANY,
             scratch_shapes=[sems(size_x)],
             compiler_params=params(4),
             name="assemble",
-        )(*[in_vmem(b) for b in blocks])
+        )(*[in_vmem(b) for b in blocks[2:] + blocks[:2]])
 
     placed = (
         P("groups", "gx"),

time: 39.8 us -> 39.8 us (level)
  no operation moved by 1% of the time
where the time goes in v20:
time: 39.8 us; the launch traced here: 39.6 us
  Pallas kernels  15.6 us (39%)
  starting transfers between devices  13.3 us (33%)
  waiting for transfers between devices  10.1 us (25%)
    ppermute x12, starting transfers between devices, swap(): return lax.ppermute(value, axis, [(i, i ^ mask) for i in range(size)])  13.3 us
    ppermute x12, waiting for transfers between devices, swap(): return lax.ppermute(value, axis, [(i, i ^ mask) for i in range(size)])  10.1 us
    pallas_call x1, Pallas kernels, shards(): pl.pallas_call(project, out_shape=pltpu.VMEM((batch, packed), F32), in_sp...  6.92 us
    pallas_call x4, Pallas kernels, product(): pl.pallas_call(functools.partial(project_out, given, len(after)), out_sha...  4.77 us
    pallas_call x1, Pallas kernels, shards(): pl.pallas_call(functools.partial(attention, size_x, depth * size_x), out_...  1.82 us
    pallas_call x1, Pallas kernels, shards(): pl.pallas_call(turn_keys, out_shape=pltpu.VMEM((rows, HD, key_cache.shape...  1.13 us
  transfers between devices with their start and end apart: 12, of which 5 were waited for; matrix products, arithmetic and copies ran while one was open for 1% of the time, Pallas kernels for 15%

profile of v20, /device:TPU:0, one launch (start us, length us, event | category | flops | bytes accessed | tf_op | source)
XLA Modules:
  0.0 39.6 jit_solution(7538389435356397521)
XLA Ops:
  0.0 6.9 %project.1.total = f32[32,2432]{1,0:T(8,128)S(1)} custom-call(bf16[32,4096]{1,0:T(8,128)(2,1)} %x.3, f32[1,4096]{1,0:T(1,128)} %bitcast.3, bf16[4096,2048]{1,0:T(8,128)(2,1)} %weights.3, bf16[4096,128]{1,0:T(8,128)(2,1)} %wk_hbm.1, bf16[4096,128]{1,0:T(8,128)(2,1)} %wv_hbm.1), custom_call_target="tpu_custom_call" | custom-call | flops 637534208 | bytes 19922944 | tf_op jit(solution)/shard_map/project/pallas_call | solution.py:260
  6.9 0.0 copy-start.3
  6.9 0.0 copy-start
  7.0 0.0 copy-start.1
  7.0 2.4 %collective-permute-start.2 = (f16[8,2432]{1,0:T(8,128)(2,1)S(1)}, f16[8,2432]{1,0:T(8,128)(2,1)S(1)}, u32[]{:S(2)}, u32[]{:S(2)}) collective-permute-start(f16[8,2432]{1,0:T(8,128)(2,1)S(1)} %convert_element_type.26), channel_id=1, source_target_pairs={{0,12},{4,8},{8,4},{12,0},{1,13},{5,9},{9,5},{13,1},{2,14},{6,10},... | collective-permute-start | bytes 116744 | tf_op jit(solution)/shard_map/ppermute | solution.py:246
  9.5 0.6 %collective-permute-start.1 = (f16[8,2432]{1,0:T(8,128)(2,1)S(1)}, f16[8,2432]{1,0:T(8,128)(2,1)S(1)}, u32[]{:S(2)}, u32[]{:S(2)}) collective-permute-start(f16[8,2432]{1,0:T(8,128)(2,1)S(1)} %convert_element_type.24), channel_id=1, source_target_pairs={{0,8},{4,12},{8,0},{12,4},{1,9},{5,13},{9,1},{13,5},{2,10},{6,14},... | collective-permute-start | bytes 116744 | tf_op jit(solution)/shard_map/ppermute | solution.py:246
  10.1 0.2 collective-permute-start
  10.3 0.0 copy-done.3
  10.3 0.1 fusion
  10.4 0.1 pad_maximum_fusion
  10.5 0.0 copy-done.1
  10.5 0.0 slice-start.1
  10.5 1.1 %turn_keys.1.k = bf16[8,128,2048]{2,1,0:T(8,128)(2,1)S(1)} custom-call(f32[8,2432]{1,0:T(8,128)S(1)} %get-tuple-element.9.after.refs_0_, bf16[8,2048,128]{2,1,0:T(8,128)(2,1)S(1)} %copy-done.1, bf16[8,2048,128]{2,1,0:T(8,128)(2,1)S(1)} %copy-done), custom_call_target="tpu_custom_call" | custom-call | bytes 4194304 | tf_op jit(solution)/shard_map/turn_keys/pallas_call | solution.py:291
  11.7 0.0 collective-permute-done.2
  11.7 1.9 %collective-permute-done.1 = f16[8,2432]{1,0:T(8,128)(2,1)S(1)} collective-permute-done((f16[8,2432]{1,0:T(8,128)(2,1)S(1)}, f16[8,2432]{1,0:T(8,128)(2,1)S(1)}, u32[]{:S(2)}, u32[]{:S(2)}) %collective-permute-start.1) | collective-permute-done | bytes 38944 | tf_op jit(solution)/shard_map/ppermute | solution.py:246
  13.7 0.0 collective-permute-done
  13.7 0.1 broadcast_in_dim.2.lengths
  13.8 1.8 %attention.1.refs_1_.refs_0_ = bf16[8,2048]{1,0:T(8,128)(2,1)S(1)} custom-call(bf16[4096,2048]{1,0:T(8,128)(2,1)} %weights.3, s32[8,128]{1,0:T(8,128)S(1)} %broadcast_in_dim.2.lengths, f32[8,128]{1,0:T(8,128)S(1)} %get-tuple-element.16.cosine, f32[8,128]{1,0:T(8,128)S(1)} %get-tuple-element.17.sine, bf16[8,128,2048]{2,1,0:T(8,128)(2,1)S(1)} %turn_keys.1.k, ...), custom_call_target="tpu_custom_call" | custom-call | flops 134217728 | bytes 8388608 | tf_op jit(solution)/shard_map/attention/pallas_call | solution.py:306
  15.6 0.1 collective-permute-start.4
  15.7 1.2 %collective-permute-start.8 = (bf16[8,2048]{1,0:T(8,128)(2,1)S(1)}, bf16[8,2048]{1,0:T(8,128)(2,1)S(1)}, u32[]{:S(2)}, u32[]{:S(2)}) collective-permute-start(bf16[8,2048]{1,0:T(8,128)(2,1)S(1)} %attention.1.refs_1_.refs_0_), channel_id=1, source_target_pairs={{0,12},{4,8},{8,4},{12,0},{1,13},{5,9},{9,5},{13,1},{2,14},{6,10},... | collective-permute-start | bytes 98312 | tf_op jit(solution)/shard_map/ppermute | solution.py:246
  16.8 1.0 %collective-permute-start.3 = (bf16[8,2048]{1,0:T(8,128)(2,1)S(1)}, bf16[8,2048]{1,0:T(8,128)(2,1)S(1)}, u32[]{:S(2)}, u32[]{:S(2)}) collective-permute-start(bf16[8,2048]{1,0:T(8,128)(2,1)S(1)} %attention.1.refs_1_.refs_0_), channel_id=1, source_target_pairs={{0,8},{4,12},{8,0},{12,4},{1,9},{5,13},{9,1},{13,5},{2,10},{6,14},... | collective-permute-start | bytes 98312 | tf_op jit(solution)/shard_map/ppermute | solution.py:246
  17.8 0.0 collective-permute-done.4.refs_2_.refs_1_
  17.8 0.0 slice-done.1
  17.8 0.0 slice-done.2
  17.8 0.0 slice-done.3
  17.8 1.2 %project_out.5 = bf16[16,2048]{1,0:T(8,128)(2,1)S(1)} custom-call(bf16[2048,4096]{1,0:T(8,128)(2,1)S(1)} %bitcast.2, bf16[8,2048]{1,0:T(8,128)(2,1)S(1)} %attention.1.refs_1_.refs_0_, bf16[8,2048]{1,0:T(8,128)(2,1)S(1)} %collective-permute-done.4.refs_2_.refs_1_), custom_call_target="tpu_custom_call" | custom-call | flops 134217728 | bytes 8388608 | tf_op jit(solution)/shard_map/project_out/pallas_call | solution.py:338
  19.0 1.7 %collective-permute-start.5 = (bf16[16,2048]{1,0:T(8,128)(2,1)S(1)}, bf16[16,2048]{1,0:T(8,128)(2,1)S(1)}, u32[]{:S(2)}, u32[]{:S(2)}) collective-permute-start(bf16[16,2048]{1,0:T(8,128)(2,1)S(1)} %project_out.5), channel_id=1, source_target_pairs={{0,1},{1,0},{2,3},{3,2},{4,5},{5,4},{6,7},{7,6},{8,9},{9,8},{10,11... | collective-permute-start | bytes 196616 | tf_op jit(solution)/shard_map/ppermute | solution.py:246
  20.7 0.0 collective-permute-done.8.refs_2_.refs_1_
  20.7 0.0 collective-permute-done.3.refs_0_.refs_1_
  20.7 1.2 %project_out.7 = bf16[16,2048]{1,0:T(8,128)(2,1)S(1)} custom-call(bf16[2048,4096]{1,0:T(8,128)(2,1)S(1)} %bitcast.2, bf16[8,2048]{1,0:T(8,128)(2,1)S(1)} %collective-permute-done.3.refs_0_.refs_1_, bf16[8,2048]{1,0:T(8,128)(2,1)S(1)} %collective-permute-done.8.refs_2_.refs_1_), custom_call_target="tpu_custom_call" | custom-call | flops 134217728 | bytes 8388608 | tf_op jit(solution)/shard_map/project_out/pallas_call | solution.py:338
  21.9 1.6 %collective-permute-start.9 = (bf16[16,2048]{1,0:T(8,128)(2,1)S(1)}, bf16[16,2048]{1,0:T(8,128)(2,1)S(1)}, u32[]{:S(2)}, u32[]{:S(2)}) collective-permute-start(bf16[16,2048]{1,0:T(8,128)(2,1)S(1)} %project_out.7), channel_id=1, source_target_pairs={{0,1},{1,0},{2,3},{3,2},{4,5},{5,4},{6,7},{7,6},{8,9},{9,8},{10,11... | collective-permute-start | bytes 196616 | tf_op jit(solution)/shard_map/ppermute | solution.py:246
  23.5 1.2 %project_out.4.own = f32[16,2048]{1,0:T(8,128)S(1)} custom-call(bf16[2048,4096]{1,0:T(8,128)(2,1)S(1)} %bitcast.2, bf16[8,2048]{1,0:T(8,128)(2,1)S(1)} %collective-permute-done.3.refs_0_.refs_1_, bf16[8,2048]{1,0:T(8,128)(2,1)S(1)} %attention.1.refs_1_.refs_0_, bf16[8,2048]{1,0:T(8,128)(2,1)S(1)} %collective-permute-done.4.refs_2_.refs_1_), custom_call_target="tpu_custom_call" | custom-call | flops 134217728 | bytes 8388608 | tf_op jit(solution)/shard_map/project_out/pallas_call | solution.py:338
  24.7 0.0 collective-permute-done.5.arrived.refs_0_
  24.8 0.0 copy-start.2
  24.8 2.7 %collective-permute-start.6 = (bf16[16,2048]{1,0:T(8,128)(2,1)S(1)}, bf16[16,2048]{1,0:T(8,128)(2,1)S(1)}, u32[]{:S(2)}, u32[]{:S(2)}) collective-permute-start(bf16[16,2048]{1,0:T(8,128)(2,1)S(1)} %add_near.2.refs_0_), channel_id=1, source_target_pairs={{0,2},{1,3},{2,0},{3,1},{4,6},{5,7},{6,4},{7,5},{8,10},{9,11},{10,... | collective-permute-start | bytes 196616 | tf_op jit(solution)/shard_map/ppermute | solution.py:246
  27.4 1.2 %project_out.6.own = f32[16,2048]{1,0:T(8,128)S(1)} custom-call(bf16[2048,4096]{1,0:T(8,128)(2,1)S(1)} %bitcast.2, bf16[16,2048]{1,0:T(8,128)(2,1)S(1)} %collective-permute-done.5.arrived.refs_0_, bf16[8,2048]{1,0:T(8,128)(2,1)S(1)} %collective-permute-done.3.refs_0_.refs_1_, bf16[8,2048]{1,0:T(8,128)(2,1)S(1)} %collective-permute-done.8.refs_2_.refs_1_), custom_call_target="tpu_custom_call" | custom-call | flops 134217728 | bytes 8388608 | tf_op jit(solution)/shard_map/project_out/pallas_call | solution.py:338
  28.6 0.0 collective-permute-done.9.arrived
  28.6 0.9 %collective-permute-start.10 = (bf16[16,2048]{1,0:T(8,128)(2,1)S(1)}, bf16[16,2048]{1,0:T(8,128)(2,1)S(1)}, u32[]{:S(2)}, u32[]{:S(2)}) collective-permute-start(bf16[16,2048]{1,0:T(8,128)(2,1)S(1)} %add_near.3.refs_0_), channel_id=1, source_target_pairs={{0,2},{1,3},{2,0},{3,1},{4,6},{5,7},{6,4},{7,5},{8,10},{9,11},{10,... | collective-permute-start | bytes 196616 | tf_op jit(solution)/shard_map/ppermute | solution.py:246
  29.5 1.1 %collective-permute-done.6.refs_1_ = bf16[16,2048]{1,0:T(8,128)(2,1)S(1)} collective-permute-done((bf16[16,2048]{1,0:T(8,128)(2,1)S(1)}, bf16[16,2048]{1,0:T(8,128)(2,1)S(1)}, u32[]{:S(2)}, u32[]{:S(2)}) %collective-permute-start.6) | collective-permute-done | bytes 65568 | tf_op jit(solution)/shard_map/ppermute | solution.py:246
  30.6 0.0 copy-done.2
  30.6 0.1 finish.2.refs_0_
  30.6 0.9 %collective-permute-start.7 = (bf16[16,2048]{1,0:T(8,128)(2,1)S(1)}, bf16[16,2048]{1,0:T(8,128)(2,1)S(1)}, u32[]{:S(2)}, u32[]{:S(2)}) collective-permute-start(bf16[16,2048]{1,0:T(8,128)(2,1)S(1)} %finish.2.refs_0_), channel_id=1, source_target_pairs={{0,1},{1,0},{2,3},{3,2},{4,5},{5,4},{6,7},{7,6},{8,9},{9,8},{10,11... | collective-permute-start | bytes 196616 | tf_op jit(solution)/shard_map/ppermute | solution.py:246
  31.6 2.9 %collective-permute-done.10.refs_1_ = bf16[16,2048]{1,0:T(8,128)(2,1)S(1)} collective-permute-done((bf16[16,2048]{1,0:T(8,128)(2,1)S(1)}, bf16[16,2048]{1,0:T(8,128)(2,1)S(1)}, u32[]{:S(2)}, u32[]{:S(2)}) %collective-permute-start.10) | collective-permute-done | bytes 65568 | tf_op jit(solution)/shard_map/ppermute | solution.py:246
  34.5 0.1 finish.3.refs_2_
  34.6 0.2 collective-permute-start.11
  34.7 0.9 %collective-permute-done.7.refs_1_ = bf16[16,2048]{1,0:T(8,128)(2,1)S(1)} collective-permute-done((bf16[16,2048]{1,0:T(8,128)(2,1)S(1)}, bf16[16,2048]{1,0:T(8,128)(2,1)S(1)}, u32[]{:S(2)}, u32[]{:S(2)}) %collective-permute-start.7) | collective-permute-done | bytes 65568 | tf_op jit(solution)/shard_map/ppermute | solution.py:246
  35.7 3.2 %collective-permute-done.11.refs_3_ = bf16[16,2048]{1,0:T(8,128)(2,1)S(1)} collective-permute-done((bf16[16,2048]{1,0:T(8,128)(2,1)S(1)}, bf16[16,2048]{1,0:T(8,128)(2,1)S(1)}, u32[]{:S(2)}, u32[]{:S(2)}) %collective-permute-start.11) | collective-permute-done | bytes 65568 | tf_op jit(solution)/shard_map/ppermute | solution.py:246
  38.9 0.7 %assemble.1 = bf16[32,4096]{1,0:T(8,128)(2,1)} custom-call(bf16[16,2048]{1,0:T(8,128)(2,1)S(1)} %finish.2.refs_0_, bf16[16,2048]{1,0:T(8,128)(2,1)S(1)} %collective-permute-done.7.refs_1_, bf16[16,2048]{1,0:T(8,128)(2,1)S(1)} %finish.3.refs_2_, bf16[16,2048]{1,0:T(8,128)(2,1)S(1)} %collective-permute-done.11.refs_3_), custom_call_target="tpu_custom_call" | custom-call | tf_op jit(solution)/shard_map/assemble/pallas_call | solution.py:378
  (17 shorter events, 0.2 us)
Async XLA Ops:
  6.9 3.4 %copy-start.3 = (s32[8]{0:T(128)S(1)}, s32[8]{0:T(128)}, u32[]{:S(2)}) copy-start(s32[8]{0:T(128)} %param.17) | copy-start | bytes 100
  6.9 3.6 %copy-start = (bf16[8,2048,128]{2,1,0:T(8,128)(2,1)S(1)}, bf16[8,2048,128]{2,1,0:T(8,128)(2,1)}, u32[]{:S(2)}) copy-start(bf16[8,2048,128]{2,1,0:T(8,128)(2,1)} %v.3) | copy-start | bytes 12582916
  7.0 3.6 %copy-start.1 = (bf16[8,2048,128]{2,1,0:T(8,128)(2,1)S(1)}, bf16[8,2048,128]{2,1,0:T(8,128)(2,1)}, u32[]{:S(2)}) copy-start(bf16[8,2048,128]{2,1,0:T(8,128)(2,1)} %k.1) | copy-start | bytes 12582916
  7.0 4.7 %collective-permute-start.2 = (f16[8,2432]{1,0:T(8,128)(2,1)S(1)}, f16[8,2432]{1,0:T(8,128)(2,1)S(1)}, u32[]{:S(2)}, u32[]{:S(2)}) collective-permute-start(f16[8,2432]{1,0:T(8,128)(2,1)S(1)} %convert_element_type.26), channel_id=1, source_target_pairs={{0,12},{4,8},{8,4},{12,0},{1,13},{5,9},{9,5},{13,1},{2,14},{6,10},... | collective-permute-start | bytes 116744 | tf_op jit(solution)/shard_map/ppermute | solution.py:246
  9.5 4.2 %collective-permute-start.1 = (f16[8,2432]{1,0:T(8,128)(2,1)S(1)}, f16[8,2432]{1,0:T(8,128)(2,1)S(1)}, u32[]{:S(2)}, u32[]{:S(2)}) collective-permute-start(f16[8,2432]{1,0:T(8,128)(2,1)S(1)} %convert_element_type.24), channel_id=1, source_target_pairs={{0,8},{4,12},{8,0},{12,4},{1,9},{5,13},{9,1},{13,5},{2,10},{6,14},... | collective-permute-start | bytes 116744 | tf_op jit(solution)/shard_map/ppermute | solution.py:246
  10.1 3.5 %collective-permute-start = (f16[8,2432]{1,0:T(8,128)(2,1)S(1)}, f16[8,2432]{1,0:T(8,128)(2,1)S(1)}, u32[]{:S(2)}, u32[]{:S(2)}) collective-permute-start(f16[8,2432]{1,0:T(8,128)(2,1)S(1)} %convert_element_type.22), channel_id=1, source_target_pairs={{0,4},{4,0},{8,12},{12,8},{1,5},{5,1},{9,13},{13,9},{2,6},{6,2},{1... | collective-permute-start | bytes 116744 | tf_op jit(solution)/shard_map/ppermute | solution.py:246
  10.5 7.3 %slice-start = ((s8[16777216]{0:T(1024)(128)(4,1)}), s8[4194304]{0:T(1024)(128)(4,1)S(1)}, s32[]{:S(2)}) async-start(s8[16777216]{0:T(1024)(128)(4,1)} %bitcast.1), calls=%async_computation | async-start | bytes 8388608
  10.5 7.3 %slice-start.1 = ((s8[16777216]{0:T(1024)(128)(4,1)}), s8[4194304]{0:T(1024)(128)(4,1)S(1)}, s32[]{:S(2)}) async-start(s8[16777216]{0:T(1024)(128)(4,1)} %bitcast.1), calls=%async_computation.1 | async-start | bytes 8388608
  13.7 4.1 %slice-start.2 = ((s8[16777216]{0:T(1024)(128)(4,1)}), s8[4194304]{0:T(1024)(128)(4,1)S(1)}, s32[]{:S(2)}) async-start(s8[16777216]{0:T(1024)(128)(4,1)} %bitcast.1), calls=%async_computation.2 | async-start | bytes 8388608
  13.8 4.1 %slice-start.3 = ((s8[16777216]{0:T(1024)(128)(4,1)}), s8[4194304]{0:T(1024)(128)(4,1)S(1)}, s32[]{:S(2)}) async-start(s8[16777216]{0:T(1024)(128)(4,1)} %bitcast.1), calls=%async_computation.3 | async-start | bytes 8388608
  15.6 2.2 %collective-permute-start.4 = (bf16[8,2048]{1,0:T(8,128)(2,1)S(1)}, bf16[8,2048]{1,0:T(8,128)(2,1)S(1)}, u32[]{:S(2)}, u32[]{:S(2)}) collective-permute-start(bf16[8,2048]{1,0:T(8,128)(2,1)S(1)} %attention.1.refs_1_.refs_0_), channel_id=1, source_target_pairs={{0,4},{4,0},{8,12},{12,8},{1,5},{5,1},{9,13},{13,9},{2,6},{6,2},{1... | collective-permute-start | bytes 98312 | tf_op jit(solution)/shard_map/ppermute | solution.py:246
  15.7 5.0 %collective-permute-start.8 = (bf16[8,2048]{1,0:T(8,128)(2,1)S(1)}, bf16[8,2048]{1,0:T(8,128)(2,1)S(1)}, u32[]{:S(2)}, u32[]{:S(2)}) collective-permute-start(bf16[8,2048]{1,0:T(8,128)(2,1)S(1)} %attention.1.refs_1_.refs_0_), channel_id=1, source_target_pairs={{0,12},{4,8},{8,4},{12,0},{1,13},{5,9},{9,5},{13,1},{2,14},{6,10},... | collective-permute-start | bytes 98312 | tf_op jit(solution)/shard_map/ppermute | solution.py:246
  16.8 3.9 %collective-permute-start.3 = (bf16[8,2048]{1,0:T(8,128)(2,1)S(1)}, bf16[8,2048]{1,0:T(8,128)(2,1)S(1)}, u32[]{:S(2)}, u32[]{:S(2)}) collective-permute-start(bf16[8,2048]{1,0:T(8,128)(2,1)S(1)} %attention.1.refs_1_.refs_0_), channel_id=1, source_target_pairs={{0,8},{4,12},{8,0},{12,4},{1,9},{5,13},{9,1},{13,5},{2,10},{6,14},... | collective-permute-start | bytes 98312 | tf_op jit(solution)/shard_map/ppermute | solution.py:246
  19.0 5.7 %collective-permute-start.5 = (bf16[16,2048]{1,0:T(8,128)(2,1)S(1)}, bf16[16,2048]{1,0:T(8,128)(2,1)S(1)}, u32[]{:S(2)}, u32[]{:S(2)}) collective-permute-start(bf16[16,2048]{1,0:T(8,128)(2,1)S(1)} %project_out.5), channel_id=1, source_target_pairs={{0,1},{1,0},{2,3},{3,2},{4,5},{5,4},{6,7},{7,6},{8,9},{9,8},{10,11... | collective-permute-start | bytes 196616 | tf_op jit(solution)/shard_map/ppermute | solution.py:246
  21.9 6.7 %collective-permute-start.9 = (bf16[16,2048]{1,0:T(8,128)(2,1)S(1)}, bf16[16,2048]{1,0:T(8,128)(2,1)S(1)}, u32[]{:S(2)}, u32[]{:S(2)}) collective-permute-start(bf16[16,2048]{1,0:T(8,128)(2,1)S(1)} %project_out.7), channel_id=1, source_target_pairs={{0,1},{1,0},{2,3},{3,2},{4,5},{5,4},{6,7},{7,6},{8,9},{9,8},{10,11... | collective-permute-start | bytes 196616 | tf_op jit(solution)/shard_map/ppermute | solution.py:246
  24.8 5.8 %copy-start.2 = (bf16[32,4096]{1,0:T(8,128)(2,1)S(1)}, bf16[32,4096]{1,0:T(8,128)(2,1)}, u32[]{:S(2)}) copy-start(bf16[32,4096]{1,0:T(8,128)(2,1)} %x.3) | copy-start | bytes 786436
  24.8 5.8 %collective-permute-start.6 = (bf16[16,2048]{1,0:T(8,128)(2,1)S(1)}, bf16[16,2048]{1,0:T(8,128)(2,1)S(1)}, u32[]{:S(2)}, u32[]{:S(2)}) collective-permute-start(bf16[16,2048]{1,0:T(8,128)(2,1)S(1)} %add_near.2.refs_0_), channel_id=1, source_target_pairs={{0,2},{1,3},{2,0},{3,1},{4,6},{5,7},{6,4},{7,5},{8,10},{9,11},{10,... | collective-permute-start | bytes 196616 | tf_op jit(solution)/shard_map/ppermute | solution.py:246
  28.6 5.9 %collective-permute-start.10 = (bf16[16,2048]{1,0:T(8,128)(2,1)S(1)}, bf16[16,2048]{1,0:T(8,128)(2,1)S(1)}, u32[]{:S(2)}, u32[]{:S(2)}) collective-permute-start(bf16[16,2048]{1,0:T(8,128)(2,1)S(1)} %add_near.3.refs_0_), channel_id=1, source_target_pairs={{0,2},{1,3},{2,0},{3,1},{4,6},{5,7},{6,4},{7,5},{8,10},{9,11},{10,... | collective-permute-start | bytes 196616 | tf_op jit(solution)/shard_map/ppermute | solution.py:246
  30.6 5.0 %collective-permute-start.7 = (bf16[16,2048]{1,0:T(8,128)(2,1)S(1)}, bf16[16,2048]{1,0:T(8,128)(2,1)S(1)}, u32[]{:S(2)}, u32[]{:S(2)}) collective-permute-start(bf16[16,2048]{1,0:T(8,128)(2,1)S(1)} %finish.2.refs_0_), channel_id=1, source_target_pairs={{0,1},{1,0},{2,3},{3,2},{4,5},{5,4},{6,7},{7,6},{8,9},{9,8},{10,11... | collective-permute-start | bytes 196616 | tf_op jit(solution)/shard_map/ppermute | solution.py:246
  34.6 4.3 %collective-permute-start.11 = (bf16[16,2048]{1,0:T(8,128)(2,1)S(1)}, bf16[16,2048]{1,0:T(8,128)(2,1)S(1)}, u32[]{:S(2)}, u32[]{:S(2)}) collective-permute-start(bf16[16,2048]{1,0:T(8,128)(2,1)S(1)} %finish.3.refs_2_), channel_id=1, source_target_pairs={{0,1},{1,0},{2,3},{3,2},{4,5},{5,4},{6,7},{7,6},{8,9},{9,8},{10,11... | collective-permute-start | bytes 196616 | tf_op jit(solution)/shard_map/ppermute | solution.py:246

commit v21 on v18

--- a/solution.py
+++ b/solution.py
@@ -43,12 +43,12 @@
 
 
 def project(x_hbm, gain_hbm, wq_hbm, wk_hbm, wv_hbm, *refs):
-    total, x, gain, wq, wk, wv, scaled, sems = refs
+    total, x, gain, wq, wkv, scaled, sems = refs
     depth = x.shape[1]
     cuts = [*range(0, depth, 2 * CHUNK), depth - CHUNK, depth]
     spans = [slice(a, b) for a, b in zip(cuts, cuts[1:])]
     steps = len(spans)
-    pairs = [(x_hbm, x), (gain_hbm, gain), (wk_hbm, wk), (wv_hbm, wv)]
+    pairs = [(x_hbm, x), (gain_hbm, gain), (wk_hbm, wkv.at[:, :HD]), (wv_hbm, wkv.at[:, HD:])]
     small = [pltpu.make_async_copy(a, b, sems.at[steps + i]) for i, (a, b) in enumerate(pairs)]
     large = []
     for step, span in enumerate(spans):
@@ -79,9 +79,8 @@
             total[:, :width] += term
         if step == 1:
             small[2].wait()
-            total[:, width : width + HD] = dot(scaled[...], wk[...])
             small[3].wait()
-            total[:, width + HD : width + 2 * HD] = dot(scaled[...], wv[...])
+            total[:, width : width + 2 * HD] = dot(scaled[...], wkv[...])
             total[:, width + 2 * HD :] = jnp.broadcast_to(squares, (squares.shape[0], HD))
 
 
@@ -103,8 +102,8 @@
             out[...] = part
 
 
-def turn_keys(after, k, v, k_turned):
-    del after, v
+def turn_keys(after, k, v, limits, k_turned):
+    del after, v, limits
     rows, slots = k.shape[0], k.shape[1]
     for row in range(rows):
         for start in range(0, slots, CHUNK):
@@ -264,8 +263,7 @@
                 pltpu.VMEM(inputs.shape, BF16),
                 pltpu.VMEM((1, depth), F32),
                 pltpu.VMEM(w_query.shape, BF16),
-                pltpu.VMEM(w_key.shape, BF16),
-                pltpu.VMEM(w_value.shape, BF16),
+                pltpu.VMEM((depth, 2 * HD), BF16),
                 pltpu.VMEM(inputs.shape, BF16),
                 sems(depth // (2 * CHUNK) + 5),
             ],
@@ -286,15 +284,16 @@
             arrived.append(swap(sums[mask].astype(F16), "gx", size_x, mask).astype(F32))
 
         values = in_vmem(value_cache)
+        limits = jnp.broadcast_to(lengths[:, None], (rows, HD))
         keys = pl.pallas_call(
             turn_keys,
             out_shape=pltpu.VMEM((rows, HD, key_cache.shape[1]), BF16),
-            in_specs=[ANY, VMEM, ANY],
+            in_specs=[ANY, VMEM, ANY, ANY],
             out_specs=VMEM,
             compiler_params=params(4),
             cost_estimate=cost(0, 2 * key_cache.size),
             name="turn_keys",
-        )(sums[0], in_vmem(key_cache), values)
+        )(sums[0], in_vmem(key_cache), values, limits)
 
         half = HD // 2
         inverse = ROPE_BASE ** (-(jnp.arange(half, dtype=F32) * 2.0 / HD))
@@ -316,7 +315,7 @@
             name="attention",
         )(
             in_hbm(w_query),
-            jnp.broadcast_to(lengths[:, None], (rows, HD)),
+            limits,
             jnp.concatenate([cosine, cosine], 1),
             jnp.concatenate([-sine, sine], 1),
             in_vmem(keys),

time: 39.1 us -> 39 us (level)
  no operation moved by 1% of the time
where the time goes in v21:
time: 39 us; the launch traced here: 38.9 us
  Pallas kernels  14.7 us (38%)
  starting transfers between devices  14.6 us (37%)
  waiting for transfers between devices  8.99 us (23%)
    ppermute x12, starting transfers between devices, swap(): return lax.ppermute(value, axis, [(i, i ^ mask) for i in range(size)])  14.6 us
    ppermute x12, waiting for transfers between devices, swap(): return lax.ppermute(value, axis, [(i, i ^ mask) for i in range(size)])  8.99 us
    pallas_call x1, Pallas kernels, shards(): pl.pallas_call(project, out_shape=pltpu.VMEM((batch, packed), F32), in_sp...  6.92 us
    pallas_call x3, Pallas kernels, product(): pl.pallas_call(functools.partial(project_out, chunk, given), out_shape=pl...  2.47 us
    pallas_call x1, Pallas kernels, shards(): pl.pallas_call(functools.partial(attention, size_x, depth * size_x), out_...  1.82 us
    pallas_call x1, Pallas kernels, shards(): pl.pallas_call(turn_keys, out_shape=pltpu.VMEM((rows, HD, key_cache.shape...  1.13 us
    pallas_call x1, Pallas kernels, shards(): pl.pallas_call(project_first, out_shape=[pltpu.VMEM((batch, block), BF16)...  0.83 us
  transfers between devices with their start and end apart: 12, of which 8 were waited for; matrix products, arithmetic and copies ran while one was open for 1% of the time, Pallas kernels for 11%

profile of v21, /device:TPU:0, one launch (start us, length us, event | category | flops | bytes accessed | tf_op | source)
XLA Modules:
  0.0 38.9 jit_solution(411090231018184826)
XLA Ops:
  0.0 6.9 %project.1.total = f32[32,2432]{1,0:T(8,128)S(1)} custom-call(bf16[32,4096]{1,0:T(8,128)(2,1)} %x.3, f32[1,4096]{1,0:T(1,128)} %bitcast.3, bf16[4096,2048]{1,0:T(8,128)(2,1)} %weights.3, bf16[4096,128]{1,0:T(8,128)(2,1)} %wk_hbm.1, bf16[4096,128]{1,0:T(8,128)(2,1)} %wv_hbm.1), custom_call_target="tpu_custom_call" | custom-call | flops 637534208 | bytes 19922944 | tf_op jit(solution)/shard_map/project/pallas_call | solution.py:257
  6.9 0.0 copy-start.3
  6.9 0.0 copy-start
  7.0 0.0 copy-start.1
  7.0 2.4 %collective-permute-start.2 = (f16[8,2432]{1,0:T(8,128)(2,1)S(1)}, f16[8,2432]{1,0:T(8,128)(2,1)S(1)}, u32[]{:S(2)}, u32[]{:S(2)}) collective-permute-start(f16[8,2432]{1,0:T(8,128)(2,1)S(1)} %convert_element_type.26), channel_id=1, source_target_pairs={{0,12},{4,8},{8,4},{12,0},{1,13},{5,9},{9,5},{13,1},{2,14},{6,10},... | collective-permute-start | bytes 116744 | tf_op jit(solution)/shard_map/ppermute | solution.py:242
  9.5 0.6 %collective-permute-start.1 = (f16[8,2432]{1,0:T(8,128)(2,1)S(1)}, f16[8,2432]{1,0:T(8,128)(2,1)S(1)}, u32[]{:S(2)}, u32[]{:S(2)}) collective-permute-start(f16[8,2432]{1,0:T(8,128)(2,1)S(1)} %convert_element_type.24), channel_id=1, source_target_pairs={{0,8},{4,12},{8,0},{12,4},{1,9},{5,13},{9,1},{13,5},{2,10},{6,14},... | collective-permute-start | bytes 116744 | tf_op jit(solution)/shard_map/ppermute | solution.py:242
  10.1 0.2 collective-permute-start
  10.3 0.0 copy-done.3
  10.3 0.1 fusion
  10.4 0.1 pad_maximum_fusion
  10.5 0.1 broadcast_in_dim.2.limits.lengths
  10.6 0.0 copy-done
  10.6 0.0 copy-done.1
  10.6 0.0 slice-start.1
  10.6 1.1 %turn_keys.1.k = bf16[8,128,2048]{2,1,0:T(8,128)(2,1)S(1)} custom-call(f32[8,2432]{1,0:T(8,128)S(1)} %get-tuple-element.11.after.refs_0_, bf16[8,2048,128]{2,1,0:T(8,128)(2,1)S(1)} %copy-done.1, bf16[8,2048,128]{2,1,0:T(8,128)(2,1)S(1)} %copy-done, s32[8,128]{1,0:T(8,128)S(1)} %broadcast_in_dim.2.limits.lengths), custom_call_target="tpu_custom_call" | custom-call | bytes 4194304 | tf_op jit(solution)/shard_map/turn_keys/pallas_call | solution.py:288
  11.7 0.0 collective-permute-done.2
  11.8 1.9 %collective-permute-done.1 = f16[8,2432]{1,0:T(8,128)(2,1)S(1)} collective-permute-done((f16[8,2432]{1,0:T(8,128)(2,1)S(1)}, f16[8,2432]{1,0:T(8,128)(2,1)S(1)}, u32[]{:S(2)}, u32[]{:S(2)}) %collective-permute-start.1) | collective-permute-done | bytes 38944 | tf_op jit(solution)/shard_map/ppermute | solution.py:242
  13.7 0.0 collective-permute-done
  13.7 0.0 slice-start.2
  13.7 0.0 slice-start.3
  13.7 1.8 %attention.1.refs_0_ = bf16[8,2048]{1,0:T(8,128)(2,1)S(1)} custom-call(bf16[4096,2048]{1,0:T(8,128)(2,1)} %weights.3, s32[8,128]{1,0:T(8,128)S(1)} %broadcast_in_dim.2.limits.lengths, f32[8,128]{1,0:T(8,128)S(1)} %get-tuple-element.20.cosine, f32[8,128]{1,0:T(8,128)S(1)} %get-tuple-element.21.sine, bf16[8,128,2048]{2,1,0:T(8,128)(2,1)S(1)} %turn_keys.1.k, ...), custom_call_target="tpu_custom_call" | custom-call | flops 134217728 | bytes 8388608 | tf_op jit(solution)/shard_map/attention/pallas_call | solution.py:303
  15.5 0.8 %collective-permute-start.5 = (bf16[8,2048]{1,0:T(8,128)(2,1)S(1)}, bf16[8,2048]{1,0:T(8,128)(2,1)S(1)}, u32[]{:S(2)}, u32[]{:S(2)}) collective-permute-start(bf16[8,2048]{1,0:T(8,128)(2,1)S(1)} %attention.1.refs_0_), channel_id=1, source_target_pairs={{0,12},{4,8},{8,4},{12,0},{1,13},{5,9},{9,5},{13,1},{2,14},{6,10},... | collective-permute-start | bytes 98312 | tf_op jit(solution)/shard_map/ppermute | solution.py:242
  16.3 0.7 %collective-permute-start.4 = (bf16[8,2048]{1,0:T(8,128)(2,1)S(1)}, bf16[8,2048]{1,0:T(8,128)(2,1)S(1)}, u32[]{:S(2)}, u32[]{:S(2)}) collective-permute-start(bf16[8,2048]{1,0:T(8,128)(2,1)S(1)} %attention.1.refs_0_), channel_id=1, source_target_pairs={{0,8},{4,12},{8,0},{12,4},{1,9},{5,13},{9,1},{13,5},{2,10},{6,14},... | collective-permute-start | bytes 98312 | tf_op jit(solution)/shard_map/ppermute | solution.py:242
  17.0 0.4 %collective-permute-start.3 = (bf16[8,2048]{1,0:T(8,128)(2,1)S(1)}, bf16[8,2048]{1,0:T(8,128)(2,1)S(1)}, u32[]{:S(2)}, u32[]{:S(2)}) collective-permute-start(bf16[8,2048]{1,0:T(8,128)(2,1)S(1)} %attention.1.refs_0_), channel_id=1, source_target_pairs={{0,4},{4,0},{8,12},{12,8},{1,5},{5,1},{9,13},{13,9},{2,6},{6,2},{1... | collective-permute-start | bytes 98312 | tf_op jit(solution)/shard_map/ppermute | solution.py:242
  17.5 1.8 %collective-permute-done.5.refs_3_ = bf16[8,2048]{1,0:T(8,128)(2,1)S(1)} collective-permute-done((bf16[8,2048]{1,0:T(8,128)(2,1)S(1)}, bf16[8,2048]{1,0:T(8,128)(2,1)S(1)}, u32[]{:S(2)}, u32[]{:S(2)}) %collective-permute-start.5) | collective-permute-done | bytes 32800 | tf_op jit(solution)/shard_map/ppermute | solution.py:242
  19.3 1.0 %collective-permute-done.4.refs_2_ = bf16[8,2048]{1,0:T(8,128)(2,1)S(1)} collective-permute-done((bf16[8,2048]{1,0:T(8,128)(2,1)S(1)}, bf16[8,2048]{1,0:T(8,128)(2,1)S(1)}, u32[]{:S(2)}, u32[]{:S(2)}) %collective-permute-start.4) | collective-permute-done | bytes 32800 | tf_op jit(solution)/shard_map/ppermute | solution.py:242
  20.3 0.0 collective-permute-done.3.refs_1_
  20.3 0.0 slice-done
  20.3 0.8 %project_first.1 = (bf16[32,1024]{1,0:T(8,128)(2,1)S(1)}, bf16[32,2048]{1,0:T(8,128)(2,1)S(1)}) custom-call(bf16[2048,4096]{1,0:T(8,128)(2,1)S(1)} %bitcast.2, bf16[8,2048]{1,0:T(8,128)(2,1)S(1)} %attention.1.refs_0_, bf16[8,2048]{1,0:T(8,128)(2,1)S(1)} %collective-permute-done.3.refs_1_, bf16[8,2048]{1,0:T(8,128)(2,1)S(1)} %collective-permute-done.4.refs_2_, ...), custom_call_target="tpu_custom_call" | custom-call | flops 134217728 | bytes 4194304 | tf_op jit(solution)/shard_map/project_first/pallas_call | solution.py:331
  21.1 1.6 %collective-permute-start.9 = (bf16[32,1024]{1,0:T(8,128)(2,1)S(1)}, bf16[32,1024]{1,0:T(8,128)(2,1)S(1)}, u32[]{:S(2)}, u32[]{:S(2)}) collective-permute-start(bf16[32,1024]{1,0:T(8,128)(2,1)S(1)} %get-tuple-element.16), channel_id=1, source_target_pairs={{0,1},{1,0},{2,3},{3,2},{4,5},{5,4},{6,7},{7,6},{8,9},{9,8},{10,11... | collective-permute-start | bytes 196616 | tf_op jit(solution)/shard_map/ppermute | solution.py:242
  22.8 0.8 %project_out.4 = bf16[32,1024]{1,0:T(8,128)(2,1)S(1)} custom-call(bf16[2048,4096]{1,0:T(8,128)(2,1)S(1)} %bitcast.2, bf16[32,2048]{1,0:T(8,128)(2,1)S(1)} %get-tuple-element.15.heads), custom_call_target="tpu_custom_call" | custom-call | flops 134217728 | bytes 4194304 | tf_op jit(solution)/shard_map/project_out/pallas_call | solution.py:343
  23.6 0.5 %collective-permute-start.6 = (bf16[32,1024]{1,0:T(8,128)(2,1)S(1)}, bf16[32,1024]{1,0:T(8,128)(2,1)S(1)}, u32[]{:S(2)}, u32[]{:S(2)}) collective-permute-start(bf16[32,1024]{1,0:T(8,128)(2,1)S(1)} %project_out.4), channel_id=1, source_target_pairs={{0,1},{1,0},{2,3},{3,2},{4,5},{5,4},{6,7},{7,6},{8,9},{9,8},{10,11... | collective-permute-start | bytes 196616 | tf_op jit(solution)/shard_map/ppermute | solution.py:242
  24.0 0.8 %project_out.5.own = f32[32,1024]{1,0:T(8,128)S(1)} custom-call(bf16[2048,4096]{1,0:T(8,128)(2,1)S(1)} %bitcast.2, bf16[32,2048]{1,0:T(8,128)(2,1)S(1)} %get-tuple-element.15.heads), custom_call_target="tpu_custom_call" | custom-call | flops 134217728 | bytes 4194304 | tf_op jit(solution)/shard_map/project_out/pallas_call | solution.py:343
  24.9 0.8 %project_out.3.own = f32[32,1024]{1,0:T(8,128)S(1)} custom-call(bf16[2048,4096]{1,0:T(8,128)(2,1)S(1)} %bitcast.2, bf16[32,2048]{1,0:T(8,128)(2,1)S(1)} %get-tuple-element.15.heads), custom_call_target="tpu_custom_call" | custom-call | flops 134217728 | bytes 4194304 | tf_op jit(solution)/shard_map/project_out/pallas_call | solution.py:343
  25.7 0.1 collective-permute-done.9.arrived
  25.8 2.7 %collective-permute-start.10 = (bf16[32,1024]{1,0:T(8,128)(2,1)S(1)}, bf16[32,1024]{1,0:T(8,128)(2,1)S(1)}, u32[]{:S(2)}, u32[]{:S(2)}) collective-permute-start(bf16[32,1024]{1,0:T(8,128)(2,1)S(1)} %add_near.3.refs_0_), channel_id=1, source_target_pairs={{0,2},{1,3},{2,0},{3,1},{4,6},{5,7},{6,4},{7,5},{8,10},{9,11},{10,... | collective-permute-start | bytes 196616 | tf_op jit(solution)/shard_map/ppermute | solution.py:242
  28.5 0.0 collective-permute-done.6.arrived
  28.5 2.6 %collective-permute-start.7 = (bf16[32,1024]{1,0:T(8,128)(2,1)S(1)}, bf16[32,1024]{1,0:T(8,128)(2,1)S(1)}, u32[]{:S(2)}, u32[]{:S(2)}) collective-permute-start(bf16[32,1024]{1,0:T(8,128)(2,1)S(1)} %add_near.2.refs_0_), channel_id=1, source_target_pairs={{0,2},{1,3},{2,0},{3,1},{4,6},{5,7},{6,4},{7,5},{8,10},{9,11},{10,... | collective-permute-start | bytes 196616 | tf_op jit(solution)/shard_map/ppermute | solution.py:242
  31.1 2.0 %collective-permute-done.10.refs_1_ = bf16[32,1024]{1,0:T(8,128)(2,1)S(1)} collective-permute-done((bf16[32,1024]{1,0:T(8,128)(2,1)S(1)}, bf16[32,1024]{1,0:T(8,128)(2,1)S(1)}, u32[]{:S(2)}, u32[]{:S(2)}) %collective-permute-start.10) | collective-permute-done | bytes 65568 | tf_op jit(solution)/shard_map/ppermute | solution.py:242
  33.1 0.0 copy-done.2
  33.1 0.1 finish.3.refs_0_
  33.1 0.2 collective-permute-start.11
  33.3 0.5 %collective-permute-done.7.refs_1_ = bf16[32,1024]{1,0:T(8,128)(2,1)S(1)} collective-permute-done((bf16[32,1024]{1,0:T(8,128)(2,1)S(1)}, bf16[32,1024]{1,0:T(8,128)(2,1)S(1)}, u32[]{:S(2)}, u32[]{:S(2)}) %collective-permute-start.7) | collective-permute-done | bytes 65568 | tf_op jit(solution)/shard_map/ppermute | solution.py:242
  33.9 1.9 %collective-permute-start.8 = (bf16[32,1024]{1,0:T(8,128)(2,1)S(1)}, bf16[32,1024]{1,0:T(8,128)(2,1)S(1)}, u32[]{:S(2)}, u32[]{:S(2)}) collective-permute-start(bf16[32,1024]{1,0:T(8,128)(2,1)S(1)} %finish.2.refs_2_), channel_id=1, source_target_pairs={{0,1},{1,0},{2,3},{3,2},{4,5},{5,4},{6,7},{7,6},{8,9},{9,8},{10,11... | collective-permute-start | bytes 196616 | tf_op jit(solution)/shard_map/ppermute | solution.py:242
  35.8 1.7 %collective-permute-done.11.refs_1_ = bf16[32,1024]{1,0:T(8,128)(2,1)S(1)} collective-permute-done((bf16[32,1024]{1,0:T(8,128)(2,1)S(1)}, bf16[32,1024]{1,0:T(8,128)(2,1)S(1)}, u32[]{:S(2)}, u32[]{:S(2)}) %collective-permute-start.11) | collective-permute-done | bytes 65568 | tf_op jit(solution)/shard_map/ppermute | solution.py:242
  37.4 0.7 %write_most.1.refs_1_ = bf16[32,4096]{1,0:T(8,128)(2,1)} custom-call(bf16[32,1024]{1,0:T(8,128)(2,1)S(1)} %finish.3.refs_0_, bf16[32,1024]{1,0:T(8,128)(2,1)S(1)} %collective-permute-done.11.refs_1_, bf16[32,1024]{1,0:T(8,128)(2,1)S(1)} %finish.2.refs_2_), custom_call_target="tpu_custom_call" | custom-call | tf_op jit(solution)/shard_map/write_most/pallas_call | solution.py:376
  38.1 0.1 collective-permute-done.8.refs_0_
  38.2 0.6 %write_last.1 = bf16[32,4096]{1,0:T(8,128)(2,1)} custom-call(bf16[32,1024]{1,0:T(8,128)(2,1)S(1)} %collective-permute-done.8.refs_0_, bf16[32,4096]{1,0:T(8,128)(2,1)} %write_most.1.refs_1_), custom_call_target="tpu_custom_call", output_to_operand_aliasing={{}: (1, {})} | custom-call | tf_op jit(solution)/shard_map/write_last/pallas_call | solution.py:385
  (18 shorter events, 0.2 us)
Async XLA Ops:
  6.9 3.4 %copy-start.3 = (s32[8]{0:T(128)S(1)}, s32[8]{0:T(128)}, u32[]{:S(2)}) copy-start(s32[8]{0:T(128)} %param.17) | copy-start | bytes 100
  6.9 3.7 %copy-start = (bf16[8,2048,128]{2,1,0:T(8,128)(2,1)S(1)}, bf16[8,2048,128]{2,1,0:T(8,128)(2,1)}, u32[]{:S(2)}) copy-start(bf16[8,2048,128]{2,1,0:T(8,128)(2,1)} %v.3) | copy-start | bytes 12582916
  7.0 3.6 %copy-start.1 = (bf16[8,2048,128]{2,1,0:T(8,128)(2,1)S(1)}, bf16[8,2048,128]{2,1,0:T(8,128)(2,1)}, u32[]{:S(2)}) copy-start(bf16[8,2048,128]{2,1,0:T(8,128)(2,1)} %k.1) | copy-start | bytes 12582916
  7.0 4.7 %collective-permute-start.2 = (f16[8,2432]{1,0:T(8,128)(2,1)S(1)}, f16[8,2432]{1,0:T(8,128)(2,1)S(1)}, u32[]{:S(2)}, u32[]{:S(2)}) collective-permute-start(f16[8,2432]{1,0:T(8,128)(2,1)S(1)} %convert_element_type.26), channel_id=1, source_target_pairs={{0,12},{4,8},{8,4},{12,0},{1,13},{5,9},{9,5},{13,1},{2,14},{6,10},... | collective-permute-start | bytes 116744 | tf_op jit(solution)/shard_map/ppermute | solution.py:242
  9.5 4.2 %collective-permute-start.1 = (f16[8,2432]{1,0:T(8,128)(2,1)S(1)}, f16[8,2432]{1,0:T(8,128)(2,1)S(1)}, u32[]{:S(2)}, u32[]{:S(2)}) collective-permute-start(f16[8,2432]{1,0:T(8,128)(2,1)S(1)} %convert_element_type.24), channel_id=1, source_target_pairs={{0,8},{4,12},{8,0},{12,4},{1,9},{5,13},{9,1},{13,5},{2,10},{6,14},... | collective-permute-start | bytes 116744 | tf_op jit(solution)/shard_map/ppermute | solution.py:242
  10.1 3.5 %collective-permute-start = (f16[8,2432]{1,0:T(8,128)(2,1)S(1)}, f16[8,2432]{1,0:T(8,128)(2,1)S(1)}, u32[]{:S(2)}, u32[]{:S(2)}) collective-permute-start(f16[8,2432]{1,0:T(8,128)(2,1)S(1)} %convert_element_type.22), channel_id=1, source_target_pairs={{0,4},{4,0},{8,12},{12,8},{1,5},{5,1},{9,13},{13,9},{2,6},{6,2},{1... | collective-permute-start | bytes 116744 | tf_op jit(solution)/shard_map/ppermute | solution.py:242
  10.6 9.7 %slice-start = ((s8[16777216]{0:T(1024)(128)(4,1)}), s8[4194304]{0:T(1024)(128)(4,1)S(1)}, s32[]{:S(2)}) async-start(s8[16777216]{0:T(1024)(128)(4,1)} %bitcast.1), calls=%async_computation | async-start | bytes 8388608
  10.6 9.7 %slice-start.1 = ((s8[16777216]{0:T(1024)(128)(4,1)}), s8[4194304]{0:T(1024)(128)(4,1)S(1)}, s32[]{:S(2)}) async-start(s8[16777216]{0:T(1024)(128)(4,1)} %bitcast.1), calls=%async_computation.1 | async-start | bytes 8388608
  13.7 6.6 %slice-start.2 = ((s8[16777216]{0:T(1024)(128)(4,1)}), s8[4194304]{0:T(1024)(128)(4,1)S(1)}, s32[]{:S(2)}) async-start(s8[16777216]{0:T(1024)(128)(4,1)} %bitcast.1), calls=%async_computation.2 | async-start | bytes 8388608
  13.7 6.6 %slice-start.3 = ((s8[16777216]{0:T(1024)(128)(4,1)}), s8[4194304]{0:T(1024)(128)(4,1)S(1)}, s32[]{:S(2)}) async-start(s8[16777216]{0:T(1024)(128)(4,1)} %bitcast.1), calls=%async_computation.3 | async-start | bytes 8388608
  15.5 3.8 %collective-permute-start.5 = (bf16[8,2048]{1,0:T(8,128)(2,1)S(1)}, bf16[8,2048]{1,0:T(8,128)(2,1)S(1)}, u32[]{:S(2)}, u32[]{:S(2)}) collective-permute-start(bf16[8,2048]{1,0:T(8,128)(2,1)S(1)} %attention.1.refs_0_), channel_id=1, source_target_pairs={{0,12},{4,8},{8,4},{12,0},{1,13},{5,9},{9,5},{13,1},{2,14},{6,10},... | collective-permute-start | bytes 98312 | tf_op jit(solution)/shard_map/ppermute | solution.py:242
  16.3 3.9 %collective-permute-start.4 = (bf16[8,2048]{1,0:T(8,128)(2,1)S(1)}, bf16[8,2048]{1,0:T(8,128)(2,1)S(1)}, u32[]{:S(2)}, u32[]{:S(2)}) collective-permute-start(bf16[8,2048]{1,0:T(8,128)(2,1)S(1)} %attention.1.refs_0_), channel_id=1, source_target_pairs={{0,8},{4,12},{8,0},{12,4},{1,9},{5,13},{9,1},{13,5},{2,10},{6,14},... | collective-permute-start | bytes 98312 | tf_op jit(solution)/shard_map/ppermute | solution.py:242
  17.0 3.2 %collective-permute-start.3 = (bf16[8,2048]{1,0:T(8,128)(2,1)S(1)}, bf16[8,2048]{1,0:T(8,128)(2,1)S(1)}, u32[]{:S(2)}, u32[]{:S(2)}) collective-permute-start(bf16[8,2048]{1,0:T(8,128)(2,1)S(1)} %attention.1.refs_0_), channel_id=1, source_target_pairs={{0,4},{4,0},{8,12},{12,8},{1,5},{5,1},{9,13},{13,9},{2,6},{6,2},{1... | collective-permute-start | bytes 98312 | tf_op jit(solution)/shard_map/ppermute | solution.py:242
  21.1 4.7 %collective-permute-start.9 = (bf16[32,1024]{1,0:T(8,128)(2,1)S(1)}, bf16[32,1024]{1,0:T(8,128)(2,1)S(1)}, u32[]{:S(2)}, u32[]{:S(2)}) collective-permute-start(bf16[32,1024]{1,0:T(8,128)(2,1)S(1)} %get-tuple-element.16), channel_id=1, source_target_pairs={{0,1},{1,0},{2,3},{3,2},{4,5},{5,4},{6,7},{7,6},{8,9},{9,8},{10,11... | collective-permute-start | bytes 196616 | tf_op jit(solution)/shard_map/ppermute | solution.py:242
  23.6 4.9 %collective-permute-start.6 = (bf16[32,1024]{1,0:T(8,128)(2,1)S(1)}, bf16[32,1024]{1,0:T(8,128)(2,1)S(1)}, u32[]{:S(2)}, u32[]{:S(2)}) collective-permute-start(bf16[32,1024]{1,0:T(8,128)(2,1)S(1)} %project_out.4), channel_id=1, source_target_pairs={{0,1},{1,0},{2,3},{3,2},{4,5},{5,4},{6,7},{7,6},{8,9},{9,8},{10,11... | collective-permute-start | bytes 196616 | tf_op jit(solution)/shard_map/ppermute | solution.py:242
  24.9 8.2 %copy-start.2 = (bf16[32,4096]{1,0:T(8,128)(2,1)S(1)}, bf16[32,4096]{1,0:T(8,128)(2,1)}, u32[]{:S(2)}) copy-start(bf16[32,4096]{1,0:T(8,128)(2,1)} %x.3) | copy-start | bytes 786436
  25.8 7.3 %collective-permute-start.10 = (bf16[32,1024]{1,0:T(8,128)(2,1)S(1)}, bf16[32,1024]{1,0:T(8,128)(2,1)S(1)}, u32[]{:S(2)}, u32[]{:S(2)}) collective-permute-start(bf16[32,1024]{1,0:T(8,128)(2,1)S(1)} %add_near.3.refs_0_), channel_id=1, source_target_pairs={{0,2},{1,3},{2,0},{3,1},{4,6},{5,7},{6,4},{7,5},{8,10},{9,11},{10,... | collective-permute-start | bytes 196616 | tf_op jit(solution)/shard_map/ppermute | solution.py:242
  28.5 5.4 %collective-permute-start.7 = (bf16[32,1024]{1,0:T(8,128)(2,1)S(1)}, bf16[32,1024]{1,0:T(8,128)(2,1)S(1)}, u32[]{:S(2)}, u32[]{:S(2)}) collective-permute-start(bf16[32,1024]{1,0:T(8,128)(2,1)S(1)} %add_near.2.refs_0_), channel_id=1, source_target_pairs={{0,2},{1,3},{2,0},{3,1},{4,6},{5,7},{6,4},{7,5},{8,10},{9,11},{10,... | collective-permute-start | bytes 196616 | tf_op jit(solution)/shard_map/ppermute | solution.py:242
  33.1 4.3 %collective-permute-start.11 = (bf16[32,1024]{1,0:T(8,128)(2,1)S(1)}, bf16[32,1024]{1,0:T(8,128)(2,1)S(1)}, u32[]{:S(2)}, u32[]{:S(2)}) collective-permute-start(bf16[32,1024]{1,0:T(8,128)(2,1)S(1)} %finish.3.refs_0_), channel_id=1, source_target_pairs={{0,1},{1,0},{2,3},{3,2},{4,5},{5,4},{6,7},{7,6},{8,9},{9,8},{10,11... | collective-permute-start | bytes 196616 | tf_op jit(solution)/shard_map/ppermute | solution.py:242
  33.9 4.3 %collective-permute-start.8 = (bf16[32,1024]{1,0:T(8,128)(2,1)S(1)}, bf16[32,1024]{1,0:T(8,128)(2,1)S(1)}, u32[]{:S(2)}, u32[]{:S(2)}) collective-permute-start(bf16[32,1024]{1,0:T(8,128)(2,1)S(1)} %finish.2.refs_2_), channel_id=1, source_target_pairs={{0,1},{1,0},{2,3},{3,2},{4,5},{5,4},{6,7},{7,6},{8,9},{9,8},{10,11... | collective-permute-start | bytes 196616 | tf_op jit(solution)/shard_map/ppermute | solution.py:242

commit v22 on v18

--- a/solution.py
+++ b/solution.py
@@ -103,8 +103,8 @@
             out[...] = part
 
 
-def turn_keys(after, k, v, k_turned):
-    del after, v
+def turn_keys(after, k, k_turned):
+    del after
     rows, slots = k.shape[0], k.shape[1]
     for row in range(rows):
         for start in range(0, slots, CHUNK):
@@ -289,12 +289,12 @@
         keys = pl.pallas_call(
             turn_keys,
             out_shape=pltpu.VMEM((rows, HD, key_cache.shape[1]), BF16),
-            in_specs=[ANY, VMEM, ANY],
+            in_specs=[ANY, VMEM],
             out_specs=VMEM,
             compiler_params=params(4),
             cost_estimate=cost(0, 2 * key_cache.size),
             name="turn_keys",
-        )(sums[0], in_vmem(key_cache), values)
+        )(sums[0], in_vmem(key_cache))
 
         half = HD // 2
         inverse = ROPE_BASE ** (-(jnp.arange(half, dtype=F32) * 2.0 / HD))

time: 39.1 us -> 39 us (level)
  no operation moved by 1% of the time
where the time goes in v22:
time: 39 us; the launch traced here: 38.9 us
  Pallas kernels  14.6 us (37%)
  starting transfers between devices  14.6 us (37%)
  waiting for transfers between devices  9.05 us (23%)
    ppermute x12, starting transfers between devices, swap(): return lax.ppermute(value, axis, [(i, i ^ mask) for i in range(size)])  14.6 us
    ppermute x12, waiting for transfers between devices, swap(): return lax.ppermute(value, axis, [(i, i ^ mask) for i in range(size)])  9.05 us
    pallas_call x1, Pallas kernels, shards(): pl.pallas_call(project, out_shape=pltpu.VMEM((batch, packed), F32), in_sp...  6.92 us
    pallas_call x3, Pallas kernels, product(): pl.pallas_call(functools.partial(project_out, chunk, given), out_shape=pl...  2.47 us
    pallas_call x1, Pallas kernels, shards(): pl.pallas_call(functools.partial(attention, size_x, depth * size_x), out_...  1.78 us
    pallas_call x1, Pallas kernels, shards(): pl.pallas_call(turn_keys, out_shape=pltpu.VMEM((rows, HD, key_cache.shape...  1.13 us
    pallas_call x1, Pallas kernels, shards(): pl.pallas_call(project_first, out_shape=[pltpu.VMEM((batch, block), BF16)...  0.83 us
  transfers between devices with their start and end apart: 12, of which 8 were waited for; matrix products, arithmetic and copies ran while one was open for 1% of the time, Pallas kernels for 11%

profile of v22, /device:TPU:0, one launch (start us, length us, event | category | flops | bytes accessed | tf_op | source)
XLA Modules:
  0.0 38.9 jit_solution(13771326842112943142)
XLA Ops:
  0.0 6.9 %project.1.total = f32[32,2432]{1,0:T(8,128)S(1)} custom-call(bf16[32,4096]{1,0:T(8,128)(2,1)} %x.3, f32[1,4096]{1,0:T(1,128)} %bitcast.3, bf16[4096,2048]{1,0:T(8,128)(2,1)} %weights.3, bf16[4096,128]{1,0:T(8,128)(2,1)} %wk_hbm.1, bf16[4096,128]{1,0:T(8,128)(2,1)} %wv_hbm.1), custom_call_target="tpu_custom_call" | custom-call | flops 637534208 | bytes 19922944 | tf_op jit(solution)/shard_map/project/pallas_call | solution.py:258
  6.9 0.0 copy-start.3
  6.9 0.0 copy-start
  7.0 2.4 %collective-permute-start.2 = (f16[8,2432]{1,0:T(8,128)(2,1)S(1)}, f16[8,2432]{1,0:T(8,128)(2,1)S(1)}, u32[]{:S(2)}, u32[]{:S(2)}) collective-permute-start(f16[8,2432]{1,0:T(8,128)(2,1)S(1)} %convert_element_type.26), channel_id=1, source_target_pairs={{0,12},{4,8},{8,4},{12,0},{1,13},{5,9},{9,5},{13,1},{2,14},{6,10},... | collective-permute-start | bytes 116744 | tf_op jit(solution)/shard_map/ppermute | solution.py:243
  9.5 0.6 %collective-permute-start.1 = (f16[8,2432]{1,0:T(8,128)(2,1)S(1)}, f16[8,2432]{1,0:T(8,128)(2,1)S(1)}, u32[]{:S(2)}, u32[]{:S(2)}) collective-permute-start(f16[8,2432]{1,0:T(8,128)(2,1)S(1)} %convert_element_type.24), channel_id=1, source_target_pairs={{0,8},{4,12},{8,0},{12,4},{1,9},{5,13},{9,1},{13,5},{2,10},{6,14},... | collective-permute-start | bytes 116744 | tf_op jit(solution)/shard_map/ppermute | solution.py:243
  10.1 0.2 collective-permute-start
  10.3 0.0 copy-done.3
  10.3 0.1 fusion
  10.4 0.1 pad_maximum_fusion
  10.5 0.0 copy-done
  10.5 0.0 slice-start
  10.5 1.1 %turn_keys.1.k = bf16[8,128,2048]{2,1,0:T(8,128)(2,1)S(1)} custom-call(f32[8,2432]{1,0:T(8,128)S(1)} %get-tuple-element.11.after.refs_0_, bf16[8,2048,128]{2,1,0:T(8,128)(2,1)S(1)} %copy-done), custom_call_target="tpu_custom_call" | custom-call | bytes 4194304 | tf_op jit(solution)/shard_map/turn_keys/pallas_call | solution.py:289
  11.7 0.0 collective-permute-done.2
  11.7 0.0 slice-start.1
  11.7 1.9 %collective-permute-done.1 = f16[8,2432]{1,0:T(8,128)(2,1)S(1)} collective-permute-done((f16[8,2432]{1,0:T(8,128)(2,1)S(1)}, f16[8,2432]{1,0:T(8,128)(2,1)S(1)}, u32[]{:S(2)}, u32[]{:S(2)}) %collective-permute-start.1) | collective-permute-done | bytes 38944 | tf_op jit(solution)/shard_map/ppermute | solution.py:243
  13.6 0.0 collective-permute-done
  13.7 0.1 broadcast_in_dim.2.lengths
  13.7 0.0 copy-done.1
  13.7 1.8 %attention.1.refs_0_ = bf16[8,2048]{1,0:T(8,128)(2,1)S(1)} custom-call(bf16[4096,2048]{1,0:T(8,128)(2,1)} %weights.3, s32[8,128]{1,0:T(8,128)S(1)} %broadcast_in_dim.2.lengths, f32[8,128]{1,0:T(8,128)S(1)} %get-tuple-element.20.cosine, f32[8,128]{1,0:T(8,128)S(1)} %get-tuple-element.21.sine, bf16[8,128,2048]{2,1,0:T(8,128)(2,1)S(1)} %turn_keys.1.k, ...), custom_call_target="tpu_custom_call" | custom-call | flops 134217728 | bytes 8388608 | tf_op jit(solution)/shard_map/attention/pallas_call | solution.py:304
  15.5 0.8 %collective-permute-start.5 = (bf16[8,2048]{1,0:T(8,128)(2,1)S(1)}, bf16[8,2048]{1,0:T(8,128)(2,1)S(1)}, u32[]{:S(2)}, u32[]{:S(2)}) collective-permute-start(bf16[8,2048]{1,0:T(8,128)(2,1)S(1)} %attention.1.refs_0_), channel_id=1, source_target_pairs={{0,12},{4,8},{8,4},{12,0},{1,13},{5,9},{9,5},{13,1},{2,14},{6,10},... | collective-permute-start | bytes 98312 | tf_op jit(solution)/shard_map/ppermute | solution.py:243
  16.3 0.7 %collective-permute-start.4 = (bf16[8,2048]{1,0:T(8,128)(2,1)S(1)}, bf16[8,2048]{1,0:T(8,128)(2,1)S(1)}, u32[]{:S(2)}, u32[]{:S(2)}) collective-permute-start(bf16[8,2048]{1,0:T(8,128)(2,1)S(1)} %attention.1.refs_0_), channel_id=1, source_target_pairs={{0,8},{4,12},{8,0},{12,4},{1,9},{5,13},{9,1},{13,5},{2,10},{6,14},... | collective-permute-start | bytes 98312 | tf_op jit(solution)/shard_map/ppermute | solution.py:243
  17.1 0.4 %collective-permute-start.3 = (bf16[8,2048]{1,0:T(8,128)(2,1)S(1)}, bf16[8,2048]{1,0:T(8,128)(2,1)S(1)}, u32[]{:S(2)}, u32[]{:S(2)}) collective-permute-start(bf16[8,2048]{1,0:T(8,128)(2,1)S(1)} %attention.1.refs_0_), channel_id=1, source_target_pairs={{0,4},{4,0},{8,12},{12,8},{1,5},{5,1},{9,13},{13,9},{2,6},{6,2},{1... | collective-permute-start | bytes 98312 | tf_op jit(solution)/shard_map/ppermute | solution.py:243
  17.5 1.8 %collective-permute-done.5.refs_3_ = bf16[8,2048]{1,0:T(8,128)(2,1)S(1)} collective-permute-done((bf16[8,2048]{1,0:T(8,128)(2,1)S(1)}, bf16[8,2048]{1,0:T(8,128)(2,1)S(1)}, u32[]{:S(2)}, u32[]{:S(2)}) %collective-permute-start.5) | collective-permute-done | bytes 32800 | tf_op jit(solution)/shard_map/ppermute | solution.py:243
  19.3 1.0 %collective-permute-done.4.refs_2_ = bf16[8,2048]{1,0:T(8,128)(2,1)S(1)} collective-permute-done((bf16[8,2048]{1,0:T(8,128)(2,1)S(1)}, bf16[8,2048]{1,0:T(8,128)(2,1)S(1)}, u32[]{:S(2)}, u32[]{:S(2)}) %collective-permute-start.4) | collective-permute-done | bytes 32800 | tf_op jit(solution)/shard_map/ppermute | solution.py:243
  20.3 0.0 collective-permute-done.3.refs_1_
  20.3 0.0 slice-done
  20.3 0.0 slice-done.1
  20.3 0.0 slice-done.2
  20.3 0.8 %project_first.1 = (bf16[32,1024]{1,0:T(8,128)(2,1)S(1)}, bf16[32,2048]{1,0:T(8,128)(2,1)S(1)}) custom-call(bf16[2048,4096]{1,0:T(8,128)(2,1)S(1)} %bitcast.2, bf16[8,2048]{1,0:T(8,128)(2,1)S(1)} %attention.1.refs_0_, bf16[8,2048]{1,0:T(8,128)(2,1)S(1)} %collective-permute-done.3.refs_1_, bf16[8,2048]{1,0:T(8,128)(2,1)S(1)} %collective-permute-done.4.refs_2_, ...), custom_call_target="tpu_custom_call" | custom-call | flops 134217728 | bytes 4194304 | tf_op jit(solution)/shard_map/project_first/pallas_call | solution.py:332
  21.1 1.6 %collective-permute-start.9 = (bf16[32,1024]{1,0:T(8,128)(2,1)S(1)}, bf16[32,1024]{1,0:T(8,128)(2,1)S(1)}, u32[]{:S(2)}, u32[]{:S(2)}) collective-permute-start(bf16[32,1024]{1,0:T(8,128)(2,1)S(1)} %get-tuple-element.16), channel_id=1, source_target_pairs={{0,1},{1,0},{2,3},{3,2},{4,5},{5,4},{6,7},{7,6},{8,9},{9,8},{10,11... | collective-permute-start | bytes 196616 | tf_op jit(solution)/shard_map/ppermute | solution.py:243
  22.8 0.8 %project_out.4 = bf16[32,1024]{1,0:T(8,128)(2,1)S(1)} custom-call(bf16[2048,4096]{1,0:T(8,128)(2,1)S(1)} %bitcast.2, bf16[32,2048]{1,0:T(8,128)(2,1)S(1)} %get-tuple-element.15.heads), custom_call_target="tpu_custom_call" | custom-call | flops 134217728 | bytes 4194304 | tf_op jit(solution)/shard_map/project_out/pallas_call | solution.py:344
  23.6 0.5 %collective-permute-start.6 = (bf16[32,1024]{1,0:T(8,128)(2,1)S(1)}, bf16[32,1024]{1,0:T(8,128)(2,1)S(1)}, u32[]{:S(2)}, u32[]{:S(2)}) collective-permute-start(bf16[32,1024]{1,0:T(8,128)(2,1)S(1)} %project_out.4), channel_id=1, source_target_pairs={{0,1},{1,0},{2,3},{3,2},{4,5},{5,4},{6,7},{7,6},{8,9},{9,8},{10,11... | collective-permute-start | bytes 196616 | tf_op jit(solution)/shard_map/ppermute | solution.py:243
  24.0 0.8 %project_out.5.own = f32[32,1024]{1,0:T(8,128)S(1)} custom-call(bf16[2048,4096]{1,0:T(8,128)(2,1)S(1)} %bitcast.2, bf16[32,2048]{1,0:T(8,128)(2,1)S(1)} %get-tuple-element.15.heads), custom_call_target="tpu_custom_call" | custom-call | flops 134217728 | bytes 4194304 | tf_op jit(solution)/shard_map/project_out/pallas_call | solution.py:344
  24.9 0.8 %project_out.3.own = f32[32,1024]{1,0:T(8,128)S(1)} custom-call(bf16[2048,4096]{1,0:T(8,128)(2,1)S(1)} %bitcast.2, bf16[32,2048]{1,0:T(8,128)(2,1)S(1)} %get-tuple-element.15.heads), custom_call_target="tpu_custom_call" | custom-call | flops 134217728 | bytes 4194304 | tf_op jit(solution)/shard_map/project_out/pallas_call | solution.py:344
  25.7 0.1 collective-permute-done.9.arrived
  25.8 2.7 %collective-permute-start.10 = (bf16[32,1024]{1,0:T(8,128)(2,1)S(1)}, bf16[32,1024]{1,0:T(8,128)(2,1)S(1)}, u32[]{:S(2)}, u32[]{:S(2)}) collective-permute-start(bf16[32,1024]{1,0:T(8,128)(2,1)S(1)} %add_near.3.refs_0_), channel_id=1, source_target_pairs={{0,2},{1,3},{2,0},{3,1},{4,6},{5,7},{6,4},{7,5},{8,10},{9,11},{10,... | collective-permute-start | bytes 196616 | tf_op jit(solution)/shard_map/ppermute | solution.py:243
  28.5 0.0 collective-permute-done.6.arrived
  28.5 2.6 %collective-permute-start.7 = (bf16[32,1024]{1,0:T(8,128)(2,1)S(1)}, bf16[32,1024]{1,0:T(8,128)(2,1)S(1)}, u32[]{:S(2)}, u32[]{:S(2)}) collective-permute-start(bf16[32,1024]{1,0:T(8,128)(2,1)S(1)} %add_near.2.refs_0_), channel_id=1, source_target_pairs={{0,2},{1,3},{2,0},{3,1},{4,6},{5,7},{6,4},{7,5},{8,10},{9,11},{10,... | collective-permute-start | bytes 196616 | tf_op jit(solution)/shard_map/ppermute | solution.py:243
  31.1 2.0 %collective-permute-done.10.refs_1_ = bf16[32,1024]{1,0:T(8,128)(2,1)S(1)} collective-permute-done((bf16[32,1024]{1,0:T(8,128)(2,1)S(1)}, bf16[32,1024]{1,0:T(8,128)(2,1)S(1)}, u32[]{:S(2)}, u32[]{:S(2)}) %collective-permute-start.10) | collective-permute-done | bytes 65568 | tf_op jit(solution)/shard_map/ppermute | solution.py:243
  33.1 0.0 copy-done.2
  33.1 0.1 finish.3.refs_0_
  33.1 0.2 collective-permute-start.11
  33.3 0.5 %collective-permute-done.7.refs_1_ = bf16[32,1024]{1,0:T(8,128)(2,1)S(1)} collective-permute-done((bf16[32,1024]{1,0:T(8,128)(2,1)S(1)}, bf16[32,1024]{1,0:T(8,128)(2,1)S(1)}, u32[]{:S(2)}, u32[]{:S(2)}) %collective-permute-start.7) | collective-permute-done | bytes 65568 | tf_op jit(solution)/shard_map/ppermute | solution.py:243
  33.9 1.9 %collective-permute-start.8 = (bf16[32,1024]{1,0:T(8,128)(2,1)S(1)}, bf16[32,1024]{1,0:T(8,128)(2,1)S(1)}, u32[]{:S(2)}, u32[]{:S(2)}) collective-permute-start(bf16[32,1024]{1,0:T(8,128)(2,1)S(1)} %finish.2.refs_2_), channel_id=1, source_target_pairs={{0,1},{1,0},{2,3},{3,2},{4,5},{5,4},{6,7},{7,6},{8,9},{9,8},{10,11... | collective-permute-start | bytes 196616 | tf_op jit(solution)/shard_map/ppermute | solution.py:243
  35.8 1.7 %collective-permute-done.11.refs_1_ = bf16[32,1024]{1,0:T(8,128)(2,1)S(1)} collective-permute-done((bf16[32,1024]{1,0:T(8,128)(2,1)S(1)}, bf16[32,1024]{1,0:T(8,128)(2,1)S(1)}, u32[]{:S(2)}, u32[]{:S(2)}) %collective-permute-start.11) | collective-permute-done | bytes 65568 | tf_op jit(solution)/shard_map/ppermute | solution.py:243
  37.4 0.7 %write_most.1.refs_1_ = bf16[32,4096]{1,0:T(8,128)(2,1)} custom-call(bf16[32,1024]{1,0:T(8,128)(2,1)S(1)} %finish.3.refs_0_, bf16[32,1024]{1,0:T(8,128)(2,1)S(1)} %collective-permute-done.11.refs_1_, bf16[32,1024]{1,0:T(8,128)(2,1)S(1)} %finish.2.refs_2_), custom_call_target="tpu_custom_call" | custom-call | tf_op jit(solution)/shard_map/write_most/pallas_call | solution.py:377
  38.2 0.1 collective-permute-done.8.refs_0_
  38.2 0.6 %write_last.1 = bf16[32,4096]{1,0:T(8,128)(2,1)} custom-call(bf16[32,1024]{1,0:T(8,128)(2,1)S(1)} %collective-permute-done.8.refs_0_, bf16[32,4096]{1,0:T(8,128)(2,1)} %write_most.1.refs_1_), custom_call_target="tpu_custom_call", output_to_operand_aliasing={{}: (1, {})} | custom-call | tf_op jit(solution)/shard_map/write_last/pallas_call | solution.py:386
  (18 shorter events, 0.2 us)
Async XLA Ops:
  6.9 3.4 %copy-start.3 = (s32[8]{0:T(128)S(1)}, s32[8]{0:T(128)}, u32[]{:S(2)}) copy-start(s32[8]{0:T(128)} %param.17) | copy-start | bytes 100
  6.9 3.6 %copy-start = (bf16[8,2048,128]{2,1,0:T(8,128)(2,1)S(1)}, bf16[8,2048,128]{2,1,0:T(8,128)(2,1)}, u32[]{:S(2)}) copy-start(bf16[8,2048,128]{2,1,0:T(8,128)(2,1)} %k.1) | copy-start | bytes 12582916
  7.0 4.6 %collective-permute-start.2 = (f16[8,2432]{1,0:T(8,128)(2,1)S(1)}, f16[8,2432]{1,0:T(8,128)(2,1)S(1)}, u32[]{:S(2)}, u32[]{:S(2)}) collective-permute-start(f16[8,2432]{1,0:T(8,128)(2,1)S(1)} %convert_element_type.26), channel_id=1, source_target_pairs={{0,12},{4,8},{8,4},{12,0},{1,13},{5,9},{9,5},{13,1},{2,14},{6,10},... | collective-permute-start | bytes 116744 | tf_op jit(solution)/shard_map/ppermute | solution.py:243
  9.5 4.2 %collective-permute-start.1 = (f16[8,2432]{1,0:T(8,128)(2,1)S(1)}, f16[8,2432]{1,0:T(8,128)(2,1)S(1)}, u32[]{:S(2)}, u32[]{:S(2)}) collective-permute-start(f16[8,2432]{1,0:T(8,128)(2,1)S(1)} %convert_element_type.24), channel_id=1, source_target_pairs={{0,8},{4,12},{8,0},{12,4},{1,9},{5,13},{9,1},{13,5},{2,10},{6,14},... | collective-permute-start | bytes 116744 | tf_op jit(solution)/shard_map/ppermute | solution.py:243
  10.1 3.5 %collective-permute-start = (f16[8,2432]{1,0:T(8,128)(2,1)S(1)}, f16[8,2432]{1,0:T(8,128)(2,1)S(1)}, u32[]{:S(2)}, u32[]{:S(2)}) collective-permute-start(f16[8,2432]{1,0:T(8,128)(2,1)S(1)} %convert_element_type.22), channel_id=1, source_target_pairs={{0,4},{4,0},{8,12},{12,8},{1,5},{5,1},{9,13},{13,9},{2,6},{6,2},{1... | collective-permute-start | bytes 116744 | tf_op jit(solution)/shard_map/ppermute | solution.py:243
  10.5 3.2 %copy-start.1 = (bf16[8,2048,128]{2,1,0:T(8,128)(2,1)S(1)}, bf16[8,2048,128]{2,1,0:T(8,128)(2,1)}, u32[]{:S(2)}) copy-start(bf16[8,2048,128]{2,1,0:T(8,128)(2,1)} %v.1) | copy-start | bytes 12582916
  10.5 9.8 %slice-start = ((s8[16777216]{0:T(1024)(128)(4,1)}), s8[4194304]{0:T(1024)(128)(4,1)S(1)}, s32[]{:S(2)}) async-start(s8[16777216]{0:T(1024)(128)(4,1)} %bitcast.1), calls=%async_computation | async-start | bytes 8388608
  11.7 8.6 %slice-start.1 = ((s8[16777216]{0:T(1024)(128)(4,1)}), s8[4194304]{0:T(1024)(128)(4,1)S(1)}, s32[]{:S(2)}) async-start(s8[16777216]{0:T(1024)(128)(4,1)} %bitcast.1), calls=%async_computation.1 | async-start | bytes 8388608
  13.7 6.5 %slice-start.2 = ((s8[16777216]{0:T(1024)(128)(4,1)}), s8[4194304]{0:T(1024)(128)(4,1)S(1)}, s32[]{:S(2)}) async-start(s8[16777216]{0:T(1024)(128)(4,1)} %bitcast.1), calls=%async_computation.2 | async-start | bytes 8388608
  13.7 6.5 %slice-start.3 = ((s8[16777216]{0:T(1024)(128)(4,1)}), s8[4194304]{0:T(1024)(128)(4,1)S(1)}, s32[]{:S(2)}) async-start(s8[16777216]{0:T(1024)(128)(4,1)} %bitcast.1), calls=%async_computation.3 | async-start | bytes 8388608
  15.5 3.8 %collective-permute-start.5 = (bf16[8,2048]{1,0:T(8,128)(2,1)S(1)}, bf16[8,2048]{1,0:T(8,128)(2,1)S(1)}, u32[]{:S(2)}, u32[]{:S(2)}) collective-permute-start(bf16[8,2048]{1,0:T(8,128)(2,1)S(1)} %attention.1.refs_0_), channel_id=1, source_target_pairs={{0,12},{4,8},{8,4},{12,0},{1,13},{5,9},{9,5},{13,1},{2,14},{6,10},... | collective-permute-start | bytes 98312 | tf_op jit(solution)/shard_map/ppermute | solution.py:243
  16.3 3.9 %collective-permute-start.4 = (bf16[8,2048]{1,0:T(8,128)(2,1)S(1)}, bf16[8,2048]{1,0:T(8,128)(2,1)S(1)}, u32[]{:S(2)}, u32[]{:S(2)}) collective-permute-start(bf16[8,2048]{1,0:T(8,128)(2,1)S(1)} %attention.1.refs_0_), channel_id=1, source_target_pairs={{0,8},{4,12},{8,0},{12,4},{1,9},{5,13},{9,1},{13,5},{2,10},{6,14},... | collective-permute-start | bytes 98312 | tf_op jit(solution)/shard_map/ppermute | solution.py:243
  17.1 3.2 %collective-permute-start.3 = (bf16[8,2048]{1,0:T(8,128)(2,1)S(1)}, bf16[8,2048]{1,0:T(8,128)(2,1)S(1)}, u32[]{:S(2)}, u32[]{:S(2)}) collective-permute-start(bf16[8,2048]{1,0:T(8,128)(2,1)S(1)} %attention.1.refs_0_), channel_id=1, source_target_pairs={{0,4},{4,0},{8,12},{12,8},{1,5},{5,1},{9,13},{13,9},{2,6},{6,2},{1... | collective-permute-start | bytes 98312 | tf_op jit(solution)/shard_map/ppermute | solution.py:243
  21.1 4.7 %collective-permute-start.9 = (bf16[32,1024]{1,0:T(8,128)(2,1)S(1)}, bf16[32,1024]{1,0:T(8,128)(2,1)S(1)}, u32[]{:S(2)}, u32[]{:S(2)}) collective-permute-start(bf16[32,1024]{1,0:T(8,128)(2,1)S(1)} %get-tuple-element.16), channel_id=1, source_target_pairs={{0,1},{1,0},{2,3},{3,2},{4,5},{5,4},{6,7},{7,6},{8,9},{9,8},{10,11... | collective-permute-start | bytes 196616 | tf_op jit(solution)/shard_map/ppermute | solution.py:243
  23.6 4.9 %collective-permute-start.6 = (bf16[32,1024]{1,0:T(8,128)(2,1)S(1)}, bf16[32,1024]{1,0:T(8,128)(2,1)S(1)}, u32[]{:S(2)}, u32[]{:S(2)}) collective-permute-start(bf16[32,1024]{1,0:T(8,128)(2,1)S(1)} %project_out.4), channel_id=1, source_target_pairs={{0,1},{1,0},{2,3},{3,2},{4,5},{5,4},{6,7},{7,6},{8,9},{9,8},{10,11... | collective-permute-start | bytes 196616 | tf_op jit(solution)/shard_map/ppermute | solution.py:243
  24.9 8.2 %copy-start.2 = (bf16[32,4096]{1,0:T(8,128)(2,1)S(1)}, bf16[32,4096]{1,0:T(8,128)(2,1)}, u32[]{:S(2)}) copy-start(bf16[32,4096]{1,0:T(8,128)(2,1)} %x.3) | copy-start | bytes 786436
  25.8 7.3 %collective-permute-start.10 = (bf16[32,1024]{1,0:T(8,128)(2,1)S(1)}, bf16[32,1024]{1,0:T(8,128)(2,1)S(1)}, u32[]{:S(2)}, u32[]{:S(2)}) collective-permute-start(bf16[32,1024]{1,0:T(8,128)(2,1)S(1)} %add_near.3.refs_0_), channel_id=1, source_target_pairs={{0,2},{1,3},{2,0},{3,1},{4,6},{5,7},{6,4},{7,5},{8,10},{9,11},{10,... | collective-permute-start | bytes 196616 | tf_op jit(solution)/shard_map/ppermute | solution.py:243
  28.5 5.4 %collective-permute-start.7 = (bf16[32,1024]{1,0:T(8,128)(2,1)S(1)}, bf16[32,1024]{1,0:T(8,128)(2,1)S(1)}, u32[]{:S(2)}, u32[]{:S(2)}) collective-permute-start(bf16[32,1024]{1,0:T(8,128)(2,1)S(1)} %add_near.2.refs_0_), channel_id=1, source_target_pairs={{0,2},{1,3},{2,0},{3,1},{4,6},{5,7},{6,4},{7,5},{8,10},{9,11},{10,... | collective-permute-start | bytes 196616 | tf_op jit(solution)/shard_map/ppermute | solution.py:243
  33.1 4.3 %collective-permute-start.11 = (bf16[32,1024]{1,0:T(8,128)(2,1)S(1)}, bf16[32,1024]{1,0:T(8,128)(2,1)S(1)}, u32[]{:S(2)}, u32[]{:S(2)}) collective-permute-start(bf16[32,1024]{1,0:T(8,128)(2,1)S(1)} %finish.3.refs_0_), channel_id=1, source_target_pairs={{0,1},{1,0},{2,3},{3,2},{4,5},{5,4},{6,7},{7,6},{8,9},{9,8},{10,11... | collective-permute-start | bytes 196616 | tf_op jit(solution)/shard_map/ppermute | solution.py:243
  33.9 4.3 %collective-permute-start.8 = (bf16[32,1024]{1,0:T(8,128)(2,1)S(1)}, bf16[32,1024]{1,0:T(8,128)(2,1)S(1)}, u32[]{:S(2)}, u32[]{:S(2)}) collective-permute-start(bf16[32,1024]{1,0:T(8,128)(2,1)S(1)} %finish.2.refs_2_), channel_id=1, source_target_pairs={{0,1},{1,0},{2,3},{3,2},{4,5},{5,4},{6,7},{7,6},{8,9},{9,8},{10,11... | collective-permute-start | bytes 196616 | tf_op jit(solution)/shard_map/ppermute | solution.py:243
